TPU v7x, 32 devices: a whole 2x2x4 slice. The times are simulated.
32 devices in a mesh: fsdp: 4 (over y, x), ctx: 4 (over z), tp: 2 (over core).
Axes of the slice: x: 2, y: 2, z: 4, core: 2. Of those that a mesh axis runs over, the one named last changes fastest.
Arguments:
- tokens: bfloat16 [8, 1024, 2048], P('fsdp', 'ctx'), may hold values from -6 to 6
- lengths: int32 [8], P('fsdp'), may hold values from 256 to 1024, as said below
- cotangent: bfloat16 [8, 1024, 2048], P('fsdp', 'ctx'), may hold values from -6 to 6
- pre_gain: bfloat16 [2048], P(('fsdp', 'ctx')), may hold values from 0.5 to 1.5
- pre_bias: bfloat16 [2048], P(('fsdp', 'ctx')), may hold values from -1 to 1
- query_weight: bfloat16 [2048, 2048], P(('fsdp', 'ctx'), 'tp'), may hold values from -0.125 to 0.125
- key_weight: bfloat16 [2048, 2048], P(('fsdp', 'ctx'), 'tp'), may hold values from -0.125 to 0.125
- value_weight: bfloat16 [2048, 4096], P(('fsdp', 'ctx'), 'tp'), may hold values from -0.125 to 0.125
- swish_weight: bfloat16 [2048, 4096], P(('fsdp', 'ctx'), 'tp'), may hold values from -0.125 to 0.125
- out_weight: bfloat16 [4096, 2048], P('tp', ('fsdp', 'ctx')), may hold values from -0.125 to 0.125
- group_gain: bfloat16 [8, 512], P('tp', ('fsdp', 'ctx')), may hold values from 0.5 to 1.5
- group_bias: bfloat16 [8, 512], P('tp', ('fsdp', 'ctx')), may hold values from -1 to 1
- mlp_gain: bfloat16 [2048], P(('fsdp', 'ctx')), may hold values from 0.5 to 1.5
- mlp_bias: bfloat16 [2048], P(('fsdp', 'ctx')), may hold values from -1 to 1
- gelu_weight: bfloat16 [2048, 4096], P(('fsdp', 'ctx'), 'tp'), may hold values from -0.125 to 0.125
- up_weight: bfloat16 [2048, 4096], P(('fsdp', 'ctx'), 'tp'), may hold values from -0.125 to 0.125
- down_weight: bfloat16 [4096, 2048], P('tp', ('fsdp', 'ctx')), may hold values from -0.125 to 0.125
Outputs:
- block_out: bfloat16 [8, 1024, 2048], P('fsdp', 'ctx')
- grad_tokens: bfloat16 [8, 1024, 2048], P('fsdp', 'ctx')
- grad_pre_gain: float32 [2048], P(('fsdp', 'ctx'))
- grad_pre_bias: float32 [2048], P(('fsdp', 'ctx'))
- grad_query: float32 [2048, 2048], P(('fsdp', 'ctx'), 'tp')
- grad_key: float32 [2048, 2048], P(('fsdp', 'ctx'), 'tp')
- grad_value: float32 [2048, 4096], P(('fsdp', 'ctx'), 'tp')
- grad_swish: float32 [2048, 4096], P(('fsdp', 'ctx'), 'tp')
- grad_out: float32 [4096, 2048], P('tp', ('fsdp', 'ctx'))
- grad_group_gain: float32 [8, 512], P('tp', ('fsdp', 'ctx'))
- grad_group_bias: float32 [8, 512], P('tp', ('fsdp', 'ctx'))
- grad_mlp_gain: float32 [2048], P(('fsdp', 'ctx'))
- grad_mlp_bias: float32 [2048], P(('fsdp', 'ctx'))
- grad_gelu: float32 [2048, 4096], P(('fsdp', 'ctx'), 'tp')
- grad_up: float32 [2048, 4096], P(('fsdp', 'ctx'), 'tp')
- grad_down: float32 [4096, 2048], P('tp', ('fsdp', 'ctx'))
Inputs may be any that keep to these rules, and one draw needn't show every extreme that they name: `lengths`: valid tokens stand at the start of a sequence; in each group of 2 consecutive sequences one sequence has 1024 valid tokens, and one sequence of the batch has 256.
All inputs are finite; a program needn't handle non-finite values.
Results may differ from a plain program's by a relative error of at most 0.018.
Values may be sent and summed in bfloat16 or wider, within the bound.
A program may use at most 256 MiB of HBM per device.

v0:
```python
import jax
import jax.numpy as jnp
from jax import lax
from jax.sharding import PartitionSpec as P

eps = 1e-05
group_floor = 1.0
highest = lax.Precision.HIGHEST


def passed_along(value, axis, by):
    length = lax.axis_size(axis)
    pairs = [(i, i + by) for i in range(length) if 0 <= i + by < length]
    return lax.ppermute(value, axis, pairs)


def layer_norm(values, norm_gain, norm_shift):
    centred = values - jnp.mean(values, -1, keepdims=True)
    spread = jnp.mean(centred * centred, -1, keepdims=True)
    return centred * lax.rsqrt(spread + eps) * norm_gain + norm_shift


def turn_tables(positions, half_size):
    frequency = jnp.power(10000.0, -jnp.arange(half_size).astype(jnp.float32) / half_size)
    angles = positions.astype(jnp.float32)[:, None] * frequency[None, :]
    return (jnp.cos(angles)[:, None, :], jnp.sin(angles)[:, None, :])


def rotate(values, cosine, sine_table):
    half_size = values.shape[-1] // 2
    first_half = values[..., :half_size]
    second = values[..., half_size:]
    return jnp.concatenate(
        [first_half * cosine - second * sine_table, second * cosine + first_half * sine_table], -1
    )


def decay_logs(first_head, head_count):
    head_ids = (first_head + jnp.arange(head_count)).astype(jnp.float32)
    return jnp.log1p(-jnp.exp2(-5.0 - head_ids))


def decay_tables(log_decay, span_len):
    offsets = jnp.arange(span_len)
    distance = (offsets[:, None] - offsets[None, :]).astype(jnp.float32)
    within_fade = jnp.where(
        distance[None] >= 0,
        jnp.exp(jnp.maximum(distance, 0.0)[None] * log_decay[:, None, None]),
        0.0,
    )
    key_fade = jnp.exp((span_len - 1 - offsets).astype(jnp.float32)[:, None] * log_decay[None, :])
    query_fade = jnp.exp((offsets + 1).astype(jnp.float32)[:, None] * log_decay[None, :])
    block_fade = jnp.exp(span_len * log_decay)
    return (within_fade, key_fade, query_fade, block_fade)


def gate_mix(mixed, swish_pre, norm_gain, norm_shift):
    centred = mixed - jnp.mean(mixed, -1, keepdims=True)
    spread = jnp.mean(centred * centred, -1, keepdims=True)
    return jax.nn.silu(swish_pre) * (
        centred * lax.rsqrt(spread + group_floor) * norm_gain + norm_shift
    )


def mlp_mix(gelu_pre, up_pre):
    return jax.nn.gelu(gelu_pre) * up_pre


def product(left, right):
    return jnp.dot(left, right, preferred_element_type=jnp.float32)


def product_left(left, right):
    return lax.dot_general(
        left, right, (((0,), (0,)), ((), ())), preferred_element_type=jnp.float32
    )


def product_right(left, right):
    return lax.dot_general(
        left, right, (((1,), (1,)), ((), ())), preferred_element_type=jnp.float32
    )


def shards(
    tokens,
    lengths,
    cotangent,
    pre_gain,
    pre_bias,
    query_weight,
    key_weight,
    value_weight,
    swish_weight,
    out_weight,
    group_gain,
    group_bias,
    mlp_gain,
    mlp_bias,
    gelu_weight,
    up_weight,
    down_weight,
):
    seq_count, span_len, model_width = tokens.shape
    row_count = seq_count * span_len
    heads_local = group_gain.shape[0]
    key_size = query_weight.shape[1] // heads_local
    value_size = value_weight.shape[1] // heads_local
    f32 = jnp.float32
    bf16 = jnp.bfloat16
    attn_full = (
        lax.all_gather(query_weight, ("fsdp", "ctx"), axis=0, tiled=True),
        lax.all_gather(key_weight, ("fsdp", "ctx"), axis=0, tiled=True),
        lax.all_gather(value_weight, ("fsdp", "ctx"), axis=0, tiled=True),
        lax.all_gather(swish_weight, ("fsdp", "ctx"), axis=0, tiled=True),
        lax.all_gather(out_weight, ("fsdp", "ctx"), axis=1, tiled=True),
        lax.all_gather(pre_gain, ("fsdp", "ctx"), axis=0, tiled=True),
        lax.all_gather(pre_bias, ("fsdp", "ctx"), axis=0, tiled=True),
        lax.all_gather(group_gain, ("fsdp", "ctx"), axis=1, tiled=True),
        lax.all_gather(group_bias, ("fsdp", "ctx"), axis=1, tiled=True),
    )
    (
        query_full,
        key_full,
        value_full,
        swish_full,
        out_full,
        pre_gain_full,
        pre_bias_full,
        group_gain_full,
        group_bias_full,
    ) = attn_full
    inputs = tokens.reshape(row_count, model_width).astype(f32)
    normed_wide, norm_in_back = jax.vjp(
        layer_norm, inputs, pre_gain_full.astype(f32), pre_bias_full.astype(f32)
    )
    normed = normed_wide.astype(bf16)
    query_pre = product(normed, query_full).reshape(seq_count, span_len, heads_local, key_size)
    key_pre = product(normed, key_full).reshape(seq_count, span_len, heads_local, key_size)
    value_pre = product(normed, value_full)
    swish_pre = product(normed, swish_full).reshape(seq_count, span_len, heads_local, value_size)
    positions = lax.axis_index("ctx") * span_len + lax.iota(jnp.int32, span_len)
    valid_mask = (positions[None, :] < lengths[:, None]).astype(f32)
    cosine, sine_table = turn_tables(positions, key_size // 2)
    key_scale = key_size ** (-0.5)

    def place_heads(query_in, key_in):
        return (
            rotate(query_in, cosine, sine_table),
            rotate(key_in, cosine, sine_table) * key_scale * valid_mask[:, :, None, None],
        )

    (query_turn, key_turn), place_back = jax.vjp(place_heads, query_pre, key_pre)
    queries = query_turn.astype(bf16)
    keys = key_turn.astype(bf16)
    values = value_pre.astype(bf16).reshape(seq_count, span_len, heads_local, value_size)
    log_decay = decay_logs(lax.axis_index("tp") * heads_local, heads_local)
    within_fade, key_fade, query_fade, block_fade = decay_tables(log_decay, span_len)
    scores = jnp.einsum("sihd,sjhd->shij", queries, keys, preferred_element_type=f32)
    probs = (scores * within_fade[None]).astype(bf16)
    inner_part = jnp.einsum("shij,sjhe->sihe", probs, values, preferred_element_type=f32)
    keys_faded = keys.astype(f32) * key_fade[None, :, :, None]
    values_wide = values.astype(f32)
    local_state = jnp.einsum("sjhd,sjhe->shde", keys_faded, values_wide, precision=highest)

    def pass_state(turn_index, received):
        return passed_along(
            (block_fade[:, None, None] * received + local_state).astype(jnp.bfloat16), "ctx", 1
        ).astype(jnp.float32)

    entering = lax.fori_loop(0, lax.axis_size("ctx") - 1, pass_state, jnp.zeros_like(local_state))
    queries_faded = queries.astype(f32) * query_fade[None, :, :, None]
    outer_part = jnp.einsum("sihd,shde->sihe", queries_faded, entering, precision=highest)
    mixed = inner_part + outer_part
    gated_wide, gate_back = jax.vjp(
        gate_mix, mixed, swish_pre, group_gain_full.astype(f32), group_bias_full.astype(f32)
    )
    gated = gated_wide.reshape(row_count, heads_local * value_size).astype(bf16)
    branch = lax.psum(product(gated, out_full), "tp")
    hidden = inputs + branch
    mlp_full = (
        lax.all_gather(gelu_weight, ("fsdp", "ctx"), axis=0, tiled=True),
        lax.all_gather(up_weight, ("fsdp", "ctx"), axis=0, tiled=True),
        lax.all_gather(down_weight, ("fsdp", "ctx"), axis=1, tiled=True),
        lax.all_gather(mlp_gain, ("fsdp", "ctx"), axis=0, tiled=True),
        lax.all_gather(mlp_bias, ("fsdp", "ctx"), axis=0, tiled=True),
    )
    gelu_full, up_full, down_full, mlp_gain_full, mlp_bias_full = mlp_full
    mlp_wide, norm_mid_back = jax.vjp(
        layer_norm, hidden, mlp_gain_full.astype(f32), mlp_bias_full.astype(f32)
    )
    mlp_in = mlp_wide.astype(bf16)
    gelu_pre = product(mlp_in, gelu_full)
    up_pre = product(mlp_in, up_full)
    inner_wide, mix_back = jax.vjp(mlp_mix, gelu_pre, up_pre)
    inner = inner_wide.astype(bf16)
    mlp_out = lax.psum(product(inner, down_full).astype(jnp.bfloat16), "tp").astype(jnp.float32)
    valid_rows = valid_mask.reshape(row_count, 1)
    block_out = (
        (valid_rows * (hidden + mlp_out)).astype(bf16).reshape(seq_count, span_len, model_width)
    )
    error = valid_rows * cotangent.reshape(row_count, model_width).astype(f32)
    error_low = error.astype(bf16)
    gelu_back_weight, up_back_weight, down_back_weight = (
        lax.all_gather(gelu_weight, ("fsdp", "ctx"), axis=0, tiled=True),
        lax.all_gather(up_weight, ("fsdp", "ctx"), axis=0, tiled=True),
        lax.all_gather(down_weight, ("fsdp", "ctx"), axis=1, tiled=True),
    )
    grad_down = product_left(inner, error_low)
    inner_grad = product_right(error_low, down_back_weight)
    gelu_grad, up_grad = mix_back(inner_grad)
    gelu_low = gelu_grad.astype(bf16)
    up_low = up_grad.astype(bf16)
    grad_gelu = product_left(mlp_in, gelu_low)
    grad_up = product_left(mlp_in, up_low)
    mlp_in_grad = lax.psum(
        product_right(gelu_low, gelu_back_weight) + product_right(up_low, up_back_weight), "tp"
    )
    hidden_norm_grad, grad_mlp_gain, grad_mlp_bias = norm_mid_back(mlp_in_grad)
    hidden_grad = error + hidden_norm_grad
    mlp_grads = (
        lax.psum_scatter(grad_gelu, ("fsdp", "ctx"), scatter_dimension=0, tiled=True),
        lax.psum_scatter(grad_up, ("fsdp", "ctx"), scatter_dimension=0, tiled=True),
        lax.psum_scatter(grad_down, ("fsdp", "ctx"), scatter_dimension=1, tiled=True),
        lax.psum_scatter(grad_mlp_gain, ("fsdp", "ctx"), scatter_dimension=0, tiled=True),
        lax.psum_scatter(grad_mlp_bias, ("fsdp", "ctx"), scatter_dimension=0, tiled=True),
    )
    query_back, key_back, value_back, swish_back, out_back = (
        lax.all_gather(query_weight, ("fsdp", "ctx"), axis=0, tiled=True),
        lax.all_gather(key_weight, ("fsdp", "ctx"), axis=0, tiled=True),
        lax.all_gather(value_weight, ("fsdp", "ctx"), axis=0, tiled=True),
        lax.all_gather(swish_weight, ("fsdp", "ctx"), axis=0, tiled=True),
        lax.all_gather(out_weight, ("fsdp", "ctx"), axis=1, tiled=True),
    )
    hidden_low = hidden_grad.astype(bf16)
    grad_out = product_left(gated, hidden_low)
    gated_grad = product_right(hidden_low, out_back).reshape(
        seq_count, span_len, heads_local, value_size
    )
    mixed_grad, swish_grad, grad_group_gain, grad_group_bias = gate_back(gated_grad)
    swish_low = swish_grad.reshape(row_count, heads_local * value_size).astype(bf16)
    mixed_low = mixed_grad.astype(bf16)
    mixed_back = mixed_low.astype(f32)
    prob_grad = jnp.einsum("sihe,sjhe->shij", mixed_low, values, preferred_element_type=f32)
    score_low = (prob_grad * within_fade[None]).astype(bf16)
    pulled_state = jnp.einsum("sihd,sihe->shde", queries_faded, mixed_back, precision=highest)

    def pass_grad(turn_index, received):
        return passed_along(
            (block_fade[:, None, None] * received + pulled_state).astype(jnp.bfloat16), "ctx", -1
        ).astype(jnp.float32)

    later_grad = lax.fori_loop(0, lax.axis_size("ctx") - 1, pass_grad, jnp.zeros_like(pulled_state))
    query_grad = jnp.einsum(
        "shij,sjhd->sihd", score_low, keys, preferred_element_type=f32
    ) + query_fade[None, :, :, None] * jnp.einsum(
        "sihe,shde->sihd", mixed_back, entering, precision=highest
    )
    key_grad = jnp.einsum(
        "shij,sihd->sjhd", score_low, queries, preferred_element_type=f32
    ) + key_fade[None, :, :, None] * jnp.einsum(
        "sjhe,shde->sjhd", values_wide, later_grad, precision=highest
    )
    value_grad = jnp.einsum(
        "shij,sihe->sjhe", probs, mixed_low, preferred_element_type=f32
    ) + jnp.einsum("sjhd,shde->sjhe", keys_faded, later_grad, precision=highest)
    query_pre_grad, key_pre_grad = place_back((query_grad, key_grad))
    query_low = query_pre_grad.reshape(row_count, heads_local * key_size).astype(bf16)
    key_low = key_pre_grad.reshape(row_count, heads_local * key_size).astype(bf16)
    value_low = value_grad.reshape(row_count, heads_local * value_size).astype(bf16)
    grad_query = product_left(normed, query_low)
    grad_key = product_left(normed, key_low)
    grad_value = product_left(normed, value_low)
    grad_swish = product_left(normed, swish_low)
    normed_partial = (
        product_right(query_low, query_back)
        + product_right(key_low, key_back)
        + product_right(value_low, value_back)
        + product_right(swish_low, swish_back)
    )
    normed_grad = lax.psum(normed_partial.astype(jnp.bfloat16), "tp").astype(jnp.float32)
    input_norm_grad, grad_pre_gain, grad_pre_bias = norm_in_back(normed_grad)
    grad_tokens = (
        (hidden_grad + input_norm_grad).astype(bf16).reshape(seq_count, span_len, model_width)
    )
    attn_grads = (
        lax.psum_scatter(grad_query, ("fsdp", "ctx"), scatter_dimension=0, tiled=True),
        lax.psum_scatter(grad_key, ("fsdp", "ctx"), scatter_dimension=0, tiled=True),
        lax.psum_scatter(grad_value, ("fsdp", "ctx"), scatter_dimension=0, tiled=True),
        lax.psum_scatter(grad_swish, ("fsdp", "ctx"), scatter_dimension=0, tiled=True),
        lax.psum_scatter(grad_out, ("fsdp", "ctx"), scatter_dimension=1, tiled=True),
        lax.psum_scatter(grad_pre_gain, ("fsdp", "ctx"), scatter_dimension=0, tiled=True),
        lax.psum_scatter(grad_pre_bias, ("fsdp", "ctx"), scatter_dimension=0, tiled=True),
        lax.psum_scatter(grad_group_gain, ("fsdp", "ctx"), scatter_dimension=1, tiled=True),
        lax.psum_scatter(grad_group_bias, ("fsdp", "ctx"), scatter_dimension=1, tiled=True),
    )
    return (
        block_out,
        grad_tokens,
        attn_grads[5],
        attn_grads[6],
        attn_grads[0],
        attn_grads[1],
        attn_grads[2],
        attn_grads[3],
        attn_grads[4],
        attn_grads[7],
        attn_grads[8],
        mlp_grads[3],
        mlp_grads[4],
        mlp_grads[0],
        mlp_grads[1],
        mlp_grads[2],
    )


def solution(mesh):
    in_specs = (
        P("fsdp", "ctx", None),
        P("fsdp"),
        P("fsdp", "ctx", None),
        P(("fsdp", "ctx")),
        P(("fsdp", "ctx")),
        P(("fsdp", "ctx"), "tp"),
        P(("fsdp", "ctx"), "tp"),
        P(("fsdp", "ctx"), "tp"),
        P(("fsdp", "ctx"), "tp"),
        P("tp", ("fsdp", "ctx")),
        P("tp", ("fsdp", "ctx")),
        P("tp", ("fsdp", "ctx")),
        P(("fsdp", "ctx")),
        P(("fsdp", "ctx")),
        P(("fsdp", "ctx"), "tp"),
        P(("fsdp", "ctx"), "tp"),
        P("tp", ("fsdp", "ctx")),
    )
    out_specs = (
        P("fsdp", "ctx", None),
        P("fsdp", "ctx", None),
        P(("fsdp", "ctx")),
        P(("fsdp", "ctx")),
        P(("fsdp", "ctx"), "tp"),
        P(("fsdp", "ctx"), "tp"),
        P(("fsdp", "ctx"), "tp"),
        P(("fsdp", "ctx"), "tp"),
        P("tp", ("fsdp", "ctx")),
        P("tp", ("fsdp", "ctx")),
        P("tp", ("fsdp", "ctx")),
        P(("fsdp", "ctx")),
        P(("fsdp", "ctx")),
        P(("fsdp", "ctx"), "tp"),
        P(("fsdp", "ctx"), "tp"),
        P("tp", ("fsdp", "ctx")),
    )
    return jax.shard_map(shards, mesh=mesh, in_specs=in_specs, out_specs=out_specs, check_vma=False)
```

profile of v0, /device:TPU:0, one launch (start us, length us, event | category | flops | bytes accessed | tf_op | source)
XLA Modules:
  0.0 4064.6 jit_solution(11655747423073126948)
XLA Ops:
  10.7 42.5 %all-gather = bf16[16,1,128]{2,1,0:T(2,128)(2,1)S(1)} all-gather(bf16[1,1,128]{2,1,0:T(2,128)(2,1)} %bitcast.263), channel_id=1, replica_groups=mesh['fsdp'=4,'ctx'=4,'tp'=2] {'fsdp','ctx'}, dimensions={0}, use_global_device_ids=true | all-gather | bytes 4352 | tf_op jit(solution)/shard_map/all_gather | solution.py:117
  53.1 35.9 all-gather.1
  92.3 37.5 all-gather.2
  129.9 36.2 all-gather.3
  196.1 85.2 %all-gather.17.cloned.1.call-done = bf16[2048,2048]{1,0:T(8,128)(2,1)} async-done(((bf16[128,2048]{1,0:T(8,128)(2,1)}), bf16[2048,2048]{1,0:T(8,128)(2,1)}) %all-gather.17.cloned.1.call-update) | async-done | bytes 8388624 | tf_op jit(solution)/shard_map/all_gather | solution.py:114
  281.3 9.8 convolution_convert_fusion.1
  295.6 99.4 %all-gather.15.cloned.1.call-done = bf16[2048,2048]{1,0:T(8,128)(2,1)} async-done(((bf16[128,2048]{1,0:T(8,128)(2,1)}), bf16[2048,2048]{1,0:T(8,128)(2,1)}) %all-gather.15.cloned.1.call-update) | async-done | bytes 8388624 | tf_op jit(solution)/shard_map/all_gather | solution.py:115
  395.0 12.9 copy.99
  413.8 260.8 %while.22 = (s32[]{:T(128)}, f32[2,4,256,512]{3,2,1,0:T(8,128)}, f32[2,4,256,512]{3,2,1,0:T(8,128)}, s32[]{:T(128)}, s32[]{:T(128)}, /*index=5*/s32[]{:T(128)}) while((s32[]{:T(128)}, f32[2,4,256,512]{3,2,1,0:T(8,128)}, f32[2,4,256,512]{3,2,1,0:T(8,128)}, s32[]{:T(128)}, s32[]{:T(128)}, /*index=5*/s32[]{:T(128)}) %tuple.75), condition=%wide.region_3.4_spmd.clone, body=%wide.region_2.3_spmd.clone.sunk | while | flops 5242907 | bytes 25165980 | solution.py:171
  422.1 82.0 %collective-permute-done = bf16[2,4,256,512]{3,2,1,0:T(8,128)(2,1)} collective-permute-done((bf16[2,4,256,512]{3,2,1,0:T(8,128)(2,1)}, bf16[2,4,256,512]{3,2,1,0:T(8,128)(2,1)}, u32[]{:S(2)}, u32[]{:S(2)}) %collective-permute-start) | collective-permute-done | bytes 2097184 | tf_op jit(solution)/shard_map/while/body/eval_jaxpr/ppermute | solution.py:14
  514.2 16.6 collective-permute-start
  530.8 80.3 %collective-permute-done = bf16[2,4,256,512]{3,2,1,0:T(8,128)(2,1)} collective-permute-done((bf16[2,4,256,512]{3,2,1,0:T(8,128)(2,1)}, bf16[2,4,256,512]{3,2,1,0:T(8,128)(2,1)}, u32[]{:S(2)}, u32[]{:S(2)}) %collective-permute-start) | collective-permute-done | bytes 2097184 | tf_op jit(solution)/shard_map/while/body/eval_jaxpr/ppermute | solution.py:14
  626.9 43.5 %collective-permute-done = bf16[2,4,256,512]{3,2,1,0:T(8,128)(2,1)} collective-permute-done((bf16[2,4,256,512]{3,2,1,0:T(8,128)(2,1)}, bf16[2,4,256,512]{3,2,1,0:T(8,128)(2,1)}, u32[]{:S(2)}, u32[]{:S(2)}) %collective-permute-start) | collective-permute-done | bytes 2097184 | tf_op jit(solution)/shard_map/while/body/eval_jaxpr/ppermute | solution.py:14
  695.9 10.7 fusion.74
  708.9 40.2 all-gather.4
  749.1 35.7 all-gather.5
  793.7 60.0 %all-gather.25.cloned.1.call-done = bf16[2048,2048]{1,0:T(8,128)(2,1)} async-done(((bf16[128,2048]{1,0:T(8,128)(2,1)}), bf16[2048,2048]{1,0:T(8,128)(2,1)}) %all-gather.25.cloned.1.call-update) | async-done | bytes 8388624 | tf_op jit(solution)/shard_map/all_gather | solution.py:182
  853.7 9.6 fusion.75
  863.4 104.6 %all-gather.27.cloned.1.call-done = bf16[2048,2048]{1,0:T(8,128)(2,1)} async-done(((bf16[128,2048]{1,0:T(8,128)(2,1)}), bf16[2048,2048]{1,0:T(8,128)(2,1)}) %all-gather.27.cloned.1.call-update) | async-done | bytes 8388624 | tf_op jit(solution)/shard_map/all_gather | solution.py:183
  968.0 10.7 fusion.76
  978.6 133.0 %all-gather.29.cloned.1.call-done = bf16[2048,2048]{1,0:T(8,128)(2,1)} async-done(((bf16[2048,128]{1,0:T(8,128)(2,1)}), bf16[2048,2048]{1,0:T(8,128)(2,1)}) %all-gather.29.cloned.1.call-update) | async-done | bytes 8388624 | tf_op jit(solution)/shard_map/all_gather | solution.py:184
  1111.6 13.2 multiply_convert_fusion
  1124.8 8.5 fusion.77
  1141.1 10.1 convolution_convert_fusion
  1151.2 15.1 all-reduce.16.cloned.1.call-done
  1213.4 171.9 %while.23 = (s32[]{:T(128)}, f32[2,4,256,512]{3,2,1,0:T(8,128)}, f32[2,4,256,512]{3,2,1,0:T(8,128)}, s32[]{:T(128)}, s32[]{:T(128)}, /*index=5*/s32[]{:T(128)}) while((s32[]{:T(128)}, f32[2,4,256,512]{3,2,1,0:T(8,128)}, f32[2,4,256,512]{3,2,1,0:T(8,128)}, s32[]{:T(128)}, s32[]{:T(128)}, /*index=5*/s32[]{:T(128)}) %tuple.78), condition=%wide.region_16.17_spmd.clone, body=%wide.region_15.16_spmd.clone.sunk | while | flops 5242907 | bytes 25165980 | solution.py:253
  1219.4 48.6 %collective-permute-done.1 = bf16[2,4,256,512]{3,2,1,0:T(8,128)(2,1)S(1)} collective-permute-done((bf16[2,4,256,512]{3,2,1,0:T(8,128)(2,1)}, bf16[2,4,256,512]{3,2,1,0:T(8,128)(2,1)S(1)}, u32[]{:S(2)}, u32[]{:S(2)}) %collective-permute-start.1) | collective-permute-done | bytes 2097184 | tf_op jit(solution)/shard_map/while/body/eval_jaxpr/ppermute | solution.py:14
  1278.0 47.8 %collective-permute-done.1 = bf16[2,4,256,512]{3,2,1,0:T(8,128)(2,1)S(1)} collective-permute-done((bf16[2,4,256,512]{3,2,1,0:T(8,128)(2,1)}, bf16[2,4,256,512]{3,2,1,0:T(8,128)(2,1)S(1)}, u32[]{:S(2)}, u32[]{:S(2)}) %collective-permute-start.1) | collective-permute-done | bytes 2097184 | tf_op jit(solution)/shard_map/while/body/eval_jaxpr/ppermute | solution.py:14
  1335.8 46.9 %collective-permute-done.1 = bf16[2,4,256,512]{3,2,1,0:T(8,128)(2,1)S(1)} collective-permute-done((bf16[2,4,256,512]{3,2,1,0:T(8,128)(2,1)}, bf16[2,4,256,512]{3,2,1,0:T(8,128)(2,1)S(1)}, u32[]{:S(2)}, u32[]{:S(2)}) %collective-permute-start.1) | collective-permute-done | bytes 2097184 | tf_op jit(solution)/shard_map/while/body/eval_jaxpr/ppermute | solution.py:14
  1385.4 8.8 fusion.51
  1434.4 10.8 add_convert_fusion.1
  1459.8 12.6 fusion.88
  1472.4 12.6 fusion.89
  1485.3 12.6 fusion.90
  1498.0 12.5 fusion.87
  1510.6 9.9 fusion.85
  1520.8 9.9 fusion.86
  1534.0 14.8 reduce-scatter.33.cloned.1.call-done
  1550.2 26.1 all-reduce.18.cloned.1.call-done
  1581.5 82.5 %all-reduce.8 = (f32[2048]{0:T(1024)S(1)}, f32[2048]{0:T(1024)S(1)}, f32[2048]{0:T(1024)S(1)}, f32[2048]{0:T(1024)S(1)}) all-reduce(f32[2048]{0:T(1024)S(1)} %get-tuple-element.102, f32[2048]{0:T(1024)S(1)} %get-tuple-element.107, f32[2048]{0:T(1024)S(1)} %copy-done.53, ...), channel_id=2, replica_groups=mesh['fsdp'=4,'ctx'=4,'tp'=2] {'fsdp','ctx'}, use_global_device_ids=true, to_apply=%region_21.22.clone | all-reduce | flops 8192 | bytes 65536
  1674.2 90.5 %reduce-scatter.17.cloned.1.call-done = f32[128,1024]{1,0:T(8,128)} async-done(((f32[2048,1024]{1,0:T(8,128)}), f32[128,1024]{1,0:T(8,128)}) %reduce-scatter.17.cloned.1.call-update) | async-done | bytes 524304 | tf_op jit(solution)/shard_map/reduce_scatter | solution.py:288
  1764.7 182.8 %reduce-scatter.15.cloned.1.call-done = f32[128,1024]{1,0:T(8,128)} async-done(((f32[2048,1024]{1,0:T(8,128)}), f32[128,1024]{1,0:T(8,128)}) %reduce-scatter.15.cloned.1.call-update) | async-done | bytes 524304 | tf_op jit(solution)/shard_map/reduce_scatter | solution.py:287
  1947.5 350.5 %reduce-scatter.25.cloned.1.call-done = f32[128,2048]{1,0:T(8,128)} async-done(((f32[2048,2048]{1,0:T(8,128)}), f32[128,2048]{1,0:T(8,128)}) %reduce-scatter.25.cloned.1.call-update) | async-done | bytes 1048592 | tf_op jit(solution)/shard_map/reduce_scatter | solution.py:222
  2297.9 351.8 %reduce-scatter.27.cloned.1.call-done = f32[128,2048]{1,0:T(8,128)} async-done(((f32[2048,2048]{1,0:T(8,128)}), f32[128,2048]{1,0:T(8,128)}) %reduce-scatter.27.cloned.1.call-update) | async-done | bytes 1048592 | tf_op jit(solution)/shard_map/reduce_scatter | solution.py:223
  2649.8 351.9 %reduce-scatter.29.cloned.1.call-done = f32[2048,128]{1,0:T(8,128)} async-done(((f32[2048,2048]{1,0:T(8,128)}), f32[2048,128]{1,0:T(8,128)}) %reduce-scatter.29.cloned.1.call-update) | async-done | bytes 1048592 | tf_op jit(solution)/shard_map/reduce_scatter | solution.py:224
  3001.6 352.0 %reduce-scatter.23.cloned.1.call-done = f32[2048,128]{1,0:T(8,128)} async-done(((f32[2048,2048]{1,0:T(8,128)}), f32[2048,128]{1,0:T(8,128)}) %reduce-scatter.23.cloned.1.call-update) | async-done | bytes 1048592 | tf_op jit(solution)/shard_map/reduce_scatter | solution.py:291
  3353.6 351.8 %reduce-scatter.19.cloned.1.call-done = f32[128,2048]{1,0:T(8,128)} async-done(((f32[2048,2048]{1,0:T(8,128)}), f32[128,2048]{1,0:T(8,128)}) %reduce-scatter.19.cloned.1.call-update) | async-done | bytes 1048592 | tf_op jit(solution)/shard_map/reduce_scatter | solution.py:289
  3705.5 352.0 %reduce-scatter.21.cloned.1.call-done = f32[128,2048]{1,0:T(8,128)} async-done(((f32[2048,2048]{1,0:T(8,128)}), f32[128,2048]{1,0:T(8,128)}) %reduce-scatter.21.cloned.1.call-update) | async-done | bytes 1048592 | tf_op jit(solution)/shard_map/reduce_scatter | solution.py:290
  (336 shorter events, 275.7 us)
Async XLA Ops:
  7.2 83.8 %copy-start.3 = (bf16[2,256,2048]{2,1,0:T(8,128)(2,1)S(1)}, bf16[2,256,2048]{2,1,0:T(8,128)(2,1)}, u32[]{:S(2)}) copy-start(bf16[2,256,2048]{2,1,0:T(8,128)(2,1)} %param.21) | copy-start | bytes 6291460
  7.2 85.1 %copy-start.62 = (bf16[4,32]{1,0:T(4,128)(2,1)S(1)}, bf16[4,32]{1,0:T(4,128)(2,1)}, u32[]{:S(2)}) copy-start(bf16[4,32]{1,0:T(4,128)(2,1)} %param.31) | copy-start | bytes 772
  7.2 122.7 %copy-start.63 = (bf16[4,32]{1,0:T(4,128)(2,1)S(1)}, bf16[4,32]{1,0:T(4,128)(2,1)}, u32[]{:S(2)}) copy-start(bf16[4,32]{1,0:T(4,128)(2,1)} %param.32) | copy-start | bytes 772
  7.2 159.1 %copy-start.61 = (s32[2]{0:T(128)S(1)}, s32[2]{0:T(128)}, u32[]{:S(2)}) copy-start(s32[2]{0:T(128)} %param.22) | copy-start | bytes 28
  7.2 164.4 %all-gather.21.cloned.1.call-start = ((), (), s32[]{:S(2)}) async-start(), calls=%async_computation.13 | async-start | bytes 4456448 | tf_op jit(solution)/shard_map/all_gather | solution.py:113
  8.0 170.4 %all-gather.19.cloned.1.call-start = ((), (), s32[]{:S(2)}) async-start(), calls=%async_computation.12 | async-start | bytes 4456448 | tf_op jit(solution)/shard_map/all_gather | solution.py:112
  8.7 272.6 %all-gather.17.cloned.1.call-start = ((), (), s32[]{:S(2)}) async-start(), calls=%async_computation.11 | async-start | bytes 8912896 | tf_op jit(solution)/shard_map/all_gather | solution.py:114
  9.4 385.6 %all-gather.15.cloned.1.call-start = ((), (), s32[]{:S(2)}) async-start(), calls=%async_computation.10 | async-start | bytes 8912896 | tf_op jit(solution)/shard_map/all_gather | solution.py:115
  10.0 685.9 %all-gather.23.cloned.1.call-start = ((), (), s32[]{:S(2)}) async-start(), calls=%async_computation.14 | async-start | bytes 8912896 | tf_op jit(solution)/shard_map/all_gather | solution.py:116
  10.6 777.6 %all-reduce.14.cloned.1.call-start = ((), (), s32[]{:S(2)}) async-start(), calls=%async_computation.15 | async-start | bytes 8388608 | tf_op jit(solution)/shard_map/psum | solution.py:179
  53.1 116.3 %copy-start.45 = (f32[16,1,128]{2,1,0:T(1,128)}, f32[16,1,128]{2,1,0:T(1,128)S(1)}, u32[]{:S(2)}) copy-start(f32[16,1,128]{2,1,0:T(1,128)S(1)} %convert_element_type.288) | copy-start | bytes 24580
  92.3 79.3 %copy-start.51 = (f32[512]{0:T(512)}, f32[512]{0:T(512)S(1)}, u32[]{:S(2)}) copy-start(f32[512]{0:T(512)S(1)} %rsqrt.34) | copy-start | bytes 6148
  92.3 79.3 %copy-start.49 = (f32[1,2,2,128]{3,1,2,0:T(2,128)}, f32[1,2,2,128]{3,1,2,0:T(2,128)S(1)}, u32[]{:S(2)}) copy-start(f32[1,2,2,128]{3,1,2,0:T(2,128)S(1)} %copy.139) | copy-start | bytes 6148
  166.5 241.4 %copy-start.47 = (f32[256,4]{0,1:T(4,128)}, f32[256,4]{0,1:T(4,128)S(1)}, u32[]{:S(2)}) copy-start(f32[256,4]{0,1:T(4,128)S(1)} %get-tuple-element.163) | copy-start | bytes 12292
  413.8 260.8 %copy-start.22 = (bf16[2,256,4,128]{1,3,2,0:T(8,128)(2,1)S(1)}, bf16[2,256,4,128]{1,3,2,0:T(8,128)(2,1)}, u32[]{:S(2)}) copy-start(bf16[2,256,4,128]{1,3,2,0:T(8,128)(2,1)} %copy-done.21) | copy-start | bytes 1572868
  413.8 260.8 %copy-start.25 = (bf16[2,256,4,128]{1,3,2,0:T(8,128)(2,1)S(1)}, bf16[2,256,4,128]{1,3,2,0:T(8,128)(2,1)}, u32[]{:S(2)}) copy-start(bf16[2,256,4,128]{1,3,2,0:T(8,128)(2,1)} %copy-done.24) | copy-start | bytes 1572868
  418.6 85.5 %collective-permute-start = (bf16[2,4,256,512]{3,2,1,0:T(8,128)(2,1)}, bf16[2,4,256,512]{3,2,1,0:T(8,128)(2,1)}, u32[]{:S(2)}, u32[]{:S(2)}) collective-permute-start(bf16[2,4,256,512]{3,2,1,0:T(8,128)(2,1)} %fusion.152), channel_id=1, source_target_pairs={{0,2},{2,4},{4,6},{1,3},{3,5},{5,7},{8,10},{10,12},{12,14},{9,11},... | collective-permute-start | bytes 6291464 | tf_op jit(solution)/shard_map/while/body/eval_jaxpr/ppermute | solution.py:14
  514.2 96.8 %collective-permute-start = (bf16[2,4,256,512]{3,2,1,0:T(8,128)(2,1)}, bf16[2,4,256,512]{3,2,1,0:T(8,128)(2,1)}, u32[]{:S(2)}, u32[]{:S(2)}) collective-permute-start(bf16[2,4,256,512]{3,2,1,0:T(8,128)(2,1)} %fusion.152), channel_id=1, source_target_pairs={{0,2},{2,4},{4,6},{1,3},{3,5},{5,7},{8,10},{10,12},{12,14},{9,11},... | collective-permute-start | bytes 6291464 | tf_op jit(solution)/shard_map/while/body/eval_jaxpr/ppermute | solution.py:14
  621.2 49.2 %collective-permute-start = (bf16[2,4,256,512]{3,2,1,0:T(8,128)(2,1)}, bf16[2,4,256,512]{3,2,1,0:T(8,128)(2,1)}, u32[]{:S(2)}, u32[]{:S(2)}) collective-permute-start(bf16[2,4,256,512]{3,2,1,0:T(8,128)(2,1)} %fusion.152), channel_id=1, source_target_pairs={{0,2},{2,4},{4,6},{1,3},{3,5},{5,7},{8,10},{10,12},{12,14},{9,11},... | collective-permute-start | bytes 6291464 | tf_op jit(solution)/shard_map/while/body/eval_jaxpr/ppermute | solution.py:14
  706.6 147.1 %all-gather.25.cloned.1.call-start = ((), (), s32[]{:S(2)}) async-start(), calls=%async_computation.16 | async-start | bytes 8912896 | tf_op jit(solution)/shard_map/all_gather | solution.py:182
  707.4 260.6 %all-gather.27.cloned.1.call-start = ((), (), s32[]{:S(2)}) async-start(), calls=%async_computation.17 | async-start | bytes 8912896 | tf_op jit(solution)/shard_map/all_gather | solution.py:183
  708.1 403.5 %all-gather.29.cloned.1.call-start = ((), (), s32[]{:S(2)}) async-start(), calls=%async_computation.18 | async-start | bytes 8912896 | tf_op jit(solution)/shard_map/all_gather | solution.py:184
  708.9 457.5 %all-reduce.16.cloned.1.call-start = ((), (), s32[]{:S(2)}) async-start(), calls=%async_computation.19 | async-start | bytes 8388608 | tf_op jit(solution)/shard_map/psum | solution.py:216
  784.9 388.6 %copy-start.55 = (f32[1,2,2,128]{3,1,2,0:T(2,128)}, f32[1,2,2,128]{3,1,2,0:T(2,128)S(1)}, u32[]{:S(2)}) copy-start(f32[1,2,2,128]{3,1,2,0:T(2,128)S(1)} %copy.138) | copy-start | bytes 6148
  793.7 60.0 %copy-start.38 = (bf16[512,2048]{1,0:T(8,128)(2,1)}, bf16[512,2048]{1,0:T(8,128)(2,1)S(1)}, u32[]{:S(2)}) copy-start(bf16[512,2048]{1,0:T(8,128)(2,1)S(1)} %add_convert_fusion.4) | copy-start | bytes 6291460
  863.4 248.2 %copy-start.37 = (bf16[512,2048]{1,0:T(8,128)(2,1)S(1)}, bf16[512,2048]{1,0:T(8,128)(2,1)}, u32[]{:S(2)}) copy-start(bf16[512,2048]{1,0:T(8,128)(2,1)} %fusion.23) | copy-start | bytes 6291460
  1139.5 393.1 %reduce-scatter.31.cloned.1.call-start = ((), (), s32[]{:S(2)}) async-start(), calls=%async_computation.28 | async-start | bytes 278528
  1213.4 171.9 %copy-start.48 = (f32[256,4]{0,1:T(4,128)S(1)}, f32[256,4]{0,1:T(4,128)}, u32[]{:S(2)}) copy-start(f32[256,4]{0,1:T(4,128)} %copy-done.47) | copy-start | bytes 12292
  1218.1 49.9 %collective-permute-start.1 = (bf16[2,4,256,512]{3,2,1,0:T(8,128)(2,1)}, bf16[2,4,256,512]{3,2,1,0:T(8,128)(2,1)S(1)}, u32[]{:S(2)}, u32[]{:S(2)}) collective-permute-start(bf16[2,4,256,512]{3,2,1,0:T(8,128)(2,1)} %fusion.153), channel_id=1, source_target_pairs={{2,0},{4,2},{6,4},{3,1},{5,3},{7,5},{10,8},{12,10},{14,12},{11,9},... | collective-permute-start | bytes 6291464 | tf_op jit(solution)/shard_map/while/body/eval_jaxpr/ppermute | solution.py:14
  1276.7 49.1 %collective-permute-start.1 = (bf16[2,4,256,512]{3,2,1,0:T(8,128)(2,1)}, bf16[2,4,256,512]{3,2,1,0:T(8,128)(2,1)S(1)}, u32[]{:S(2)}, u32[]{:S(2)}) collective-permute-start(bf16[2,4,256,512]{3,2,1,0:T(8,128)(2,1)} %fusion.153), channel_id=1, source_target_pairs={{2,0},{4,2},{6,4},{3,1},{5,3},{7,5},{10,8},{12,10},{14,12},{11,9},... | collective-permute-start | bytes 6291464 | tf_op jit(solution)/shard_map/while/body/eval_jaxpr/ppermute | solution.py:14
  1334.5 48.2 %collective-permute-start.1 = (bf16[2,4,256,512]{3,2,1,0:T(8,128)(2,1)}, bf16[2,4,256,512]{3,2,1,0:T(8,128)(2,1)S(1)}, u32[]{:S(2)}, u32[]{:S(2)}) collective-permute-start(bf16[2,4,256,512]{3,2,1,0:T(8,128)(2,1)} %fusion.153), channel_id=1, source_target_pairs={{2,0},{4,2},{6,4},{3,1},{5,3},{7,5},{10,8},{12,10},{14,12},{11,9},... | collective-permute-start | bytes 6291464 | tf_op jit(solution)/shard_map/while/body/eval_jaxpr/ppermute | solution.py:14
  1397.3 151.5 %reduce-scatter.33.cloned.1.call-start = ((), (), s32[]{:S(2)}) async-start(), calls=%async_computation.29 | async-start | bytes 278528
  1416.5 159.7 %all-reduce.18.cloned.1.call-start = ((), (), s32[]{:S(2)}) async-start(), calls=%async_computation.30 | async-start | bytes 8388608 | tf_op jit(solution)/shard_map/psum | solution.py:197
  1445.3 319.4 %reduce-scatter.17.cloned.1.call-start = ((), (), s32[]{:S(2)}) async-start(), calls=%async_computation.21 | async-start | bytes 8912896 | tf_op jit(solution)/shard_map/reduce_scatter | solution.py:288
  1453.8 493.7 %reduce-scatter.15.cloned.1.call-start = ((), (), s32[]{:S(2)}) async-start(), calls=%async_computation.20 | async-start | bytes 8912896 | tf_op jit(solution)/shard_map/reduce_scatter | solution.py:287
  1459.7 838.2 %reduce-scatter.25.cloned.1.call-start = ((), (), s32[]{:S(2)}) async-start(), calls=%async_computation.25 | async-start | bytes 17825792 | tf_op jit(solution)/shard_map/reduce_scatter | solution.py:222
  1472.4 1177.4 %reduce-scatter.27.cloned.1.call-start = ((), (), s32[]{:S(2)}) async-start(), calls=%async_computation.26 | async-start | bytes 17825792 | tf_op jit(solution)/shard_map/reduce_scatter | solution.py:223
  1485.0 1516.6 %reduce-scatter.29.cloned.1.call-start = ((), (), s32[]{:S(2)}) async-start(), calls=%async_computation.27 | async-start | bytes 17825792 | tf_op jit(solution)/shard_map/reduce_scatter | solution.py:224
  1498.0 1855.7 %reduce-scatter.23.cloned.1.call-start = ((), (), s32[]{:S(2)}) async-start(), calls=%async_computation.24 | async-start | bytes 17825792 | tf_op jit(solution)/shard_map/reduce_scatter | solution.py:291
  1510.6 2194.9 %reduce-scatter.19.cloned.1.call-start = ((), (), s32[]{:S(2)}) async-start(), calls=%async_computation.22 | async-start | bytes 17825792 | tf_op jit(solution)/shard_map/reduce_scatter | solution.py:289
  1520.5 2537.0 %reduce-scatter.21.cloned.1.call-start = ((), (), s32[]{:S(2)}) async-start(), calls=%async_computation.23 | async-start | bytes 17825792 | tf_op jit(solution)/shard_map/reduce_scatter | solution.py:290
  1530.7 45.6 %copy-start.4 = (bf16[2,256,2048]{2,1,0:T(8,128)(2,1)S(1)}, bf16[2,256,2048]{2,1,0:T(8,128)(2,1)}, u32[]{:S(2)}) copy-start(bf16[2,256,2048]{2,1,0:T(8,128)(2,1)} %param.21) | copy-start | bytes 6291460
  1530.7 45.6 %copy-start.46 = (f32[16,1,128]{2,1,0:T(1,128)S(1)}, f32[16,1,128]{2,1,0:T(1,128)}, u32[]{:S(2)}) copy-start(f32[16,1,128]{2,1,0:T(1,128)} %copy-done.45) | copy-start | bytes 24580
  1530.7 45.6 %copy-start.50 = (f32[1,2,2,128]{3,1,2,0:T(2,128)S(1)}, f32[1,2,2,128]{3,1,2,0:T(2,128)}, u32[]{:S(2)}) copy-start(f32[1,2,2,128]{3,1,2,0:T(2,128)} %copy-done.49) | copy-start | bytes 6148
  1530.7 48.5 %copy-start.58 = (f32[1,2,2,128]{3,1,2,0:T(2,128)S(1)}, f32[1,2,2,128]{3,1,2,0:T(2,128)}, u32[]{:S(2)}) copy-start(f32[1,2,2,128]{3,1,2,0:T(2,128)} %copy-done.57) | copy-start | bytes 6148
  1530.8 48.5 %copy-start.52 = (f32[512]{0:T(512)S(1)}, f32[512]{0:T(512)}, u32[]{:S(2)}) copy-start(f32[512]{0:T(512)} %copy-done.51) | copy-start | bytes 6148
  1576.3 90.0 %copy-start.56 = (f32[1,2,2,128]{3,1,2,0:T(2,128)S(1)}, f32[1,2,2,128]{3,1,2,0:T(2,128)}, u32[]{:S(2)}) copy-start(f32[1,2,2,128]{3,1,2,0:T(2,128)} %copy-done.55) | copy-start | bytes 6148
  1576.3 90.0 %copy-start.60 = (f32[512]{0:T(512)S(1)}, f32[512]{0:T(512)}, u32[]{:S(2)}) copy-start(f32[512]{0:T(512)} %copy-done.59) | copy-start | bytes 6148
  (58 other events, 387.0 us)
Sparse Core Ops, SparseCore 0:
  10.8 78.7 all-gather.20
  92.3 74.6 all-gather.18
  169.8 111.4 all-gather.16
  283.9 111.0 all-gather.14
  397.5 206.0 all-gather.22
  706.7 29.6 all-reduce.13
  739.6 114.0 all-gather.24
  856.9 111.0 all-gather.26
  971.0 140.5 all-gather.28
  1139.7 26.6 all-reduce.15
  1397.4 76.5 reduce-scatter.30
  1476.2 72.5 reduce-scatter.32
  1551.4 24.8 all-reduce.17
  1579.1 185.5 reduce-scatter.16
  1767.5 179.9 reduce-scatter.14
  1950.3 347.5 reduce-scatter.24
  2300.8 348.9 reduce-scatter.26
  2652.6 348.9 reduce-scatter.28
  3004.6 348.9 reduce-scatter.22
  3356.5 348.9 reduce-scatter.18
  3708.5 348.9 reduce-scatter.20
where the time goes:
time: 4070 us; the launch traced here: 4060 us
  waiting for transfers between devices  3280 us (81%)
  blocking collectives  310 us (8%)
  matrix products  252 us (6%)
  other arithmetic  104 us (3%)
  local copies, waits for them, and re-layouts  74.4 us (2%)
    reduce_scatter x1, waiting for transfers between devices, shards(): lax.psum_scatter(grad_swish, ('fsdp', 'ctx'), scatter_dimension=0, tiled=...  352 us
    reduce_scatter x1, waiting for transfers between devices, shards(): lax.psum_scatter(grad_out, ('fsdp', 'ctx'), scatter_dimension=1, tiled=True)  352 us
    reduce_scatter x1, waiting for transfers between devices, shards(): lax.psum_scatter(grad_down, ('fsdp', 'ctx'), scatter_dimension=1, tiled=T...  352 us
    reduce_scatter x1, waiting for transfers between devices, shards(): lax.psum_scatter(grad_up, ('fsdp', 'ctx'), scatter_dimension=0, tiled=True)  352 us
    reduce_scatter x1, waiting for transfers between devices, shards(): lax.psum_scatter(grad_value, ('fsdp', 'ctx'), scatter_dimension=0, tiled=...  352 us
    reduce_scatter x1, waiting for transfers between devices, shards(): lax.psum_scatter(grad_gelu, ('fsdp', 'ctx'), scatter_dimension=0, tiled=T...  350 us
    ppermute x6, waiting for transfers between devices, passed_along(): return lax.ppermute(value, axis, pairs)  349 us
    reduce_scatter x1, waiting for transfers between devices, shards(): lax.psum_scatter(grad_query, ('fsdp', 'ctx'), scatter_dimension=0, tiled=...  183 us
  transfers between devices with their start and end apart: 27, of which 22 were waited for; matrix products, arithmetic and copies ran while one was open for 7% of the time, Pallas kernels for 0%

commit v1 on v0

v1 whole, which is shorter than its diff:
```python
import jax
import jax.numpy as jnp
from jax import lax
from jax.sharding import PartitionSpec as P

eps = 1e-05
group_floor = 1.0
f32 = jnp.float32
bf16 = jnp.bfloat16


def layer_norm(values, norm_gain, norm_shift):
    centred = values - jnp.mean(values, -1, keepdims=True)
    spread = jnp.mean(centred * centred, -1, keepdims=True)
    return centred * lax.rsqrt(spread + eps) * norm_gain + norm_shift


def turn_tables(positions, half_size):
    frequency = jnp.power(10000.0, -jnp.arange(half_size).astype(f32) / half_size)
    angles = positions.astype(f32)[:, None] * frequency[None, :]
    return jnp.cos(angles), jnp.sin(angles)


def rotate(values, cosine, sine):
    half_size = values.shape[-1] // 2
    first = values[..., :half_size]
    second = values[..., half_size:]
    return jnp.concatenate([first * cosine - second * sine, second * cosine + first * sine], -1)


def rotate_back(values, cosine, sine):
    return rotate(values, cosine, -sine)


def gate_mix(mixed, swish_pre, norm_gain, norm_shift):
    centred = mixed - jnp.mean(mixed, -1, keepdims=True)
    spread = jnp.mean(centred * centred, -1, keepdims=True)
    return jax.nn.silu(swish_pre) * (
        centred * lax.rsqrt(spread + group_floor) * norm_gain + norm_shift
    )


def mlp_mix(gelu_pre, up_pre):
    return jax.nn.gelu(gelu_pre) * up_pre


def product(left, right):
    return jnp.dot(left, right, preferred_element_type=f32)


def product_left(left, right):
    return lax.dot_general(left, right, (((0,), (0,)), ((), ())), preferred_element_type=f32)


def product_right(left, right):
    return lax.dot_general(left, right, (((1,), (1,)), ((), ())), preferred_element_type=f32)


def blocks(spec, left, right):
    return jnp.einsum(spec, left, right, preferred_element_type=f32)


def gather_rows(own):
    return lax.all_gather(own, ("fsdp", "tp"), axis=0, tiled=True)


def scatter_rows(partial):
    return lax.psum_scatter(partial, ("fsdp", "tp"), scatter_dimension=0, tiled=True)


def pass_states(local, fade, by):
    length = lax.axis_size("ctx")
    pairs = [(i, i + by) for i in range(length) if 0 <= i + by < length]

    def step(turn, received):
        return lax.ppermute((fade * received.astype(f32) + local).astype(bf16), "ctx", pairs)

    return lax.fori_loop(0, length - 1, step, jnp.zeros(local.shape, bf16))


def shards(
    tokens,
    lengths,
    cotangent,
    pre_gain,
    pre_bias,
    query_weight,
    key_weight,
    value_weight,
    swish_weight,
    out_weight,
    group_gain,
    group_bias,
    mlp_gain,
    mlp_bias,
    gelu_weight,
    up_weight,
    down_weight,
):
    seq_count, span, width = tokens.shape
    nf, nc, nt = lax.axis_size("fsdp"), lax.axis_size("ctx"), lax.axis_size("tp")
    f, c, t = lax.axis_index("fsdp"), lax.axis_index("ctx"), lax.axis_index("tp")
    block_rows = seq_count * span
    own_rows = block_rows // nt
    depth = query_weight.shape[0]
    heads_local = group_gain.shape[0]
    assert heads_local == nf
    key_size = query_weight.shape[1] // heads_local
    value_size = value_weight.shape[1] // heads_local
    hidden_size = gelu_weight.shape[1] // nf
    seqs = nf * seq_count
    rows = seqs * span
    head = t * heads_local + f

    def perm(v):
        return v.reshape(-1, nf, nc, depth).transpose(0, 2, 1, 3).reshape(-1, width)

    def unperm(v):
        return v.reshape(-1, nc, nf, depth).transpose(0, 2, 1, 3).reshape(-1, width)

    def own_part(v):
        return lax.dynamic_slice_in_dim(v.reshape(block_rows, width), t * own_rows, own_rows, 0)

    def spread(w):
        return w.reshape(depth, nf, -1).transpose(1, 0, 2)

    def full_weights(*ws):
        mine = jnp.concatenate([spread(w) for w in ws], -1)
        mine = lax.all_to_all(mine, "fsdp", 0, 0, tiled=True)
        return lax.all_gather(mine, "ctx", axis=0, tiled=True).reshape(width, -1)

    attn_w = full_weights(query_weight, key_weight, value_weight, swish_weight)
    rest_w = full_weights(out_weight.T, gelu_weight, up_weight, down_weight.T)
    out_t = rest_w[:, :value_size]
    gelu_up = rest_w[:, value_size : value_size + 2 * hidden_size]
    down_t = rest_w[:, value_size + 2 * hidden_size :]

    small = jnp.concatenate(
        [
            jnp.stack([pre_gain, pre_bias, mlp_gain, mlp_bias]).astype(f32).reshape(-1),
            group_gain.astype(f32).reshape(-1),
            group_bias.astype(f32).reshape(-1),
            lengths.astype(f32),
        ]
    )
    small = lax.all_gather(small, ("fsdp", "ctx"), axis=0)
    pre_gain_full, pre_bias_full, mlp_gain_full, mlp_bias_full = (
        small[:, i * depth : (i + 1) * depth].reshape(width) for i in range(4)
    )
    group = small[:, 4 * depth : 4 * depth + 2 * group_gain.size].reshape(
        nf * nc, 2, heads_local, -1
    )
    group = lax.dynamic_index_in_dim(group, f, 2, False).transpose(1, 0, 2).reshape(2, value_size)
    all_lengths = small.reshape(nf, nc, -1)[:, 0, -seq_count:].reshape(seqs)

    inputs = own_part(tokens).astype(f32)
    normed_wide, norm_in_back = jax.vjp(layer_norm, inputs, pre_gain_full, pre_bias_full)
    normed = gather_rows(perm(normed_wide.astype(bf16)))
    positions = c * span + lax.iota(jnp.int32, span)
    own_ids = t * own_rows + lax.iota(jnp.int32, own_rows)
    own_valid = (c * span + own_ids % span < lengths[own_ids // span]).astype(f32)[:, None]
    error = own_valid * own_part(cotangent).astype(f32)
    error_all = gather_rows(perm(error.astype(bf16)))

    pre = product(normed, attn_w)
    valid = (positions.astype(f32)[None, :] < all_lengths[:, None]).astype(f32)[:, :, None]
    cosine, sine = turn_tables(positions, key_size // 2)
    key_scale = key_size ** (-0.5)
    query_pre = pre[:, :key_size].reshape(seqs, span, key_size)
    key_pre = pre[:, key_size : 2 * key_size].reshape(seqs, span, key_size)
    value_pre = pre[:, 2 * key_size : 2 * key_size + value_size]
    swish_pre = pre[:, 2 * key_size + value_size :]
    queries = rotate(query_pre, cosine, sine).astype(bf16)
    keys = (rotate(key_pre, cosine, sine) * key_scale * valid).astype(bf16)
    values = value_pre.astype(bf16).reshape(seqs, span, value_size)

    log_decay = jnp.log1p(-jnp.exp2(-5.0 - head.astype(f32)))
    offsets = jnp.arange(span)
    distance = (offsets[:, None] - offsets[None, :]).astype(f32)
    within_fade = jnp.where(distance >= 0, jnp.exp(jnp.maximum(distance, 0.0) * log_decay), 0.0)
    key_fade = jnp.exp((span - 1 - offsets).astype(f32) * log_decay)[:, None]
    query_fade = jnp.exp((offsets + 1).astype(f32) * log_decay)[:, None]
    block_fade = jnp.exp(span * log_decay)

    keys_faded = (keys.astype(f32) * key_fade).astype(bf16)
    queries_faded = (queries.astype(f32) * query_fade).astype(bf16)
    local_state = blocks("sjd,sje->sde", keys_faded, values)
    entering = pass_states(local_state, block_fade, 1)
    probs = (blocks("sid,sjd->sij", queries, keys) * within_fade).astype(bf16)
    mixed = blocks("sij,sje->sie", probs, values) + blocks("sid,sde->sie", queries_faded, entering)
    gated_wide, gate_back = jax.vjp(
        gate_mix, mixed.reshape(rows, value_size), swish_pre, group[0], group[1]
    )
    gated = gated_wide.astype(bf16)
    branch = scatter_rows(product_right(gated, out_t).astype(bf16))
    hidden = inputs + unperm(branch.astype(f32))

    mlp_wide, norm_mid_back = jax.vjp(layer_norm, hidden, mlp_gain_full, mlp_bias_full)
    mlp_in = gather_rows(perm(mlp_wide.astype(bf16)))
    pre_ff = product(mlp_in, gelu_up)
    inner_wide, mix_back = jax.vjp(mlp_mix, pre_ff[:, :hidden_size], pre_ff[:, hidden_size:])
    inner = inner_wide.astype(bf16)
    mlp_out = scatter_rows(product_right(inner, down_t).astype(bf16))
    block_own = (own_valid * (hidden + unperm(mlp_out.astype(f32)))).astype(bf16)
    block_out = lax.all_gather(block_own, "tp", axis=0, tiled=True).reshape(tokens.shape)

    def to_owners(grads):
        mine = lax.psum_scatter(grads.astype(bf16), "ctx", scatter_dimension=0, tiled=True)
        return lax.all_to_all(mine.reshape(nf, depth, -1), "fsdp", 0, 0, tiled=True).astype(f32)

    def along(grads):
        return grads.transpose(1, 0, 2).reshape(depth, -1)

    def across(grads):
        return grads.transpose(0, 2, 1).reshape(-1, depth)

    grad_down_t = product_left(error_all, inner)
    gelu_grad, up_grad = mix_back(product(error_all, down_t))
    ff_low = jnp.concatenate([gelu_grad.astype(bf16), up_grad.astype(bf16)], -1)
    grad_gelu_up = product_left(mlp_in, ff_low)
    ff_grads = to_owners(jnp.concatenate([grad_gelu_up, grad_down_t], -1))
    mlp_in_grad = unperm(scatter_rows(product_right(ff_low, gelu_up).astype(bf16)).astype(f32))
    hidden_norm_grad, grad_mlp_gain, grad_mlp_bias = norm_mid_back(mlp_in_grad)
    hidden_grad = error + hidden_norm_grad

    hidden_low = gather_rows(perm(hidden_grad.astype(bf16)))
    grad_out_t = product_left(hidden_low, gated)
    gated_grad = product(hidden_low, out_t)
    mixed_grad, swish_grad, grad_group_gain, grad_group_bias = gate_back(gated_grad)
    swish_low = swish_grad.astype(bf16)
    mixed_low = mixed_grad.astype(bf16).reshape(seqs, span, value_size)
    score_low = (blocks("sie,sje->sij", mixed_low, values) * within_fade).astype(bf16)
    pulled_state = blocks("sid,sie->sde", queries_faded, mixed_low)
    later = pass_states(pulled_state, block_fade, -1)
    query_grad = blocks("sij,sjd->sid", score_low, keys) + query_fade * blocks(
        "sie,sde->sid", mixed_low, entering
    )
    key_grad = blocks("sij,sid->sjd", score_low, queries) + key_fade * blocks(
        "sje,sde->sjd", values, later
    )
    value_grad = blocks("sij,sie->sje", probs, mixed_low) + blocks(
        "sjd,sde->sje", keys_faded, later
    )
    query_low = rotate_back(query_grad, cosine, sine).astype(bf16).reshape(rows, key_size)
    key_low = rotate_back(key_grad * key_scale * valid, cosine, sine).astype(bf16)
    low = jnp.concatenate(
        [
            query_low,
            key_low.reshape(rows, key_size),
            value_grad.astype(bf16).reshape(rows, value_size),
            swish_low,
        ],
        -1,
    )
    grad_attn = product_left(normed, low)
    attn_grads = to_owners(jnp.concatenate([grad_attn, grad_out_t], -1))
    normed_grad = unperm(scatter_rows(product_right(low, attn_w).astype(bf16)).astype(f32))
    input_norm_grad, grad_pre_gain, grad_pre_bias = norm_in_back(normed_grad)
    tokens_own = (hidden_grad + input_norm_grad).astype(bf16)
    grad_tokens = lax.all_gather(tokens_own, "tp", axis=0, tiled=True).reshape(tokens.shape)

    mine = (lax.iota(jnp.int32, nt * heads_local) == head).astype(f32)[:, None]
    sums = jnp.concatenate(
        [
            grad_pre_gain,
            grad_pre_bias,
            grad_mlp_gain,
            grad_mlp_bias,
            (mine * grad_group_gain[None]).reshape(-1),
            (mine * grad_group_bias[None]).reshape(-1),
        ]
    )
    sums = lax.psum(sums, ("fsdp", "ctx", "tp"))
    place = f * nc + c
    norm_sums = lax.dynamic_index_in_dim(
        sums[: 4 * width].reshape(4, nf * nc, depth), place, 1, False
    )
    group_sums = sums[4 * width :].reshape(2, nt, heads_local, nf * nc, -1)
    group_sums = lax.dynamic_index_in_dim(group_sums, t, 1, False)
    group_sums = lax.dynamic_index_in_dim(group_sums, place, 2, False)

    at = [0, key_size, 2 * key_size, 2 * key_size + value_size, 2 * key_size + 2 * value_size]
    return (
        block_out,
        grad_tokens,
        norm_sums[0],
        norm_sums[1],
        along(attn_grads[..., : at[1]]),
        along(attn_grads[..., at[1] : at[2]]),
        along(attn_grads[..., at[2] : at[3]]),
        along(attn_grads[..., at[3] : at[4]]),
        across(attn_grads[..., at[4] :]),
        group_sums[0],
        group_sums[1],
        norm_sums[2],
        norm_sums[3],
        along(ff_grads[..., :hidden_size]),
        along(ff_grads[..., hidden_size : 2 * hidden_size]),
        across(ff_grads[..., 2 * hidden_size :]),
    )


def solution(mesh):
    rows = P("fsdp", "ctx", None)
    vector = P(("fsdp", "ctx"))
    tall = P(("fsdp", "ctx"), "tp")
    wide = P("tp", ("fsdp", "ctx"))
    in_specs = (rows, P("fsdp"), rows, vector, vector, tall, tall, tall, tall, wide)
    in_specs += (wide, wide, vector, vector, tall, tall, wide)
    out_specs = (rows, rows, vector, vector, tall, tall, tall, tall, wide)
    out_specs += (wide, wide, vector, vector, tall, tall, wide)
    return jax.shard_map(shards, mesh=mesh, in_specs=in_specs, out_specs=out_specs, check_vma=False)
```

time: 4070 us -> 1660 us (0.41)
  waiting for transfers between devices: 3280 us -> 1100 us
  blocking collectives: 310 us -> 122 us
  matrix products: 252 us -> 178 us
    reduce_scatter x8 -> x6, waiting for transfers between devices: 2380 us -> 367 us  [the longest x4 236 us: scatter_rows(): lax.psum_scatter(partial, ('fsdp', 'tp'), scatter_dimension=0, tiled=True)]
    all_gather x8, waiting for transfers between devices: 482 us -> 194 us  [the longest x4 181 us: gather_rows(): return lax.all_gather(own, ('fsdp', 'tp'), axis=0, tiled=True)]
    all_gather x6 -> x0, blocking collectives: 228 us -> none  [the longest x1 42.5 us: shards(): lax.all_gather(pre_gain, ('fsdp', 'ctx'), axis=0, tiled=True)]
    psum x3 -> x1, waiting for transfers between devices: 41.2 us -> 121 us  [shards(): sums = lax.psum(sums, ('fsdp', 'ctx', 'tp'))]
    ppermute x6, waiting for transfers between devices: 349 us -> 415 us  [step(): lax.ppermute((fade * received.astype(f32) + local).astype(bf16), 'ctx', p...]
    all_to_all x0 -> x2, blocking collectives: none -> 43.6 us  [full_weights(): mine = lax.all_to_all(mine, 'fsdp', 0, 0, tiled=True)]
    dot_general x8 -> x4, matrix products: 82.7 us -> 49 us  [product_left(): lax.dot_general(left, right, (((0,), (0,)), ((), ())), preferred_element_...]
    dot_general x20 -> x16, matrix products: 107 us -> 81.9 us  [the longest x4 59 us: product(): return jnp.dot(left, right, preferred_element_type=f32)]
  transfers between devices with their start and end apart: 27 -> 23, of which waited for: 22 -> 18; matrix products, arithmetic and copies ran while one was open for 7% -> 16% of each run, Pallas kernels for 0% -> 0%
where the time goes in v1:
time: 1660 us; the launch traced here: 1650 us
  waiting for transfers between devices  1100 us (66%)
  matrix products  178 us (11%)
  blocking collectives  122 us (7%)
  local copies, waits for them, and re-layouts  105 us (6%)
  other arithmetic  69.6 us (4%)
  starting transfers between devices  65.6 us (4%)
    ppermute x6, waiting for transfers between devices, step(): lax.ppermute((fade * received.astype(f32) + local).astype(bf16), 'ctx', p...  415 us
    reduce_scatter x4, waiting for transfers between devices, scatter_rows(): lax.psum_scatter(partial, ('fsdp', 'tp'), scatter_dimension=0, tiled=True)  236 us
    all_gather x4, waiting for transfers between devices, gather_rows(): return lax.all_gather(own, ('fsdp', 'tp'), axis=0, tiled=True)  181 us
    reduce_scatter x2, waiting for transfers between devices, to_owners(): lax.psum_scatter(grads.astype(bf16), 'ctx', scatter_dimension=0, tiled=True)  130 us
    psum x1, waiting for transfers between devices, shards(): sums = lax.psum(sums, ('fsdp', 'ctx', 'tp'))  121 us
    unnamed x1, blocking collectives  78.4 us
    dot_general x4, matrix products, product(): return jnp.dot(left, right, preferred_element_type=f32)  59 us
    ppermute x6, starting transfers between devices, step(): lax.ppermute((fade * received.astype(f32) + local).astype(bf16), 'ctx', p...  56.5 us
  transfers between devices with their start and end apart: 23, of which 18 were waited for; matrix products, arithmetic and copies ran while one was open for 16% of the time, Pallas kernels for 0%

profile of v1, /device:TPU:0, one launch (start us, length us, event | category | flops | bytes accessed | tf_op | source)
XLA Modules:
  0.0 1654.9 jit_solution(7174689534238034317)
XLA Ops:
  14.0 24.8 %all_to_all.20 = bf16[4,128,1536]{1,2,0:T(8,128)(2,1)} all-to-all(bf16[4,128,1536]{1,2,0:T(8,128)(2,1)S(1)} %pad_maximum_fusion.6), channel_id=1, replica_groups=mesh['fsdp'=4,'ctx'=4,'tp'=2] {'fsdp'}, dimensions={0} | all-to-all | bytes 3145728 | tf_op jit(solution)/shard_map/all_to_all | solution.py:129
  45.9 78.4 %all-reduce = f32[12320]{0:T(1024)S(1)} all-reduce(f32[12320]{0:T(1024)S(1)} %maximum_dynamic-update-slice_fusion), channel_id=2, replica_groups=mesh['fsdp'=4,'ctx'=4,'tp'=2] {'fsdp','ctx'}, use_global_device_ids=true, to_apply=%add | all-reduce | flops 12320 | bytes 98560
  131.2 18.8 %all_to_all.21 = bf16[4,128,2048]{1,2,0:T(8,128)(2,1)} all-to-all(bf16[4,128,2048]{1,2,0:T(8,128)(2,1)S(1)} %pad_maximum_fusion.5), channel_id=1, replica_groups=mesh['fsdp'=4,'ctx'=4,'tp'=2] {'fsdp'}, dimensions={0} | all-to-all | bytes 4194304 | tf_op jit(solution)/shard_map/all_to_all | solution.py:129
  150.0 3.9 copy.124
  158.9 56.8 %all-gather.10.cloned.1.call-done = bf16[2048,2048]{0,1:T(8,128)(2,1)} async-done(((bf16[256,2048]{0,1:T(8,128)(2,1)}), bf16[2048,2048]{0,1:T(8,128)(2,1)}) %all-gather.10.cloned.1.call-update) | async-done | bytes 8388624 | tf_op jit(solution)/shard_map/all_gather | solution.py:64
  215.7 17.5 %fusion.66 = f32[2048,1536]{1,0:T(8,128)S(1)} fusion(bf16[2048,2048]{0,1:T(8,128)(2,1)} %all-gather.10.cloned.1.call-done, bf16[2048,1536]{1,0:T(8,128)(2,1)} %bitcast.296), kind=kOutput, calls=%fused_computation.197 | convolution fusion | flops 12884901888 | bytes 27262976 | tf_op jit(solution)/shard_map/dot_general | solution.py:48
  245.8 260.8 %while.20 = (s32[]{:T(128)}, bf16[8,256,512]{2,1,0:T(8,128)(2,1)S(1)}, f32[]{:T(128)}, f32[8,256,512]{2,1,0:T(8,128)}, s32[]{:T(128)}) while((s32[]{:T(128)}, bf16[8,256,512]{2,1,0:T(8,128)(2,1)S(1)}, f32[]{:T(128)}, f32[8,256,512]{2,1,0:T(8,128)}, s32[]{:T(128)}) %tuple.82), condition=%wide.region_3.4_spmd, body=%wide.region_2.3_spmd.sunk | while | flops 4194306 | bytes 16777320 | solution.py:78
  245.8 4.3 add_convert_fusion.12
  253.6 90.8 %collective-permute-done = bf16[8,256,512]{2,1,0:T(8,128)(2,1)S(1)} collective-permute-done((bf16[8,256,512]{2,1,0:T(8,128)(2,1)}, bf16[8,256,512]{2,1,0:T(8,128)(2,1)S(1)}, u32[]{:S(2)}, u32[]{:S(2)}) %collective-permute-start) | collective-permute-done | bytes 2097184 | tf_op jit(solution)/shard_map/while/body/eval_jaxpr/ppermute | solution.py:76
  344.4 4.2 add_convert_fusion.12
  348.6 44.7 %collective-permute-start = (bf16[8,256,512]{2,1,0:T(8,128)(2,1)}, bf16[8,256,512]{2,1,0:T(8,128)(2,1)S(1)}, u32[]{:S(2)}, u32[]{:S(2)}) collective-permute-start(bf16[8,256,512]{2,1,0:T(8,128)(2,1)} %add_convert_fusion.12), channel_id=1, source_target_pairs={{0,2},{2,4},{4,6},{1,3},{3,5},{5,7},{8,10},{10,12},{12,14},{9,11},... | collective-permute-start | bytes 6291464 | tf_op jit(solution)/shard_map/while/body/eval_jaxpr/ppermute | solution.py:76
  393.4 59.6 %collective-permute-done = bf16[8,256,512]{2,1,0:T(8,128)(2,1)S(1)} collective-permute-done((bf16[8,256,512]{2,1,0:T(8,128)(2,1)}, bf16[8,256,512]{2,1,0:T(8,128)(2,1)S(1)}, u32[]{:S(2)}, u32[]{:S(2)}) %collective-permute-start) | collective-permute-done | bytes 2097184 | tf_op jit(solution)/shard_map/while/body/eval_jaxpr/ppermute | solution.py:76
  453.0 4.2 add_convert_fusion.12
  457.2 4.4 collective-permute-start
  461.6 44.9 %collective-permute-done = bf16[8,256,512]{2,1,0:T(8,128)(2,1)S(1)} collective-permute-done((bf16[8,256,512]{2,1,0:T(8,128)(2,1)}, bf16[8,256,512]{2,1,0:T(8,128)(2,1)S(1)}, u32[]{:S(2)}, u32[]{:S(2)}) %collective-permute-start) | collective-permute-done | bytes 2097184 | tf_op jit(solution)/shard_map/while/body/eval_jaxpr/ppermute | solution.py:76
  506.5 4.1 fusion.65
  516.0 9.1 convolution_convert_fusion.3
  525.2 73.3 %reduce-scatter.7.cloned.1.call-done = bf16[256,2048]{1,0:T(8,128)(2,1)} async-done(((bf16[2048,2048]{1,0:T(8,128)(2,1)}), bf16[256,2048]{1,0:T(8,128)(2,1)}) %reduce-scatter.7.cloned.1.call-update) | async-done | bytes 1048592 | tf_op jit(solution)/shard_map/reduce_scatter | solution.py:68
  614.8 48.9 %all-gather.16.cloned.1.call-done = bf16[2048,2048]{0,1:T(8,128)(2,1)} async-done(((bf16[256,2048]{0,1:T(8,128)(2,1)}), bf16[2048,2048]{0,1:T(8,128)(2,1)}) %all-gather.16.cloned.1.call-update) | async-done | bytes 8388624 | tf_op jit(solution)/shard_map/all_gather | solution.py:64
  663.7 14.7 fusion.12
  678.4 43.8 %all-gather.20.cloned.1.call-done = bf16[2048,2048]{0,1:T(8,128)(2,1)} async-done(((bf16[256,2048]{0,1:T(8,128)(2,1)}), bf16[2048,2048]{0,1:T(8,128)(2,1)}) %all-gather.20.cloned.1.call-update) | async-done | bytes 8388624 | tf_op jit(solution)/shard_map/all_gather | solution.py:64
  722.2 13.6 fusion.6
  737.0 8.4 convolution_convert_fusion.2
  745.5 14.4 convolution_convert_fusion.1
  760.0 57.0 %reduce-scatter.9.cloned.1.call-done = bf16[256,2048]{1,0:T(8,128)(2,1)} async-done(((bf16[2048,2048]{1,0:T(8,128)(2,1)}), bf16[256,2048]{1,0:T(8,128)(2,1)}) %reduce-scatter.9.cloned.1.call-update) | async-done | bytes 1048592 | tf_op jit(solution)/shard_map/reduce_scatter | solution.py:68
  823.6 68.1 %reduce-scatter.11.cloned.1.call-done = bf16[256,2048]{1,0:T(8,128)(2,1)} async-done(((bf16[2048,2048]{1,0:T(8,128)(2,1)}), bf16[256,2048]{1,0:T(8,128)(2,1)}) %reduce-scatter.11.cloned.1.call-update) | async-done | bytes 1048592 | tf_op jit(solution)/shard_map/reduce_scatter | solution.py:68
  905.9 8.7 convolution_convert_fusion.6
  914.6 11.8 convolution_convert_fusion.5
  930.4 31.3 %all-gather.22.cloned.1.call-done = bf16[2048,2048]{0,1:T(8,128)(2,1)} async-done(((bf16[256,2048]{0,1:T(8,128)(2,1)}), bf16[2048,2048]{0,1:T(8,128)(2,1)}) %all-gather.22.cloned.1.call-update) | async-done | bytes 8388624 | tf_op jit(solution)/shard_map/all_gather | solution.py:64
  961.7 13.2 multiply_reduce_fusion
  988.2 236.9 %while.21 = (s32[]{:T(128)}, bf16[8,256,512]{2,1,0:T(8,128)(2,1)S(1)}, f32[]{:T(128)}, f32[8,256,512]{2,1,0:T(8,128)}, s32[]{:T(128)}) while((s32[]{:T(128)}, bf16[8,256,512]{2,1,0:T(8,128)(2,1)S(1)}, f32[]{:T(128)}, f32[8,256,512]{2,1,0:T(8,128)}, s32[]{:T(128)}) %tuple.85), condition=%wide.region_16.17_spmd, body=%wide.region_15.16_spmd.sunk | while | flops 4194306 | bytes 16777320 | solution.py:78
  988.2 4.3 add_convert_fusion.13
  993.8 124.2 %collective-permute-done.1 = bf16[8,256,512]{2,1,0:T(8,128)(2,1)S(1)} collective-permute-done((bf16[8,256,512]{2,1,0:T(8,128)(2,1)}, bf16[8,256,512]{2,1,0:T(8,128)(2,1)S(1)}, u32[]{:S(2)}, u32[]{:S(2)}) %collective-permute-start.1) | collective-permute-done | bytes 2097184 | tf_op jit(solution)/shard_map/while/body/eval_jaxpr/ppermute | solution.py:76
  1118.0 4.3 add_convert_fusion.13
  1123.6 48.2 %collective-permute-done.1 = bf16[8,256,512]{2,1,0:T(8,128)(2,1)S(1)} collective-permute-done((bf16[8,256,512]{2,1,0:T(8,128)(2,1)}, bf16[8,256,512]{2,1,0:T(8,128)(2,1)S(1)}, u32[]{:S(2)}, u32[]{:S(2)}) %collective-permute-start.1) | collective-permute-done | bytes 2097184 | tf_op jit(solution)/shard_map/while/body/eval_jaxpr/ppermute | solution.py:76
  1171.8 4.3 add_convert_fusion.13
  1177.4 47.4 %collective-permute-done.1 = bf16[8,256,512]{2,1,0:T(8,128)(2,1)S(1)} collective-permute-done((bf16[8,256,512]{2,1,0:T(8,128)(2,1)}, bf16[8,256,512]{2,1,0:T(8,128)(2,1)S(1)}, u32[]{:S(2)}, u32[]{:S(2)}) %collective-permute-start.1) | collective-permute-done | bytes 2097184 | tf_op jit(solution)/shard_map/while/body/eval_jaxpr/ppermute | solution.py:76
  1237.1 15.3 convolution_convert_fusion
  1254.0 10.1 convolution_convert_fusion.7
  1264.1 18.3 %convolution_convert_fusion.4 = bf16[2048,1536]{0,1:T(8,128)(2,1)} fusion(bf16[2048,2048]{0,1:T(8,128)(2,1)} %all-gather.10.cloned.1.call-done, bf16[2048,1536]{1,0:T(8,128)(2,1)S(1)} %copy-done.49), kind=kOutput, calls=%fused_computation.7 | convolution fusion | flops 12888047616 | bytes 20971520 | tf_op jit(solution)/shard_map/dot_general | solution.py:52
  1282.4 8.0 pad_maximum_fusion
  1293.4 4.5 all-to-all-start.3
  1298.8 38.1 %reduce-scatter.13.cloned.1.call-done = bf16[256,2048]{1,0:T(8,128)(2,1)} async-done(((bf16[2048,2048]{1,0:T(8,128)(2,1)}), bf16[256,2048]{1,0:T(8,128)(2,1)}) %reduce-scatter.13.cloned.1.call-update) | async-done | bytes 1048592 | tf_op jit(solution)/shard_map/reduce_scatter | solution.py:68
  1336.9 3.9 reshape.692
  1349.0 4.1 add_convert_fusion.4
  1353.2 130.4 %reduce-scatter.15.cloned.1.call-done = bf16[512,2048]{0,1:T(8,128)(2,1)} async-done(((bf16[2048,2048]{0,1:T(8,128)(2,1)}), bf16[512,2048]{0,1:T(8,128)(2,1)}) %reduce-scatter.15.cloned.1.call-update) | async-done | bytes 2097168 | tf_op jit(solution)/shard_map/reduce_scatter | solution.py:208
  1501.3 120.8 %all-reduce.3.cloned.1.call-done = f32[16384]{0:T(1024)} async-done(((f32[16384]{0:T(1024)}), f32[16384]{0:T(1024)}) %all-reduce.3.cloned.1.call-update) | async-done | bytes 65552 | tf_op jit(solution)/shard_map/psum | solution.py:273
  1624.1 11.1 all-gather.24.cloned.1.call-done
  (334 shorter events, 163.1 us)
Async XLA Ops:
  7.2 34.3 %copy-start = (bf16[2,256,2048]{2,1,0:T(8,128)(2,1)S(1)}, bf16[2,256,2048]{2,1,0:T(8,128)(2,1)}, u32[]{:S(2)}) copy-start(bf16[2,256,2048]{2,1,0:T(8,128)(2,1)} %param.21) | copy-start | bytes 6291460
  7.2 151.7 %all-gather.12.cloned.1.call-start = ((), (), s32[]{:S(2)}) async-start(), calls=%async_computation.11 | async-start | bytes 7864320 | tf_op jit(solution)/shard_map/all_gather | solution.py:130
  41.4 174.3 %all-gather.10.cloned.1.call-start = ((), (), s32[]{:S(2)}) async-start(), calls=%async_computation.10 | async-start | bytes 9437184 | tf_op jit(solution)/shard_map/all_gather | solution.py:64
  44.2 559.4 %copy-start.6 = (bf16[256,2048]{0,1:T(8,128)(2,1)}, bf16[256,2048]{0,1:T(8,128)(2,1)S(1)}, u32[]{:S(2)}) copy-start(bf16[256,2048]{0,1:T(8,128)(2,1)S(1)} %copy.160) | copy-start | bytes 3145732
  127.5 388.5 %all-gather.14.cloned.1.call-start = ((), (), s32[]{:S(2)}) async-start(), calls=%async_computation.12 | async-start | bytes 10485760 | tf_op jit(solution)/shard_map/all_gather | solution.py:130
  153.9 444.6 %reduce-scatter.7.cloned.1.call-start = ((), (), s32[]{:S(2)}) async-start(), calls=%async_computation.13 | async-start | bytes 9437184 | tf_op jit(solution)/shard_map/reduce_scatter | solution.py:68
  154.7 88.0 %copy-start.57 = (f32[256]{0:T(256)}, f32[256]{0:T(256)S(1)}, u32[]{:S(2)}) copy-start(f32[256]{0:T(256)S(1)} %get-tuple-element.192) | copy-start | bytes 3076
  154.8 351.8 %copy-start.59 = (f32[256]{0:T(256)}, f32[256]{0:T(256)S(1)}, u32[]{:S(2)}) copy-start(f32[256]{0:T(256)S(1)} %get-tuple-element.193) | copy-start | bytes 3076
  155.6 82.8 %copy-start.44 = (f32[8,256]{1,0:T(8,128)}, f32[8,256]{1,0:T(8,128)S(1)}, u32[]{:S(2)}) copy-start(f32[8,256]{1,0:T(8,128)S(1)} %compare_select_fusion) | copy-start | bytes 24580
  156.8 81.0 %copy-start.34 = (f32[256,128]{1,0:T(8,128)}, f32[256,128]{1,0:T(8,128)S(1)}, u32[]{:S(2)}) copy-start(f32[256,128]{1,0:T(8,128)S(1)} %get-tuple-element.185) | copy-start | bytes 393220
  233.2 4.6 copy-start.21
  233.5 9.2 copy-start.9
  250.1 94.3 %collective-permute-start = (bf16[8,256,512]{2,1,0:T(8,128)(2,1)}, bf16[8,256,512]{2,1,0:T(8,128)(2,1)S(1)}, u32[]{:S(2)}, u32[]{:S(2)}) collective-permute-start(bf16[8,256,512]{2,1,0:T(8,128)(2,1)} %add_convert_fusion.12), channel_id=1, source_target_pairs={{0,2},{2,4},{4,6},{1,3},{3,5},{5,7},{8,10},{10,12},{12,14},{9,11},... | collective-permute-start | bytes 6291464 | tf_op jit(solution)/shard_map/while/body/eval_jaxpr/ppermute | solution.py:76
  348.6 104.3 %collective-permute-start = (bf16[8,256,512]{2,1,0:T(8,128)(2,1)}, bf16[8,256,512]{2,1,0:T(8,128)(2,1)S(1)}, u32[]{:S(2)}, u32[]{:S(2)}) collective-permute-start(bf16[8,256,512]{2,1,0:T(8,128)(2,1)} %add_convert_fusion.12), channel_id=1, source_target_pairs={{0,2},{2,4},{4,6},{1,3},{3,5},{5,7},{8,10},{10,12},{12,14},{9,11},... | collective-permute-start | bytes 6291464 | tf_op jit(solution)/shard_map/while/body/eval_jaxpr/ppermute | solution.py:76
  457.2 49.3 %collective-permute-start = (bf16[8,256,512]{2,1,0:T(8,128)(2,1)}, bf16[8,256,512]{2,1,0:T(8,128)(2,1)S(1)}, u32[]{:S(2)}, u32[]{:S(2)}) collective-permute-start(bf16[8,256,512]{2,1,0:T(8,128)(2,1)} %add_convert_fusion.12), channel_id=1, source_target_pairs={{0,2},{2,4},{4,6},{1,3},{3,5},{5,7},{8,10},{10,12},{12,14},{9,11},... | collective-permute-start | bytes 6291464 | tf_op jit(solution)/shard_map/while/body/eval_jaxpr/ppermute | solution.py:76
  511.5 4.5 copy-start.46
  516.0 9.2 copy-start.30
  525.2 138.5 %all-gather.16.cloned.1.call-start = ((), (), s32[]{:S(2)}) async-start(), calls=%async_computation.14 | async-start | bytes 9437184 | tf_op jit(solution)/shard_map/all_gather | solution.py:64
  607.6 114.5 %all-gather.20.cloned.1.call-start = ((), (), s32[]{:S(2)}) async-start(), calls=%async_computation.17 | async-start | bytes 9437184 | tf_op jit(solution)/shard_map/all_gather | solution.py:64
  611.4 291.8 %copy-start.19 = (bf16[256,2048]{0,1:T(8,128)(2,1)}, bf16[256,2048]{0,1:T(8,128)(2,1)S(1)}, u32[]{:S(2)}) copy-start(bf16[256,2048]{0,1:T(8,128)(2,1)S(1)} %copy.161) | copy-start | bytes 3145732
  613.5 289.7 %copy-start.53 = (f32[256]{0:T(256)}, f32[256]{0:T(256)S(1)}, u32[]{:S(2)}) copy-start(f32[256]{0:T(256)S(1)} %compare_convert_fusion.1) | copy-start | bytes 3076
  614.8 202.2 %reduce-scatter.9.cloned.1.call-start = ((), (), s32[]{:S(2)}) async-start(), calls=%async_computation.15 | async-start | bytes 9437184 | tf_op jit(solution)/shard_map/reduce_scatter | solution.py:68
  745.5 146.2 %reduce-scatter.11.cloned.1.call-start = ((), (), s32[]{:S(2)}) async-start(), calls=%async_computation.18 | async-start | bytes 9437184 | tf_op jit(solution)/shard_map/reduce_scatter | solution.py:68
  759.9 201.8 %all-gather.22.cloned.1.call-start = ((), (), s32[]{:S(2)}) async-start(), calls=%async_computation.19 | async-start | bytes 9437184 | tf_op jit(solution)/shard_map/all_gather | solution.py:64
  905.6 384.9 %reduce-scatter.17.cloned.1.call-start = ((), (), s32[]{:S(2)}) async-start(), calls=%async_computation.24 | async-start | bytes 7864320 | tf_op jit(solution)/shard_map/reduce_scatter | solution.py:208
  905.9 8.7 copy-start.74
  905.9 8.7 copy-start.75
  930.1 44.8 %copy-start.47 = (f32[1,2,8,128]{3,1,2,0:T(2,128)S(1)}, f32[1,2,8,128]{3,1,2,0:T(2,128)}, u32[]{:S(2)}) copy-start(f32[1,2,8,128]{3,1,2,0:T(2,128)} %copy-done.46) | copy-start | bytes 24580
  930.1 406.7 %reduce-scatter.13.cloned.1.call-start = ((), (), s32[]{:S(2)}) async-start(), calls=%async_computation.20 | async-start | bytes 9437184 | tf_op jit(solution)/shard_map/reduce_scatter | solution.py:68
  961.7 13.2 copy-start.5
  977.2 8.5 copy-start.11
  988.2 237.0 %copy-start.45 = (f32[8,256]{1,0:T(8,128)S(1)}, f32[8,256]{1,0:T(8,128)}, u32[]{:S(2)}) copy-start(f32[8,256]{1,0:T(8,128)} %copy-done.44) | copy-start | bytes 24580
  988.2 237.0 %copy-start.58 = (f32[256]{0:T(256)S(1)}, f32[256]{0:T(256)}, u32[]{:S(2)}) copy-start(f32[256]{0:T(256)} %copy-done.57) | copy-start | bytes 3076
  992.5 125.5 %collective-permute-start.1 = (bf16[8,256,512]{2,1,0:T(8,128)(2,1)}, bf16[8,256,512]{2,1,0:T(8,128)(2,1)S(1)}, u32[]{:S(2)}, u32[]{:S(2)}) collective-permute-start(bf16[8,256,512]{2,1,0:T(8,128)(2,1)} %add_convert_fusion.13), channel_id=1, source_target_pairs={{2,0},{4,2},{6,4},{3,1},{5,3},{7,5},{10,8},{12,10},{14,12},{11,9},... | collective-permute-start | bytes 6291464 | tf_op jit(solution)/shard_map/while/body/eval_jaxpr/ppermute | solution.py:76
  1122.3 49.5 %collective-permute-start.1 = (bf16[8,256,512]{2,1,0:T(8,128)(2,1)}, bf16[8,256,512]{2,1,0:T(8,128)(2,1)S(1)}, u32[]{:S(2)}, u32[]{:S(2)}) collective-permute-start(bf16[8,256,512]{2,1,0:T(8,128)(2,1)} %add_convert_fusion.13), channel_id=1, source_target_pairs={{2,0},{4,2},{6,4},{3,1},{5,3},{7,5},{10,8},{12,10},{14,12},{11,9},... | collective-permute-start | bytes 6291464 | tf_op jit(solution)/shard_map/while/body/eval_jaxpr/ppermute | solution.py:76
  1176.1 48.7 %collective-permute-start.1 = (bf16[8,256,512]{2,1,0:T(8,128)(2,1)}, bf16[8,256,512]{2,1,0:T(8,128)(2,1)S(1)}, u32[]{:S(2)}, u32[]{:S(2)}) collective-permute-start(bf16[8,256,512]{2,1,0:T(8,128)(2,1)} %add_convert_fusion.13), channel_id=1, source_target_pairs={{2,0},{4,2},{6,4},{3,1},{5,3},{7,5},{10,8},{12,10},{14,12},{11,9},... | collective-permute-start | bytes 6291464 | tf_op jit(solution)/shard_map/while/body/eval_jaxpr/ppermute | solution.py:76
  1230.8 6.2 slice-start
  1231.6 5.5 slice-start.1
  1252.4 231.2 %reduce-scatter.15.cloned.1.call-start = ((), (), s32[]{:S(2)}) async-start(), calls=%async_computation.23 | async-start | bytes 10485760 | tf_op jit(solution)/shard_map/reduce_scatter | solution.py:208
  1254.0 10.1 copy-start.49
  1264.1 18.3 %copy-start.33 = (bf16[2048,512]{0,1:T(8,128)(2,1)S(1)}, bf16[2048,512]{0,1:T(8,128)(2,1)}, u32[]{:S(2)}) copy-start(bf16[2048,512]{0,1:T(8,128)(2,1)} %convolution_convert_fusion.7) | copy-start | bytes 6291460
  1293.4 4.5 copy-start.14
  1293.4 193.4 %all-to-all-start.3 = ((bf16[4,128,1536]{1,2,0:T(8,128)(2,1)}), bf16[4,128,1536]{1,2,0:T(8,128)(2,1)}, u32[]{:S(2)}, u32[]{:S(2)}) async-start(bf16[4,128,1536]{1,2,0:T(8,128)(2,1)} %copy_bitcast_fusion.1), calls=%async_computation.9 | async-start | bytes 3145728 | tf_op jit(solution)/shard_map/all_to_all | solution.py:209
  1297.9 199.5 %all-gather.18.cloned.1.call-start = ((), (), s32[]{:S(2)}) async-start(), calls=%async_computation.16 | async-start | bytes 3145728 | tf_op jit(solution)/shard_map/all_gather | solution.py:205
  1298.7 323.4 %all-reduce.3.cloned.1.call-start = ((), (), s32[]{:S(2)}) async-start(), calls=%async_computation.22 | async-start | bytes 131072 | tf_op jit(solution)/shard_map/psum | solution.py:273
  1349.0 286.2 %all-gather.24.cloned.1.call-start = ((), (), s32[]{:S(2)}) async-start(), calls=%async_computation.21 | async-start | bytes 3145728 | tf_op jit(solution)/shard_map/all_gather | solution.py:260
  1486.9 152.2 %all-to-all-start.2 = ((bf16[4,128,2048]{1,2,0:T(8,128)(2,1)}), bf16[4,128,2048]{1,2,0:T(8,128)(2,1)S(1)}, u32[]{:S(2)}, u32[]{:S(2)}) async-start(bf16[4,128,2048]{1,2,0:T(8,128)(2,1)} %copy_bitcast_fusion), calls=%async_computation.7 | async-start | bytes 4194304 | tf_op jit(solution)/shard_map/all_to_all | solution.py:209
  1643.7 4.4 copy-start.1
  (53 other events, 124.5 us)
Sparse Core Ops, SparseCore 0:
  41.5 117.3 all-gather.11
  161.4 54.2 all-gather.9
  217.8 204.4 all-gather.13
  525.3 73.2 reduce-scatter.6
  607.7 55.9 all-gather.15
  666.2 55.9 all-gather.19
  745.6 71.3 reduce-scatter.8
  820.4 71.2 reduce-scatter.10
  905.7 55.9 all-gather.21
  964.0 153.8 reduce-scatter.16
  1252.5 84.2 reduce-scatter.12
  1339.1 144.4 reduce-scatter.14
  1485.7 11.0 all-gather.17
  1502.8 119.2 all-reduce.2
  1624.0 11.1 all-gather.23

commit v2 on v1

--- a/solution.py
+++ b/solution.py
@@ -1,6 +1,10 @@
+import functools
+
 import jax
 import jax.numpy as jnp
 from jax import lax
+from jax.experimental import pallas as pl
+from jax.experimental.pallas import tpu as pltpu
 from jax.sharding import PartitionSpec as P
 
 eps = 1e-05
@@ -60,22 +64,356 @@
     return jnp.einsum(spec, left, right, preferred_element_type=f32)
 
 
-def gather_rows(own):
-    return lax.all_gather(own, ("fsdp", "tp"), axis=0, tiled=True)
-
-
-def scatter_rows(partial):
-    return lax.psum_scatter(partial, ("fsdp", "tp"), scatter_dimension=0, tiled=True)
-
-
-def pass_states(local, fade, by):
+MESH = pl.DeviceIdType.MESH
+
+
+def beside(f):
+    return f + 1 - 2 * (f % 2), (f + 2) % 4, 3 - f
+
+
+def greet(devices):
+    barrier = pltpu.get_barrier_semaphore()
+    for device in devices:
+        pl.semaphore_signal(barrier, inc=1, device_id=device, device_id_type=MESH)
+    pl.semaphore_wait(barrier, len(devices))
+
+
+def remote(src, dst, send, recv, device):
+    return pltpu.make_async_remote_copy(
+        src_ref=src, dst_ref=dst, send_sem=send, recv_sem=recv, device_id=device, device_id_type=MESH
+    )
+
+
+def gather_kernel(own, out, keep, send, recv):
+    f, t = lax.axis_index("fsdp"), lax.axis_index("tp")
+    fx, fy, fd = beside(f)
+    x, y, core = {"fsdp": fx}, {"fsdp": fy}, {"tp": 1 - t}
+    greet([x, y, core])
+    half = own.shape[0] // 2
+
+    def part(ref, h):
+        return ref.at[pl.ds(h * half, half)]
+
+    def slot(who, h):
+        return part(out.at[2 * who + t], h)
+
+    local = pltpu.make_async_copy(own, out.at[2 * f + t], keep)
+    local.start()
+    first = [
+        remote(part(own, 0), slot(f, 0), send.at[0], recv.at[0], x),
+        remote(part(own, 1), slot(f, 1), send.at[1], recv.at[3], y),
+        remote(part(own, 1), slot(f, 1), send.at[2], recv.at[1], x),
+        remote(part(own, 0), slot(f, 0), send.at[3], recv.at[2], y),
+        remote(part(own, 0), slot(f, 0), send.at[4], recv.at[6], core),
+        remote(part(own, 1), slot(f, 1), send.at[5], recv.at[7], core),
+    ]
+    for copy in first:
+        copy.start()
+
+    def pass_on(who, h, s, r, device):
+        return remote(slot(who, h), slot(who, h), send.at[s], recv.at[r], device)
+
+    sent = list(first)
+
+    def go(copy):
+        copy.start()
+        sent.append(copy)
+
+    first[0].wait_recv()
+    go(pass_on(fx, 0, 6, 4, y))
+    go(pass_on(fx, 0, 7, 8, core))
+    first[1].wait_recv()
+    go(pass_on(fy, 1, 8, 5, x))
+    go(pass_on(fy, 1, 9, 11, core))
+    first[2].wait_recv()
+    go(pass_on(fx, 1, 10, 9, core))
+    first[3].wait_recv()
+    go(pass_on(fy, 0, 11, 10, core))
+    remote(slot(fd, 0), slot(fd, 0), send.at[12], recv.at[4], y).wait_recv()
+    go(pass_on(fd, 0, 12, 12, core))
+    remote(slot(fd, 1), slot(fd, 1), send.at[13], recv.at[5], x).wait_recv()
+    go(pass_on(fd, 1, 13, 13, core))
+    for r in range(6, 14):
+        remote(slot(f, 0), slot(f, 0), send.at[0], recv.at[r], core).wait_recv()
+    for copy in sent:
+        copy.wait_send()
+    local.wait()
+
+
+def gather_rows(own, collective_id):
+    rows, width = own.shape
+    out = pl.pallas_call(
+        gather_kernel,
+        out_shape=jax.ShapeDtypeStruct((8, rows, width), own.dtype),
+        in_specs=[pl.BlockSpec(memory_space=pl.ANY)],
+        out_specs=pl.BlockSpec(memory_space=pl.ANY),
+        scratch_shapes=[
+            pltpu.SemaphoreType.DMA,
+            pltpu.SemaphoreType.DMA((14,)),
+            pltpu.SemaphoreType.DMA((14,)),
+        ],
+        compiler_params=pltpu.CompilerParams(collective_id=collective_id, has_side_effects=True),
+        cost_estimate=pl.CostEstimate(flops=0, bytes_accessed=160_000_000, transcendentals=0),
+    )(own)
+    return out.reshape(8 * rows, width)
+
+
+def scatter_kernel(partial, out, mine, theirs, total, diag, last, keep, send, recv):
+    f, t = lax.axis_index("fsdp"), lax.axis_index("tp")
+    fx, fy, fd = beside(f)
+    x, y, core = {"fsdp": fx}, {"fsdp": fy}, {"tp": 1 - t}
+    greet([x, y, core])
+    half = out.shape[0] // 2
+    order = [fd, fy, fx, f]
+    kept, crossing = [], []
+    for i, who in enumerate(order):
+        crossing.append(
+            remote(partial.at[2 * who + 1 - t], theirs.at[i], send.at[i], recv.at[i], core)
+        )
+        kept.append(pltpu.make_async_copy(partial.at[2 * who + t], mine.at[i], keep.at[i]))
+        crossing[i].start()
+        kept[i].start()
+
+    def part(ref, h):
+        return ref.at[pl.ds(h * half, half)]
+
+    def add(i):
+        kept[i].wait()
+        crossing[i].wait_recv()
+        total[i] = (mine[i].astype(f32) + theirs[i].astype(f32)).astype(total.dtype)
+
+    add(0)
+    d0 = remote(part(total.at[0], 0), diag.at[0], send.at[4], recv.at[4], x)
+    d1 = remote(part(total.at[0], 1), diag.at[1], send.at[5], recv.at[5], y)
+    d0.start()
+    d1.start()
+    add(1)
+    y1 = remote(part(total.at[1], 1), part(last.at[1], 1), send.at[6], recv.at[6], y)
+    y1.start()
+    add(2)
+    x0 = remote(part(total.at[2], 0), part(last.at[0], 0), send.at[7], recv.at[7], x)
+    x0.start()
+    d0.wait_recv()
+    total[1, :half] = (total[1, :half].astype(f32) + diag[0].astype(f32)).astype(total.dtype)
+    y0 = remote(part(total.at[1], 0), part(last.at[1], 0), send.at[8], recv.at[8], y)
+    y0.start()
+    d1.wait_recv()
+    total[2, half:] = (total[2, half:].astype(f32) + diag[1].astype(f32)).astype(total.dtype)
+    x1 = remote(part(total.at[2], 1), part(last.at[0], 1), send.at[9], recv.at[9], x)
+    x1.start()
+    kept[3].wait()
+    crossing[3].wait_recv()
+    for copy in (y1, x0, y0, x1):
+        copy.wait_recv()
+    out[...] = (mine[3].astype(f32) + theirs[3].astype(f32)) + (
+        last[0].astype(f32) + last[1].astype(f32)
+    )
+    for copy in (*crossing, d0, d1, y1, x0, y0, x1):
+        copy.wait_send()
+
+
+def scatter_rows(partial, collective_id):
+    rows, width = partial.shape[0] // 8, partial.shape[1]
+    dt = partial.dtype
+    return pl.pallas_call(
+        scatter_kernel,
+        out_shape=jax.ShapeDtypeStruct((rows, width), f32),
+        in_specs=[pl.BlockSpec(memory_space=pl.ANY)],
+        out_specs=pl.BlockSpec(memory_space=pltpu.VMEM),
+        scratch_shapes=[
+            pltpu.VMEM((4, rows, width), dt),
+            pltpu.VMEM((4, rows, width), dt),
+            pltpu.VMEM((3, rows, width), dt),
+            pltpu.VMEM((2, rows // 2, width), dt),
+            pltpu.VMEM((2, rows, width), dt),
+            pltpu.SemaphoreType.DMA((4,)),
+            pltpu.SemaphoreType.DMA((10,)),
+            pltpu.SemaphoreType.DMA((10,)),
+        ],
+        compiler_params=pltpu.CompilerParams(
+            collective_id=collective_id, has_side_effects=True, vmem_limit_bytes=40 << 20
+        ),
+        cost_estimate=pl.CostEstimate(flops=0, bytes_accessed=160_000_000, transcendentals=0),
+    )(partial.reshape(8, rows, width))
+
+
+def pass_kernel(by, local, fade, out, held, send, recv):
     length = lax.axis_size("ctx")
-    pairs = [(i, i + by) for i in range(length) if 0 <= i + by < length]
-
-    def step(turn, received):
-        return lax.ppermute((fade * received.astype(f32) + local).astype(bf16), "ctx", pairs)
-
-    return lax.fori_loop(0, length - 1, step, jnp.zeros(local.shape, bf16))
+    c = lax.axis_index("ctx")
+    pieces = local.shape[0]
+    first = c == (0 if by > 0 else length - 1)
+    last = c == (length - 1 if by > 0 else 0)
+    target = lax.rem(c + by + length, length)
+    source = lax.rem(c - by + length, length)
+    barrier = pltpu.get_barrier_semaphore()
+
+    @pl.when(jnp.logical_not(first))
+    def _():
+        pl.semaphore_signal(barrier, inc=1, device_id={"ctx": source}, device_id_type=MESH)
+
+    @pl.when(jnp.logical_not(last))
+    def _():
+        pl.semaphore_wait(barrier, 1)
+
+    def copy(p):
+        return remote(held.at[p], out.at[p], send.at[p], recv.at[p], {"ctx": target})
+
+    def step(p, carry):
+        @pl.when(first)
+        def _():
+            out[p] = jnp.zeros(out.shape[1:], out.dtype)
+
+        @pl.when(jnp.logical_not(first))
+        def _():
+            copy(p).wait_recv()
+
+        @pl.when(jnp.logical_not(last))
+        def _():
+            held[p] = (fade[...] * out[p].astype(f32) + local[p]).astype(held.dtype)
+            copy(p).start()
+
+        return carry
+
+    lax.fori_loop(0, pieces, step, 0)
+
+    @pl.when(jnp.logical_not(last))
+    def _():
+        def done(p, carry):
+            copy(p).wait_send()
+            return carry
+
+        lax.fori_loop(0, pieces, done, 0)
+
+
+def pass_states(local, fade, by, collective_id):
+    pieces = local.shape[0]
+    return pl.pallas_call(
+        functools.partial(pass_kernel, by),
+        out_shape=jax.ShapeDtypeStruct(local.shape, bf16),
+        in_specs=[pl.BlockSpec(memory_space=pltpu.VMEM)] * 2,
+        out_specs=pl.BlockSpec(memory_space=pltpu.VMEM),
+        scratch_shapes=[
+            pltpu.VMEM(local.shape, bf16),
+            pltpu.SemaphoreType.DMA((pieces,)),
+            pltpu.SemaphoreType.DMA((pieces,)),
+        ],
+        compiler_params=pltpu.CompilerParams(
+            collective_id=collective_id, has_side_effects=True, vmem_limit_bytes=40 << 20
+        ),
+        cost_estimate=pl.CostEstimate(flops=0, bytes_accessed=200_000_000, transcendentals=0),
+    )(local, jnp.full((1, local.shape[2]), fade, f32))
+
+def peer_of(place, nc, nt):
+    return {"fsdp": place // (nc * nt), "ctx": place // nt % nc, "tp": place % nt}
+
+
+def spread_kernel(own, out, keep, send, recv):
+    nc = lax.axis_size("ctx")
+    count = out.shape[0]
+    t = lax.axis_index("tp")
+    place = lax.axis_index("fsdp") * nc + lax.axis_index("ctx")
+    barrier = pltpu.get_barrier_semaphore()
+
+    def peer(i):
+        other = lax.rem(place + i, count)
+        return {"fsdp": other // nc, "ctx": other % nc}
+
+    def hello(i, carry):
+        pl.semaphore_signal(barrier, inc=1, device_id=peer(i), device_id_type=MESH)
+        return carry
+
+    lax.fori_loop(1, count, hello, 0)
+    pl.semaphore_wait(barrier, count - 1)
+
+    def copy(i):
+        return remote(own, out.at[place], send.at[i], recv.at[i], peer(i))
+
+    def go(i, carry):
+        copy(i).start()
+        return carry
+
+    lax.fori_loop(1, count, go, 0)
+    local = pltpu.make_async_copy(own, out.at[place], keep)
+    local.start()
+    local.wait()
+
+    def done(i, carry):
+        copy(i).wait()
+        return carry
+
+    lax.fori_loop(1, count, done, 0)
+
+
+def spread_small(own, collective_id):
+    count = lax.axis_size("fsdp") * lax.axis_size("ctx")
+    return pl.pallas_call(
+        spread_kernel,
+        out_shape=jax.ShapeDtypeStruct((count, *own.shape), own.dtype),
+        in_specs=[pl.BlockSpec(memory_space=pltpu.VMEM)],
+        out_specs=pl.BlockSpec(memory_space=pltpu.VMEM),
+        scratch_shapes=[
+            pltpu.SemaphoreType.DMA,
+            pltpu.SemaphoreType.DMA((count,)),
+            pltpu.SemaphoreType.DMA((count,)),
+        ],
+        compiler_params=pltpu.CompilerParams(collective_id=collective_id, has_side_effects=True),
+        cost_estimate=pl.CostEstimate(flops=0, bytes_accessed=30_000_000, transcendentals=0),
+    )(own)
+
+
+def total_kernel(parts, out, slots, send, recv):
+    nc, nt = lax.axis_size("ctx"), lax.axis_size("tp")
+    count = parts.shape[0]
+    place = (lax.axis_index("fsdp") * nc + lax.axis_index("ctx")) * nt + lax.axis_index("tp")
+    barrier = pltpu.get_barrier_semaphore()
+
+    def hello(i, carry):
+        other = peer_of(lax.rem(place + i, count), nc, nt)
+        pl.semaphore_signal(barrier, inc=1, device_id=other, device_id_type=MESH)
+        return carry
+
+    lax.fori_loop(1, count, hello, 0)
+    pl.semaphore_wait(barrier, count - 1)
+
+    def copy(i):
+        other = lax.rem(place + i, count)
+        return remote(
+            parts.at[other], slots.at[i], send.at[i], recv.at[i], peer_of(other, nc, nt)
+        )
+
+    def go(i, carry):
+        copy(i).start()
+        return carry
+
+    lax.fori_loop(1, count, go, 0)
+
+    def add(i, carry):
+        copy(i).wait()
+        return carry + slots[i]
+
+    out[...] = lax.fori_loop(1, count, add, parts[place])
+
+
+def total_small(parts, collective_id):
+    count = parts.shape[0]
+    return pl.pallas_call(
+        total_kernel,
+        out_shape=jax.ShapeDtypeStruct(parts.shape[1:], parts.dtype),
+        in_specs=[pl.BlockSpec(memory_space=pltpu.VMEM)],
+        out_specs=pl.BlockSpec(memory_space=pltpu.VMEM),
+        scratch_shapes=[
+            pltpu.VMEM(parts.shape, parts.dtype),
+            pltpu.SemaphoreType.DMA((count,)),
+            pltpu.SemaphoreType.DMA((count,)),
+        ],
+        compiler_params=pltpu.CompilerParams(collective_id=collective_id, has_side_effects=True),
+        cost_estimate=pl.CostEstimate(flops=0, bytes_accessed=30_000_000, transcendentals=0),
+    )(parts)
+
+
+def both_halves(own, t):
+    other = lax.ppermute(own, "tp", [(0, 1), (1, 0)])
+    return jnp.where(t == 0, jnp.concatenate([own, other]), jnp.concatenate([other, own]))
 
 
 def shards(
@@ -112,6 +450,11 @@
     rows = seqs * span
     head = t * heads_local + f
 
+    def pad_tile(v):
+        return jnp.pad(v, [(0, 0)] * (v.ndim - 1) + [(0, -v.shape[-1] % 1024)]).reshape(
+            *v.shape[:-1], 8, -1
+        )
+
     def perm(v):
         return v.reshape(-1, nf, nc, depth).transpose(0, 2, 1, 3).reshape(-1, width)
 
@@ -143,7 +486,8 @@
             lengths.astype(f32),
         ]
     )
-    small = lax.all_gather(small, ("fsdp", "ctx"), axis=0)
+    small_size = small.size
+    small = spread_small(pad_tile(small), 4).reshape(nf * nc, -1)[:, :small_size]
     pre_gain_full, pre_bias_full, mlp_gain_full, mlp_bias_full = (
         small[:, i * depth : (i + 1) * depth].reshape(width) for i in range(4)
     )
@@ -155,12 +499,12 @@
 
     inputs = own_part(tokens).astype(f32)
     normed_wide, norm_in_back = jax.vjp(layer_norm, inputs, pre_gain_full, pre_bias_full)
-    normed = gather_rows(perm(normed_wide.astype(bf16)))
+    normed = gather_rows(perm(normed_wide.astype(bf16)), 0)
     positions = c * span + lax.iota(jnp.int32, span)
     own_ids = t * own_rows + lax.iota(jnp.int32, own_rows)
     own_valid = (c * span + own_ids % span < lengths[own_ids // span]).astype(f32)[:, None]
     error = own_valid * own_part(cotangent).astype(f32)
-    error_all = gather_rows(perm(error.astype(bf16)))
+    error_all = gather_rows(perm(error.astype(bf16)), 0)
 
     pre = product(normed, attn_w)
     valid = (positions.astype(f32)[None, :] < all_lengths[:, None]).astype(f32)[:, :, None]
@@ -185,24 +529,24 @@
     keys_faded = (keys.astype(f32) * key_fade).astype(bf16)
     queries_faded = (queries.astype(f32) * query_fade).astype(bf16)
     local_state = blocks("sjd,sje->sde", keys_faded, values)
-    entering = pass_states(local_state, block_fade, 1)
+    entering = pass_states(local_state, block_fade, 1, 2)
     probs = (blocks("sid,sjd->sij", queries, keys) * within_fade).astype(bf16)
     mixed = blocks("sij,sje->sie", probs, values) + blocks("sid,sde->sie", queries_faded, entering)
     gated_wide, gate_back = jax.vjp(
         gate_mix, mixed.reshape(rows, value_size), swish_pre, group[0], group[1]
     )
     gated = gated_wide.astype(bf16)
-    branch = scatter_rows(product_right(gated, out_t).astype(bf16))
-    hidden = inputs + unperm(branch.astype(f32))
+    branch = scatter_rows(product_right(gated, out_t).astype(bf16), 1)
+    hidden = inputs + unperm(branch)
 
     mlp_wide, norm_mid_back = jax.vjp(layer_norm, hidden, mlp_gain_full, mlp_bias_full)
-    mlp_in = gather_rows(perm(mlp_wide.astype(bf16)))
+    mlp_in = gather_rows(perm(mlp_wide.astype(bf16)), 0)
     pre_ff = product(mlp_in, gelu_up)
     inner_wide, mix_back = jax.vjp(mlp_mix, pre_ff[:, :hidden_size], pre_ff[:, hidden_size:])
     inner = inner_wide.astype(bf16)
-    mlp_out = scatter_rows(product_right(inner, down_t).astype(bf16))
-    block_own = (own_valid * (hidden + unperm(mlp_out.astype(f32)))).astype(bf16)
-    block_out = lax.all_gather(block_own, "tp", axis=0, tiled=True).reshape(tokens.shape)
+    mlp_out = scatter_rows(product_right(inner, down_t).astype(bf16), 1)
+    block_own = (own_valid * (hidden + unperm(mlp_out))).astype(bf16)
+    block_out = both_halves(block_own, t).reshape(tokens.shape)
 
     def to_owners(grads):
         mine = lax.psum_scatter(grads.astype(bf16), "ctx", scatter_dimension=0, tiled=True)
@@ -219,11 +563,11 @@
     ff_low = jnp.concatenate([gelu_grad.astype(bf16), up_grad.astype(bf16)], -1)
     grad_gelu_up = product_left(mlp_in, ff_low)
     ff_grads = to_owners(jnp.concatenate([grad_gelu_up, grad_down_t], -1))
-    mlp_in_grad = unperm(scatter_rows(product_right(ff_low, gelu_up).astype(bf16)).astype(f32))
+    mlp_in_grad = unperm(scatter_rows(product_right(ff_low, gelu_up).astype(bf16), 1))
     hidden_norm_grad, grad_mlp_gain, grad_mlp_bias = norm_mid_back(mlp_in_grad)
     hidden_grad = error + hidden_norm_grad
 
-    hidden_low = gather_rows(perm(hidden_grad.astype(bf16)))
+    hidden_low = gather_rows(perm(hidden_grad.astype(bf16)), 0)
     grad_out_t = product_left(hidden_low, gated)
     gated_grad = product(hidden_low, out_t)
     mixed_grad, swish_grad, grad_group_gain, grad_group_bias = gate_back(gated_grad)
@@ -231,7 +575,7 @@
     mixed_low = mixed_grad.astype(bf16).reshape(seqs, span, value_size)
     score_low = (blocks("sie,sje->sij", mixed_low, values) * within_fade).astype(bf16)
     pulled_state = blocks("sid,sie->sde", queries_faded, mixed_low)
-    later = pass_states(pulled_state, block_fade, -1)
+    later = pass_states(pulled_state, block_fade, -1, 3)
     query_grad = blocks("sij,sjd->sid", score_low, keys) + query_fade * blocks(
         "sie,sde->sid", mixed_low, entering
     )
@@ -254,30 +598,23 @@
     )
     grad_attn = product_left(normed, low)
     attn_grads = to_owners(jnp.concatenate([grad_attn, grad_out_t], -1))
-    normed_grad = unperm(scatter_rows(product_right(low, attn_w).astype(bf16)).astype(f32))
+    normed_grad = unperm(scatter_rows(product_right(low, attn_w).astype(bf16), 1))
     input_norm_grad, grad_pre_gain, grad_pre_bias = norm_in_back(normed_grad)
     tokens_own = (hidden_grad + input_norm_grad).astype(bf16)
-    grad_tokens = lax.all_gather(tokens_own, "tp", axis=0, tiled=True).reshape(tokens.shape)
-
-    mine = (lax.iota(jnp.int32, nt * heads_local) == head).astype(f32)[:, None]
-    sums = jnp.concatenate(
-        [
-            grad_pre_gain,
-            grad_pre_bias,
-            grad_mlp_gain,
-            grad_mlp_bias,
-            (mine * grad_group_gain[None]).reshape(-1),
-            (mine * grad_group_bias[None]).reshape(-1),
-        ]
-    )
-    sums = lax.psum(sums, ("fsdp", "ctx", "tp"))
-    place = f * nc + c
-    norm_sums = lax.dynamic_index_in_dim(
-        sums[: 4 * width].reshape(4, nf * nc, depth), place, 1, False
-    )
-    group_sums = sums[4 * width :].reshape(2, nt, heads_local, nf * nc, -1)
-    group_sums = lax.dynamic_index_in_dim(group_sums, t, 1, False)
-    group_sums = lax.dynamic_index_in_dim(group_sums, place, 2, False)
+    grad_tokens = both_halves(tokens_own, t).reshape(tokens.shape)
+
+    norm_parts = jnp.stack([grad_pre_gain, grad_pre_bias, grad_mlp_gain, grad_mlp_bias])
+    norm_parts = norm_parts.reshape(4, nf * nc, 1, depth).transpose(1, 2, 0, 3)
+    norm_parts = jnp.broadcast_to(norm_parts, (nf * nc, nt, 4, depth)).reshape(nf * nc, nt, -1)
+    mine = lax.iota(jnp.int32, nt * heads_local) == head
+    group_parts = jnp.stack([grad_group_gain, grad_group_bias]).reshape(1, 2, nf * nc, -1)
+    group_parts = jnp.where(mine[:, None, None, None], group_parts, 0.0)
+    group_parts = group_parts.reshape(nt, heads_local, 2, nf * nc, -1).transpose(3, 0, 2, 1, 4)
+    parts = jnp.concatenate([norm_parts, group_parts.reshape(nf * nc, nt, -1)], -1)
+    parts = parts.reshape(nf * nc * nt, -1)
+    sums = total_small(pad_tile(parts), 5).reshape(-1)[: parts.shape[1]]
+    norm_sums = sums[: 4 * depth].reshape(4, depth)
+    group_sums = sums[4 * depth :].reshape(2, heads_local, -1)
 
     at = [0, key_size, 2 * key_size, 2 * key_size + value_size, 2 * key_size + 2 * value_size]
     return (

time: 1660 us -> 1010 us (0.61)
  waiting for transfers between devices: 1100 us -> 107 us
  Pallas kernels: 0 us -> 531 us
  blocking collectives: 122 us -> 51.3 us
  starting transfers between devices: 65.6 us -> 9.3 us
  matrix products: 178 us -> 147 us
  other arithmetic: 69.6 us -> 45.2 us
    pallas_call x0 -> x12, Pallas kernels: none -> 531 us  [the longest x2 172 us: pass_states(): pl.pallas_call(functools.partial(pass_kernel, by), out_shape=jax.ShapeDty...]
    ppermute x6 -> x2, waiting for transfers between devices: 415 us -> 0.01 us  [both_halves(): other = lax.ppermute(own, 'tp', [(0, 1), (1, 0)])]
    reduce_scatter x4 -> x0, waiting for transfers between devices: 236 us -> none  [scatter_rows(): lax.psum_scatter(partial, ('fsdp', 'tp'), scatter_dimension=0, tiled=True)]
    all_gather x6 -> x0, waiting for transfers between devices: 192 us -> none  [the longest x4 181 us: gather_rows(): return lax.all_gather(own, ('fsdp', 'tp'), axis=0, tiled=True)]
    psum x1 -> x0, waiting for transfers between devices: 121 us -> none  [shards(): sums = lax.psum(sums, ('fsdp', 'ctx', 'tp'))]
    unnamed x1 -> x0, blocking collectives: 78.4 us -> none
    reduce_scatter x2, waiting for transfers between devices: 130 us -> 66.5 us  [to_owners(): lax.psum_scatter(grads.astype(bf16), 'ctx', scatter_dimension=0, tiled=True)]
    ppermute x6 -> x2, starting transfers between devices: 56.5 us -> 0.14 us  [both_halves(): other = lax.ppermute(own, 'tp', [(0, 1), (1, 0)])]
  transfers between devices with their start and end apart: 23 -> 8, of which waited for: 18 -> 2; matrix products, arithmetic and copies ran while one was open for 16% -> 17% of each run, Pallas kernels for 0% -> 45%
where the time goes in v2:
time: 1010 us; the launch traced here: 1000 us
  Pallas kernels  531 us (53%)
  matrix products  147 us (15%)
  waiting for transfers between devices  107 us (11%)
  local copies, waits for them, and re-layouts  97.4 us (10%)
  blocking collectives  51.3 us (5%)
  other arithmetic  45.2 us (4%)
  between operations  15.6 us (2%)
    pallas_call x2, Pallas kernels, pass_states(): pl.pallas_call(functools.partial(pass_kernel, by), out_shape=jax.ShapeDty...  172 us
    pallas_call x4, Pallas kernels, scatter_rows(): pl.pallas_call(scatter_kernel, out_shape=jax.ShapeDtypeStruct((rows, widt...  161 us
    pallas_call x4, Pallas kernels, gather_rows(): pl.pallas_call(gather_kernel, out_shape=jax.ShapeDtypeStruct((8, rows, wi...  159 us
    reduce_scatter x2, waiting for transfers between devices, to_owners(): lax.psum_scatter(grads.astype(bf16), 'ctx', scatter_dimension=0, tiled=True)  66.5 us
    dot_general x4, matrix products, product(): return jnp.dot(left, right, preferred_element_type=f32)  54.3 us
    all_to_all x2, blocking collectives, full_weights(): mine = lax.all_to_all(mine, 'fsdp', 0, 0, tiled=True)  51.3 us
    dot_general x4, matrix products, product_right(): lax.dot_general(left, right, (((1,), (1,)), ((), ())), preferred_element_...  46.2 us
    unnamed x172, local copies, waits for them, and re-layouts  41.9 us
  transfers between devices with their start and end apart: 8, of which 2 were waited for; matrix products, arithmetic and copies ran while one was open for 17% of the time, Pallas kernels for 45%

profile of v2, /device:TPU:0, one launch (start us, length us, event | category | flops | bytes accessed | tf_op | source)
XLA Modules:
  0.0 1003.6 jit_solution(14401923642743716367)
XLA Ops:
  11.3 24.7 %all_to_all.20 = bf16[4,128,1536]{1,2,0:T(8,128)(2,1)S(1)} all-to-all(bf16[4,128,1536]{1,2,0:T(8,128)(2,1)S(1)} %pad_maximum_fusion.6), channel_id=1, replica_groups=mesh['fsdp'=4,'ctx'=4,'tp'=2] {'fsdp'}, dimensions={0} | all-to-all | bytes 3145728 | tf_op jit(solution)/shard_map/all_to_all | solution.py:472
  39.0 26.6 %all_to_all.21 = bf16[4,128,2048]{1,2,0:T(8,128)(2,1)S(1)} all-to-all(bf16[4,128,2048]{1,2,0:T(8,128)(2,1)S(1)} %pad_maximum_fusion.5), channel_id=1, replica_groups=mesh['fsdp'=4,'ctx'=4,'tp'=2] {'fsdp'}, dimensions={0} | all-to-all | bytes 4194304 | tf_op jit(solution)/shard_map/all_to_all | solution.py:472
  65.6 2.6 copy.125
  69.7 13.7 %shard_map.288 = f32[16,8,128]{2,1,0:T(8,128)} custom-call(f32[8,128]{1,0:T(8,128)} %fusion.43.own), custom_call_target="tpu_custom_call" | custom-call | bytes 30000000 | tf_op jit(solution)/shard_map/pallas_call | solution.py:349
  92.0 2.6 reshape.658.own
  99.5 39.3 %shard_map.294 = bf16[8,256,2048]{2,1,0:T(8,128)(2,1)} custom-call(bf16[256,2048]{1,0:T(8,128)(2,1)} %reshape.687.own), custom_call_target="tpu_custom_call" | custom-call | bytes 160000000 | tf_op jit(solution)/shard_map/pallas_call | solution.py:145
  138.8 40.4 %shard_map.289 = bf16[8,256,2048]{2,1,0:T(8,128)(2,1)} custom-call(bf16[256,2048]{1,0:T(8,128)(2,1)} %reshape.658.own), custom_call_target="tpu_custom_call" | custom-call | bytes 160000000 | tf_op jit(solution)/shard_map/pallas_call | solution.py:145
  180.6 17.5 %fusion.63 = f32[2048,1536]{1,0:T(8,128)S(1)} fusion(bf16[2048,2048]{1,0:T(8,128)(2,1)} %bitcast.258, bf16[2048,1536]{1,0:T(8,128)(2,1)} %bitcast.330), kind=kOutput, calls=%fused_computation.196 | convolution fusion | flops 12884901888 | bytes 27262976 | tf_op jit(solution)/shard_map/dot_general | solution.py:52
  198.7 3.9 copy-done.20
  204.4 92.1 %shard_map.290 = bf16[8,256,512]{2,1,0:T(8,128)(2,1)S(1)} custom-call(f32[8,256,512]{2,1,0:T(8,128)S(1)} %fusion.39.local, f32[1,512]{1,0:T(1,128)S(1)} %broadcast_in_dim.37.fade), custom_call_target="tpu_custom_call" | custom-call | bytes 200000000 | tf_op jit(solution)/shard_map/pallas_call | solution.py:290
  301.2 3.3 multiply_convert_fusion.2
  304.5 40.2 %all-gather.5.cloned.1.call-done = bf16[16,128,2048]{2,1,0:T(8,128)(2,1)} async-done(((bf16[4,128,2048]{2,1,0:T(8,128)(2,1)}), bf16[16,128,2048]{2,1,0:T(8,128)(2,1)}) %all-gather.5.cloned.1.call-update) | async-done | bytes 8388624 | tf_op jit(solution)/shard_map/all_gather | solution.py:473
  344.7 6.4 convolution_convert_fusion.3
  351.1 40.9 %shard_map.291 = f32[256,2048]{1,0:T(8,128)S(1)} custom-call(bf16[8,256,2048]{2,1,0:T(8,128)(2,1)S(1)} %bitcast.248), custom_call_target="tpu_custom_call" | custom-call | bytes 160000000 | tf_op jit(solution)/shard_map/pallas_call | solution.py:218
  400.8 39.6 %shard_map.292 = bf16[8,256,2048]{2,1,0:T(8,128)(2,1)} custom-call(bf16[256,2048]{1,0:T(8,128)(2,1)} %reshape.680.own), custom_call_target="tpu_custom_call" | custom-call | bytes 160000000 | tf_op jit(solution)/shard_map/pallas_call | solution.py:145
  440.4 12.5 %fusion.12 = f32[2048,1024]{1,0:T(8,128)S(1)} fusion(bf16[2048,2048]{1,0:T(8,128)(2,1)} %bitcast.270, bf16[2048,2048]{1,0:T(8,128)(2,1)} %bitcast.325), kind=kOutput, calls=%fused_computation.38 | convolution fusion | flops 8589934592 | bytes 20971520 | tf_op jit(solution)/shard_map/dot_general | solution.py:52
  452.9 12.0 %fusion.6 = (bf16[2048,512]{1,0:T(8,128)(2,1)}, bf16[2048,512]{1,0:T(8,128)(2,1)}, bf16[2048,512]{1,0:T(8,128)(2,1)S(1)}) fusion(f32[2048,1024]{1,0:T(8,128)S(1)} %fusion.12, bf16[2048,2048]{1,0:T(8,128)(2,1)} %bitcast.262, bf16[2048,2048]{1,0:T(8,128)(2,1)} %bitcast.326), kind=kOutput, calls=%fused_computation.17 | convolution fusion | flops 4322230272 | bytes 25165824 | tf_op jit(solution)/shard_map/dot_general | solution.py:52
  464.9 11.8 %convolution_convert_fusion.5 = bf16[2048,1024]{0,1:T(8,128)(2,1)S(1)} fusion(bf16[2048,2048]{1,0:T(8,128)(2,1)S(1)} %bitcast.271, bf16[2048,512]{1,0:T(8,128)(2,1)} %get-tuple-element.84, bf16[2048,512]{1,0:T(8,128)(2,1)} %get-tuple-element.83), kind=kOutput, calls=%fused_computation.36 | convolution fusion | flops 8600420352 | bytes 16777216 | tf_op jit(solution)/shard_map/dot_general | solution.py:56
  476.8 14.0 %convolution_convert_fusion.1 = bf16[2048,2048]{1,0:T(8,128)(2,1)} fusion(bf16[2048,2048]{1,0:T(8,128)(2,1)} %bitcast.327, bf16[2048,512]{1,0:T(8,128)(2,1)} %get-tuple-element.84, bf16[2048,512]{1,0:T(8,128)(2,1)} %get-tuple-element.83), kind=kOutput, calls=%fused_computation.2 | convolution fusion | flops 8602517504 | bytes 16777216 | tf_op jit(solution)/shard_map/dot_general | solution.py:60
  490.8 4.9 convolution_convert_fusion.6
  495.7 8.4 convolution_convert_fusion.2
  504.1 3.4 pad_maximum_fusion.1
  507.7 3.4 copy-done.3
  511.0 40.2 %shard_map.295 = f32[256,2048]{1,0:T(8,128)S(1)} custom-call(bf16[8,256,2048]{2,1,0:T(8,128)(2,1)S(1)} %bitcast.246), custom_call_target="tpu_custom_call" | custom-call | bytes 160000000 | tf_op jit(solution)/shard_map/pallas_call | solution.py:218
  553.7 3.0 copy.135
  559.1 3.4 copy-done.2
  562.6 40.0 %shard_map.293 = f32[256,2048]{1,0:T(8,128)S(1)} custom-call(bf16[8,256,2048]{2,1,0:T(8,128)(2,1)S(1)} %bitcast.245), custom_call_target="tpu_custom_call" | custom-call | bytes 160000000 | tf_op jit(solution)/shard_map/pallas_call | solution.py:218
  605.0 3.0 copy.130
  608.0 4.1 fusion.55
  616.1 40.0 %shard_map.296 = bf16[8,256,2048]{2,1,0:T(8,128)(2,1)} custom-call(bf16[256,2048]{1,0:T(8,128)(2,1)} %reshape.693.own), custom_call_target="tpu_custom_call" | custom-call | bytes 160000000 | tf_op jit(solution)/shard_map/pallas_call | solution.py:145
  656.0 12.3 %multiply_reduce_fusion = (f32[512]{0:T(512)S(1)}, f32[2048]{0:T(1024)S(1)}, f32[512]{0:T(512)S(1)}, f32[2048,512]{1,0:T(8,128)S(1)}, bf16[2048,512]{1,0:T(8,128)(2,1)S(1)}) fusion(f32[8,256,512]{2,1,0:T(8,128)} %copy-done.6, f32[2048]{0:T(1024)S(1)} %rsqrt.31, f32[2048]{0:T(1024)S(1)} %bitcast.312, f32[512]{0:T(512)S(1)} %mul.534, ...), kind=kOutput, calls=%fused_computation.24 | convolution fusion | flops 4319081472 | bytes 25198592 | tf_op jit(solution)/shard_map/dot_general | solution.py:52
  672.8 79.5 %shard_map.297 = bf16[8,256,512]{2,1,0:T(8,128)(2,1)S(1)} custom-call(f32[8,256,512]{2,1,0:T(8,128)S(1)} %fusion.38.local, f32[1,512]{1,0:T(1,128)S(1)} %copy-done.5), custom_call_target="tpu_custom_call" | custom-call | bytes 200000000 | tf_op jit(solution)/shard_map/pallas_call | solution.py:290
  763.7 5.0 convolution_convert_fusion.7
  768.8 16.1 %convolution_convert_fusion.4 = bf16[2048,1536]{0,1:T(8,128)(2,1)} fusion(bf16[2048,2048]{1,0:T(8,128)(2,1)S(1)} %bitcast.261, bf16[2048,1536]{1,0:T(8,128)(2,1)S(1)} %constant_dynamic-update-slice_fusion), kind=kOutput, calls=%fused_computation.5 | convolution fusion | flops 12888047616 | bytes 20971520 | tf_op jit(solution)/shard_map/dot_general | solution.py:56
  785.0 7.7 pad_maximum_fusion
  792.8 17.3 %convolution_convert_fusion = bf16[2048,2048]{1,0:T(8,128)(2,1)S(1)} fusion(bf16[2048,1536]{1,0:T(8,128)(2,1)} %copy-done.47, bf16[2048,1536]{1,0:T(8,128)(2,1)} %bitcast.331), kind=kOutput, calls=%fused_computation.1 | convolution fusion | flops 12889096192 | bytes 20971520 | tf_op jit(solution)/shard_map/dot_general | solution.py:60
  810.1 40.2 %shard_map.298 = f32[256,2048]{1,0:T(8,128)S(1)} custom-call(bf16[8,256,2048]{2,1,0:T(8,128)(2,1)S(1)} %bitcast.247), custom_call_target="tpu_custom_call" | custom-call | bytes 160000000 | tf_op jit(solution)/shard_map/pallas_call | solution.py:218
  850.4 2.5 reshape.698
  856.7 2.8 copy_bitcast_fusion.1
  859.5 4.4 all-to-all-start.3
  863.9 3.8 add_convert_fusion.2
  868.0 66.5 %reduce-scatter.3.cloned.1.call-done = bf16[512,2048]{0,1:T(8,128)(2,1)} async-done(((bf16[2048,2048]{0,1:T(8,128)(2,1)}), bf16[512,2048]{0,1:T(8,128)(2,1)}) %reduce-scatter.3.cloned.1.call-update) | async-done | bytes 2097168 | tf_op jit(solution)/shard_map/reduce_scatter | solution.py:552
  934.5 3.3 copy_bitcast_fusion
  937.8 4.5 all-to-all-start.2
  945.6 25.2 %shard_map.299 = f32[8,128]{1,0:T(8,128)} custom-call(f32[32,8,128]{2,1,0:T(8,128)} %bitcast.300), custom_call_target="tpu_custom_call" | custom-call | bytes 30000000 | tf_op jit(solution)/shard_map/pallas_call | solution.py:399
  973.5 3.0 maximum_select_fusion
  983.3 2.6 fusion.60
  991.6 2.6 fusion.58
  (292 shorter events, 90.7 us)
Async XLA Ops:
  7.2 3.7 copy-start.34
  7.2 173.4 %all-gather.3.cloned.1.call-start = ((), (), s32[]{:S(2)}) async-start(), calls=%async_computation.6 | async-start | bytes 7864320 | tf_op jit(solution)/shard_map/all_gather | solution.py:473
  37.6 307.1 %all-gather.5.cloned.1.call-start = ((), (), s32[]{:S(2)}) async-start(), calls=%async_computation.7 | async-start | bytes 10485760 | tf_op jit(solution)/shard_map/all_gather | solution.py:473
  68.3 788.4 %reduce-scatter.5.cloned.1.call-start = ((), (), s32[]{:S(2)}) async-start(), calls=%async_computation.9 | async-start | bytes 7864320 | tf_op jit(solution)/shard_map/reduce_scatter | solution.py:552
  87.1 9.5 copy-start.18
  87.6 308.7 %copy-start.8 = (bf16[256,2048]{0,1:T(8,128)(2,1)}, bf16[256,2048]{0,1:T(8,128)(2,1)S(1)}, u32[]{:S(2)}) copy-start(bf16[256,2048]{0,1:T(8,128)(2,1)S(1)} %copy.161) | copy-start | bytes 3145732
  88.0 2.3 copy-start.48
  179.2 24.4 %copy-start.54 = (f32[256]{0:T(256)}, f32[256]{0:T(256)S(1)}, u32[]{:S(2)}) copy-start(f32[256]{0:T(256)S(1)} %get-tuple-element.130) | copy-start | bytes 3076
  179.2 119.0 %copy-start.56 = (f32[256]{0:T(256)}, f32[256]{0:T(256)S(1)}, u32[]{:S(2)}) copy-start(f32[256]{0:T(256)S(1)} %get-tuple-element.131) | copy-start | bytes 3076
  179.3 117.3 %copy-start.39 = (f32[256,256]{1,0:T(8,128)}, f32[256,256]{1,0:T(8,128)S(1)}, u32[]{:S(2)}) copy-start(f32[256,256]{1,0:T(8,128)S(1)} %exponential_select_fusion) | copy-start | bytes 786436
  179.4 23.8 %copy-start.43 = (f32[8,256]{1,0:T(8,128)}, f32[8,256]{1,0:T(8,128)S(1)}, u32[]{:S(2)}) copy-start(f32[8,256]{1,0:T(8,128)S(1)} %compare_select_fusion) | copy-start | bytes 24580
  180.6 22.0 %copy-start.31 = (f32[256,128]{1,0:T(8,128)}, f32[256,128]{1,0:T(8,128)S(1)}, u32[]{:S(2)}) copy-start(f32[256,128]{1,0:T(8,128)S(1)} %get-tuple-element.123) | copy-start | bytes 393220
  198.1 4.5 copy-start.20
  198.4 98.7 %copy-start.13 = (bf16[2048,512]{1,0:T(8,128)(2,1)}, bf16[2048,512]{1,0:T(8,128)(2,1)S(1)}, u32[]{:S(2)}) copy-start(bf16[2048,512]{1,0:T(8,128)(2,1)S(1)} %slice.283) | copy-start | bytes 6291460
  203.2 95.1 %copy-start.22 = (bf16[8,256,128]{2,1,0:T(8,128)(2,1)}, bf16[8,256,128]{2,1,0:T(8,128)(2,1)S(1)}, u32[]{:S(2)}) copy-start(bf16[8,256,128]{2,1,0:T(8,128)(2,1)S(1)} %get-tuple-element.92) | copy-start | bytes 1572868
  203.2 95.1 %copy-start.24 = (bf16[8,256,128]{2,1,0:T(8,128)(2,1)}, bf16[8,256,128]{2,1,0:T(8,128)(2,1)S(1)}, u32[]{:S(2)}) copy-start(bf16[8,256,128]{2,1,0:T(8,128)(2,1)S(1)} %get-tuple-element.93) | copy-start | bytes 1572868
  203.6 93.1 %copy-start.16 = (bf16[8,256,256]{2,1,0:T(8,128)(2,1)}, bf16[8,256,256]{2,1,0:T(8,128)(2,1)S(1)}, u32[]{:S(2)}) copy-start(bf16[8,256,256]{2,1,0:T(8,128)(2,1)S(1)} %fusion.25) | copy-start | bytes 3145732
  204.4 92.2 %copy-start.4 = (f32[1,512]{1,0:T(1,128)}, f32[1,512]{1,0:T(1,128)S(1)}, u32[]{:S(2)}) copy-start(f32[1,512]{1,0:T(1,128)S(1)} %broadcast_in_dim.37.fade) | copy-start | bytes 6148
  299.2 2.0 copy-start.6
  304.5 46.6 %copy-start.29 = (bf16[2048,512]{1,0:T(8,128)(2,1)}, bf16[2048,512]{1,0:T(8,128)(2,1)S(1)}, u32[]{:S(2)}) copy-start(bf16[2048,512]{1,0:T(8,128)(2,1)S(1)} %multiply_convert_fusion.2) | copy-start | bytes 6291460
  452.9 12.1 %copy-start.21 = (bf16[8,256,2048]{2,1,0:T(8,128)(2,1)S(1)}, bf16[8,256,2048]{2,1,0:T(8,128)(2,1)}, u32[]{:S(2)}) copy-start(bf16[8,256,2048]{2,1,0:T(8,128)(2,1)} %shard_map.292) | copy-start | bytes 25165828
  464.9 25.9 %slice-start.2 = ((s8[8388608]{0:T(1024)(128)(4,1)}), s8[4194304]{0:T(1024)(128)(4,1)S(1)}, s32[]{:S(2)}) async-start(s8[8388608]{0:T(1024)(128)(4,1)} %bitcast.263), calls=%async_computation.12 | async-start | bytes 8388608
  476.8 14.0 %slice-start.3 = ((s8[8388608]{0:T(1024)(128)(4,1)}), s8[4194304]{0:T(1024)(128)(4,1)S(1)}, s32[]{:S(2)}) async-start(s8[8388608]{0:T(1024)(128)(4,1)} %bitcast.263), calls=%async_computation.13 | async-start | bytes 8388608
  507.6 426.9 %reduce-scatter.3.cloned.1.call-start = ((), (), s32[]{:S(2)}) async-start(), calls=%async_computation.8 | async-start | bytes 10485760 | tf_op jit(solution)/shard_map/reduce_scatter | solution.py:552
  507.7 3.4 copy-start.3
  553.7 3.0 copy-start.11
  559.1 3.4 copy-start.2
  604.9 3.0 copy-start.12
  605.0 3.0 copy-start.51
  608.0 4.1 copy-start.19
  656.0 12.4 %copy-start.46 = (f32[1,2,8,128]{3,1,2,0:T(2,128)S(1)}, f32[1,2,8,128]{3,1,2,0:T(2,128)}, u32[]{:S(2)}) copy-start(f32[1,2,8,128]{3,1,2,0:T(2,128)} %copy-done.45) | copy-start | bytes 24580
  656.0 12.4 %copy-start.7 = (f32[8,256,512]{2,1,0:T(8,128)S(1)}, f32[8,256,512]{2,1,0:T(8,128)}, u32[]{:S(2)}) copy-start(f32[8,256,512]{2,1,0:T(8,128)} %copy-done.6) | copy-start | bytes 12582916
  672.8 79.5 %copy-start.14 = (bf16[2048,512]{1,0:T(8,128)(2,1)S(1)}, bf16[2048,512]{1,0:T(8,128)(2,1)}, u32[]{:S(2)}) copy-start(bf16[2048,512]{1,0:T(8,128)(2,1)} %copy-done.13) | copy-start | bytes 6291460
  672.8 79.5 %copy-start.40 = (f32[256,256]{1,0:T(8,128)S(1)}, f32[256,256]{1,0:T(8,128)}, u32[]{:S(2)}) copy-start(f32[256,256]{1,0:T(8,128)} %copy-done.39) | copy-start | bytes 786436
  759.4 2.2 slice-start.4
  760.2 3.5 slice-start.5
  761.0 7.8 slice-start
  761.1 2.6 copy-start.30
  763.7 5.1 copy-start.47
  763.7 5.1 slice-start.1
  792.7 180.8 %collective-permute-start = (bf16[256,2048]{0,1:T(8,128)(2,1)}, bf16[256,2048]{0,1:T(8,128)(2,1)}, u32[]{:S(2)}, u32[]{:S(2)}) collective-permute-start(bf16[256,2048]{0,1:T(8,128)(2,1)} %get-tuple-element.101), channel_id=1, source_target_pairs={{0,1},{1,0},{2,3},{3,2},{4,5},{5,4},{6,7},{7,6},{8,9},{9,8},{10,11... | collective-permute-start | bytes 3145736 | tf_op jit(solution)/shard_map/ppermute | solution.py:415
  852.8 2.0 copy-start.9
  852.8 2.1 copy-start.42
  852.8 2.1 copy-start.49
  859.5 78.3 %all-to-all-start.3 = ((bf16[4,128,1536]{1,2,0:T(8,128)(2,1)}), bf16[4,128,1536]{1,2,0:T(8,128)(2,1)}, u32[]{:S(2)}, u32[]{:S(2)}) async-start(bf16[4,128,1536]{1,2,0:T(8,128)(2,1)} %copy_bitcast_fusion.1), calls=%async_computation.5 | async-start | bytes 3145728 | tf_op jit(solution)/shard_map/all_to_all | solution.py:553
  867.8 111.1 %collective-permute-start.1 = (bf16[256,2048]{0,1:T(8,128)(2,1)}, bf16[256,2048]{0,1:T(8,128)(2,1)}, u32[]{:S(2)}, u32[]{:S(2)}) collective-permute-start(bf16[256,2048]{0,1:T(8,128)(2,1)} %add_convert_fusion.2), channel_id=1, source_target_pairs={{0,1},{1,0},{2,3},{3,2},{4,5},{5,4},{6,7},{7,6},{8,9},{9,8},{10,11... | collective-permute-start | bytes 3145736 | tf_op jit(solution)/shard_map/ppermute | solution.py:415
  937.8 50.7 %all-to-all-start.2 = ((bf16[4,128,2048]{1,2,0:T(8,128)(2,1)}), bf16[4,128,2048]{1,2,0:T(8,128)(2,1)}, u32[]{:S(2)}, u32[]{:S(2)}) async-start(bf16[4,128,2048]{1,2,0:T(8,128)(2,1)} %copy_bitcast_fusion), calls=%async_computation.3 | async-start | bytes 4194304 | tf_op jit(solution)/shard_map/all_to_all | solution.py:553
  976.5 2.4 copy-start.28
  (33 other events, 34.5 us)
Sparse Core Ops, SparseCore 0:
  37.7 116.3 all-gather.2
  156.3 188.3 all-gather.4
  507.7 127.3 reduce-scatter.4
  792.8 141.6 reduce-scatter.2

commit v3 on v2

--- a/solution.py
+++ b/solution.py
@@ -4,6 +4,7 @@
 import jax.numpy as jnp
 from jax import lax
 from jax.experimental import pallas as pl
+from jax.experimental.layout import Layout, with_layout_constraint
 from jax.experimental.pallas import tpu as pltpu
 from jax.sharding import PartitionSpec as P
 
@@ -71,24 +72,16 @@
     return f + 1 - 2 * (f % 2), (f + 2) % 4, 3 - f
 
 
-def greet(devices):
-    barrier = pltpu.get_barrier_semaphore()
-    for device in devices:
-        pl.semaphore_signal(barrier, inc=1, device_id=device, device_id_type=MESH)
-    pl.semaphore_wait(barrier, len(devices))
-
-
 def remote(src, dst, send, recv, device):
     return pltpu.make_async_remote_copy(
         src_ref=src, dst_ref=dst, send_sem=send, recv_sem=recv, device_id=device, device_id_type=MESH
     )
 
 
-def gather_kernel(own, out, keep, send, recv):
+def gather_steps(own, out, keep, send, recv):
     f, t = lax.axis_index("fsdp"), lax.axis_index("tp")
     fx, fy, fd = beside(f)
     x, y, core = {"fsdp": fx}, {"fsdp": fy}, {"tp": 1 - t}
-    greet([x, y, core])
     half = own.shape[0] // 2
 
     def part(ref, h):
@@ -98,7 +91,6 @@
         return part(out.at[2 * who + t], h)
 
     local = pltpu.make_async_copy(own, out.at[2 * f + t], keep)
-    local.start()
     first = [
         remote(part(own, 0), slot(f, 0), send.at[0], recv.at[0], x),
         remote(part(own, 1), slot(f, 1), send.at[1], recv.at[3], y),
@@ -107,153 +99,142 @@
         remote(part(own, 0), slot(f, 0), send.at[4], recv.at[6], core),
         remote(part(own, 1), slot(f, 1), send.at[5], recv.at[7], core),
     ]
-    for copy in first:
-        copy.start()
+    sent = list(first)
 
     def pass_on(who, h, s, r, device):
-        return remote(slot(who, h), slot(who, h), send.at[s], recv.at[r], device)
-
-    sent = list(first)
-
-    def go(copy):
+        copy = remote(slot(who, h), slot(who, h), send.at[s], recv.at[r], device)
         copy.start()
         sent.append(copy)
 
-    first[0].wait_recv()
-    go(pass_on(fx, 0, 6, 4, y))
-    go(pass_on(fx, 0, 7, 8, core))
-    first[1].wait_recv()
-    go(pass_on(fy, 1, 8, 5, x))
-    go(pass_on(fy, 1, 9, 11, core))
-    first[2].wait_recv()
-    go(pass_on(fx, 1, 10, 9, core))
-    first[3].wait_recv()
-    go(pass_on(fy, 0, 11, 10, core))
-    remote(slot(fd, 0), slot(fd, 0), send.at[12], recv.at[4], y).wait_recv()
-    go(pass_on(fd, 0, 12, 12, core))
-    remote(slot(fd, 1), slot(fd, 1), send.at[13], recv.at[5], x).wait_recv()
-    go(pass_on(fd, 1, 13, 13, core))
-    for r in range(6, 14):
-        remote(slot(f, 0), slot(f, 0), send.at[0], recv.at[r], core).wait_recv()
-    for copy in sent:
-        copy.wait_send()
-    local.wait()
-
-
-def gather_rows(own, collective_id):
-    rows, width = own.shape
-    out = pl.pallas_call(
-        gather_kernel,
-        out_shape=jax.ShapeDtypeStruct((8, rows, width), own.dtype),
-        in_specs=[pl.BlockSpec(memory_space=pl.ANY)],
-        out_specs=pl.BlockSpec(memory_space=pl.ANY),
-        scratch_shapes=[
-            pltpu.SemaphoreType.DMA,
-            pltpu.SemaphoreType.DMA((14,)),
-            pltpu.SemaphoreType.DMA((14,)),
-        ],
-        compiler_params=pltpu.CompilerParams(collective_id=collective_id, has_side_effects=True),
-        cost_estimate=pl.CostEstimate(flops=0, bytes_accessed=160_000_000, transcendentals=0),
-    )(own)
-    return out.reshape(8 * rows, width)
-
-
-def scatter_kernel(partial, out, mine, theirs, total, diag, last, keep, send, recv):
+    def begin():
+        local.start()
+        for copy in first:
+            copy.start()
+
+    def relay():
+        first[0].wait_recv()
+        pass_on(fx, 0, 6, 4, y)
+        pass_on(fx, 0, 7, 8, core)
+        first[1].wait_recv()
+        pass_on(fy, 1, 8, 5, x)
+        pass_on(fy, 1, 9, 11, core)
+
+    def rest():
+        first[2].wait_recv()
+        pass_on(fx, 1, 10, 9, core)
+        first[3].wait_recv()
+        pass_on(fy, 0, 11, 10, core)
+
+    def diagonal():
+        remote(slot(fd, 0), slot(fd, 0), send.at[12], recv.at[4], y).wait_recv()
+        pass_on(fd, 0, 12, 12, core)
+        remote(slot(fd, 1), slot(fd, 1), send.at[13], recv.at[5], x).wait_recv()
+        pass_on(fd, 1, 13, 13, core)
+
+    def end():
+        for r in range(6, 14):
+            remote(slot(f, 0), slot(f, 0), send.at[0], recv.at[r], core).wait_recv()
+        for copy in sent:
+            copy.wait_send()
+        local.wait()
+
+    return begin, relay, rest, diagonal, end
+
+
+def gather_scratch():
+    return [
+        pltpu.SemaphoreType.DMA,
+        pltpu.SemaphoreType.DMA((14,)),
+        pltpu.SemaphoreType.DMA((14,)),
+    ]
+
+
+def scatter_steps(partial, out, mine, theirs, total, diag, last, keep, send, recv):
     f, t = lax.axis_index("fsdp"), lax.axis_index("tp")
     fx, fy, fd = beside(f)
     x, y, core = {"fsdp": fx}, {"fsdp": fy}, {"tp": 1 - t}
-    greet([x, y, core])
     half = out.shape[0] // 2
-    order = [fd, fy, fx, f]
-    kept, crossing = [], []
-    for i, who in enumerate(order):
-        crossing.append(
-            remote(partial.at[2 * who + 1 - t], theirs.at[i], send.at[i], recv.at[i], core)
-        )
-        kept.append(pltpu.make_async_copy(partial.at[2 * who + t], mine.at[i], keep.at[i]))
-        crossing[i].start()
-        kept[i].start()
 
     def part(ref, h):
         return ref.at[pl.ds(h * half, half)]
+
+    crossing = [
+        remote(partial.at[2 * who + 1 - t], theirs.at[i], send.at[i], recv.at[i], core)
+        for i, who in enumerate([fd, fy, fx, f])
+    ]
+    kept = [
+        pltpu.make_async_copy(partial.at[2 * who + t], mine.at[i], keep.at[i])
+        for i, who in enumerate([fd, fy, fx, f])
+    ]
+    d0 = remote(part(total.at[0], 0), diag.at[0], send.at[4], recv.at[4], x)
+    d1 = remote(part(total.at[0], 1), diag.at[1], send.at[5], recv.at[5], y)
+    y1 = remote(part(total.at[1], 1), part(last.at[1], 1), send.at[6], recv.at[6], y)
+    x0 = remote(part(total.at[2], 0), part(last.at[0], 0), send.at[7], recv.at[7], x)
+    y0 = remote(part(total.at[1], 0), part(last.at[1], 0), send.at[8], recv.at[8], y)
+    x1 = remote(part(total.at[2], 1), part(last.at[0], 1), send.at[9], recv.at[9], x)
+
+    def begin():
+        for a, b in zip(crossing, kept):
+            a.start()
+            b.start()
 
     def add(i):
         kept[i].wait()
         crossing[i].wait_recv()
         total[i] = (mine[i].astype(f32) + theirs[i].astype(f32)).astype(total.dtype)
 
-    add(0)
-    d0 = remote(part(total.at[0], 0), diag.at[0], send.at[4], recv.at[4], x)
-    d1 = remote(part(total.at[0], 1), diag.at[1], send.at[5], recv.at[5], y)
-    d0.start()
-    d1.start()
-    add(1)
-    y1 = remote(part(total.at[1], 1), part(last.at[1], 1), send.at[6], recv.at[6], y)
-    y1.start()
-    add(2)
-    x0 = remote(part(total.at[2], 0), part(last.at[0], 0), send.at[7], recv.at[7], x)
-    x0.start()
-    d0.wait_recv()
-    total[1, :half] = (total[1, :half].astype(f32) + diag[0].astype(f32)).astype(total.dtype)
-    y0 = remote(part(total.at[1], 0), part(last.at[1], 0), send.at[8], recv.at[8], y)
-    y0.start()
-    d1.wait_recv()
-    total[2, half:] = (total[2, half:].astype(f32) + diag[1].astype(f32)).astype(total.dtype)
-    x1 = remote(part(total.at[2], 1), part(last.at[0], 1), send.at[9], recv.at[9], x)
-    x1.start()
-    kept[3].wait()
-    crossing[3].wait_recv()
-    for copy in (y1, x0, y0, x1):
-        copy.wait_recv()
-    out[...] = (mine[3].astype(f32) + theirs[3].astype(f32)) + (
-        last[0].astype(f32) + last[1].astype(f32)
-    )
-    for copy in (*crossing, d0, d1, y1, x0, y0, x1):
-        copy.wait_send()
-
-
-def scatter_rows(partial, collective_id):
-    rows, width = partial.shape[0] // 8, partial.shape[1]
-    dt = partial.dtype
-    return pl.pallas_call(
-        scatter_kernel,
-        out_shape=jax.ShapeDtypeStruct((rows, width), f32),
-        in_specs=[pl.BlockSpec(memory_space=pl.ANY)],
-        out_specs=pl.BlockSpec(memory_space=pltpu.VMEM),
-        scratch_shapes=[
-            pltpu.VMEM((4, rows, width), dt),
-            pltpu.VMEM((4, rows, width), dt),
-            pltpu.VMEM((3, rows, width), dt),
-            pltpu.VMEM((2, rows // 2, width), dt),
-            pltpu.VMEM((2, rows, width), dt),
-            pltpu.SemaphoreType.DMA((4,)),
-            pltpu.SemaphoreType.DMA((10,)),
-            pltpu.SemaphoreType.DMA((10,)),
-        ],
-        compiler_params=pltpu.CompilerParams(
-            collective_id=collective_id, has_side_effects=True, vmem_limit_bytes=40 << 20
-        ),
-        cost_estimate=pl.CostEstimate(flops=0, bytes_accessed=160_000_000, transcendentals=0),
-    )(partial.reshape(8, rows, width))
-
-
-def pass_kernel(by, local, fade, out, held, send, recv):
+    def diagonal():
+        add(0)
+        d0.start()
+        d1.start()
+
+    def straight():
+        add(1)
+        y1.start()
+        add(2)
+        x0.start()
+
+    def relay():
+        d0.wait_recv()
+        total[1, :half] = (total[1, :half].astype(f32) + diag[0].astype(f32)).astype(total.dtype)
+        y0.start()
+        d1.wait_recv()
+        total[2, half:] = (total[2, half:].astype(f32) + diag[1].astype(f32)).astype(total.dtype)
+        x1.start()
+
+    def end():
+        kept[3].wait()
+        crossing[3].wait_recv()
+        for copy in (y1, x0, y0, x1):
+            copy.wait_recv()
+        out[...] = (mine[3].astype(f32) + theirs[3].astype(f32)) + (
+            last[0].astype(f32) + last[1].astype(f32)
+        )
+        for copy in (*crossing, d0, d1, y1, x0, y0, x1):
+            copy.wait_send()
+
+    return begin, diagonal, straight, relay, end
+
+
+def scatter_scratch(rows, width, kind):
+    return [
+        pltpu.VMEM((4, rows, width), kind),
+        pltpu.VMEM((4, rows, width), kind),
+        pltpu.VMEM((3, rows, width), kind),
+        pltpu.VMEM((2, rows // 2, width), kind),
+        pltpu.VMEM((2, rows, width), kind),
+        pltpu.SemaphoreType.DMA((4,)),
+        pltpu.SemaphoreType.DMA((10,)),
+        pltpu.SemaphoreType.DMA((10,)),
+    ]
+
+
+def pass_steps(by, local, fade, out, held, send, recv):
     length = lax.axis_size("ctx")
     c = lax.axis_index("ctx")
-    pieces = local.shape[0]
     first = c == (0 if by > 0 else length - 1)
     last = c == (length - 1 if by > 0 else 0)
     target = lax.rem(c + by + length, length)
-    source = lax.rem(c - by + length, length)
-    barrier = pltpu.get_barrier_semaphore()
-
-    @pl.when(jnp.logical_not(first))
-    def _():
-        pl.semaphore_signal(barrier, inc=1, device_id={"ctx": source}, device_id_type=MESH)
-
-    @pl.when(jnp.logical_not(last))
-    def _():
-        pl.semaphore_wait(barrier, 1)
 
     def copy(p):
         return remote(held.at[p], out.at[p], send.at[p], recv.at[p], {"ctx": target})
@@ -274,34 +255,178 @@
 
         return carry
 
-    lax.fori_loop(0, pieces, step, 0)
-
-    @pl.when(jnp.logical_not(last))
-    def _():
-        def done(p, carry):
-            copy(p).wait_send()
-            return carry
-
-        lax.fori_loop(0, pieces, done, 0)
-
-
-def pass_states(local, fade, by, collective_id):
+    def end():
+        @pl.when(jnp.logical_not(last))
+        def _():
+            def done(p, carry):
+                copy(p).wait_send()
+                return carry
+
+            lax.fori_loop(0, local.shape[0], done, 0)
+
+    return step, end
+
+
+def greet_plane(by=0):
+    f, c, t = lax.axis_index("fsdp"), lax.axis_index("ctx"), lax.axis_index("tp")
+    length = lax.axis_size("ctx")
+    fx, fy, _ = beside(f)
+    barrier = pltpu.get_barrier_semaphore()
+    for device in ({"fsdp": fx}, {"fsdp": fy}, {"tp": 1 - t}):
+        pl.semaphore_signal(barrier, inc=1, device_id=device, device_id_type=MESH)
+    if by != 0:
+        first = c == (0 if by > 0 else length - 1)
+        last = c == (length - 1 if by > 0 else 0)
+        source = {"ctx": lax.rem(c - by + length, length)}
+
+        @pl.when(jnp.logical_not(first))
+        def _():
+            pl.semaphore_signal(barrier, inc=1, device_id=source, device_id_type=MESH)
+
+        @pl.when(jnp.logical_not(last))
+        def _():
+            pl.semaphore_wait(barrier, 4)
+
+        @pl.when(last)
+        def _():
+            pl.semaphore_wait(barrier, 3)
+    else:
+        pl.semaphore_wait(barrier, 3)
+
+
+def gather_kernel(*refs):
+    steps = gather_steps(*refs)
+    greet_plane()
+    for step in steps:
+        step()
+
+
+def scatter_kernel(*refs):
+    steps = scatter_steps(*refs)
+    greet_plane()
+    for step in steps:
+        step()
+
+
+def pass_gather_kernel(by, local, fade, own, out, full, held, send, recv, *scratch):
+    begin, relay, rest, diagonal, end = gather_steps(own, full, *scratch)
+    step, done = pass_steps(by, local, fade, out, held, send, recv)
     pieces = local.shape[0]
+    greet_plane(by)
+    begin()
+    lax.fori_loop(0, pieces // 4, step, 0)
+    relay()
+    lax.fori_loop(pieces // 4, pieces // 2, step, 0)
+    rest()
+    lax.fori_loop(pieces // 2, pieces, step, 0)
+    diagonal()
+    end()
+    done()
+
+
+def pass_scatter_kernel(by, local, fade, partial, out, own, held, send, recv, *scratch):
+    begin, diagonal, straight, relay, end = scatter_steps(partial, own, *scratch)
+    step, done = pass_steps(by, local, fade, out, held, send, recv)
+    pieces = local.shape[0]
+    greet_plane(by)
+    begin()
+    lax.fori_loop(0, pieces // 4, step, 0)
+    diagonal()
+    straight()
+    lax.fori_loop(pieces // 4, 3 * pieces // 4, step, 0)
+    relay()
+    lax.fori_loop(3 * pieces // 4, pieces, step, 0)
+    end()
+    done()
+
+
+def call(kernel, collective_id, outs, ins, scratch, *args):
+    shapes, spaces = zip(*outs)
     return pl.pallas_call(
-        functools.partial(pass_kernel, by),
-        out_shape=jax.ShapeDtypeStruct(local.shape, bf16),
-        in_specs=[pl.BlockSpec(memory_space=pltpu.VMEM)] * 2,
-        out_specs=pl.BlockSpec(memory_space=pltpu.VMEM),
-        scratch_shapes=[
-            pltpu.VMEM(local.shape, bf16),
-            pltpu.SemaphoreType.DMA((pieces,)),
-            pltpu.SemaphoreType.DMA((pieces,)),
-        ],
+        kernel,
+        out_shape=shapes,
+        in_specs=[pl.BlockSpec(memory_space=space) for space in ins],
+        out_specs=tuple(pl.BlockSpec(memory_space=space) for space in spaces),
+        scratch_shapes=scratch,
         compiler_params=pltpu.CompilerParams(
-            collective_id=collective_id, has_side_effects=True, vmem_limit_bytes=40 << 20
+            collective_id=collective_id, has_side_effects=True, vmem_limit_bytes=44 << 20
         ),
-        cost_estimate=pl.CostEstimate(flops=0, bytes_accessed=200_000_000, transcendentals=0),
-    )(local, jnp.full((1, local.shape[2]), fade, f32))
+        cost_estimate=pl.CostEstimate(flops=0, bytes_accessed=2_000_000, transcendentals=0),
+    )(*args)
+
+
+def gathered(own):
+    rows, width = own.shape
+    return jax.ShapeDtypeStruct((8, rows, width), own.dtype), pl.ANY
+
+
+def scattered(partial):
+    rows, width = partial.shape
+    return jax.ShapeDtypeStruct((rows // 8, width), f32), pltpu.VMEM
+
+
+def passed(local):
+    return jax.ShapeDtypeStruct(local.shape, bf16), pltpu.VMEM
+
+
+def pass_scratch(local):
+    pieces = local.shape[0]
+    return [
+        pltpu.VMEM(local.shape, bf16),
+        pltpu.SemaphoreType.DMA((pieces,)),
+        pltpu.SemaphoreType.DMA((pieces,)),
+    ]
+
+
+def in_eights(partial):
+    return partial.reshape(8, -1, partial.shape[1])
+
+
+def gather_rows(own, collective_id):
+    (out,) = call(gather_kernel, collective_id, [gathered(own)], [pl.ANY], gather_scratch(), own)
+    return out.reshape(-1, own.shape[1])
+
+
+def scatter_rows(partial, collective_id):
+    scratch = scatter_scratch(partial.shape[0] // 8, partial.shape[1], partial.dtype)
+    (out,) = call(
+        scatter_kernel,
+        collective_id,
+        [scattered(partial)],
+        [pl.ANY],
+        scratch,
+        in_eights(partial),
+    )
+    return out
+
+
+def pass_and_gather(local, fade, own, by, collective_id):
+    out, full = call(
+        functools.partial(pass_gather_kernel, by),
+        collective_id,
+        [passed(local), gathered(own)],
+        [pltpu.VMEM, pltpu.VMEM, pl.ANY],
+        pass_scratch(local) + gather_scratch(),
+        local,
+        jnp.full((1, local.shape[2]), fade, f32),
+        own,
+    )
+    return out, full.reshape(-1, own.shape[1])
+
+
+def pass_and_scatter(local, fade, partial, by, collective_id):
+    rows, width = partial.shape
+    return call(
+        functools.partial(pass_scatter_kernel, by),
+        collective_id,
+        [passed(local), scattered(partial)],
+        [pltpu.VMEM, pltpu.VMEM, pl.ANY],
+        pass_scratch(local) + scatter_scratch(rows // 8, width, partial.dtype),
+        local,
+        jnp.full((1, local.shape[2]), fade, f32),
+        in_eights(partial),
+    )
+
 
 def peer_of(place, nc, nt):
     return {"fsdp": place // (nc * nt), "ctx": place // nt % nc, "tp": place % nt}
@@ -357,7 +482,7 @@
             pltpu.SemaphoreType.DMA((count,)),
         ],
         compiler_params=pltpu.CompilerParams(collective_id=collective_id, has_side_effects=True),
-        cost_estimate=pl.CostEstimate(flops=0, bytes_accessed=30_000_000, transcendentals=0),
+        cost_estimate=pl.CostEstimate(flops=0, bytes_accessed=1_000_000, transcendentals=0),
     )(own)
 
 
@@ -407,7 +532,7 @@
             pltpu.SemaphoreType.DMA((count,)),
         ],
         compiler_params=pltpu.CompilerParams(collective_id=collective_id, has_side_effects=True),
-        cost_estimate=pl.CostEstimate(flops=0, bytes_accessed=30_000_000, transcendentals=0),
+        cost_estimate=pl.CostEstimate(flops=0, bytes_accessed=1_000_000, transcendentals=0),
     )(parts)
 
 
@@ -467,16 +592,16 @@
     def spread(w):
         return w.reshape(depth, nf, -1).transpose(1, 0, 2)
 
-    def full_weights(*ws):
+    def head_columns(*ws):
         mine = jnp.concatenate([spread(w) for w in ws], -1)
-        mine = lax.all_to_all(mine, "fsdp", 0, 0, tiled=True)
+        return lax.all_to_all(mine, "fsdp", 0, 0, tiled=True)
+
+    def all_depths(mine):
         return lax.all_gather(mine, "ctx", axis=0, tiled=True).reshape(width, -1)
 
-    attn_w = full_weights(query_weight, key_weight, value_weight, swish_weight)
-    rest_w = full_weights(out_weight.T, gelu_weight, up_weight, down_weight.T)
-    out_t = rest_w[:, :value_size]
-    gelu_up = rest_w[:, value_size : value_size + 2 * hidden_size]
-    down_t = rest_w[:, value_size + 2 * hidden_size :]
+    attn_w = all_depths(head_columns(query_weight, key_weight, value_weight, swish_weight))
+    rest = head_columns(out_weight.T, gelu_weight, up_weight, down_weight.T)
+    out_t = all_depths(rest[..., :value_size])
 
     small = jnp.concatenate(
         [
@@ -504,7 +629,6 @@
     own_ids = t * own_rows + lax.iota(jnp.int32, own_rows)
     own_valid = (c * span + own_ids % span < lengths[own_ids // span]).astype(f32)[:, None]
     error = own_valid * own_part(cotangent).astype(f32)
-    error_all = gather_rows(perm(error.astype(bf16)), 0)
 
     pre = product(normed, attn_w)
     valid = (positions.astype(f32)[None, :] < all_lengths[:, None]).astype(f32)[:, :, None]
@@ -529,7 +653,12 @@
     keys_faded = (keys.astype(f32) * key_fade).astype(bf16)
     queries_faded = (queries.astype(f32) * query_fade).astype(bf16)
     local_state = blocks("sjd,sje->sde", keys_faded, values)
-    entering = pass_states(local_state, block_fade, 1, 2)
+    error_low = perm(error.astype(bf16))
+    entering, error_all = pass_and_gather(local_state, block_fade, error_low, 1, 2)
+    rest, entering = lax.optimization_barrier((rest, entering))
+    ff_w = all_depths(rest[..., value_size:])
+    gelu_up = ff_w[:, : 2 * hidden_size]
+    down_t = ff_w[:, 2 * hidden_size :]
     probs = (blocks("sid,sjd->sij", queries, keys) * within_fade).astype(bf16)
     mixed = blocks("sij,sje->sie", probs, values) + blocks("sid,sde->sie", queries_faded, entering)
     gated_wide, gate_back = jax.vjp(
@@ -544,13 +673,15 @@
     pre_ff = product(mlp_in, gelu_up)
     inner_wide, mix_back = jax.vjp(mlp_mix, pre_ff[:, :hidden_size], pre_ff[:, hidden_size:])
     inner = inner_wide.astype(bf16)
-    mlp_out = scatter_rows(product_right(inner, down_t).astype(bf16), 1)
-    block_own = (own_valid * (hidden + unperm(mlp_out))).astype(bf16)
-    block_out = both_halves(block_own, t).reshape(tokens.shape)
-
-    def to_owners(grads):
-        mine = lax.psum_scatter(grads.astype(bf16), "ctx", scatter_dimension=0, tiled=True)
-        return lax.all_to_all(mine.reshape(nf, depth, -1), "fsdp", 0, 0, tiled=True).astype(f32)
+    mlp_part = product_right(inner, down_t).astype(bf16)
+
+    def sum_depths(grads):
+        grads = with_layout_constraint(grads.astype(bf16), Layout((0, 1)))
+        mine = lax.psum_scatter(grads, "ctx", scatter_dimension=0, tiled=True)
+        return mine.reshape(nf, depth, -1)
+
+    def all_heads(mine):
+        return lax.all_to_all(mine, "fsdp", 0, 0, tiled=True).astype(f32)
 
     def along(grads):
         return grads.transpose(1, 0, 2).reshape(depth, -1)
@@ -562,7 +693,9 @@
     gelu_grad, up_grad = mix_back(product(error_all, down_t))
     ff_low = jnp.concatenate([gelu_grad.astype(bf16), up_grad.astype(bf16)], -1)
     grad_gelu_up = product_left(mlp_in, ff_low)
-    ff_grads = to_owners(jnp.concatenate([grad_gelu_up, grad_down_t], -1))
+    ff_parts = jnp.concatenate([grad_gelu_up, grad_down_t], -1).astype(bf16)
+    ff_parts, ff_low = lax.optimization_barrier((ff_parts, ff_low))
+    ff_sum = sum_depths(ff_parts)
     mlp_in_grad = unperm(scatter_rows(product_right(ff_low, gelu_up).astype(bf16), 1))
     hidden_norm_grad, grad_mlp_gain, grad_mlp_bias = norm_mid_back(mlp_in_grad)
     hidden_grad = error + hidden_norm_grad
@@ -575,7 +708,13 @@
     mixed_low = mixed_grad.astype(bf16).reshape(seqs, span, value_size)
     score_low = (blocks("sie,sje->sij", mixed_low, values) * within_fade).astype(bf16)
     pulled_state = blocks("sid,sie->sde", queries_faded, mixed_low)
-    later = pass_states(pulled_state, block_fade, -1, 3)
+    early = jnp.concatenate([product_left(normed, swish_low), grad_out_t], -1).astype(bf16)
+    early, pulled_state, ff_sum = lax.optimization_barrier((early, pulled_state, ff_sum))
+    later, mlp_out = pass_and_scatter(pulled_state, block_fade, mlp_part, -1, 3)
+    early, later = lax.optimization_barrier((early, later))
+    early_sum = sum_depths(early)
+    block_own = (own_valid * (hidden + unperm(mlp_out))).astype(bf16)
+    block_out = both_halves(block_own, t).reshape(tokens.shape)
     query_grad = blocks("sij,sjd->sid", score_low, keys) + query_fade * blocks(
         "sie,sde->sid", mixed_low, entering
     )
@@ -592,13 +731,15 @@
             query_low,
             key_low.reshape(rows, key_size),
             value_grad.astype(bf16).reshape(rows, value_size),
-            swish_low,
         ],
         -1,
     )
-    grad_attn = product_left(normed, low)
-    attn_grads = to_owners(jnp.concatenate([grad_attn, grad_out_t], -1))
+    attn_part = product_left(normed, low).astype(bf16)
+    attn_part, low = lax.optimization_barrier((attn_part, low))
+    attn_sum = sum_depths(attn_part)
+    low = jnp.concatenate([low, swish_low], -1)
     normed_grad = unperm(scatter_rows(product_right(low, attn_w).astype(bf16), 1))
+    early_sum, normed_grad = lax.optimization_barrier((early_sum, normed_grad))
     input_norm_grad, grad_pre_gain, grad_pre_bias = norm_in_back(normed_grad)
     tokens_own = (hidden_grad + input_norm_grad).astype(bf16)
     grad_tokens = both_halves(tokens_own, t).reshape(tokens.shape)
@@ -613,10 +754,12 @@
     parts = jnp.concatenate([norm_parts, group_parts.reshape(nf * nc, nt, -1)], -1)
     parts = parts.reshape(nf * nc * nt, -1)
     sums = total_small(pad_tile(parts), 5).reshape(-1)[: parts.shape[1]]
+    sums, attn_sum = lax.optimization_barrier((sums, attn_sum))
+    ff_grads, early_grads, attn_grads = (all_heads(v) for v in (ff_sum, early_sum, attn_sum))
     norm_sums = sums[: 4 * depth].reshape(4, depth)
     group_sums = sums[4 * depth :].reshape(2, heads_local, -1)
 
-    at = [0, key_size, 2 * key_size, 2 * key_size + value_size, 2 * key_size + 2 * value_size]
+    at = [0, key_size, 2 * key_size]
     return (
         block_out,
         grad_tokens,
@@ -624,9 +767,9 @@
         norm_sums[1],
         along(attn_grads[..., : at[1]]),
         along(attn_grads[..., at[1] : at[2]]),
-        along(attn_grads[..., at[2] : at[3]]),
-        along(attn_grads[..., at[3] : at[4]]),
-        across(attn_grads[..., at[4] :]),
+        along(attn_grads[..., at[2] :]),
+        along(early_grads[..., :value_size]),
+        across(early_grads[..., value_size:]),
         group_sums[0],
         group_sums[1],
         norm_sums[2],

time: 1010 us -> 861 us (0.85)
  Pallas kernels: 531 us -> 403 us
  blocking collectives: 51.3 us -> 24.7 us
  waiting for transfers between devices: 107 us -> 85.3 us
    pallas_call x10 -> x8, Pallas kernels: 492 us -> 364 us  [call(): pl.pallas_call(kernel, out_shape=shapes, in_specs=[pl.BlockSpec(memory_sp...]
    reduce_scatter x2 -> x3, waiting for transfers between devices: 66.5 us -> 31.9 us  [sum_depths(): mine = lax.psum_scatter(grads, 'ctx', scatter_dimension=0, tiled=True)]
    all_to_all x2 -> x1, blocking collectives: 51.3 us -> 24.7 us  [head_columns(): return lax.all_to_all(mine, 'fsdp', 0, 0, tiled=True)]
    pallas_call x1, Pallas kernels: 13.7 us -> 25.2 us  [spread_small(): pl.pallas_call(spread_kernel, out_shape=jax.ShapeDtypeStruct((count, *own...]
    pallas_call x1, Pallas kernels: 25.2 us -> 13.9 us  [total_small(): pl.pallas_call(total_kernel, out_shape=jax.ShapeDtypeStruct(parts.shape[1...]
    all_gather x2 -> x3, waiting for transfers between devices: 40.2 us -> 43.9 us  [all_depths(): return lax.all_gather(mine, 'ctx', axis=0, tiled=True).reshape(width, -1)]
    unnamed x172 -> x189, local copies, waits for them, and re-layouts: 41.9 us -> 41.1 us
    dot_general x4 -> x5, matrix products: 37.9 us -> 38.2 us  [product_left(): lax.dot_general(left, right, (((0,), (0,)), ((), ())), preferred_element_...]
  transfers between devices with their start and end apart: 8 -> 12, of which waited for: 2 -> 4; matrix products, arithmetic and copies ran while one was open for 17% -> 26% of each run, Pallas kernels for 45% -> 40%
where the time goes in v3:
time: 861 us; the launch traced here: 853 us
  Pallas kernels  403 us (47%)
  matrix products  154 us (18%)
  local copies, waits for them, and re-layouts  101 us (12%)
  waiting for transfers between devices  85.3 us (10%)
  other arithmetic  51.1 us (6%)
  blocking collectives  24.7 us (3%)
  starting transfers between devices  18.2 us (2%)
  between operations  16.2 us (2%)
    pallas_call x8, Pallas kernels, call(): pl.pallas_call(kernel, out_shape=shapes, in_specs=[pl.BlockSpec(memory_sp...  364 us
    dot_general x4, matrix products, product_right(): lax.dot_general(left, right, (((1,), (1,)), ((), ())), preferred_element_...  51.3 us
    dot_general x4, matrix products, product(): return jnp.dot(left, right, preferred_element_type=f32)  50.6 us
    all_gather x3, waiting for transfers between devices, all_depths(): return lax.all_gather(mine, 'ctx', axis=0, tiled=True).reshape(width, -1)  43.9 us
    unnamed x189, local copies, waits for them, and re-layouts  41.1 us
    dot_general x5, matrix products, product_left(): lax.dot_general(left, right, (((0,), (0,)), ((), ())), preferred_element_...  38.2 us
    reduce_scatter x3, waiting for transfers between devices, sum_depths(): mine = lax.psum_scatter(grads, 'ctx', scatter_dimension=0, tiled=True)  31.9 us
    pallas_call x1, Pallas kernels, spread_small(): pl.pallas_call(spread_kernel, out_shape=jax.ShapeDtypeStruct((count, *own...  25.2 us
  transfers between devices with their start and end apart: 12, of which 4 were waited for; matrix products, arithmetic and copies ran while one was open for 26% of the time, Pallas kernels for 40%

profile of v3, /device:TPU:0, one launch (start us, length us, event | category | flops | bytes accessed | tf_op | source)
XLA Modules:
  0.0 853.4 jit_solution(5210815104306225027)
XLA Ops:
  11.3 24.7 %all_to_all.25 = bf16[4,128,1536]{1,2,0:T(8,128)(2,1)S(1)} all-to-all(bf16[4,128,1536]{1,2,0:T(8,128)(2,1)S(1)} %pad_maximum_fusion.4), channel_id=1, replica_groups=mesh['fsdp'=4,'ctx'=4,'tp'=2] {'fsdp'}, dimensions={0} | all-to-all | bytes 3145728 | tf_op jit(solution)/shard_map/all_to_all | solution.py:597
  40.4 4.6 all-to-all-start.1
  45.9 25.2 %shard_map.288 = f32[16,8,128]{2,1,0:T(8,128)} custom-call(f32[8,128]{1,0:T(8,128)} %fusion.43.own), custom_call_target="tpu_custom_call" | custom-call | bytes 1000000 | tf_op jit(solution)/shard_map/pallas_call | solution.py:474
  86.6 38.3 %shard_map.289 = bf16[8,256,2048]{2,1,0:T(8,128)(2,1)S(1)} custom-call(bf16[256,2048]{1,0:T(8,128)(2,1)S(1)} %reshape.682.refs_0_), custom_call_target="tpu_custom_call" | custom-call | bytes 2000000 | tf_op jit(solution)/shard_map/pallas_call | solution.py:345
  125.0 3.2 copy-done.1
  132.3 21.9 %all-gather.4.cloned.1.call-done = bf16[16,128,1536]{2,1,0:T(8,128)(2,1)} async-done(((bf16[4,128,1536]{2,1,0:T(8,128)(2,1)}), bf16[16,128,1536]{2,1,0:T(8,128)(2,1)}) %all-gather.4.cloned.1.call-update) | async-done | bytes 6291472 | tf_op jit(solution)/shard_map/all_gather | solution.py:600
  154.2 17.4 %fusion.60 = f32[2048,1536]{1,0:T(8,128)S(1)} fusion(bf16[2048,2048]{1,0:T(8,128)(2,1)} %bitcast.232, bf16[2048,1536]{1,0:T(8,128)(2,1)} %bitcast.316), kind=kOutput, calls=%fused_computation.192 | convolution fusion | flops 12884901888 | bytes 27262976 | tf_op jit(solution)/shard_map/dot_general | solution.py:53
  172.2 3.9 copy-done.32
  179.0 63.0 %shard_map.290 = (bf16[8,256,512]{2,1,0:T(8,128)(2,1)S(1)}, bf16[8,256,2048]{2,1,0:T(8,128)(2,1)}) custom-call(f32[8,256,512]{2,1,0:T(8,128)S(1)} %fusion.39.local, f32[1,512]{1,0:T(1,128)S(1)} %broadcast_in_dim.37.fade, bf16[256,2048]{1,0:T(8,128)(2,1)S(1)} %reshape.699.own), custom_call_target="tpu_custom_call" | custom-call | bytes 2000000 | tf_op jit(solution)/shard_map/pallas_call | solution.py:345
  242.0 3.4 slice.191
  255.1 3.4 multiply_convert_fusion.2
  258.5 9.1 %convolution_convert_fusion.3 = bf16[2048,2048]{1,0:T(8,128)(2,1)} fusion(bf16[2048,512]{1,0:T(8,128)(2,1)S(1)} %multiply_convert_fusion.2, bf16[2048,512]{1,0:T(8,128)(2,1)} %bitcast.322), kind=kOutput, calls=%fused_computation.3 | convolution fusion | flops 4299161600 | bytes 12582912 | tf_op jit(solution)/shard_map/dot_general | solution.py:61
  267.7 40.8 %shard_map.291 = f32[256,2048]{1,0:T(8,128)S(1)} custom-call(bf16[8,256,2048]{2,1,0:T(8,128)(2,1)} %bitcast.256), custom_call_target="tpu_custom_call" | custom-call | bytes 2000000 | tf_op jit(solution)/shard_map/pallas_call | solution.py:345
  316.6 39.5 %shard_map.292 = bf16[8,256,2048]{2,1,0:T(8,128)(2,1)S(1)} custom-call(bf16[256,2048]{1,0:T(8,128)(2,1)S(1)} %reshape.707.refs_0_), custom_call_target="tpu_custom_call" | custom-call | bytes 2000000 | tf_op jit(solution)/shard_map/pallas_call | solution.py:345
  356.1 3.3 copy-done.2
  359.4 22.0 %all-gather.8.cloned.1.call-done = bf16[16,128,1536]{2,1,0:T(8,128)(2,1)} async-done(((bf16[4,128,1536]{2,1,0:T(8,128)(2,1)}), bf16[16,128,1536]{2,1,0:T(8,128)(2,1)}) %all-gather.8.cloned.1.call-update) | async-done | bytes 6291472 | tf_op jit(solution)/shard_map/all_gather | solution.py:600
  381.4 12.5 %fusion.15 = f32[2048,1024]{1,0:T(8,128)S(1)} fusion(bf16[2048,2048]{1,0:T(8,128)(2,1)} %bitcast.241, bf16[2048,1536]{1,0:T(8,128)(2,1)} %bitcast.318), kind=kOutput, calls=%fused_computation.41 | convolution fusion | flops 8589934592 | bytes 20971520 | tf_op jit(solution)/shard_map/dot_general | solution.py:53
  393.9 10.8 %fusion.9 = (bf16[2048,512]{1,0:T(8,128)(2,1)S(1)}, bf16[2048,512]{1,0:T(8,128)(2,1)S(1)}, bf16[2048,512]{1,0:T(8,128)(2,1)S(1)}) fusion(f32[2048,1024]{1,0:T(8,128)S(1)} %fusion.15, bf16[2048,2048]{1,0:T(8,128)(2,1)} %bitcast.314, bf16[2048,1536]{1,0:T(8,128)(2,1)} %bitcast.319), kind=kOutput, calls=%fused_computation.18 | convolution fusion | flops 4322230272 | bytes 25165824 | tf_op jit(solution)/shard_map/dot_general | solution.py:53
  404.7 9.3 %convolution_convert_fusion.5 = bf16[2048,1024]{1,0:T(8,128)(2,1)S(1)} fusion(bf16[2048,2048]{1,0:T(8,128)(2,1)S(1)} %bitcast.242, bf16[2048,512]{1,0:T(8,128)(2,1)S(1)} %get-tuple-element.121, bf16[2048,512]{1,0:T(8,128)(2,1)S(1)} %get-tuple-element.120), kind=kOutput, calls=%fused_computation.39 | convolution fusion | flops 8600420352 | bytes 16777216 | tf_op jit(solution)/shard_map/dot_general | solution.py:57
  416.6 8.4 convolution_convert_fusion.8
  425.1 3.2 pad_maximum_fusion
  428.3 14.4 %convolution_convert_fusion.2 = bf16[2048,2048]{1,0:T(8,128)(2,1)} fusion(bf16[2048,1024]{1,0:T(8,128)(2,1)} %pad_maximum_fusion.1, bf16[2048,1536]{1,0:T(8,128)(2,1)} %bitcast.320), kind=kOutput, calls=%fused_computation.2 | convolution fusion | flops 8594128896 | bytes 16777216 | tf_op jit(solution)/shard_map/dot_general | solution.py:61
  442.8 41.2 %shard_map.293 = f32[256,2048]{1,0:T(8,128)S(1)} custom-call(bf16[8,256,2048]{2,1,0:T(8,128)(2,1)} %bitcast.255), custom_call_target="tpu_custom_call" | custom-call | bytes 2000000 | tf_op jit(solution)/shard_map/pallas_call | solution.py:345
  486.4 3.1 copy.150
  495.9 39.2 %shard_map.294 = bf16[8,256,2048]{2,1,0:T(8,128)(2,1)S(1)} custom-call(bf16[256,2048]{1,0:T(8,128)(2,1)S(1)} %reshape.715.refs_0_), custom_call_target="tpu_custom_call" | custom-call | bytes 2000000 | tf_op jit(solution)/shard_map/pallas_call | solution.py:345
  535.2 10.0 %multiply_reduce_fusion = (f32[512]{0:T(512)S(1)}, f32[2048]{0:T(1024)S(1)}, f32[512]{0:T(512)S(1)}, f32[2048,512]{1,0:T(8,128)S(1)}, bf16[2048,512]{1,0:T(8,128)(2,1)S(1)}) fusion(f32[8,256,512]{2,1,0:T(8,128)S(1)} %copy-done.14, f32[2048]{0:T(1024)S(1)} %rsqrt.31, f32[2048]{0:T(1024)S(1)} %bitcast.302, f32[512]{0:T(512)S(1)} %mul.535, ...), kind=kOutput, calls=%fused_computation.26 | convolution fusion | flops 4319081472 | bytes 25198592 | tf_op jit(solution)/shard_map/dot_general | solution.py:53
  545.2 3.4 fusion.52
  548.7 4.8 convolution_convert_fusion.6
  553.5 4.8 convolution_convert_fusion.7
  558.3 2.7 pad_maximum_fusion.2
  565.0 2.8 fusion.38.local
  567.9 8.4 convolution_convert_fusion.1
  578.5 61.5 %shard_map.295 = (bf16[8,256,512]{2,1,0:T(8,128)(2,1)S(1)}, f32[256,2048]{1,0:T(8,128)S(1)}) custom-call(f32[8,256,512]{2,1,0:T(8,128)S(1)} %copy-done, f32[1,512]{1,0:T(1,128)S(1)} %copy-done.9, bf16[8,256,2048]{2,1,0:T(8,128)(2,1)} %bitcast.258), custom_call_target="tpu_custom_call" | custom-call | bytes 2000000 | tf_op jit(solution)/shard_map/pallas_call | solution.py:345
  642.3 3.0 multiply_convert_fusion.3
  657.0 10.9 %convolution_convert_fusion.4 = bf16[2048,1024]{1,0:T(8,128)(2,1)} fusion(bf16[2048,2048]{1,0:T(8,128)(2,1)S(1)} %bitcast.238, bf16[2048,1024]{1,0:T(8,128)(2,1)S(1)} %constant_dynamic-update-slice_fusion), kind=kOutput, calls=%fused_computation.38 | convolution fusion | flops 8592031744 | bytes 16777216 | tf_op jit(solution)/shard_map/dot_general | solution.py:57
  669.8 4.6 all-to-all-start.4
  674.4 19.3 %convolution_convert_fusion = bf16[2048,2048]{1,0:T(8,128)(2,1)} fusion(bf16[2048,1536]{1,0:T(8,128)(2,1)} %bitcast.317, bf16[2048,512]{1,0:T(8,128)(2,1)} %copy-done.79, bf16[2048,1024]{1,0:T(8,128)(2,1)} %copy-done.56), kind=kOutput, calls=%fused_computation | convolution fusion | flops 12901679104 | bytes 20971520 | tf_op jit(solution)/shard_map/dot_general | solution.py:61
  696.1 2.9 copy.155
  699.0 40.3 %shard_map.296 = f32[256,2048]{1,0:T(8,128)S(1)} custom-call(bf16[8,256,2048]{2,1,0:T(8,128)(2,1)} %bitcast.254), custom_call_target="tpu_custom_call" | custom-call | bytes 2000000 | tf_op jit(solution)/shard_map/pallas_call | solution.py:345
  743.7 4.2 convert_element_type.210
  750.7 13.9 %shard_map.297 = f32[8,128]{1,0:T(8,128)} custom-call(f32[32,8,128]{2,1,0:T(8,128)} %bitcast.290), custom_call_target="tpu_custom_call" | custom-call | bytes 1000000 | tf_op jit(solution)/shard_map/pallas_call | solution.py:524
  765.3 31.9 %reduce-scatter.8.cloned.1.call-done = bf16[512,1024]{1,0:T(8,128)(2,1)} async-done(((bf16[2048,1024]{1,0:T(8,128)(2,1)}), bf16[512,1024]{1,0:T(8,128)(2,1)}) %reduce-scatter.8.cloned.1.call-update) | async-done | bytes 1048592 | tf_op jit(solution)/shard_map/reduce_scatter | solution.py:680
  797.2 4.3 all-to-all-start.2
  801.5 4.6 add_convert_fusion.2
  806.1 9.4 %all-to-all-done.2 = bf16[4,128,1024]{2,1,0:T(8,128)(2,1)} async-done(((bf16[4,128,1024]{2,1,0:T(8,128)(2,1)}), bf16[4,128,1024]{2,1,0:T(8,128)(2,1)}, u32[]{:S(2)}, u32[]{:S(2)}) %all-to-all-start.2) | async-done | bytes 1048608 | tf_op jit(solution)/shard_map/all_to_all | solution.py:684
  815.5 3.8 all-to-all-start.3
  819.3 3.3 slice_bitcast_fusion
  836.4 2.8 maximum_select_fusion.1
  (328 shorter events, 113.7 us)
Async XLA Ops:
  7.2 3.7 copy-start.45
  7.2 147.0 %all-gather.4.cloned.1.call-start = ((), (), s32[]{:S(2)}) async-start(), calls=%async_computation.8 | async-start | bytes 7864320 | tf_op jit(solution)/shard_map/all_gather | solution.py:600
  40.4 4.7 copy-start.75
  40.4 4.8 copy-start.76
  40.4 4.9 copy-start.69
  40.4 4.9 copy-start.70
  40.4 4.9 copy-start.71
  40.4 4.9 copy-start.72
  40.4 4.9 copy-start.73
  40.4 89.1 %all-to-all-start.1 = ((bf16[4,128,2048]{1,2,0:T(8,128)(2,1)}), bf16[4,128,2048]{1,2,0:T(8,128)(2,1)}, u32[]{:S(2)}, u32[]{:S(2)}) async-start(bf16[4,128,2048]{1,2,0:T(8,128)(2,1)} %pad_maximum_fusion.3), calls=%async_computation.1 | async-start | bytes 4194304 | tf_op jit(solution)/shard_map/all_to_all | solution.py:597
  45.0 213.6 %all-gather.6.cloned.1.call-start = ((), (), s32[]{:S(2)}) async-start(), calls=%async_computation.9 | async-start | bytes 2621440 | tf_op jit(solution)/shard_map/all_gather | solution.py:600
  79.0 3.7 copy-start.30
  128.2 49.8 %copy-start.63 = (f32[256]{0:T(256)}, f32[256]{0:T(256)S(1)}, u32[]{:S(2)}) copy-start(f32[256]{0:T(256)S(1)} %get-tuple-element.167) | copy-start | bytes 3076
  128.2 123.2 %copy-start.65 = (f32[256]{0:T(256)}, f32[256]{0:T(256)S(1)}, u32[]{:S(2)}) copy-start(f32[256]{0:T(256)S(1)} %get-tuple-element.168) | copy-start | bytes 3076
  128.3 49.3 %copy-start.54 = (f32[8,256]{1,0:T(8,128)}, f32[8,256]{1,0:T(8,128)S(1)}, u32[]{:S(2)}) copy-start(f32[8,256]{1,0:T(8,128)S(1)} %compare_select_fusion) | copy-start | bytes 24580
  129.5 46.6 %copy-start.42 = (f32[256,128]{1,0:T(8,128)}, f32[256,128]{1,0:T(8,128)S(1)}, u32[]{:S(2)}) copy-start(f32[256,128]{1,0:T(8,128)S(1)} %get-tuple-element.158) | copy-start | bytes 393220
  131.7 249.7 %all-gather.8.cloned.1.call-start = ((), (), s32[]{:S(2)}) async-start(), calls=%async_computation.10 | async-start | bytes 7864320 | tf_op jit(solution)/shard_map/all_gather | solution.py:600
  171.5 4.6 copy-start.32
  171.8 6.2 copy-start.18
  179.0 63.0 %copy-start.8 = (f32[1,512]{1,0:T(1,128)}, f32[1,512]{1,0:T(1,128)S(1)}, u32[]{:S(2)}) copy-start(f32[1,512]{1,0:T(1,128)S(1)} %broadcast_in_dim.37.fade) | copy-start | bytes 6148
  242.0 9.5 %copy-start.4 = (bf16[8,256,512]{2,1,0:T(8,128)(2,1)}, bf16[8,256,512]{2,1,0:T(8,128)(2,1)S(1)}, u32[]{:S(2)}) copy-start(bf16[8,256,512]{2,1,0:T(8,128)(2,1)S(1)} %get-tuple-element.36) | copy-start | bytes 6291460
  248.1 328.2 %reduce-scatter.4.cloned.1.call-start = ((), (), s32[]{:S(2)}) async-start(), calls=%async_computation.11 | async-start | bytes 7864320 | tf_op jit(solution)/shard_map/reduce_scatter | solution.py:680
  258.5 9.2 %copy-start.40 = (bf16[2048,512]{1,0:T(8,128)(2,1)}, bf16[2048,512]{1,0:T(8,128)(2,1)S(1)}, u32[]{:S(2)}) copy-start(bf16[2048,512]{1,0:T(8,128)(2,1)S(1)} %multiply_convert_fusion.2) | copy-start | bytes 6291460
  393.9 10.8 %copy-start.3 = (bf16[8,256,2048]{2,1,0:T(8,128)(2,1)S(1)}, bf16[8,256,2048]{2,1,0:T(8,128)(2,1)}, u32[]{:S(2)}) copy-start(bf16[8,256,2048]{2,1,0:T(8,128)(2,1)} %copy-done.2) | copy-start | bytes 25165828
  404.7 12.0 %copy-start.77 = (bf16[2048,512]{1,0:T(8,128)(2,1)}, bf16[2048,512]{1,0:T(8,128)(2,1)S(1)}, u32[]{:S(2)}) copy-start(bf16[2048,512]{1,0:T(8,128)(2,1)S(1)} %get-tuple-element.124) | copy-start | bytes 6291460
  428.3 319.7 %reduce-scatter.6.cloned.1.call-start = ((), (), s32[]{:S(2)}) async-start(), calls=%async_computation.12 | async-start | bytes 5242880 | tf_op jit(solution)/shard_map/reduce_scatter | solution.py:680
  495.9 39.3 %copy-start.14 = (f32[8,256,512]{2,1,0:T(8,128)S(1)}, f32[8,256,512]{2,1,0:T(8,128)}, u32[]{:S(2)}) copy-start(f32[8,256,512]{2,1,0:T(8,128)} %copy-done.13) | copy-start | bytes 12582916
  495.9 39.3 %copy-start.74 = (bf16[16,128,512]{2,1,0:T(8,128)(2,1)S(1)}, bf16[16,128,512]{2,1,0:T(8,128)(2,1)}, u32[]{:S(2)}) copy-start(bf16[16,128,512]{2,1,0:T(8,128)(2,1)} %all-gather.6.cloned.1.call-done) | copy-start | bytes 6291460
  545.2 8.3 copy-start.79
  545.2 8.3 slice-start
  548.7 4.8 slice-start.1
  561.1 4.0 copy-start.34
  561.1 4.0 copy-start.36
  561.1 4.0 copy-start.66
  567.9 8.4 copy-start.9
  641.4 155.8 %reduce-scatter.8.cloned.1.call-start = ((), (), s32[]{:S(2)}) async-start(), calls=%async_computation.13 | async-start | bytes 5242880 | tf_op jit(solution)/shard_map/reduce_scatter | solution.py:680
  652.6 4.4 slice-start.2
  669.8 73.9 %all-to-all-start.4 = ((bf16[4,128,1536]{2,1,0:T(8,128)(2,1)}), bf16[4,128,1536]{2,1,0:T(8,128)(2,1)}, u32[]{:S(2)}, u32[]{:S(2)}) async-start(bf16[4,128,1536]{2,1,0:T(8,128)(2,1)} %bitcast.275), calls=%async_computation.7 | async-start | bytes 3145728 | tf_op jit(solution)/shard_map/all_to_all | solution.py:684
  674.4 19.3 %copy-start.7 = (f32[256,2048]{1,0:T(8,128)S(1)}, f32[256,2048]{1,0:T(8,128)}, u32[]{:S(2)}) copy-start(f32[256,2048]{1,0:T(8,128)} %copy-done.6) | copy-start | bytes 6291460
  743.7 5.0 copy-start.25
  743.7 4.3 copy-start.17
  743.7 4.3 copy-start.53
  743.7 4.3 copy-start.58
  749.9 51.6 %copy-start.12 = (f32[256,2048]{0,1:T(8,128)S(1)}, f32[256,2048]{0,1:T(8,128)}, u32[]{:S(2)}) copy-start(f32[256,2048]{0,1:T(8,128)} %copy-done.10) | copy-start | bytes 6291460
  797.2 18.3 %all-to-all-start.2 = ((bf16[4,128,1024]{2,1,0:T(8,128)(2,1)}), bf16[4,128,1024]{2,1,0:T(8,128)(2,1)}, u32[]{:S(2)}, u32[]{:S(2)}) async-start(bf16[4,128,1024]{2,1,0:T(8,128)(2,1)} %bitcast.279), calls=%async_computation.5 | async-start | bytes 2097152 | tf_op jit(solution)/shard_map/all_to_all | solution.py:684
  806.1 30.3 %collective-permute-start.1 = (bf16[256,2048]{0,1:T(8,128)(2,1)}, bf16[256,2048]{0,1:T(8,128)(2,1)}, u32[]{:S(2)}, u32[]{:S(2)}) collective-permute-start(bf16[256,2048]{0,1:T(8,128)(2,1)} %get-tuple-element.159), channel_id=1, source_target_pairs={{0,1},{1,0},{2,3},{3,2},{4,5},{5,4},{6,7},{7,6},{8,9},{9,8},{10,11... | collective-permute-start | bytes 3145736 | tf_op jit(solution)/shard_map/ppermute | solution.py:540
  815.5 18.1 %all-to-all-start.3 = ((bf16[4,128,1024]{2,1,0:T(8,128)(2,1)}), bf16[4,128,1024]{2,1,0:T(8,128)(2,1)S(1)}, u32[]{:S(2)}, u32[]{:S(2)}) async-start(bf16[4,128,1024]{2,1,0:T(8,128)(2,1)} %bitcast.278), calls=%async_computation.6 | async-start | bytes 2097152 | tf_op jit(solution)/shard_map/all_to_all | solution.py:684
  829.1 12.5 %collective-permute-start = (bf16[256,2048]{0,1:T(8,128)(2,1)S(1)}, bf16[256,2048]{0,1:T(8,128)(2,1)}, u32[]{:S(2)}, u32[]{:S(2)}) collective-permute-start(bf16[256,2048]{0,1:T(8,128)(2,1)S(1)} %copy-done.39), channel_id=1, source_target_pairs={{0,1},{1,0},{2,3},{3,2},{4,5},{5,4},{6,7},{7,6},{8,9},{9,8},{10,11... | collective-permute-start | bytes 3145736 | tf_op jit(solution)/shard_map/ppermute | solution.py:540
  (48 other events, 87.4 us)
Sparse Core Ops, SparseCore 0:
  37.7 116.4 all-gather.3
  156.3 56.2 all-gather.5
  248.2 133.1 all-gather.7
  428.4 108.9 reduce-scatter.3
  641.5 73.9 reduce-scatter.5
  717.8 79.3 reduce-scatter.7

commit v4 on v3

--- a/solution.py
+++ b/solution.py
@@ -78,7 +78,19 @@
     )
 
 
-def gather_steps(own, out, keep, send, recv):
+def reorder(src, dst, kind, back):
+    nf, nc = lax.axis_size("fsdp"), lax.axis_size("ctx")
+    depth = src.shape[-1] // (nf * nc)
+    for f in range(nf):
+        for c in range(nc):
+            plain, mixed = (f * nc + c) * depth, (c * nf + f) * depth
+            if back:
+                plain, mixed = mixed, plain
+            dst[:, mixed : mixed + depth] = src[:, plain : plain + depth].astype(kind)
+
+
+def gather_steps(plain, out, mixed, keep, send, recv):
+    own = plain if mixed is None else mixed
     f, t = lax.axis_index("fsdp"), lax.axis_index("tp")
     fx, fy, fd = beside(f)
     x, y, core = {"fsdp": fx}, {"fsdp": fy}, {"tp": 1 - t}
@@ -107,6 +119,8 @@
         sent.append(copy)
 
     def begin():
+        if mixed is not None:
+            reorder(plain, mixed, mixed.dtype, False)
         local.start()
         for copy in first:
             copy.start()
@@ -141,30 +155,32 @@
     return begin, relay, rest, diagonal, end
 
 
-def gather_scratch():
+def in_kernel(width):
+    return width // (lax.axis_size("fsdp") * lax.axis_size("ctx")) % 128 == 0
+
+
+def gather_scratch(own):
     return [
+        pltpu.VMEM(own.shape if in_kernel(own.shape[1]) else (16, 128), own.dtype),
         pltpu.SemaphoreType.DMA,
         pltpu.SemaphoreType.DMA((14,)),
         pltpu.SemaphoreType.DMA((14,)),
     ]
 
 
-def scatter_steps(partial, out, mine, theirs, total, diag, last, keep, send, recv):
+def scatter_steps(start, left, right, out, mine, sent, theirs, total, diag, last, send, recv):
     f, t = lax.axis_index("fsdp"), lax.axis_index("tp")
     fx, fy, fd = beside(f)
     x, y, core = {"fsdp": fx}, {"fsdp": fy}, {"tp": 1 - t}
     half = out.shape[0] // 2
+    order = [fd, fy, fx, f]
+    tile, size = 512, left.shape[2]
 
     def part(ref, h):
         return ref.at[pl.ds(h * half, half)]
 
     crossing = [
-        remote(partial.at[2 * who + 1 - t], theirs.at[i], send.at[i], recv.at[i], core)
-        for i, who in enumerate([fd, fy, fx, f])
-    ]
-    kept = [
-        pltpu.make_async_copy(partial.at[2 * who + t], mine.at[i], keep.at[i])
-        for i, who in enumerate([fd, fy, fx, f])
+        remote(sent.at[i], theirs.at[i], send.at[i], recv.at[i], core) for i in range(4)
     ]
     d0 = remote(part(total.at[0], 0), diag.at[0], send.at[4], recv.at[4], x)
     d1 = remote(part(total.at[0], 1), diag.at[1], send.at[5], recv.at[5], y)
@@ -173,26 +189,46 @@
     y0 = remote(part(total.at[1], 0), part(last.at[1], 0), send.at[8], recv.at[8], y)
     x1 = remote(part(total.at[2], 1), part(last.at[0], 1), send.at[9], recv.at[9], x)
 
-    def begin():
-        for a, b in zip(crossing, kept):
-            a.start()
-            b.start()
+    def make(block, put):
+        def piece(j, carry):
+            columns = pl.ds(pl.multiple_of(j * tile, tile), tile)
+            put(columns, product_right(left[block], right[columns, start : start + size]))
+            return carry
+
+        lax.fori_loop(0, out.shape[1] // tile, piece, 0)
+
+    def cross(i):
+        def put(columns, value):
+            sent[i, :, columns] = value.astype(sent.dtype)
+
+        make(2 * order[i] + 1 - t, put)
+        crossing[i].start()
+
+    def keep(i):
+        def put(columns, value):
+            mine[:, columns] = value
+
+        make(2 * order[i] + t, put)
 
     def add(i):
-        kept[i].wait()
+        keep(i)
         crossing[i].wait_recv()
-        total[i] = (mine[i].astype(f32) + theirs[i].astype(f32)).astype(total.dtype)
+        total[i] = (mine[...] + theirs[i].astype(f32)).astype(total.dtype)
 
     def diagonal():
+        cross(0)
+        cross(1)
         add(0)
         d0.start()
         d1.start()
 
     def straight():
+        cross(2)
         add(1)
         y1.start()
         add(2)
         x0.start()
+        cross(3)
 
     def relay():
         d0.wait_recv()
@@ -201,29 +237,32 @@
         d1.wait_recv()
         total[2, half:] = (total[2, half:].astype(f32) + diag[1].astype(f32)).astype(total.dtype)
         x1.start()
+        keep(3)
+        crossing[3].wait_recv()
+        mine[...] += theirs[3].astype(f32)
 
     def end():
-        kept[3].wait()
-        crossing[3].wait_recv()
         for copy in (y1, x0, y0, x1):
             copy.wait_recv()
-        out[...] = (mine[3].astype(f32) + theirs[3].astype(f32)) + (
-            last[0].astype(f32) + last[1].astype(f32)
-        )
+        mine[...] += last[0].astype(f32) + last[1].astype(f32)
+        if in_kernel(out.shape[1]):
+            reorder(mine, out, out.dtype, True)
+        else:
+            out[...] = mine[...]
         for copy in (*crossing, d0, d1, y1, x0, y0, x1):
             copy.wait_send()
 
-    return begin, diagonal, straight, relay, end
-
-
-def scatter_scratch(rows, width, kind):
+    return diagonal, straight, relay, end
+
+
+def scatter_scratch(rows, width):
     return [
-        pltpu.VMEM((4, rows, width), kind),
-        pltpu.VMEM((4, rows, width), kind),
-        pltpu.VMEM((3, rows, width), kind),
-        pltpu.VMEM((2, rows // 2, width), kind),
-        pltpu.VMEM((2, rows, width), kind),
-        pltpu.SemaphoreType.DMA((4,)),
+        pltpu.VMEM((rows, width), f32),
+        pltpu.VMEM((4, rows, width), bf16),
+        pltpu.VMEM((4, rows, width), bf16),
+        pltpu.VMEM((3, rows, width), bf16),
+        pltpu.VMEM((2, rows // 2, width), bf16),
+        pltpu.VMEM((2, rows, width), bf16),
         pltpu.SemaphoreType.DMA((10,)),
         pltpu.SemaphoreType.DMA((10,)),
     ]
@@ -294,22 +333,26 @@
         pl.semaphore_wait(barrier, 3)
 
 
+def gather_with(own, full, mixed, *scratch):
+    return gather_steps(own, full, mixed if in_kernel(own.shape[1]) else None, *scratch)
+
+
 def gather_kernel(*refs):
-    steps = gather_steps(*refs)
+    steps = gather_with(*refs)
     greet_plane()
     for step in steps:
         step()
 
 
-def scatter_kernel(*refs):
-    steps = scatter_steps(*refs)
+def scatter_kernel(start, *refs):
+    steps = scatter_steps(start, *refs)
     greet_plane()
     for step in steps:
         step()
 
 
 def pass_gather_kernel(by, local, fade, own, out, full, held, send, recv, *scratch):
-    begin, relay, rest, diagonal, end = gather_steps(own, full, *scratch)
+    begin, relay, rest, diagonal, end = gather_with(own, full, *scratch)
     step, done = pass_steps(by, local, fade, out, held, send, recv)
     pieces = local.shape[0]
     greet_plane(by)
@@ -324,16 +367,16 @@
     done()
 
 
-def pass_scatter_kernel(by, local, fade, partial, out, own, held, send, recv, *scratch):
-    begin, diagonal, straight, relay, end = scatter_steps(partial, own, *scratch)
+def pass_scatter_kernel(by, start, local, fade, left, right, out, own, held, send, recv, *scratch):
+    diagonal, straight, relay, end = scatter_steps(start, left, right, own, *scratch)
     step, done = pass_steps(by, local, fade, out, held, send, recv)
     pieces = local.shape[0]
     greet_plane(by)
-    begin()
     lax.fori_loop(0, pieces // 4, step, 0)
     diagonal()
+    lax.fori_loop(pieces // 4, pieces // 2, step, 0)
     straight()
-    lax.fori_loop(pieces // 4, 3 * pieces // 4, step, 0)
+    lax.fori_loop(pieces // 2, 3 * pieces // 4, step, 0)
     relay()
     lax.fori_loop(3 * pieces // 4, pieces, step, 0)
     end()
@@ -345,24 +388,37 @@
     return pl.pallas_call(
         kernel,
         out_shape=shapes,
-        in_specs=[pl.BlockSpec(memory_space=space) for space in ins],
+        in_specs=ins,
         out_specs=tuple(pl.BlockSpec(memory_space=space) for space in spaces),
         scratch_shapes=scratch,
         compiler_params=pltpu.CompilerParams(
-            collective_id=collective_id, has_side_effects=True, vmem_limit_bytes=44 << 20
+            collective_id=collective_id, has_side_effects=True, vmem_limit_bytes=52 << 20
         ),
         cost_estimate=pl.CostEstimate(flops=0, bytes_accessed=2_000_000, transcendentals=0),
     )(*args)
 
 
+def vmem():
+    return pl.BlockSpec(memory_space=pltpu.VMEM)
+
+
+def perm(v):
+    nf, nc = lax.axis_size("fsdp"), lax.axis_size("ctx")
+    return v.reshape(len(v), nf, nc, -1).transpose(0, 2, 1, 3).reshape(v.shape)
+
+
+def unperm(v):
+    nf, nc = lax.axis_size("fsdp"), lax.axis_size("ctx")
+    return v.reshape(len(v), nc, nf, -1).transpose(0, 2, 1, 3).reshape(v.shape)
+
+
 def gathered(own):
     rows, width = own.shape
     return jax.ShapeDtypeStruct((8, rows, width), own.dtype), pl.ANY
 
 
-def scattered(partial):
-    rows, width = partial.shape
-    return jax.ShapeDtypeStruct((rows // 8, width), f32), pltpu.VMEM
+def scattered(left, right):
+    return jax.ShapeDtypeStruct((left.shape[0] // 8, right.shape[0]), f32), pltpu.VMEM
 
 
 def passed(local):
@@ -378,35 +434,45 @@
     ]
 
 
-def in_eights(partial):
-    return partial.reshape(8, -1, partial.shape[1])
+def in_eights(left):
+    return left.reshape(8, -1, left.shape[1])
+
+
+def ready(own):
+    return own if in_kernel(own.shape[1]) else perm(own)
+
+
+def plain(own):
+    return own if in_kernel(own.shape[1]) else unperm(own)
 
 
 def gather_rows(own, collective_id):
-    (out,) = call(gather_kernel, collective_id, [gathered(own)], [pl.ANY], gather_scratch(), own)
+    own = ready(own)
+    (out,) = call(gather_kernel, collective_id, [gathered(own)], [vmem()], gather_scratch(own), own)
     return out.reshape(-1, own.shape[1])
 
 
-def scatter_rows(partial, collective_id):
-    scratch = scatter_scratch(partial.shape[0] // 8, partial.shape[1], partial.dtype)
+def scatter_product(left, right, start, collective_id):
     (out,) = call(
-        scatter_kernel,
+        functools.partial(scatter_kernel, start),
         collective_id,
-        [scattered(partial)],
-        [pl.ANY],
-        scratch,
-        in_eights(partial),
-    )
-    return out
+        [scattered(left, right)],
+        [vmem(), vmem()],
+        scatter_scratch(left.shape[0] // 8, right.shape[0]),
+        in_eights(left),
+        right,
+    )
+    return plain(out)
 
 
 def pass_and_gather(local, fade, own, by, collective_id):
+    own = ready(own)
     out, full = call(
         functools.partial(pass_gather_kernel, by),
         collective_id,
         [passed(local), gathered(own)],
-        [pltpu.VMEM, pltpu.VMEM, pl.ANY],
-        pass_scratch(local) + gather_scratch(),
+        [vmem(), vmem(), vmem()],
+        pass_scratch(local) + gather_scratch(own),
         local,
         jnp.full((1, local.shape[2]), fade, f32),
         own,
@@ -414,76 +480,269 @@
     return out, full.reshape(-1, own.shape[1])
 
 
-def pass_and_scatter(local, fade, partial, by, collective_id):
-    rows, width = partial.shape
-    return call(
-        functools.partial(pass_scatter_kernel, by),
+def pass_and_scatter(local, fade, left, right, start, by, collective_id):
+    out, own = call(
+        functools.partial(pass_scatter_kernel, by, start),
         collective_id,
-        [passed(local), scattered(partial)],
-        [pltpu.VMEM, pltpu.VMEM, pl.ANY],
-        pass_scratch(local) + scatter_scratch(rows // 8, width, partial.dtype),
+        [passed(local), scattered(left, right)],
+        [vmem(), vmem(), vmem(), vmem()],
+        pass_scratch(local) + scatter_scratch(left.shape[0] // 8, right.shape[0]),
         local,
         jnp.full((1, local.shape[2]), fade, f32),
-        in_eights(partial),
-    )
+        in_eights(left),
+        right,
+    )
+    return out, plain(own)
 
 
 def peer_of(place, nc, nt):
     return {"fsdp": place // (nc * nt), "ctx": place // nt % nc, "tp": place % nt}
 
 
-def spread_kernel(own, out, keep, send, recv):
-    nc = lax.axis_size("ctx")
-    count = out.shape[0]
-    t = lax.axis_index("tp")
-    place = lax.axis_index("fsdp") * nc + lax.axis_index("ctx")
+def line_steps(home, place, arrived, send, recv):
+    nf, nc = lax.axis_size("fsdp"), lax.axis_size("ctx")
+    f, c = lax.axis_index("fsdp"), lax.axis_index("ctx")
+    order = [f, *beside(f)]
+    above, below = c < nc - 1, c > 0
+
+    def copy(src, place_of, who, up):
+        chunk = place_of * nf + who
+        return remote(
+            src,
+            place(place_of, who),
+            send.at[chunk if up else nc * nf + chunk],
+            recv.at[chunk],
+            {"ctx": lax.rem(c + 1, nc) if up else lax.rem(c + nc - 1, nc)},
+        )
+
+    def first(i):
+        who = order[i]
+        arrived(i)
+
+        @pl.when(above)
+        def _():
+            copy(home(who), c, who, True).start()
+
+        @pl.when(below)
+        def _():
+            copy(home(who), c, who, False).start()
+
+    def step(k, carry):
+        for who in order:
+
+            @pl.when(c - k >= 0)
+            def _():
+                copy(place(c - k, who), c - k, who, True).wait_recv()
+
+                @pl.when(above)
+                def _():
+                    copy(place(c - k, who), c - k, who, True).start()
+
+            @pl.when(c + k < nc)
+            def _():
+                copy(place(c + k, who), c + k, who, False).wait_recv()
+
+                @pl.when(below)
+                def _():
+                    copy(place(c + k, who), c + k, who, False).start()
+
+        return carry
+
+    def end():
+        def one(other, carry):
+            for who in order:
+
+                @pl.when(above & (other <= c))
+                def _():
+                    copy(place(other, who), other, who, True).wait_send()
+
+                @pl.when(below & (other >= c))
+                def _():
+                    copy(place(other, who), other, who, False).wait_send()
+
+            return carry
+
+        lax.fori_loop(0, nc, one, 0)
+
+    return first, step, end
+
+
+def line_scratch():
+    count = lax.axis_size("fsdp") * lax.axis_size("ctx")
+    return [pltpu.SemaphoreType.DMA((2 * count,)), pltpu.SemaphoreType.DMA((count,))]
+
+
+def start_kernel(sizes, split, turned, own, small, *refs):
+    count = len(sizes)
+    weights = list(refs[:count])
+    attn, rest, full, everyone = refs[count : count + 4]
+    (
+        turns,
+        gains,
+        normed,
+        mixed,
+        gather_keep,
+        gather_send,
+        gather_recv,
+        line_send,
+        line_recv,
+        keep,
+        send,
+        recv,
+        small_send,
+        small_recv,
+    ) = refs[count + 4 :]
+    nf, nc = lax.axis_size("fsdp"), lax.axis_size("ctx")
+    f, c, t = lax.axis_index("fsdp"), lax.axis_index("ctx"), lax.axis_index("tp")
+    here, places = f * nc + c, nf * nc
+    depth = weights[0].shape[0]
+    across = [weights[i] for i in turned]
+    for n, i in enumerate(turned):
+        weights[i] = turns.at[n]
+    near = beside(f)
+    starts = [sum(sizes[:i]) if i < split else sum(sizes[split:i]) for i in range(count)]
+
+    def peer(i):
+        other = lax.rem(here + i, places)
+        return {"fsdp": other // nc, "ctx": other % nc}
+
     barrier = pltpu.get_barrier_semaphore()
-
-    def peer(i):
-        other = lax.rem(place + i, count)
-        return {"fsdp": other // nc, "ctx": other % nc}
+    pl.semaphore_signal(barrier, inc=1, device_id={"tp": 1 - t}, device_id_type=MESH)
 
     def hello(i, carry):
         pl.semaphore_signal(barrier, inc=1, device_id=peer(i), device_id_type=MESH)
         return carry
 
-    lax.fori_loop(1, count, hello, 0)
-    pl.semaphore_wait(barrier, count - 1)
-
-    def copy(i):
-        return remote(own, out.at[place], send.at[i], recv.at[i], peer(i))
+    lax.fori_loop(1, places, hello, 0)
+    pl.semaphore_wait(barrier, places)
+
+    def chunk(place_of, who):
+        rows = pl.multiple_of((place_of * nf + who) * depth, depth)
+        return attn.at[pl.ds(rows, depth)]
+
+    def columns(i, who):
+        return weights[i].at[:, pl.ds(pl.multiple_of(who * sizes[i], sizes[i]), sizes[i])]
+
+    def target(i):
+        where = chunk(c, f) if i < split else rest.at[f]
+        return where.at[:, pl.ds(starts[i], sizes[i])]
+
+    def hand_out(i, n):
+        return remote(
+            columns(i, near[n]),
+            target(i),
+            send.at[3 * i + n],
+            recv.at[n if i < split else 3 + n],
+            {"fsdp": near[n]},
+        )
+
+    def hold(i):
+        return pltpu.make_async_copy(columns(i, f), target(i), keep.at[0 if i < split else 1])
+
+    for i in range(split):
+        hold(i).start()
+    for n in range(3):
+        for i in range(split):
+            hand_out(i, n).start()
+
+    def arrived(i):
+        if i == 0:
+            pltpu.make_async_copy(chunk(c, f), chunk(c, f), keep.at[0]).wait()
+        else:
+            who = near[i - 1]
+            remote(
+                chunk(c, who), chunk(c, who), send.at[0], recv.at[i - 1], {"fsdp": who}
+            ).wait_recv()
+
+    first, step, end = line_steps(lambda who: chunk(c, who), chunk, arrived, line_send, line_recv)
+    first(0)
+
+    def tell(i):
+        return remote(small, everyone.at[here], small_send.at[i], small_recv.at[i], peer(i))
 
     def go(i, carry):
-        copy(i).start()
+        tell(i).start()
         return carry
 
-    lax.fori_loop(1, count, go, 0)
-    local = pltpu.make_async_copy(own, out.at[place], keep)
-    local.start()
-    local.wait()
-
-    def done(i, carry):
-        copy(i).wait()
+    def told(i, carry):
+        tell(i).wait()
         return carry
 
-    lax.fori_loop(1, count, done, 0)
-
-
-def spread_small(own, collective_id):
-    count = lax.axis_size("fsdp") * lax.axis_size("ctx")
-    return pl.pallas_call(
-        spread_kernel,
-        out_shape=jax.ShapeDtypeStruct((count, *own.shape), own.dtype),
-        in_specs=[pl.BlockSpec(memory_space=pltpu.VMEM)],
-        out_specs=pl.BlockSpec(memory_space=pltpu.VMEM),
-        scratch_shapes=[
-            pltpu.SemaphoreType.DMA,
+    lax.fori_loop(1, places, go, 0)
+    everyone[here] = small[...]
+    first(1)
+    lax.fori_loop(1, places, told, 0)
+    for i in range(places):
+        for j in range(2):
+            gains[j : j + 1, i * depth : (i + 1) * depth] = everyone[i, j : j + 1, :depth]
+    rows = normed.shape[0]
+    mine = own[pl.ds(pl.multiple_of(t * rows, rows), rows), :].astype(f32)
+    normed[...] = layer_norm(mine, gains[0:1, :], gains[1:2, :]).astype(bf16)
+    begin, relay, others, diagonal, finish = gather_steps(
+        normed, full, mixed, gather_keep, gather_send, gather_recv
+    )
+    begin()
+    first(2)
+    first(3)
+    step(1, 0)
+    relay()
+    for n in range(len(turned)):
+        turns[n] = across[n][...].T
+    for i in range(split, count):
+        hold(i).start()
+        for n in range(3):
+            hand_out(i, n).start()
+    lax.fori_loop(2, 3, step, 0)
+    others()
+    diagonal()
+    lax.fori_loop(3, nc, step, 0)
+    finish()
+    pltpu.make_async_copy(rest.at[f], rest.at[f], keep.at[1]).wait()
+    for n in range(3):
+        where = rest.at[near[n]]
+        remote(where, where, send.at[0], recv.at[3 + n], {"fsdp": near[n]}).wait_recv()
+    for i in range(count):
+        for n in range(3):
+            hand_out(i, n).wait_send()
+    end()
+
+
+def start(tokens, small, weights, split, turned, collective_id):
+    nf, nc = lax.axis_size("fsdp"), lax.axis_size("ctx")
+    rows, width = tokens.shape
+    rows //= lax.axis_size("tp")
+    depth = weights[0].shape[0]
+    sizes = [w.size // depth // nf for w in weights]
+    anywhere = pl.BlockSpec(memory_space=pl.ANY)
+    count = nf * nc
+    return call(
+        functools.partial(start_kernel, sizes, split, turned),
+        collective_id,
+        [
+            (jax.ShapeDtypeStruct((width, sum(sizes[:split])), bf16), pl.ANY),
+            (jax.ShapeDtypeStruct((nf, depth, sum(sizes[split:])), bf16), pl.ANY),
+            (jax.ShapeDtypeStruct((8, rows, width), bf16), pl.ANY),
+            (jax.ShapeDtypeStruct((count, *small.shape), f32), pltpu.VMEM),
+        ],
+        [vmem(), vmem()]
+        + [vmem() if i in turned else anywhere for i in range(len(weights))],
+        [
+            pltpu.VMEM((len(turned), depth, sizes[turned[0]] * nf), bf16),
+            pltpu.VMEM((8, width), f32),
+            pltpu.VMEM((rows, width), bf16),
+            pltpu.VMEM((rows, width), bf16),
+            *gather_scratch(tokens)[1:],
+            *line_scratch(),
+            pltpu.SemaphoreType.DMA((2,)),
+            pltpu.SemaphoreType.DMA((3 * len(weights),)),
+            pltpu.SemaphoreType.DMA((6,)),
             pltpu.SemaphoreType.DMA((count,)),
             pltpu.SemaphoreType.DMA((count,)),
         ],
-        compiler_params=pltpu.CompilerParams(collective_id=collective_id, has_side_effects=True),
-        cost_estimate=pl.CostEstimate(flops=0, bytes_accessed=1_000_000, transcendentals=0),
-    )(own)
+        tokens,
+        small,
+        *weights,
+    )
 
 
 def total_kernel(parts, out, slots, send, recv):
@@ -580,51 +839,34 @@
             *v.shape[:-1], 8, -1
         )
 
-    def perm(v):
-        return v.reshape(-1, nf, nc, depth).transpose(0, 2, 1, 3).reshape(-1, width)
-
-    def unperm(v):
-        return v.reshape(-1, nc, nf, depth).transpose(0, 2, 1, 3).reshape(-1, width)
-
     def own_part(v):
         return lax.dynamic_slice_in_dim(v.reshape(block_rows, width), t * own_rows, own_rows, 0)
 
-    def spread(w):
-        return w.reshape(depth, nf, -1).transpose(1, 0, 2)
-
-    def head_columns(*ws):
-        mine = jnp.concatenate([spread(w) for w in ws], -1)
-        return lax.all_to_all(mine, "fsdp", 0, 0, tiled=True)
-
     def all_depths(mine):
         return lax.all_gather(mine, "ctx", axis=0, tiled=True).reshape(width, -1)
 
-    attn_w = all_depths(head_columns(query_weight, key_weight, value_weight, swish_weight))
-    rest = head_columns(out_weight.T, gelu_weight, up_weight, down_weight.T)
+    def padded(v):
+        return jnp.pad(v.astype(f32).reshape(-1), (0, 128 - v.size))
+
+    kinds = [pre_gain, pre_bias, mlp_gain, mlp_bias, group_gain, group_bias, lengths]
+    small = jnp.stack([padded(v) for v in kinds] + [jnp.zeros(128, f32)])
+    weights = [query_weight, key_weight, value_weight, swish_weight]
+    weights += [out_weight, gelu_weight, up_weight, down_weight]
+    attn_w, rest, normed, small = start(
+        tokens.reshape(block_rows, width), small, weights, 4, (4, 7), 0
+    )
+    small, tokens, cotangent = lax.optimization_barrier((small, tokens, cotangent))
+    normed = normed.reshape(rows, width)
     out_t = all_depths(rest[..., :value_size])
-
-    small = jnp.concatenate(
-        [
-            jnp.stack([pre_gain, pre_bias, mlp_gain, mlp_bias]).astype(f32).reshape(-1),
-            group_gain.astype(f32).reshape(-1),
-            group_bias.astype(f32).reshape(-1),
-            lengths.astype(f32),
-        ]
-    )
-    small_size = small.size
-    small = spread_small(pad_tile(small), 4).reshape(nf * nc, -1)[:, :small_size]
     pre_gain_full, pre_bias_full, mlp_gain_full, mlp_bias_full = (
-        small[:, i * depth : (i + 1) * depth].reshape(width) for i in range(4)
-    )
-    group = small[:, 4 * depth : 4 * depth + 2 * group_gain.size].reshape(
-        nf * nc, 2, heads_local, -1
-    )
+        small[:, i, :depth].reshape(width) for i in range(4)
+    )
+    group = small[:, 4:6, : group_gain.size].reshape(nf * nc, 2, heads_local, -1)
     group = lax.dynamic_index_in_dim(group, f, 2, False).transpose(1, 0, 2).reshape(2, value_size)
-    all_lengths = small.reshape(nf, nc, -1)[:, 0, -seq_count:].reshape(seqs)
+    all_lengths = small.reshape(nf, nc, 8, 128)[:, 0, 6, :seq_count].reshape(seqs)
 
     inputs = own_part(tokens).astype(f32)
-    normed_wide, norm_in_back = jax.vjp(layer_norm, inputs, pre_gain_full, pre_bias_full)
-    normed = gather_rows(perm(normed_wide.astype(bf16)), 0)
+    _, norm_in_back = jax.vjp(layer_norm, inputs, pre_gain_full, pre_bias_full)
     positions = c * span + lax.iota(jnp.int32, span)
     own_ids = t * own_rows + lax.iota(jnp.int32, own_rows)
     own_valid = (c * span + own_ids % span < lengths[own_ids // span]).astype(f32)[:, None]
@@ -653,7 +895,7 @@
     keys_faded = (keys.astype(f32) * key_fade).astype(bf16)
     queries_faded = (queries.astype(f32) * query_fade).astype(bf16)
     local_state = blocks("sjd,sje->sde", keys_faded, values)
-    error_low = perm(error.astype(bf16))
+    error_low = error.astype(bf16)
     entering, error_all = pass_and_gather(local_state, block_fade, error_low, 1, 2)
     rest, entering = lax.optimization_barrier((rest, entering))
     ff_w = all_depths(rest[..., value_size:])
@@ -665,15 +907,14 @@
         gate_mix, mixed.reshape(rows, value_size), swish_pre, group[0], group[1]
     )
     gated = gated_wide.astype(bf16)
-    branch = scatter_rows(product_right(gated, out_t).astype(bf16), 1)
-    hidden = inputs + unperm(branch)
+    branch = scatter_product(gated, out_t, 0, 1)
+    hidden = inputs + branch
 
     mlp_wide, norm_mid_back = jax.vjp(layer_norm, hidden, mlp_gain_full, mlp_bias_full)
-    mlp_in = gather_rows(perm(mlp_wide.astype(bf16)), 0)
+    mlp_in = gather_rows(mlp_wide.astype(bf16), 4)
     pre_ff = product(mlp_in, gelu_up)
     inner_wide, mix_back = jax.vjp(mlp_mix, pre_ff[:, :hidden_size], pre_ff[:, hidden_size:])
     inner = inner_wide.astype(bf16)
-    mlp_part = product_right(inner, down_t).astype(bf16)
 
     def sum_depths(grads):
         grads = with_layout_constraint(grads.astype(bf16), Layout((0, 1)))
@@ -689,18 +930,20 @@
     def across(grads):
         return grads.transpose(0, 2, 1).reshape(-1, depth)
 
-    grad_down_t = product_left(error_all, inner)
+    down_part = product_left(error_all, inner).astype(bf16)
+    down_part, down_t = lax.optimization_barrier((down_part, down_t))
+    down_sum = sum_depths(down_part)
     gelu_grad, up_grad = mix_back(product(error_all, down_t))
     ff_low = jnp.concatenate([gelu_grad.astype(bf16), up_grad.astype(bf16)], -1)
     grad_gelu_up = product_left(mlp_in, ff_low)
-    ff_parts = jnp.concatenate([grad_gelu_up, grad_down_t], -1).astype(bf16)
+    ff_parts = grad_gelu_up.astype(bf16)
     ff_parts, ff_low = lax.optimization_barrier((ff_parts, ff_low))
     ff_sum = sum_depths(ff_parts)
-    mlp_in_grad = unperm(scatter_rows(product_right(ff_low, gelu_up).astype(bf16), 1))
+    mlp_in_grad = scatter_product(ff_low, ff_w, 0, 6)
     hidden_norm_grad, grad_mlp_gain, grad_mlp_bias = norm_mid_back(mlp_in_grad)
     hidden_grad = error + hidden_norm_grad
 
-    hidden_low = gather_rows(perm(hidden_grad.astype(bf16)), 0)
+    hidden_low = gather_rows(hidden_grad.astype(bf16), 4)
     grad_out_t = product_left(hidden_low, gated)
     gated_grad = product(hidden_low, out_t)
     mixed_grad, swish_grad, grad_group_gain, grad_group_bias = gate_back(gated_grad)
@@ -708,12 +951,17 @@
     mixed_low = mixed_grad.astype(bf16).reshape(seqs, span, value_size)
     score_low = (blocks("sie,sje->sij", mixed_low, values) * within_fade).astype(bf16)
     pulled_state = blocks("sid,sie->sde", queries_faded, mixed_low)
-    early = jnp.concatenate([product_left(normed, swish_low), grad_out_t], -1).astype(bf16)
-    early, pulled_state, ff_sum = lax.optimization_barrier((early, pulled_state, ff_sum))
-    later, mlp_out = pass_and_scatter(pulled_state, block_fade, mlp_part, -1, 3)
-    early, later = lax.optimization_barrier((early, later))
-    early_sum = sum_depths(early)
-    block_own = (own_valid * (hidden + unperm(mlp_out))).astype(bf16)
+    out_sum = sum_depths(grad_out_t)
+    swish_part = product_left(normed, swish_low).astype(bf16)
+    swish_part, pulled_state, ff_sum, down_sum = lax.optimization_barrier(
+        (swish_part, pulled_state, ff_sum, down_sum)
+    )
+    later, mlp_out = pass_and_scatter(
+        pulled_state, block_fade, inner, ff_w, 2 * hidden_size, -1, 3
+    )
+    swish_part, later, out_sum = lax.optimization_barrier((swish_part, later, out_sum))
+    swish_sum = sum_depths(swish_part)
+    block_own = (own_valid * (hidden + mlp_out)).astype(bf16)
     block_out = both_halves(block_own, t).reshape(tokens.shape)
     query_grad = blocks("sij,sjd->sid", score_low, keys) + query_fade * blocks(
         "sie,sde->sid", mixed_low, entering
@@ -738,8 +986,8 @@
     attn_part, low = lax.optimization_barrier((attn_part, low))
     attn_sum = sum_depths(attn_part)
     low = jnp.concatenate([low, swish_low], -1)
-    normed_grad = unperm(scatter_rows(product_right(low, attn_w).astype(bf16), 1))
-    early_sum, normed_grad = lax.optimization_barrier((early_sum, normed_grad))
+    normed_grad = scatter_product(low, attn_w, 0, 7)
+    swish_sum, normed_grad = lax.optimization_barrier((swish_sum, normed_grad))
     input_norm_grad, grad_pre_gain, grad_pre_bias = norm_in_back(normed_grad)
     tokens_own = (hidden_grad + input_norm_grad).astype(bf16)
     grad_tokens = both_halves(tokens_own, t).reshape(tokens.shape)
@@ -755,28 +1003,30 @@
     parts = parts.reshape(nf * nc * nt, -1)
     sums = total_small(pad_tile(parts), 5).reshape(-1)[: parts.shape[1]]
     sums, attn_sum = lax.optimization_barrier((sums, attn_sum))
-    ff_grads, early_grads, attn_grads = (all_heads(v) for v in (ff_sum, early_sum, attn_sum))
+    ready_sums = jnp.concatenate([ff_sum, down_sum, out_sum], -1)
+    ff_grads = all_heads(ready_sums)
+    attn_grads = all_heads(jnp.concatenate([swish_sum, attn_sum], -1))
     norm_sums = sums[: 4 * depth].reshape(4, depth)
     group_sums = sums[4 * depth :].reshape(2, heads_local, -1)
 
-    at = [0, key_size, 2 * key_size]
+    at = [value_size, value_size + key_size, value_size + 2 * key_size]
     return (
         block_out,
         grad_tokens,
         norm_sums[0],
         norm_sums[1],
-        along(attn_grads[..., : at[1]]),
+        along(attn_grads[..., at[0] : at[1]]),
         along(attn_grads[..., at[1] : at[2]]),
         along(attn_grads[..., at[2] :]),
-        along(early_grads[..., :value_size]),
-        across(early_grads[..., value_size:]),
+        along(attn_grads[..., : at[0]]),
+        across(ff_grads[..., 3 * hidden_size :]),
         group_sums[0],
         group_sums[1],
         norm_sums[2],
         norm_sums[3],
         along(ff_grads[..., :hidden_size]),
         along(ff_grads[..., hidden_size : 2 * hidden_size]),
-        across(ff_grads[..., 2 * hidden_size :]),
+        across(ff_grads[..., 2 * hidden_size : 3 * hidden_size]),
     )
 
 

time: 861 us -> 806 us (0.936)
  Pallas kernels: 403 us -> 498 us
  local copies, waits for them, and re-layouts: 101 us -> 51.3 us
  waiting for transfers between devices: 85.3 us -> 41.8 us
  matrix products: 154 us -> 120 us
  blocking collectives: 24.7 us -> 0 us
  other arithmetic: 51.1 us -> 61.2 us
    pallas_call x9 -> x8, Pallas kernels: 389 us -> 486 us  [call(): pl.pallas_call(kernel, out_shape=shapes, in_specs=ins, out_specs=tuple((p...]
    dot_general x4 -> x0, matrix products: 51.3 us -> none  [product_right(): lax.dot_general(left, right, (((1,), (1,)), ((), ())), preferred_element_...]
    all_to_all x1 -> x0, blocking collectives: 24.7 us -> none  [head_columns(): return lax.all_to_all(mine, 'fsdp', 0, 0, tiled=True)]
    reshape x16 -> x1, local copies, waits for them, and re-layouts: 24.2 us -> 0.1 us  [shards(): group = small[:, 4:6, :group_gain.size].reshape(nf * nc, 2, heads_local, -1)]
    reduce_scatter x3 -> x5, waiting for transfers between devices: 31.9 us -> 8.14 us  [sum_depths(): mine = lax.psum_scatter(grads, 'ctx', scatter_dimension=0, tiled=True)]
    unnamed x189 -> x106, local copies, waits for them, and re-layouts: 41.1 us -> 18.3 us
    all_gather x3 -> x2, waiting for transfers between devices: 43.9 us -> 33.6 us  [all_depths(): return lax.all_gather(mine, 'ctx', axis=0, tiled=True).reshape(width, -1)]
    all_to_all x3 -> x2, waiting for transfers between devices: 9.36 us -> 0.01 us  [all_heads(): return lax.all_to_all(mine, 'fsdp', 0, 0, tiled=True).astype(f32)]
  transfers between devices with their start and end apart: 12 -> 11, of which waited for: 4 -> 2; matrix products, arithmetic and copies ran while one was open for 26% -> 23% of each run, Pallas kernels for 40% -> 48%
where the time goes in v4:
time: 806 us; the launch traced here: 798 us
  Pallas kernels  498 us (62%)
  matrix products  120 us (15%)
  other arithmetic  61.2 us (8%)
  local copies, waits for them, and re-layouts  51.3 us (6%)
  waiting for transfers between devices  41.8 us (5%)
  between operations  15.4 us (2%)
  starting transfers between devices  9.86 us (1%)
    pallas_call x8, Pallas kernels, call(): pl.pallas_call(kernel, out_shape=shapes, in_specs=ins, out_specs=tuple((p...  486 us
    dot_general x4, matrix products, product(): return jnp.dot(left, right, preferred_element_type=f32)  56.6 us
    dot_general x5, matrix products, product_left(): lax.dot_general(left, right, (((0,), (0,)), ((), ())), preferred_element_...  40.8 us
    all_gather x2, waiting for transfers between devices, all_depths(): return lax.all_gather(mine, 'ctx', axis=0, tiled=True).reshape(width, -1)  33.6 us
    dot_general x12, matrix products, blocks(): return jnp.einsum(spec, left, right, preferred_element_type=f32)  22.5 us
    unnamed x106, local copies, waits for them, and re-layouts  18.3 us
  transfers between devices with their start and end apart: 11, of which 2 were waited for; matrix products, arithmetic and copies ran while one was open for 23% of the time, Pallas kernels for 48%

profile of v4, /device:TPU:0, one launch (start us, length us, event | category | flops | bytes accessed | tf_op | source)
XLA Modules:
  0.0 797.9 jit_solution(14842540253249867393)
XLA Ops:
  14.8 114.8 %shard_map.288 = (bf16[2048,1536]{1,0:T(8,128)(2,1)}, bf16[4,128,2048]{2,1,0:T(8,128)(2,1)}, bf16[8,256,2048]{2,1,0:T(8,128)(2,1)}, f32[16,8,128]{2,1,0:T(8,128)S(1)}) custom-call(bf16[512,2048]{1,0:T(8,128)(2,1)} %bitcast.173, f32[8,128]{1,0:T(8,128)S(1)} %stack.79.small, bf16[128,1024]{1,0:T(8,128)(2,1)S(1)} %copy-done.2, bf16[128,1024]{1,0:T(8,128)(2,1)S(1)} %copy-done.3, ...), custom_call_target="tpu_custom_call" | custom-call | bytes 2000000 | tf_op jit(solution)/shard_map/pallas_call | solution.py:388
  131.6 19.2 %fusion.45 = f32[2048,1536]{1,0:T(8,128)} fusion(bf16[2048,2048]{1,0:T(8,128)(2,1)} %bitcast.234, bf16[2048,1536]{1,0:T(8,128)(2,1)} %get-tuple-element.49.refs_1_), kind=kOutput, calls=%fused_computation.162 | convolution fusion | flops 12884901888 | bytes 27262976 | tf_op jit(solution)/shard_map/dot_general | solution.py:53
  151.0 2.5 slice.284
  156.9 2.6 fusion.40
  161.4 2.8 fusion.26.local
  164.5 55.1 %shard_map.289 = (bf16[8,256,512]{2,1,0:T(8,128)(2,1)}, bf16[8,256,2048]{2,1,0:T(8,128)(2,1)}) custom-call(f32[8,256,512]{2,1,0:T(8,128)} %fusion.26.local, f32[1,512]{1,0:T(1,128)S(1)} %broadcast_in_dim.37.fade, bf16[256,2048]{1,0:T(8,128)(2,1)S(1)} %fusion.22.own), custom_call_target="tpu_custom_call" | custom-call | bytes 2000000 | tf_op jit(solution)/shard_map/pallas_call | solution.py:388
  222.2 2.7 fusion.46
  227.8 4.2 multiply_convert_fusion.2
  232.1 46.2 %shard_map.290 = f32[256,2048]{1,0:T(8,128)} custom-call(bf16[8,256,512]{2,1,0:T(8,128)(2,1)} %bitcast.179, bf16[2048,512]{1,0:T(8,128)(2,1)} %bitcast.191), custom_call_target="tpu_custom_call" | custom-call | bytes 2000000 | tf_op jit(solution)/shard_map/pallas_call | solution.py:388
  278.3 2.7 fusion.39
  281.8 39.1 %shard_map.291 = bf16[8,256,2048]{2,1,0:T(8,128)(2,1)} custom-call(bf16[256,2048]{1,0:T(8,128)(2,1)S(1)} %add_convert_fusion.3.refs_0_), custom_call_target="tpu_custom_call" | custom-call | bytes 2000000 | tf_op jit(solution)/shard_map/pallas_call | solution.py:388
  320.9 33.6 %all-gather.5.cloned.1.call-done = bf16[16,128,1536]{2,1,0:T(8,128)(2,1)} async-done(((bf16[4,128,1536]{2,1,0:T(8,128)(2,1)}), bf16[16,128,1536]{2,1,0:T(8,128)(2,1)}) %all-gather.5.cloned.1.call-update) | async-done | bytes 6291472 | tf_op jit(solution)/shard_map/all_gather | solution.py:846
  354.4 3.2 slice.222
  357.7 12.6 %fusion.10 = f32[2048,1024]{1,0:T(8,128)S(1)} fusion(bf16[2048,2048]{1,0:T(8,128)(2,1)} %bitcast.181, bf16[2048,1536]{1,0:T(8,128)(2,1)} %bitcast.161), kind=kOutput, calls=%fused_computation.15 | convolution fusion | flops 8589934592 | bytes 20971520 | tf_op jit(solution)/shard_map/dot_general | solution.py:53
  374.8 5.7 convolution_convert_fusion.4
  380.6 12.8 %fusion.6 = (bf16[2048,512]{1,0:T(8,128)(2,1)S(1)}, bf16[2048,512]{1,0:T(8,128)(2,1)S(1)}) fusion(f32[2048,1024]{1,0:T(8,128)} %copy-done.18, bf16[2048,2048]{1,0:T(8,128)(2,1)} %bitcast.241, bf16[2048,512]{1,0:T(8,128)(2,1)} %slice.222), kind=kOutput, calls=%fused_computation.11 | convolution fusion | flops 4320133120 | bytes 23068672 | tf_op jit(solution)/shard_map/dot_general | solution.py:53
  393.4 2.6 pad_maximum_fusion.1
  396.0 12.8 %convolution_convert_fusion.1 = bf16[2048,1024]{1,0:T(8,128)(2,1)} fusion(bf16[2048,2048]{1,0:T(8,128)(2,1)} %bitcast.182, bf16[2048,512]{1,0:T(8,128)(2,1)S(1)} %get-tuple-element.98, bf16[2048,512]{1,0:T(8,128)(2,1)S(1)} %get-tuple-element.97), kind=kOutput, calls=%fused_computation.33 | convolution fusion | flops 8600420352 | bytes 16777216 | tf_op jit(solution)/shard_map/dot_general | solution.py:57
  408.9 49.4 %shard_map.292 = f32[256,2048]{1,0:T(8,128)} custom-call(bf16[8,256,1024]{2,1,0:T(8,128)(2,1)} %bitcast.178, bf16[2048,1536]{1,0:T(8,128)(2,1)} %bitcast.162), custom_call_target="tpu_custom_call" | custom-call | bytes 2000000 | tf_op jit(solution)/shard_map/pallas_call | solution.py:388
  458.3 2.5 multiply_reduce_fusion.3
  462.9 39.1 %shard_map.293 = bf16[8,256,2048]{2,1,0:T(8,128)(2,1)} custom-call(bf16[256,2048]{1,0:T(8,128)(2,1)S(1)} %fusion.23.refs_0_), custom_call_target="tpu_custom_call" | custom-call | bytes 2000000 | tf_op jit(solution)/shard_map/pallas_call | solution.py:388
  502.0 11.9 %multiply_reduce_fusion = (f32[512]{0:T(512)S(1)}, f32[2048]{0:T(1024)S(1)}, f32[512]{0:T(512)S(1)}, f32[2048,512]{1,0:T(8,128)S(1)}, bf16[2048,512]{1,0:T(8,128)(2,1)}) fusion(f32[8,256,512]{2,1,0:T(8,128)S(1)} %copy-done.5, f32[2048]{0:T(1024)S(1)} %rsqrt.30, f32[2048]{0:T(1024)S(1)} %bitcast.224, f32[512]{0:T(512)S(1)} %mul.523, ...), kind=kOutput, calls=%fused_computation.20 | convolution fusion | flops 4319081472 | bytes 25198592 | tf_op jit(solution)/shard_map/dot_general | solution.py:53
  513.9 3.2 fusion.36
  517.2 2.3 copy-done.19
  519.5 6.0 convolution_convert_fusion.2
  525.5 2.7 add_convert_fusion.1
  532.0 3.0 fusion.25.local
  535.0 2.9 fusion.48
  541.0 5.7 convolution_convert_fusion.3
  546.7 88.1 %shard_map.294 = (bf16[8,256,512]{2,1,0:T(8,128)(2,1)}, f32[256,2048]{1,0:T(8,128)}) custom-call(f32[8,256,512]{2,1,0:T(8,128)} %fusion.25.local, f32[1,512]{1,0:T(1,128)S(1)} %broadcast_in_dim.37.fade, bf16[8,256,512]{2,1,0:T(8,128)(2,1)} %bitcast.185, bf16[2048,1536]{1,0:T(8,128)(2,1)} %bitcast.163), custom_call_target="tpu_custom_call" | custom-call | bytes 2000000 | tf_op jit(solution)/shard_map/pallas_call | solution.py:388
  635.3 3.9 add_multiply_fusion
  645.5 10.6 %convolution_convert_fusion = bf16[2048,1024]{1,0:T(8,128)(2,1)} fusion(bf16[2048,2048]{1,0:T(8,128)(2,1)S(1)} %bitcast.240, bf16[2048,1024]{1,0:T(8,128)(2,1)S(1)} %constant_dynamic-update-slice_fusion), kind=kOutput, calls=%fused_computation.32 | convolution fusion | flops 8592031744 | bytes 16777216 | tf_op jit(solution)/shard_map/dot_general | solution.py:57
  657.3 2.8 pad_maximum_fusion.2
  660.0 4.6 all-to-all-start.1
  664.7 6.0 pad_maximum_fusion
  670.7 54.4 %shard_map.295 = f32[256,2048]{1,0:T(8,128)} custom-call(bf16[8,256,1536]{2,1,0:T(8,128)(2,1)} %bitcast.172, bf16[2048,1536]{1,0:T(8,128)(2,1)} %get-tuple-element.49.refs_1_), custom_call_target="tpu_custom_call" | custom-call | bytes 2000000 | tf_op jit(solution)/shard_map/pallas_call | solution.py:388
  725.2 2.8 fusion.17
  728.0 2.4 fusion.20
  730.4 4.0 add_convert_fusion.2
  735.2 12.2 %shard_map.296 = f32[8,128]{1,0:T(8,128)} custom-call(f32[32,8,128]{2,1,0:T(8,128)} %bitcast.209), custom_call_target="tpu_custom_call" | custom-call | bytes 1000000 | tf_op jit(solution)/shard_map/pallas_call | solution.py:783
  748.5 8.1 %reduce-scatter.14.cloned.1.call-done = bf16[512,1024]{1,0:T(8,128)(2,1)} async-done(((bf16[2048,1024]{1,0:T(8,128)(2,1)}), bf16[512,1024]{1,0:T(8,128)(2,1)}) %reduce-scatter.14.cloned.1.call-update) | async-done | bytes 1048592 | tf_op jit(solution)/shard_map/reduce_scatter | solution.py:921
  756.6 2.6 pad_maximum_fusion.3
  759.3 3.9 all-to-all-start
  767.5 2.5 copy.77
  770.0 2.4 copy.89
  773.4 2.5 copy.74
  776.0 4.7 maximum_select_fusion.1
  780.7 3.8 maximum_select_fusion
  (214 shorter events, 56.2 us)
Async XLA Ops:
  7.2 224.9 %all-gather.3.cloned.1.call-start = ((), (), s32[]{:S(2)}) async-start(), calls=%async_computation.7 | async-start | bytes 2621440 | tf_op jit(solution)/shard_map/all_gather | solution.py:846
  131.5 223.0 %all-gather.5.cloned.1.call-start = ((), (), s32[]{:S(2)}) async-start(), calls=%async_computation.8 | async-start | bytes 7864320 | tf_op jit(solution)/shard_map/all_gather | solution.py:846
  151.0 2.6 copy-start.41
  153.6 7.8 copy-start.6
  156.9 2.6 copy-start.35
  161.4 2.8 copy-start.28
  164.5 55.2 %copy-start.33 = (bf16[4,128,2048]{2,1,0:T(8,128)(2,1)S(1)}, bf16[4,128,2048]{2,1,0:T(8,128)(2,1)}, u32[]{:S(2)}) copy-start(bf16[4,128,2048]{2,1,0:T(8,128)(2,1)} %get-tuple-element.56) | copy-start | bytes 6291460
  219.6 2.0 copy-start.23
  219.7 2.0 copy-start.25
  221.0 325.7 %reduce-scatter.8.cloned.1.call-start = ((), (), s32[]{:S(2)}) async-start(), calls=%async_computation.10 | async-start | bytes 2621440 | tf_op jit(solution)/shard_map/reduce_scatter | solution.py:921
  222.2 2.7 copy-start.30
  222.2 2.7 copy-start.20
  225.8 2.0 copy-start.4
  232.1 46.2 %copy-start.9 = (bf16[2,256,2048]{2,1,0:T(8,128)(2,1)S(1)}, bf16[2,256,2048]{2,1,0:T(8,128)(2,1)}, u32[]{:S(2)}) copy-start(bf16[2,256,2048]{2,1,0:T(8,128)(2,1)} %param.17) | copy-start | bytes 6291460
  354.4 20.4 %slice-start.4 = ((s8[8388608]{0:T(1024)(128)(4,1)}), s8[4194304]{0:T(1024)(128)(4,1)S(1)}, s32[]{:S(2)}) async-start(s8[8388608]{0:T(1024)(128)(4,1)} %bitcast.242), calls=%async_computation.18 | async-start | bytes 8388608
  357.7 17.1 %slice-start.5 = ((s8[8388608]{0:T(1024)(128)(4,1)}), s8[4194304]{0:T(1024)(128)(4,1)S(1)}, s32[]{:S(2)}) async-start(s8[8388608]{0:T(1024)(128)(4,1)} %bitcast.242), calls=%async_computation.19 | async-start | bytes 8388608
  370.3 3.2 copy-start.18
  380.6 166.1 %reduce-scatter.6.cloned.1.call-start = ((), (), s32[]{:S(2)}) async-start(), calls=%async_computation.9 | async-start | bytes 5242880 | tf_op jit(solution)/shard_map/reduce_scatter | solution.py:921
  408.8 226.0 %reduce-scatter.10.cloned.1.call-start = ((), (), s32[]{:S(2)}) async-start(), calls=%async_computation.11 | async-start | bytes 2621440 | tf_op jit(solution)/shard_map/reduce_scatter | solution.py:921
  458.3 2.5 copy-start.13
  462.9 39.1 %copy-start.5 = (f32[8,256,512]{2,1,0:T(8,128)S(1)}, f32[8,256,512]{2,1,0:T(8,128)}, u32[]{:S(2)}) copy-start(f32[8,256,512]{2,1,0:T(8,128)} %copy-done.4) | copy-start | bytes 12582916
  513.9 3.2 copy-start.15
  513.9 5.5 copy-start.19
  525.5 199.7 %reduce-scatter.12.cloned.1.call-start = ((), (), s32[]{:S(2)}) async-start(), calls=%async_computation.12 | async-start | bytes 2621440 | tf_op jit(solution)/shard_map/reduce_scatter | solution.py:921
  525.5 2.9 copy-start.7
  532.0 3.0 copy-start.31
  532.0 8.1 %slice-start = ((s8[8388608]{0:T(1024)(128)(4,1)}), s8[4194304]{0:T(1024)(128)(4,1)S(1)}, s32[]{:S(2)}) async-start(s8[8388608]{0:T(1024)(128)(4,1)} %bitcast.235), calls=%async_computation.14 | async-start | bytes 8388608
  535.0 2.9 copy-start.21
  535.0 5.1 slice-start.1
  537.9 3.0 copy-start.34
  634.8 4.4 copy-start.36
  634.8 4.4 copy-start.38
  634.9 121.8 %reduce-scatter.14.cloned.1.call-start = ((), (), s32[]{:S(2)}) async-start(), calls=%async_computation.13 | async-start | bytes 5242880 | tf_op jit(solution)/shard_map/reduce_scatter | solution.py:921
  635.3 3.9 copy-start.17
  635.3 10.1 %slice-start.2 = ((s8[8388608]{0:T(1024)(128)(4,1)}), s8[4194304]{0:T(1024)(128)(4,1)S(1)}, s32[]{:S(2)}) async-start(s8[8388608]{0:T(1024)(128)(4,1)} %bitcast.238), calls=%async_computation.16 | async-start | bytes 8388608
  639.2 1.8 copy-start.16
  639.8 2.5 copy-start.14
  640.0 5.5 slice-start.3
  643.4 2.0 copy-start.27
  660.0 99.2 %all-to-all-start.1 = ((bf16[4,128,2048]{2,1,0:T(8,128)(2,1)}), bf16[4,128,2048]{2,1,0:T(8,128)(2,1)}, u32[]{:S(2)}, u32[]{:S(2)}) async-start(bf16[4,128,2048]{2,1,0:T(8,128)(2,1)} %pad_maximum_fusion.2), calls=%async_computation.6 | async-start | bytes 4194304 | tf_op jit(solution)/shard_map/all_to_all | solution.py:925
  670.7 54.5 %copy-start.39 = (f32[16,1,128]{2,1,0:T(1,128)S(1)}, f32[16,1,128]{2,1,0:T(1,128)}, u32[]{:S(2)}) copy-start(f32[16,1,128]{2,1,0:T(1,128)} %get-tuple-element.122) | copy-start | bytes 24580
  725.2 2.9 copy-start.8
  725.2 5.2 copy-start.12
  728.0 2.4 copy-start.10
  734.4 41.6 %collective-permute-start.1 = (bf16[256,2048]{1,0:T(8,128)(2,1)}, bf16[256,2048]{1,0:T(8,128)(2,1)}, u32[]{:S(2)}, u32[]{:S(2)}) collective-permute-start(bf16[256,2048]{1,0:T(8,128)(2,1)} %get-tuple-element.136), channel_id=1, source_target_pairs={{0,1},{1,0},{2,3},{3,2},{4,5},{5,4},{6,7},{7,6},{8,9},{9,8},{10,11... | collective-permute-start | bytes 3145736 | tf_op jit(solution)/shard_map/ppermute | solution.py:799
  747.4 33.3 %collective-permute-start = (bf16[256,2048]{1,0:T(8,128)(2,1)S(1)}, bf16[256,2048]{1,0:T(8,128)(2,1)}, u32[]{:S(2)}, u32[]{:S(2)}) collective-permute-start(bf16[256,2048]{1,0:T(8,128)(2,1)S(1)} %get-tuple-element.137), channel_id=1, source_target_pairs={{0,1},{1,0},{2,3},{3,2},{4,5},{5,4},{6,7},{7,6},{8,9},{9,8},{10,11... | collective-permute-start | bytes 3145736 | tf_op jit(solution)/shard_map/ppermute | solution.py:799
  759.3 27.1 %all-to-all-start = ((bf16[4,128,1536]{2,1,0:T(8,128)(2,1)}), bf16[4,128,1536]{2,1,0:T(8,128)(2,1)S(1)}, u32[]{:S(2)}, u32[]{:S(2)}) async-start(bf16[4,128,1536]{2,1,0:T(8,128)(2,1)} %pad_maximum_fusion.3), calls=%async_computation.5 | async-start | bytes 3145728 | tf_op jit(solution)/shard_map/all_to_all | solution.py:925
  770.0 2.4 copy-start.32
  (11 other events, 12.7 us)
Sparse Core Ops, SparseCore 0:
  131.6 45.8 all-gather.2
  221.1 133.3 all-gather.4
  380.7 42.0 reduce-scatter.7
  425.0 76.1 reduce-scatter.5
  525.6 52.0 reduce-scatter.9
  635.0 41.0 reduce-scatter.11
  678.4 78.1 reduce-scatter.13

commit v5 on v4

--- a/solution.py
+++ b/solution.py
@@ -145,12 +145,13 @@
         remote(slot(fd, 1), slot(fd, 1), send.at[13], recv.at[5], x).wait_recv()
         pass_on(fd, 1, 13, 13, core)
 
-    def end():
-        for r in range(6, 14):
-            remote(slot(f, 0), slot(f, 0), send.at[0], recv.at[r], core).wait_recv()
+    def end(crossed=False):
+        if not crossed:
+            for r in range(6, 14):
+                remote(slot(f, 0), slot(f, 0), send.at[0], recv.at[r], core).wait_recv()
+            local.wait()
         for copy in sent:
             copy.wait_send()
-        local.wait()
 
     return begin, relay, rest, diagonal, end
 
@@ -168,13 +169,13 @@
     ]
 
 
-def scatter_steps(start, left, right, out, mine, sent, theirs, total, diag, last, send, recv):
+def scatter_steps(start, lefts, right, out, mine, sent, theirs, total, diag, last, send, recv):
     f, t = lax.axis_index("fsdp"), lax.axis_index("tp")
     fx, fy, fd = beside(f)
     x, y, core = {"fsdp": fx}, {"fsdp": fy}, {"tp": 1 - t}
     half = out.shape[0] // 2
     order = [fd, fy, fx, f]
-    tile, size = 512, left.shape[2]
+    tile = 512
 
     def part(ref, h):
         return ref.at[pl.ds(h * half, half)]
@@ -192,7 +193,12 @@
     def make(block, put):
         def piece(j, carry):
             columns = pl.ds(pl.multiple_of(j * tile, tile), tile)
-            put(columns, product_right(left[block], right[columns, start : start + size]))
+            at, value = start, 0.0
+            for left in lefts:
+                size = left.shape[2]
+                value += product_right(left[block], right[columns, at : at + size])
+                at += size
+            put(columns, value)
             return carry
 
         lax.fori_loop(0, out.shape[1] // tile, piece, 0)
@@ -294,6 +300,11 @@
 
         return carry
 
+    def run(quarter):
+        count = local.shape[0]
+        low = 0 if quarter == 0 else jnp.where(first, count, quarter * count // 4)
+        lax.fori_loop(low, jnp.where(first, count, (quarter + 1) * count // 4), step, 0)
+
     def end():
         @pl.when(jnp.logical_not(last))
         def _():
@@ -303,15 +314,16 @@
 
             lax.fori_loop(0, local.shape[0], done, 0)
 
-    return step, end
-
-
-def greet_plane(by=0):
+    return run, end
+
+
+def greet_plane(by=0, diagonal=False):
     f, c, t = lax.axis_index("fsdp"), lax.axis_index("ctx"), lax.axis_index("tp")
     length = lax.axis_size("ctx")
-    fx, fy, _ = beside(f)
+    fx, fy, fd = beside(f)
     barrier = pltpu.get_barrier_semaphore()
-    for device in ({"fsdp": fx}, {"fsdp": fy}, {"tp": 1 - t}):
+    peers = [{"fsdp": fx}, {"fsdp": fy}, {"tp": 1 - t}] + [{"fsdp": fd}] * diagonal
+    for device in peers:
         pl.semaphore_signal(barrier, inc=1, device_id=device, device_id_type=MESH)
     if by != 0:
         first = c == (0 if by > 0 else length - 1)
@@ -324,13 +336,13 @@
 
         @pl.when(jnp.logical_not(last))
         def _():
-            pl.semaphore_wait(barrier, 4)
+            pl.semaphore_wait(barrier, len(peers) + 1)
 
         @pl.when(last)
         def _():
-            pl.semaphore_wait(barrier, 3)
+            pl.semaphore_wait(barrier, len(peers))
     else:
-        pl.semaphore_wait(barrier, 3)
+        pl.semaphore_wait(barrier, len(peers))
 
 
 def gather_with(own, full, mixed, *scratch):
@@ -344,42 +356,118 @@
         step()
 
 
-def scatter_kernel(start, *refs):
-    steps = scatter_steps(start, *refs)
+def scatter_kernel(count, start, *refs):
+    steps = scatter_steps(start, refs[:count], *refs[count:])
     greet_plane()
     for step in steps:
         step()
 
 
+def gather_products_kernel(own, left, right, grad, back, full, total, mixed, *scratch):
+    f, t = lax.axis_index("fsdp"), lax.axis_index("tp")
+    fx, fy, fd = beside(f)
+    recv = scratch[2]
+    begin, relay, rest, diagonal, end = gather_with(own, full, mixed, *scratch)
+    tile = 512
+
+    def use(block, fresh=False):
+        back[block] = product(full[block], right[...])
+
+        def piece(j, carry):
+            columns = pl.ds(pl.multiple_of(j * tile, tile), tile)
+            value = product_left(full[block, :, columns], left[block])
+            total[columns, :] = value if fresh else total[columns, :] + value
+            return carry
+
+        lax.fori_loop(0, total.shape[0] // tile, piece, 0)
+
+    def crossed(who, r):
+        block = full.at[2 * who + 1 - t]
+        half = block.shape[0] // 2
+        for h in range(2):
+            where = block.at[pl.ds(h * half, half)]
+            remote(where, where, scratch[1].at[0], recv.at[r + h], {"tp": 1 - t}).wait_recv()
+
+    greet_plane()
+    begin()
+    pltpu.make_async_copy(full.at[2 * f + t], full.at[2 * f + t], scratch[0]).wait()
+    use(2 * f + t, True)
+    relay()
+    crossed(f, 6)
+    use(2 * f + 1 - t)
+    rest()
+    use(2 * fx + t)
+    use(2 * fy + t)
+    crossed(fx, 8)
+    use(2 * fx + 1 - t)
+    crossed(fy, 10)
+    use(2 * fy + 1 - t)
+    diagonal()
+    use(2 * fd + t)
+    crossed(fd, 12)
+    use(2 * fd + 1 - t)
+    end(True)
+    grad[...] = total[...].astype(grad.dtype)
+
+
+def gather_products(own, left, right, collective_id):
+    own = ready(own)
+    rows, width = own.shape
+    size = left.shape[1]
+    grad, back = call(
+        gather_products_kernel,
+        collective_id,
+        [
+            (jax.ShapeDtypeStruct((width, size), bf16), pltpu.VMEM),
+            (jax.ShapeDtypeStruct((8, rows, size), f32), pltpu.VMEM),
+        ],
+        [vmem()] * 3,
+        [
+            pltpu.VMEM((8, rows, width), bf16),
+            pltpu.VMEM((width, size), f32),
+            *gather_scratch(own),
+        ],
+        own,
+        in_eights(left),
+        right,
+    )
+    return grad, back.reshape(8 * rows, size)
+
+
 def pass_gather_kernel(by, local, fade, own, out, full, held, send, recv, *scratch):
     begin, relay, rest, diagonal, end = gather_with(own, full, *scratch)
-    step, done = pass_steps(by, local, fade, out, held, send, recv)
-    pieces = local.shape[0]
+    run, done = pass_steps(by, local, fade, out, held, send, recv)
     greet_plane(by)
     begin()
-    lax.fori_loop(0, pieces // 4, step, 0)
+    run(0)
     relay()
-    lax.fori_loop(pieces // 4, pieces // 2, step, 0)
+    run(1)
     rest()
-    lax.fori_loop(pieces // 2, pieces, step, 0)
+    run(2)
+    run(3)
     diagonal()
     end()
     done()
 
 
-def pass_scatter_kernel(by, start, local, fade, left, right, out, own, held, send, recv, *scratch):
-    diagonal, straight, relay, end = scatter_steps(start, left, right, own, *scratch)
-    step, done = pass_steps(by, local, fade, out, held, send, recv)
-    pieces = local.shape[0]
-    greet_plane(by)
-    lax.fori_loop(0, pieces // 4, step, 0)
+def pass_scatter_kernel(by, start, local, fade, left, right, ff, down, out, own, *refs):
+    gelu_grad, up_grad, down_grad, held, send, recv = refs[:6]
+    scratch, hand = refs[6:-3], refs[-3:]
+    targets = [[(gelu_grad, False), (up_grad, False)], [(down_grad, True)]]
+    hand_over, take = hand_steps([ff, down], targets, *hand)
+    diagonal, straight, relay, end = scatter_steps(start, [left], right, own, *scratch)
+    run, done = pass_steps(by, local, fade, out, held, send, recv)
+    greet_plane(by, True)
+    run(0)
     diagonal()
-    lax.fori_loop(pieces // 4, pieces // 2, step, 0)
+    run(1)
     straight()
-    lax.fori_loop(pieces // 2, 3 * pieces // 4, step, 0)
+    run(2)
     relay()
-    lax.fori_loop(3 * pieces // 4, pieces, step, 0)
+    hand_over()
+    run(3)
     end()
+    take()
     done()
 
 
@@ -452,20 +540,23 @@
     return out.reshape(-1, own.shape[1])
 
 
-def scatter_product(left, right, start, collective_id):
+def scatter_product(lefts, right, start, collective_id):
+    rows, width = lefts[0].shape[0] // 8, right.shape[0]
     (out,) = call(
-        functools.partial(scatter_kernel, start),
+        functools.partial(scatter_kernel, len(lefts), start),
         collective_id,
-        [scattered(left, right)],
-        [vmem(), vmem()],
-        scatter_scratch(left.shape[0] // 8, right.shape[0]),
-        in_eights(left),
+        [(jax.ShapeDtypeStruct((rows, width), f32), pltpu.VMEM)],
+        [vmem()] * (len(lefts) + 1),
+        scatter_scratch(rows, width),
+        *(in_eights(left) for left in lefts),
         right,
     )
     return plain(out)
 
 
 def pass_and_gather(local, fade, own, by, collective_id):
+    shape = local.shape
+    local = local.reshape(2 * shape[0], -1, shape[2])
     own = ready(own)
     out, full = call(
         functools.partial(pass_gather_kernel, by),
@@ -477,22 +568,33 @@
         jnp.full((1, local.shape[2]), fade, f32),
         own,
     )
-    return out, full.reshape(-1, own.shape[1])
-
-
-def pass_and_scatter(local, fade, left, right, start, by, collective_id):
-    out, own = call(
+    return out.reshape(shape), full.reshape(-1, own.shape[1])
+
+
+def pass_and_scatter(local, fade, left, right, start, ff, down, by, collective_id):
+    shape = local.shape
+    local = local.reshape(2 * shape[0], -1, shape[2])
+    out, own, *grads = call(
         functools.partial(pass_scatter_kernel, by, start),
         collective_id,
-        [passed(local), scattered(left, right)],
-        [vmem(), vmem(), vmem(), vmem()],
-        pass_scratch(local) + scatter_scratch(left.shape[0] // 8, right.shape[0]),
+        [
+            passed(local),
+            scattered(left, right),
+            *handed(ff, [down.shape[2]] * 2),
+            *handed(down, [down.shape[2]], True),
+        ],
+        [vmem()] * 6,
+        pass_scratch(local)
+        + scatter_scratch(left.shape[0] // 8, right.shape[0])
+        + hand_scratch([ff, down]),
         local,
         jnp.full((1, local.shape[2]), fade, f32),
         in_eights(left),
         right,
-    )
-    return out, plain(own)
+        ff,
+        down,
+    )
+    return out.reshape(shape), plain(own), *(grad.astype(f32) for grad in grads)
 
 
 def peer_of(place, nc, nt):
@@ -745,6 +847,124 @@
     )
 
 
+def hand_steps(parts, outs, slots, send, recv):
+    f = lax.axis_index("fsdp")
+    near = beside(f)
+    starts = [sum(part.shape[2] for part in parts[:i]) for i in range(len(parts))]
+
+    def copies(n):
+        return [
+            remote(
+                part.at[near[n]],
+                slots.at[n, :, pl.ds(at, part.shape[2])],
+                send.at[len(parts) * n + i],
+                recv.at[len(parts) * n + i],
+                {"fsdp": near[n]},
+            )
+            for i, (part, at) in enumerate(zip(parts, starts))
+        ]
+
+    def begin():
+        for n in range(3):
+            for copy in copies(n):
+                copy.start()
+
+    def put(who, blocks):
+        for block, targets in zip(blocks, outs):
+            at = 0
+            for out, turned in targets:
+                size = out.shape[0 if turned else 1] // lax.axis_size("fsdp")
+                where = pl.ds(pl.multiple_of(who * size, size), size)
+                if turned:
+                    out[where, :] = block[:, at : at + size].T
+                else:
+                    out[:, where] = block[:, at : at + size]
+                at += size
+
+    def end():
+        put(f, [part[f] for part in parts])
+        for n in range(3):
+            for copy in copies(n):
+                copy.wait()
+            put(
+                near[n],
+                [slots[n, :, at : at + part.shape[2]] for part, at in zip(parts, starts)],
+            )
+
+    return begin, end
+
+
+def hand_scratch(parts):
+    size = sum(part.shape[2] for part in parts)
+    return [
+        pltpu.VMEM((3, parts[0].shape[1], size), bf16),
+        pltpu.SemaphoreType.DMA((3 * len(parts),)),
+        pltpu.SemaphoreType.DMA((3 * len(parts),)),
+    ]
+
+
+def handed(part, sizes, turned=False):
+    nf, depth = part.shape[:2]
+    shapes = [(nf * n, depth) if turned else (depth, nf * n) for n in sizes]
+    return [(jax.ShapeDtypeStruct(shape, bf16), pltpu.VMEM) for shape in shapes]
+
+
+def finish_kernel(turned, counts, *refs):
+    parts, outs, scratch = refs[: len(turned)], list(refs[len(turned) : -3]), refs[-3:]
+    targets = [[(outs.pop(0), turn) for _ in range(n)] for turn, n in zip(turned, counts)]
+    begin, end = hand_steps(parts, targets, *scratch)
+    greet_fsdp()
+    begin()
+    end()
+
+
+def greet_fsdp():
+    near = beside(lax.axis_index("fsdp"))
+    barrier = pltpu.get_barrier_semaphore()
+    for who in near:
+        pl.semaphore_signal(barrier, inc=1, device_id={"fsdp": who}, device_id_type=MESH)
+    pl.semaphore_wait(barrier, 3)
+
+
+def finish(parts, sizes, turned, collective_id):
+    outs = [one for n in zip(parts, sizes, turned) for one in handed(*n)]
+    outs = call(
+        functools.partial(finish_kernel, turned, [len(size) for size in sizes]),
+        collective_id,
+        outs,
+        [vmem()] * len(parts),
+        hand_scratch(parts),
+        *parts,
+    )
+    return [out.astype(f32) for out in outs]
+
+
+def halves_kernel(own, out, keep, send, recv):
+    t = lax.axis_index("tp")
+    core = {"tp": 1 - t}
+    barrier = pltpu.get_barrier_semaphore()
+    pl.semaphore_signal(barrier, inc=1, device_id=core, device_id_type=MESH)
+    pl.semaphore_wait(barrier, 1)
+    copy = remote(own, out.at[t], send, recv, core)
+    copy.start()
+    local = pltpu.make_async_copy(own, out.at[t], keep)
+    local.start()
+    local.wait()
+    copy.wait()
+
+
+def both_halves(own, collective_id):
+    (out,) = call(
+        halves_kernel,
+        collective_id,
+        [(jax.ShapeDtypeStruct((2, *own.shape), own.dtype), pl.ANY)],
+        [pl.BlockSpec(memory_space=pl.ANY)],
+        [pltpu.SemaphoreType.DMA] * 3,
+        own,
+    )
+    return out
+
+
 def total_kernel(parts, out, slots, send, recv):
     nc, nt = lax.axis_size("ctx"), lax.axis_size("tp")
     count = parts.shape[0]
@@ -793,11 +1013,6 @@
         compiler_params=pltpu.CompilerParams(collective_id=collective_id, has_side_effects=True),
         cost_estimate=pl.CostEstimate(flops=0, bytes_accessed=1_000_000, transcendentals=0),
     )(parts)
-
-
-def both_halves(own, t):
-    other = lax.ppermute(own, "tp", [(0, 1), (1, 0)])
-    return jnp.where(t == 0, jnp.concatenate([own, other]), jnp.concatenate([other, own]))
 
 
 def shards(
@@ -907,7 +1122,7 @@
         gate_mix, mixed.reshape(rows, value_size), swish_pre, group[0], group[1]
     )
     gated = gated_wide.astype(bf16)
-    branch = scatter_product(gated, out_t, 0, 1)
+    branch = scatter_product([gated], out_t, 0, 1)
     hidden = inputs + branch
 
     mlp_wide, norm_mid_back = jax.vjp(layer_norm, hidden, mlp_gain_full, mlp_bias_full)
@@ -920,15 +1135,6 @@
         grads = with_layout_constraint(grads.astype(bf16), Layout((0, 1)))
         mine = lax.psum_scatter(grads, "ctx", scatter_dimension=0, tiled=True)
         return mine.reshape(nf, depth, -1)
-
-    def all_heads(mine):
-        return lax.all_to_all(mine, "fsdp", 0, 0, tiled=True).astype(f32)
-
-    def along(grads):
-        return grads.transpose(1, 0, 2).reshape(depth, -1)
-
-    def across(grads):
-        return grads.transpose(0, 2, 1).reshape(-1, depth)
 
     down_part = product_left(error_all, inner).astype(bf16)
     down_part, down_t = lax.optimization_barrier((down_part, down_t))
@@ -939,30 +1145,28 @@
     ff_parts = grad_gelu_up.astype(bf16)
     ff_parts, ff_low = lax.optimization_barrier((ff_parts, ff_low))
     ff_sum = sum_depths(ff_parts)
-    mlp_in_grad = scatter_product(ff_low, ff_w, 0, 6)
+    mlp_in_grad = scatter_product([ff_low], ff_w, 0, 6)
     hidden_norm_grad, grad_mlp_gain, grad_mlp_bias = norm_mid_back(mlp_in_grad)
     hidden_grad = error + hidden_norm_grad
 
-    hidden_low = gather_rows(hidden_grad.astype(bf16), 4)
-    grad_out_t = product_left(hidden_low, gated)
-    gated_grad = product(hidden_low, out_t)
+    out_part, gated_grad = gather_products(hidden_grad.astype(bf16), gated, out_t, 10)
+    out_sum = sum_depths(out_part)
     mixed_grad, swish_grad, grad_group_gain, grad_group_bias = gate_back(gated_grad)
     swish_low = swish_grad.astype(bf16)
     mixed_low = mixed_grad.astype(bf16).reshape(seqs, span, value_size)
     score_low = (blocks("sie,sje->sij", mixed_low, values) * within_fade).astype(bf16)
     pulled_state = blocks("sid,sie->sde", queries_faded, mixed_low)
-    out_sum = sum_depths(grad_out_t)
     swish_part = product_left(normed, swish_low).astype(bf16)
     swish_part, pulled_state, ff_sum, down_sum = lax.optimization_barrier(
         (swish_part, pulled_state, ff_sum, down_sum)
     )
-    later, mlp_out = pass_and_scatter(
-        pulled_state, block_fade, inner, ff_w, 2 * hidden_size, -1, 3
-    )
-    swish_part, later, out_sum = lax.optimization_barrier((swish_part, later, out_sum))
+    later, mlp_out, grad_gelu, grad_up, grad_down = pass_and_scatter(
+        pulled_state, block_fade, inner, ff_w, 2 * hidden_size, ff_sum, down_sum, -1, 3
+    )
+    out_sum, swish_part, later = lax.optimization_barrier((out_sum, swish_part, later))
     swish_sum = sum_depths(swish_part)
     block_own = (own_valid * (hidden + mlp_out)).astype(bf16)
-    block_out = both_halves(block_own, t).reshape(tokens.shape)
+    block_out = both_halves(block_own, 8).reshape(tokens.shape)
     query_grad = blocks("sij,sjd->sid", score_low, keys) + query_fade * blocks(
         "sie,sde->sid", mixed_low, entering
     )
@@ -985,13 +1189,18 @@
     attn_part = product_left(normed, low).astype(bf16)
     attn_part, low = lax.optimization_barrier((attn_part, low))
     attn_sum = sum_depths(attn_part)
-    low = jnp.concatenate([low, swish_low], -1)
-    normed_grad = scatter_product(low, attn_w, 0, 7)
+    normed_grad = scatter_product([low, swish_low], attn_w, 0, 7)
     swish_sum, normed_grad = lax.optimization_barrier((swish_sum, normed_grad))
     input_norm_grad, grad_pre_gain, grad_pre_bias = norm_in_back(normed_grad)
     tokens_own = (hidden_grad + input_norm_grad).astype(bf16)
-    grad_tokens = both_halves(tokens_own, t).reshape(tokens.shape)
-
+    grad_tokens = both_halves(tokens_own, 8).reshape(tokens.shape)
+
+    early_grads = finish(
+        [out_sum, swish_sum],
+        [[value_size], [value_size]],
+        [True, False],
+        9,
+    )
     norm_parts = jnp.stack([grad_pre_gain, grad_pre_bias, grad_mlp_gain, grad_mlp_bias])
     norm_parts = norm_parts.reshape(4, nf * nc, 1, depth).transpose(1, 2, 0, 3)
     norm_parts = jnp.broadcast_to(norm_parts, (nf * nc, nt, 4, depth)).reshape(nf * nc, nt, -1)
@@ -1002,31 +1211,33 @@
     parts = jnp.concatenate([norm_parts, group_parts.reshape(nf * nc, nt, -1)], -1)
     parts = parts.reshape(nf * nc * nt, -1)
     sums = total_small(pad_tile(parts), 5).reshape(-1)[: parts.shape[1]]
-    sums, attn_sum = lax.optimization_barrier((sums, attn_sum))
-    ready_sums = jnp.concatenate([ff_sum, down_sum, out_sum], -1)
-    ff_grads = all_heads(ready_sums)
-    attn_grads = all_heads(jnp.concatenate([swish_sum, attn_sum], -1))
+    sums, attn_sum, block_out, grad_tokens, early_grads = lax.optimization_barrier(
+        (sums, attn_sum, block_out, grad_tokens, early_grads)
+    )
+    grad_out, grad_swish = early_grads
+    grad_query, grad_key, grad_value = finish(
+        [attn_sum], [[key_size, key_size, value_size]], [False], 11
+    )
     norm_sums = sums[: 4 * depth].reshape(4, depth)
     group_sums = sums[4 * depth :].reshape(2, heads_local, -1)
 
-    at = [value_size, value_size + key_size, value_size + 2 * key_size]
     return (
         block_out,
         grad_tokens,
         norm_sums[0],
         norm_sums[1],
-        along(attn_grads[..., at[0] : at[1]]),
-        along(attn_grads[..., at[1] : at[2]]),
-        along(attn_grads[..., at[2] :]),
-        along(attn_grads[..., : at[0]]),
-        across(ff_grads[..., 3 * hidden_size :]),
+        grad_query,
+        grad_key,
+        grad_value,
+        grad_swish,
+        grad_out,
         group_sums[0],
         group_sums[1],
         norm_sums[2],
         norm_sums[3],
-        along(ff_grads[..., :hidden_size]),
-        along(ff_grads[..., hidden_size : 2 * hidden_size]),
-        across(ff_grads[..., 2 * hidden_size : 3 * hidden_size]),
+        grad_gelu,
+        grad_up,
+        grad_down,
     )
 
 

time: 806 us -> 799 us (level)
  Pallas kernels: 498 us -> 553 us
  matrix products: 120 us -> 101 us
  waiting for transfers between devices: 41.8 us -> 26.1 us
  local copies, waits for them, and re-layouts: 51.3 us -> 40.6 us
  starting transfers between devices: 9.86 us -> 0.67 us
    pallas_call x8 -> x12, Pallas kernels: 486 us -> 540 us  [call(): pl.pallas_call(kernel, out_shape=shapes, in_specs=ins, out_specs=tuple((p...]
    dot_general x4 -> x3, matrix products: 56.6 us -> 44.6 us  [product(): return jnp.dot(left, right, preferred_element_type=f32)]
    concatenate x3 -> x0, other arithmetic: 11.4 us -> none  [the longest x1 6.01 us: shards(): low = jnp.concatenate([low, swish_low], -1)]
    select_n x2 -> x0, other arithmetic: 8.51 us -> none  [both_halves(): jnp.where(t == 0, jnp.concatenate([own, other]), jnp.concatenate([other,...]
    all_to_all x2 -> x0, starting transfers between devices: 8.5 us -> none  [all_heads(): return lax.all_to_all(mine, 'fsdp', 0, 0, tiled=True).astype(f32)]
    reduce_scatter x5, waiting for transfers between devices: 8.14 us -> 0.07 us  [sum_depths(): mine = lax.psum_scatter(grads, 'ctx', scatter_dimension=0, tiled=True)]
    dot_general x5 -> x4, matrix products: 40.8 us -> 34.8 us  [product_left(): lax.dot_general(left, right, (((0,), (0,)), ((), ())), preferred_element_...]
    unnamed x106 -> x118, local copies, waits for them, and re-layouts: 18.3 us -> 22.6 us
  transfers between devices with their start and end apart: 11 -> 7, of which waited for: 2 -> 1; matrix products, arithmetic and copies ran while one was open for 23% -> 18% of each run, Pallas kernels for 48% -> 53%
where the time goes in v5:
time: 799 us; the launch traced here: 792 us
  Pallas kernels  553 us (69%)
  matrix products  101 us (13%)
  other arithmetic  54.3 us (7%)
  local copies, waits for them, and re-layouts  40.6 us (5%)
  waiting for transfers between devices  26.1 us (3%)
  between operations  15.4 us (2%)
    pallas_call x12, Pallas kernels, call(): pl.pallas_call(kernel, out_shape=shapes, in_specs=ins, out_specs=tuple((p...  540 us
    dot_general x3, matrix products, product(): return jnp.dot(left, right, preferred_element_type=f32)  44.6 us
    dot_general x4, matrix products, product_left(): lax.dot_general(left, right, (((0,), (0,)), ((), ())), preferred_element_...  34.8 us
    all_gather x2, waiting for transfers between devices, all_depths(): return lax.all_gather(mine, 'ctx', axis=0, tiled=True).reshape(width, -1)  25.9 us
    unnamed x118, local copies, waits for them, and re-layouts  22.6 us
    dot_general x12, matrix products, blocks(): return jnp.einsum(spec, left, right, preferred_element_type=f32)  21.8 us
  transfers between devices with their start and end apart: 7, of which 1 were waited for; matrix products, arithmetic and copies ran while one was open for 18% of the time, Pallas kernels for 53%

profile of v5, /device:TPU:0, one launch (start us, length us, event | category | flops | bytes accessed | tf_op | source)
XLA Modules:
  0.0 791.7 jit_solution(14047764855062690729)
XLA Ops:
  14.8 114.8 %shard_map.288 = (bf16[2048,1536]{1,0:T(8,128)(2,1)}, bf16[4,128,2048]{2,1,0:T(8,128)(2,1)}, bf16[8,256,2048]{2,1,0:T(8,128)(2,1)}, f32[16,8,128]{2,1,0:T(8,128)S(1)}) custom-call(bf16[512,2048]{1,0:T(8,128)(2,1)} %bitcast.149, f32[8,128]{1,0:T(8,128)S(1)} %stack.79.small, bf16[128,1024]{1,0:T(8,128)(2,1)S(1)} %copy-done.3, bf16[128,1024]{1,0:T(8,128)(2,1)S(1)} %copy-done.4, ...), custom_call_target="tpu_custom_call" | custom-call | bytes 2000000 | tf_op jit(solution)/shard_map/pallas_call | solution.py:476
  129.6 1.9 slice.150
  131.6 19.2 %fusion.43 = f32[2048,1536]{1,0:T(8,128)} fusion(bf16[2048,2048]{1,0:T(8,128)(2,1)} %bitcast.204, bf16[2048,1536]{1,0:T(8,128)(2,1)} %get-tuple-element.64.refs_2_), kind=kOutput, calls=%fused_computation.149 | convolution fusion | flops 12884901888 | bytes 27262976 | tf_op jit(solution)/shard_map/dot_general | solution.py:53
  151.0 2.5 slice.236
  154.3 1.3 compare_select_fusion.2
  156.8 2.5 fusion.38
  159.4 1.5 subtract_convert_fusion.2
  161.3 2.8 fusion.25
  164.4 55.4 %shard_map.289 = (bf16[16,128,512]{2,1,0:T(8,128)(2,1)}, bf16[8,256,2048]{2,1,0:T(8,128)(2,1)}) custom-call(f32[16,128,512]{2,1,0:T(8,128)} %bitcast.155, f32[1,512]{1,0:T(1,128)S(1)} %broadcast_in_dim.37.fade, bf16[256,2048]{1,0:T(8,128)(2,1)S(1)} %fusion.22.own), custom_call_target="tpu_custom_call" | custom-call | bytes 2000000 | tf_op jit(solution)/shard_map/pallas_call | solution.py:476
  223.1 1.8 multiply_convert_fusion.7
  230.0 4.3 multiply_convert_fusion.2
  234.2 46.2 %shard_map.290 = f32[256,2048]{1,0:T(8,128)} custom-call(bf16[8,256,512]{2,1,0:T(8,128)(2,1)} %bitcast.147, bf16[2048,512]{1,0:T(8,128)(2,1)} %bitcast.160), custom_call_target="tpu_custom_call" | custom-call | bytes 2000000 | tf_op jit(solution)/shard_map/pallas_call | solution.py:476
  280.5 2.1 fusion.37
  283.9 39.1 %shard_map.291 = bf16[8,256,2048]{2,1,0:T(8,128)(2,1)} custom-call(bf16[256,2048]{1,0:T(8,128)(2,1)S(1)} %add_convert_fusion.3.refs_0_), custom_call_target="tpu_custom_call" | custom-call | bytes 2000000 | tf_op jit(solution)/shard_map/pallas_call | solution.py:476
  323.0 25.9 %all-gather.5.cloned.1.call-done = bf16[16,128,1536]{2,1,0:T(8,128)(2,1)} async-done(((bf16[4,128,1536]{2,1,0:T(8,128)(2,1)}), bf16[16,128,1536]{2,1,0:T(8,128)(2,1)}) %all-gather.5.cloned.1.call-update) | async-done | bytes 6291472 | tf_op jit(solution)/shard_map/all_gather | solution.py:1061
  348.9 3.2 slice.190
  352.1 12.6 %fusion.10 = f32[2048,1024]{1,0:T(8,128)S(1)} fusion(bf16[2048,2048]{1,0:T(8,128)(2,1)} %bitcast.163, bf16[2048,1536]{1,0:T(8,128)(2,1)} %bitcast.136), kind=kOutput, calls=%fused_computation.14 | convolution fusion | flops 8589934592 | bytes 20971520 | tf_op jit(solution)/shard_map/dot_general | solution.py:53
  364.7 1.5 multiply_convert_fusion.1
  366.3 1.7 copy-done.19
  367.9 1.3 copy-done.24
  369.3 5.8 convolution_convert_fusion.3
  375.1 12.8 %fusion.6 = (bf16[2048,512]{1,0:T(8,128)(2,1)S(1)}, bf16[2048,512]{1,0:T(8,128)(2,1)S(1)}) fusion(f32[2048,1024]{1,0:T(8,128)} %copy-done.19, bf16[2048,2048]{1,0:T(8,128)(2,1)} %bitcast.211, bf16[2048,512]{1,0:T(8,128)(2,1)} %slice.190), kind=kOutput, calls=%fused_computation.10 | convolution fusion | flops 4320133120 | bytes 23068672 | tf_op jit(solution)/shard_map/dot_general | solution.py:53
  387.9 2.7 pad_maximum_fusion
  390.6 12.8 %convolution_convert_fusion.1 = bf16[2048,1024]{1,0:T(8,128)(2,1)} fusion(bf16[2048,2048]{1,0:T(8,128)(2,1)} %bitcast.164, bf16[2048,512]{1,0:T(8,128)(2,1)S(1)} %get-tuple-element.126, bf16[2048,512]{1,0:T(8,128)(2,1)S(1)} %get-tuple-element.125), kind=kOutput, calls=%fused_computation.34 | convolution fusion | flops 8600420352 | bytes 16777216 | tf_op jit(solution)/shard_map/dot_general | solution.py:57
  403.5 49.5 %shard_map.292 = f32[256,2048]{1,0:T(8,128)} custom-call(bf16[8,256,1024]{2,1,0:T(8,128)(2,1)} %bitcast.154, bf16[2048,1536]{1,0:T(8,128)(2,1)} %bitcast.137), custom_call_target="tpu_custom_call" | custom-call | bytes 2000000 | tf_op jit(solution)/shard_map/pallas_call | solution.py:476
  453.1 2.5 multiply_reduce_fusion.3
  458.0 45.5 %shard_map.293 = (bf16[2048,512]{1,0:T(8,128)(2,1)}, f32[8,256,512]{2,1,0:T(8,128)}) custom-call(bf16[256,2048]{1,0:T(8,128)(2,1)S(1)} %fusion.23.own, bf16[8,256,512]{2,1,0:T(8,128)(2,1)} %bitcast.148, bf16[2048,512]{1,0:T(8,128)(2,1)} %bitcast.161), custom_call_target="tpu_custom_call" | custom-call | bytes 2000000 | tf_op jit(solution)/shard_map/pallas_call | solution.py:476
  503.5 7.5 multiply_reduce_fusion.1
  511.1 3.1 fusion.35
  514.3 2.6 add_convert_fusion.1
  518.2 1.9 fusion.33
  520.8 3.0 fusion.24
  523.8 2.9 fusion.46
  526.7 2.2 multiply_add_fusion.1
  529.8 5.7 convolution_convert_fusion.2
  535.5 100.3 %shard_map.294 = (bf16[16,128,512]{2,1,0:T(8,128)(2,1)}, f32[256,2048]{1,0:T(8,128)}, bf16[128,2048]{1,0:T(8,128)(2,1)S(1)}, bf16[128,2048]{1,0:T(8,128)(2,1)S(1)}, bf16[2048,128]{1,0:T(8,128)(2,1)S(1)}) custom-call(f32[16,128,512]{2,1,0:T(8,128)} %bitcast.156, f32[1,512]{1,0:T(1,128)S(1)} %broadcast_in_dim.37.fade, bf16[8,256,512]{2,1,0:T(8,128)(2,1)} %bitcast.167, ...), custom_call_target="tpu_custom_call" | custom-call | bytes 2000000 | tf_op jit(solution)/shard_map/pallas_call | solution.py:476
  636.4 3.8 add_multiply_fusion
  644.5 2.0 copy-done.29
  646.6 10.5 %convolution_convert_fusion = bf16[2048,1024]{1,0:T(8,128)(2,1)} fusion(bf16[2048,2048]{1,0:T(8,128)(2,1)S(1)} %bitcast.210, bf16[2048,1024]{1,0:T(8,128)(2,1)S(1)} %constant_dynamic-update-slice_fusion), kind=kOutput, calls=%fused_computation.33 | convolution fusion | flops 8592031744 | bytes 16777216 | tf_op jit(solution)/shard_map/dot_general | solution.py:57
  660.7 51.1 %shard_map.295 = f32[256,2048]{1,0:T(8,128)} custom-call(bf16[8,256,1024]{2,1,0:T(8,128)(2,1)} %bitcast.170, bf16[8,256,512]{2,1,0:T(8,128)(2,1)} %bitcast.157, bf16[2048,1536]{1,0:T(8,128)(2,1)} %get-tuple-element.64.refs_2_), custom_call_target="tpu_custom_call" | custom-call | bytes 2000000 | tf_op jit(solution)/shard_map/pallas_call | solution.py:476
  711.8 2.7 fusion.20
  714.5 2.3 fusion.34
  717.7 13.3 %shard_map.296 = f32[8,128]{1,0:T(8,128)} custom-call(f32[32,8,128]{2,1,0:T(8,128)} %bitcast.181), custom_call_target="tpu_custom_call" | custom-call | bytes 1000000 | tf_op jit(solution)/shard_map/pallas_call | solution.py:1003
  731.1 16.1 %shard_map.299 = (bf16[2048,128]{1,0:T(8,128)(2,1)S(1)}, bf16[128,2048]{1,0:T(8,128)(2,1)S(1)}) custom-call(bf16[4,128,512]{2,1,0:T(8,128)(2,1)S(1)} %bitcast.133, bf16[4,128,512]{2,1,0:T(8,128)(2,1)} %bitcast.180), custom_call_target="tpu_custom_call" | custom-call | bytes 2000000 | tf_op jit(solution)/shard_map/pallas_call | solution.py:476
  748.2 5.0 add_convert_fusion.2
  753.2 2.9 shard_map.298
  757.1 2.8 shard_map.297
  761.9 16.3 %shard_map.300 = (bf16[128,1024]{1,0:T(8,128)(2,1)S(1)}, bf16[128,1024]{1,0:T(8,128)(2,1)S(1)}, bf16[128,2048]{1,0:T(8,128)(2,1)S(1)}) custom-call(bf16[4,128,1024]{2,1,0:T(8,128)(2,1)} %bitcast.178), custom_call_target="tpu_custom_call" | custom-call | bytes 2000000 | tf_op jit(solution)/shard_map/pallas_call | solution.py:476
  (213 shorter events, 45.0 us)
Async XLA Ops:
  7.2 227.0 %all-gather.3.cloned.1.call-start = ((), (), s32[]{:S(2)}) async-start(), calls=%async_computation.5 | async-start | bytes 2621440 | tf_op jit(solution)/shard_map/all_gather | solution.py:1061
  131.5 217.4 %all-gather.5.cloned.1.call-start = ((), (), s32[]{:S(2)}) async-start(), calls=%async_computation.6 | async-start | bytes 7864320 | tf_op jit(solution)/shard_map/all_gather | solution.py:1061
  151.0 2.6 copy-start.47
  153.6 363.3 %copy-start.10 = (bf16[2048,512]{1,0:T(8,128)(2,1)}, bf16[2048,512]{1,0:T(8,128)(2,1)S(1)}, u32[]{:S(2)}) copy-start(bf16[2048,512]{1,0:T(8,128)(2,1)S(1)} %slice.236) | copy-start | bytes 6291460
  156.2 5.1 copy-start.41
  156.2 7.9 copy-start.38
  161.3 2.8 copy-start.30
  164.3 55.4 %copy-start.34 = (bf16[4,128,2048]{2,1,0:T(8,128)(2,1)S(1)}, bf16[4,128,2048]{2,1,0:T(8,128)(2,1)}, u32[]{:S(2)}) copy-start(bf16[4,128,2048]{2,1,0:T(8,128)(2,1)} %get-tuple-element.70) | copy-start | bytes 6291460
  221.1 314.4 %reduce-scatter.10.cloned.1.call-start = ((), (), s32[]{:S(2)}) async-start(), calls=%async_computation.9 | async-start | bytes 2621440 | tf_op jit(solution)/shard_map/reduce_scatter | solution.py:1136
  223.1 2.6 copy-start.35
  224.9 2.0 copy-start.20
  224.9 2.0 copy-start.25
  225.0 2.2 copy-start.27
  225.0 2.2 copy-start.43
  228.0 2.0 copy-start.5
  234.2 46.2 %copy-start.12 = (bf16[2,256,2048]{2,1,0:T(8,128)(2,1)S(1)}, bf16[2,256,2048]{2,1,0:T(8,128)(2,1)}, u32[]{:S(2)}) copy-start(bf16[2,256,2048]{2,1,0:T(8,128)(2,1)} %param.17) | copy-start | bytes 6291460
  348.9 20.4 %slice-start.4 = ((s8[8388608]{0:T(1024)(128)(4,1)}), s8[4194304]{0:T(1024)(128)(4,1)S(1)}, s32[]{:S(2)}) async-start(s8[8388608]{0:T(1024)(128)(4,1)} %bitcast.212), calls=%async_computation.16 | async-start | bytes 8388608
  352.1 17.2 %slice-start.5 = ((s8[8388608]{0:T(1024)(128)(4,1)}), s8[4194304]{0:T(1024)(128)(4,1)S(1)}, s32[]{:S(2)}) async-start(s8[8388608]{0:T(1024)(128)(4,1)} %bitcast.212), calls=%async_computation.17 | async-start | bytes 8388608
  364.7 3.2 copy-start.19
  375.1 160.4 %reduce-scatter.8.cloned.1.call-start = ((), (), s32[]{:S(2)}) async-start(), calls=%async_computation.8 | async-start | bytes 5242880 | tf_op jit(solution)/shard_map/reduce_scatter | solution.py:1136
  403.4 232.3 %reduce-scatter.6.cloned.1.call-start = ((), (), s32[]{:S(2)}) async-start(), calls=%async_computation.7 | async-start | bytes 2621440 | tf_op jit(solution)/shard_map/reduce_scatter | solution.py:1136
  403.5 49.6 %copy-start.8 = (f32[256,2048]{1,0:T(8,128)S(1)}, f32[256,2048]{1,0:T(8,128)}, u32[]{:S(2)}) copy-start(f32[256,2048]{1,0:T(8,128)} %copy-done.7) | copy-start | bytes 6291460
  453.0 2.5 copy-start.14
  455.6 2.0 copy-start.31
  455.6 2.0 copy-start.39
  458.0 45.5 %copy-start.6 = (f32[8,256,512]{2,1,0:T(8,128)S(1)}, f32[8,256,512]{2,1,0:T(8,128)}, u32[]{:S(2)}) copy-start(f32[8,256,512]{2,1,0:T(8,128)} %copy-done.5) | copy-start | bytes 12582916
  514.2 197.6 %reduce-scatter.12.cloned.1.call-start = ((), (), s32[]{:S(2)}) async-start(), calls=%async_computation.10 | async-start | bytes 2621440 | tf_op jit(solution)/shard_map/reduce_scatter | solution.py:1136
  514.3 2.6 copy-start.36
  520.8 3.0 copy-start.33
  520.8 8.1 %slice-start = ((s8[8388608]{0:T(1024)(128)(4,1)}), s8[4194304]{0:T(1024)(128)(4,1)S(1)}, s32[]{:S(2)}) async-start(s8[8388608]{0:T(1024)(128)(4,1)} %bitcast.205), calls=%async_computation.12 | async-start | bytes 8388608
  523.8 2.9 copy-start.21
  523.8 5.1 slice-start.1
  526.7 3.1 copy-start.16
  635.8 124.2 %reduce-scatter.14.cloned.1.call-start = ((), (), s32[]{:S(2)}) async-start(), calls=%async_computation.11 | async-start | bytes 5242880 | tf_op jit(solution)/shard_map/reduce_scatter | solution.py:1136
  636.4 3.8 copy-start.18
  636.4 10.1 %slice-start.2 = ((s8[8388608]{0:T(1024)(128)(4,1)}), s8[4194304]{0:T(1024)(128)(4,1)S(1)}, s32[]{:S(2)}) async-start(s8[8388608]{0:T(1024)(128)(4,1)} %bitcast.208), calls=%async_computation.14 | async-start | bytes 8388608
  640.2 1.9 copy-start.17
  640.8 2.6 copy-start.15
  641.0 5.6 slice-start.3
  644.5 2.0 copy-start.29
  711.8 2.7 copy-start.11
  714.5 16.6 %copy-start.2 = (bf16[512,512]{1,0:T(8,128)(2,1)S(1)}, bf16[512,512]{1,0:T(8,128)(2,1)}, u32[]{:S(2)}) copy-start(bf16[512,512]{1,0:T(8,128)(2,1)} %reduce-scatter.6.cloned.1.call-done) | copy-start | bytes 1572868
  716.8 31.4 %copy-start.9 = (f32[256,2048]{1,0:T(8,128)S(1)}, f32[256,2048]{1,0:T(8,128)}, u32[]{:S(2)}) copy-start(f32[256,2048]{1,0:T(8,128)} %copy-done.7) | copy-start | bytes 6291460
  716.8 31.4 %copy-start.40 = (f32[256]{0:T(256)S(1)}, f32[256]{0:T(256)}, u32[]{:S(2)}) copy-start(f32[256]{0:T(256)} %copy-done.38) | copy-start | bytes 3076
  716.9 31.4 %copy-start.46 = (f32[256]{0:T(256)S(1)}, f32[256]{0:T(256)}, u32[]{:S(2)}) copy-start(f32[256]{0:T(256)} %copy-done.45) | copy-start | bytes 3076
  756.0 3.9 copy-start.37
  761.9 19.1 %copy-start.23 = (bf16[2,256,2048]{2,1,0:T(8,128)(2,1)S(1)}, bf16[2,256,2048]{2,1,0:T(8,128)(2,1)}, u32[]{:S(2)}) copy-start(bf16[2,256,2048]{2,1,0:T(8,128)(2,1)} %shard_map.297) | copy-start | bytes 6291460
  781.0 2.3 copy-start.22
  (13 other events, 14.5 us)
Sparse Core Ops, SparseCore 0:
  131.6 45.9 all-gather.2
  221.2 127.6 all-gather.4
  375.2 41.9 reduce-scatter.9
  419.5 76.1 reduce-scatter.7
  514.3 51.9 reduce-scatter.5
  635.9 41.5 reduce-scatter.11
  679.8 78.0 reduce-scatter.13

commit v6 on v5

--- a/solution.py
+++ b/solution.py
@@ -302,8 +302,11 @@
 
     def run(quarter):
         count = local.shape[0]
-        low = 0 if quarter == 0 else jnp.where(first, count, quarter * count // 4)
-        lax.fori_loop(low, jnp.where(first, count, (quarter + 1) * count // 4), step, 0)
+        if quarter < 0:
+            lax.fori_loop(0, jnp.where(first, count, 0), step, 0)
+        else:
+            low, high = quarter * count // 4, (quarter + 1) * count // 4
+            lax.fori_loop(jnp.where(first, count, low), jnp.where(first, count, high), step, 0)
 
     def end():
         @pl.when(jnp.logical_not(last))
@@ -439,6 +442,7 @@
     run, done = pass_steps(by, local, fade, out, held, send, recv)
     greet_plane(by)
     begin()
+    run(-1)
     run(0)
     relay()
     run(1)
@@ -450,21 +454,22 @@
     done()
 
 
-def pass_scatter_kernel(by, start, local, fade, left, right, ff, down, out, own, *refs):
+def pass_scatter_kernel(by, start, local, fade, left, right, ff, out, own, *refs):
     gelu_grad, up_grad, down_grad, held, send, recv = refs[:6]
     scratch, hand = refs[6:-3], refs[-3:]
-    targets = [[(gelu_grad, False), (up_grad, False)], [(down_grad, True)]]
-    hand_over, take = hand_steps([ff, down], targets, *hand)
+    targets = [[(gelu_grad, False), (up_grad, False), (down_grad, True)]]
+    hand_over, take = hand_steps([ff], targets, *hand)
     diagonal, straight, relay, end = scatter_steps(start, [left], right, own, *scratch)
     run, done = pass_steps(by, local, fade, out, held, send, recv)
     greet_plane(by, True)
+    run(-1)
+    diagonal()
+    straight()
     run(0)
-    diagonal()
     run(1)
-    straight()
-    run(2)
     relay()
     hand_over()
+    run(2)
     run(3)
     end()
     take()
@@ -571,7 +576,77 @@
     return out.reshape(shape), full.reshape(-1, own.shape[1])
 
 
-def pass_and_scatter(local, fade, left, right, start, ff, down, by, collective_id):
+def feed_forward_kernel(rows, error, weight, inner, low, grads, total):
+    step = pl.program_id(0)
+    size, tile, deep = inner.shape[1], 512, 1024
+    root = (2.0 / jnp.pi) ** 0.5
+
+    def units(j, carry):
+        at = pl.multiple_of(j * tile, tile)
+        gelu_pre = product(rows[...], weight[:, pl.ds(at, tile)])
+        up_pre = product(rows[...], weight[:, pl.ds(at + size, tile)])
+        square = gelu_pre * gelu_pre
+        bend = jnp.tanh(root * gelu_pre * (1.0 + 0.044715 * square))
+        half = 0.5 * (1.0 + bend)
+        gelu = gelu_pre * half
+        slope = half + 0.5 * gelu_pre * (1.0 - bend * bend) * root * (1.0 + 0.134145 * square)
+        inner[:, pl.ds(at, tile)] = (gelu * up_pre).astype(bf16)
+        inner_grad = product(error[...], weight[:, pl.ds(at + 2 * size, tile)])
+        low[:, pl.ds(at, tile)] = (inner_grad * up_pre * slope).astype(bf16)
+        low[:, pl.ds(at + size, tile)] = (inner_grad * gelu).astype(bf16)
+        return carry
+
+    lax.fori_loop(0, size // tile, units, 0)
+
+    def depths(first, last):
+        def piece(j, carry):
+            at = pl.ds(pl.multiple_of(j * deep, deep), deep)
+            into = grads if last else total
+            for left, right, columns in (
+                (rows, low, slice(0, 2 * size)),
+                (error, inner, slice(2 * size, 3 * size)),
+            ):
+                value = product_left(left[:, at], right[...])
+                if not first:
+                    value += total[at, columns]
+                into[at, columns] = value.astype(into.dtype)
+            return carry
+
+        lax.fori_loop(0, total.shape[0] // deep, piece, 0)
+
+    steps = pl.num_programs(0)
+    pl.when(step == 0)(lambda: depths(True, False))
+    pl.when((step > 0) & (step < steps - 1))(lambda: depths(False, False))
+    pl.when(step == steps - 1)(lambda: depths(False, True))
+
+
+def feed_forward(rows, error, weight):
+    count, width = rows.shape
+    size, block = weight.shape[1] // 3, 512
+    whole = pl.BlockSpec(weight.shape, lambda i: (0, 0))
+
+    def some(columns):
+        return pl.BlockSpec((block, columns), lambda i: (i, 0))
+
+    return pl.pallas_call(
+        feed_forward_kernel,
+        grid=(count // block,),
+        out_shape=(
+            jax.ShapeDtypeStruct((count, size), bf16),
+            jax.ShapeDtypeStruct((count, 2 * size), bf16),
+            jax.ShapeDtypeStruct(weight.shape, bf16),
+        ),
+        in_specs=[some(width), some(width), whole],
+        out_specs=(some(size), some(2 * size), whole),
+        scratch_shapes=[pltpu.VMEM(weight.shape, f32)],
+        compiler_params=pltpu.CompilerParams(vmem_limit_bytes=56 << 20),
+        cost_estimate=pl.CostEstimate(
+            flops=14 * count * width * size, bytes_accessed=40_000_000, transcendentals=count * size
+        ),
+    )(rows, error, weight)
+
+
+def pass_and_scatter(local, fade, left, right, start, ff, by, collective_id):
     shape = local.shape
     local = local.reshape(2 * shape[0], -1, shape[2])
     out, own, *grads = call(
@@ -580,19 +655,18 @@
         [
             passed(local),
             scattered(left, right),
-            *handed(ff, [down.shape[2]] * 2),
-            *handed(down, [down.shape[2]], True),
+            *handed(ff, [left.shape[1]] * 2),
+            *handed(ff, [left.shape[1]], True),
         ],
-        [vmem()] * 6,
+        [vmem()] * 5,
         pass_scratch(local)
         + scatter_scratch(left.shape[0] // 8, right.shape[0])
-        + hand_scratch([ff, down]),
+        + hand_scratch([ff]),
         local,
         jnp.full((1, local.shape[2]), fade, f32),
         in_eights(left),
         right,
         ff,
-        down,
     )
     return out.reshape(shape), plain(own), *(grad.astype(f32) for grad in grads)
 
@@ -1114,8 +1188,6 @@
     entering, error_all = pass_and_gather(local_state, block_fade, error_low, 1, 2)
     rest, entering = lax.optimization_barrier((rest, entering))
     ff_w = all_depths(rest[..., value_size:])
-    gelu_up = ff_w[:, : 2 * hidden_size]
-    down_t = ff_w[:, 2 * hidden_size :]
     probs = (blocks("sid,sjd->sij", queries, keys) * within_fade).astype(bf16)
     mixed = blocks("sij,sje->sie", probs, values) + blocks("sid,sde->sie", queries_faded, entering)
     gated_wide, gate_back = jax.vjp(
@@ -1127,24 +1199,14 @@
 
     mlp_wide, norm_mid_back = jax.vjp(layer_norm, hidden, mlp_gain_full, mlp_bias_full)
     mlp_in = gather_rows(mlp_wide.astype(bf16), 4)
-    pre_ff = product(mlp_in, gelu_up)
-    inner_wide, mix_back = jax.vjp(mlp_mix, pre_ff[:, :hidden_size], pre_ff[:, hidden_size:])
-    inner = inner_wide.astype(bf16)
+    inner, ff_low, ff_part = feed_forward(mlp_in, error_all, ff_w)
 
     def sum_depths(grads):
         grads = with_layout_constraint(grads.astype(bf16), Layout((0, 1)))
         mine = lax.psum_scatter(grads, "ctx", scatter_dimension=0, tiled=True)
         return mine.reshape(nf, depth, -1)
 
-    down_part = product_left(error_all, inner).astype(bf16)
-    down_part, down_t = lax.optimization_barrier((down_part, down_t))
-    down_sum = sum_depths(down_part)
-    gelu_grad, up_grad = mix_back(product(error_all, down_t))
-    ff_low = jnp.concatenate([gelu_grad.astype(bf16), up_grad.astype(bf16)], -1)
-    grad_gelu_up = product_left(mlp_in, ff_low)
-    ff_parts = grad_gelu_up.astype(bf16)
-    ff_parts, ff_low = lax.optimization_barrier((ff_parts, ff_low))
-    ff_sum = sum_depths(ff_parts)
+    ff_sum = sum_depths(ff_part)
     mlp_in_grad = scatter_product([ff_low], ff_w, 0, 6)
     hidden_norm_grad, grad_mlp_gain, grad_mlp_bias = norm_mid_back(mlp_in_grad)
     hidden_grad = error + hidden_norm_grad
@@ -1157,11 +1219,11 @@
     score_low = (blocks("sie,sje->sij", mixed_low, values) * within_fade).astype(bf16)
     pulled_state = blocks("sid,sie->sde", queries_faded, mixed_low)
     swish_part = product_left(normed, swish_low).astype(bf16)
-    swish_part, pulled_state, ff_sum, down_sum = lax.optimization_barrier(
-        (swish_part, pulled_state, ff_sum, down_sum)
+    swish_part, pulled_state, ff_sum = lax.optimization_barrier(
+        (swish_part, pulled_state, ff_sum)
     )
     later, mlp_out, grad_gelu, grad_up, grad_down = pass_and_scatter(
-        pulled_state, block_fade, inner, ff_w, 2 * hidden_size, ff_sum, down_sum, -1, 3
+        pulled_state, block_fade, inner, ff_w, 2 * hidden_size, ff_sum, -1, 3
     )
     out_sum, swish_part, later = lax.optimization_barrier((out_sum, swish_part, later))
     swish_sum = sum_depths(swish_part)

time: 799 us -> 767 us (0.960)
  matrix products: 101 us -> 58.1 us
  Pallas kernels: 553 us -> 575 us
    pallas_call x0 -> x1, Pallas kernels: none -> 36.3 us  [feed_forward(): pl.pallas_call(feed_forward_kernel, grid=(count // block,), out_shape=(ja...]
    dot_general x3 -> x1, matrix products: 44.6 us -> 19.2 us  [product(): return jnp.dot(left, right, preferred_element_type=f32)]
    dot_general x4 -> x2, matrix products: 34.8 us -> 16.6 us  [product_left(): lax.dot_general(left, right, (((0,), (0,)), ((), ())), preferred_element_...]
    pallas_call x12, Pallas kernels: 540 us -> 526 us  [call(): pl.pallas_call(kernel, out_shape=shapes, in_specs=ins, out_specs=tuple((p...]
    unnamed x118 -> x110, local copies, waits for them, and re-layouts: 22.6 us -> 19.1 us
  transfers between devices with their start and end apart: 7 -> 6, of which waited for: 1 -> 1; matrix products, arithmetic and copies ran while one was open for 18% -> 15% of each run, Pallas kernels for 53% -> 54%
where the time goes in v6:
time: 767 us; the launch traced here: 759 us
  Pallas kernels  575 us (75%)
  matrix products  58.1 us (8%)
  other arithmetic  50.3 us (7%)
  local copies, waits for them, and re-layouts  33.8 us (4%)
  waiting for transfers between devices  25.9 us (3%)
  between operations  15.4 us (2%)
    pallas_call x12, Pallas kernels, call(): pl.pallas_call(kernel, out_shape=shapes, in_specs=ins, out_specs=tuple((p...  526 us
    pallas_call x1, Pallas kernels, feed_forward(): pl.pallas_call(feed_forward_kernel, grid=(count // block,), out_shape=(ja...  36.3 us
    all_gather x2, waiting for transfers between devices, all_depths(): return lax.all_gather(mine, 'ctx', axis=0, tiled=True).reshape(width, -1)  25.7 us
    dot_general x12, matrix products, blocks(): return jnp.einsum(spec, left, right, preferred_element_type=f32)  22.2 us
    dot_general x1, matrix products, product(): return jnp.dot(left, right, preferred_element_type=f32)  19.2 us
    unnamed x110, local copies, waits for them, and re-layouts  19.1 us
    dot_general x2, matrix products, product_left(): lax.dot_general(left, right, (((0,), (0,)), ((), ())), preferred_element_...  16.6 us
  transfers between devices with their start and end apart: 6, of which 1 were waited for; matrix products, arithmetic and copies ran while one was open for 15% of the time, Pallas kernels for 54%

profile of v6, /device:TPU:0, one launch (start us, length us, event | category | flops | bytes accessed | tf_op | source)
XLA Modules:
  0.0 758.9 jit_solution(2243719785505772937)
XLA Ops:
  14.8 114.8 %shard_map.288 = (bf16[2048,1536]{1,0:T(8,128)(2,1)}, bf16[4,128,2048]{2,1,0:T(8,128)(2,1)}, bf16[8,256,2048]{2,1,0:T(8,128)(2,1)}, f32[16,8,128]{2,1,0:T(8,128)S(1)}) custom-call(bf16[512,2048]{1,0:T(8,128)(2,1)} %bitcast.141, f32[8,128]{1,0:T(8,128)S(1)} %stack.79.small, bf16[128,1024]{1,0:T(8,128)(2,1)S(1)} %copy-done.3, bf16[128,1024]{1,0:T(8,128)(2,1)S(1)} %copy-done.4, ...), custom_call_target="tpu_custom_call" | custom-call | bytes 2000000 | tf_op jit(solution)/shard_map/pallas_call | solution.py:481
  129.6 1.9 slice.138
  131.6 19.2 %fusion.34 = f32[2048,1536]{1,0:T(8,128)} fusion(bf16[2048,2048]{1,0:T(8,128)(2,1)} %bitcast.194, bf16[2048,1536]{1,0:T(8,128)(2,1)} %get-tuple-element.62.refs_2_), kind=kOutput, calls=%fused_computation.132 | convolution fusion | flops 12884901888 | bytes 27262976 | tf_op jit(solution)/shard_map/dot_general | solution.py:53
  151.0 2.5 slice.201
  154.2 1.3 compare_select_fusion.2
  156.8 2.5 fusion.29
  159.3 1.5 subtract_convert_fusion.2
  161.2 2.8 fusion.16
  164.3 55.4 %shard_map.289 = (bf16[16,128,512]{2,1,0:T(8,128)(2,1)}, bf16[8,256,2048]{2,1,0:T(8,128)(2,1)}) custom-call(f32[16,128,512]{2,1,0:T(8,128)} %bitcast.146, f32[1,512]{1,0:T(1,128)S(1)} %broadcast_in_dim.37.fade, bf16[256,2048]{1,0:T(8,128)(2,1)S(1)} %fusion.13.own), custom_call_target="tpu_custom_call" | custom-call | bytes 2000000 | tf_op jit(solution)/shard_map/pallas_call | solution.py:481
  219.8 1.3 slice.141
  223.4 1.8 multiply_convert_fusion.5
  229.1 1.1 copy-done.5
  230.2 4.2 multiply_convert_fusion
  234.5 46.1 %shard_map.290 = f32[256,2048]{1,0:T(8,128)} custom-call(bf16[8,256,512]{2,1,0:T(8,128)(2,1)} %bitcast.139, bf16[2048,512]{1,0:T(8,128)(2,1)} %bitcast.151), custom_call_target="tpu_custom_call" | custom-call | bytes 2000000 | tf_op jit(solution)/shard_map/pallas_call | solution.py:481
  280.7 2.1 fusion.28
  284.1 39.1 %shard_map.291 = bf16[8,256,2048]{2,1,0:T(8,128)(2,1)} custom-call(bf16[256,2048]{1,0:T(8,128)(2,1)S(1)} %add_convert_fusion.3.refs_0_), custom_call_target="tpu_custom_call" | custom-call | bytes 2000000 | tf_op jit(solution)/shard_map/pallas_call | solution.py:481
  323.2 25.7 %all-gather.5.cloned.1.call-done = bf16[16,128,1536]{2,1,0:T(8,128)(2,1)} async-done(((bf16[4,128,1536]{2,1,0:T(8,128)(2,1)}), bf16[16,128,1536]{2,1,0:T(8,128)(2,1)}) %all-gather.5.cloned.1.call-update) | async-done | bytes 6291472 | tf_op jit(solution)/shard_map/all_gather | solution.py:1135
  348.9 36.3 %shard_map.292 = (bf16[2048,512]{1,0:T(8,128)(2,1)}, bf16[2048,1024]{1,0:T(8,128)(2,1)}, bf16[2048,1536]{1,0:T(8,128)(2,1)}) custom-call(bf16[2048,2048]{1,0:T(8,128)(2,1)} %bitcast.154, bf16[2048,2048]{1,0:T(8,128)(2,1)} %bitcast.201, bf16[2048,1536]{1,0:T(8,128)(2,1)} %bitcast.136), custom_call_target="tpu_custom_call" | custom-call | flops 30064771072 | bytes 40000000 | tf_op jit(solution)/shard_map/pallas_call | solution.py:631
  385.3 49.8 %shard_map.293 = f32[256,2048]{1,0:T(8,128)} custom-call(bf16[8,256,1024]{2,1,0:T(8,128)(2,1)} %bitcast.163, bf16[2048,1536]{1,0:T(8,128)(2,1)} %bitcast.137), custom_call_target="tpu_custom_call" | custom-call | bytes 2000000 | tf_op jit(solution)/shard_map/pallas_call | solution.py:481
  435.1 2.5 multiply_reduce_fusion.3
  438.4 1.3 copy-done.13
  440.0 45.6 %shard_map.294 = (bf16[2048,512]{1,0:T(8,128)(2,1)}, f32[8,256,512]{2,1,0:T(8,128)}) custom-call(bf16[256,2048]{1,0:T(8,128)(2,1)S(1)} %fusion.14.own, bf16[8,256,512]{2,1,0:T(8,128)(2,1)} %bitcast.140, bf16[2048,512]{1,0:T(8,128)(2,1)} %bitcast.152), custom_call_target="tpu_custom_call" | custom-call | bytes 2000000 | tf_op jit(solution)/shard_map/pallas_call | solution.py:481
  485.6 7.6 %multiply_reduce_fusion.1 = (f32[2048]{0:T(1024)S(1)}, f32[512]{0:T(512)S(1)}, f32[512]{0:T(512)S(1)}, f32[2048,512]{1,0:T(8,128)S(1)}, bf16[2048,512]{1,0:T(8,128)(2,1)}) fusion(f32[8,256,512]{2,1,0:T(8,128)S(1)} %copy-done.6, f32[512]{0:T(512)S(1)} %mul.473, f32[2048]{0:T(1024)S(1)} %bitcast.182, f32[2048]{0:T(1024)S(1)} %rsqrt.31, ...), kind=kLoop, calls=%fused_computation.12 | loop fusion | flops 24114176 | bytes 18907136 | tf_op jit(solution)/shard_map/transpose(jvp())/reduce_sum | solution.py:44
  493.3 3.2 fusion.26
  496.6 2.6 add_convert_fusion.1
  500.4 1.9 fusion.24
  502.9 3.0 fusion.15
  505.9 2.9 fusion.37
  508.8 2.2 multiply_add_fusion.1
  511.9 5.8 convolution_convert_fusion.1
  517.6 86.6 %shard_map.295 = (bf16[16,128,512]{2,1,0:T(8,128)(2,1)}, f32[256,2048]{1,0:T(8,128)}, bf16[128,2048]{1,0:T(8,128)(2,1)S(1)}, bf16[128,2048]{1,0:T(8,128)(2,1)S(1)}, bf16[2048,128]{1,0:T(8,128)(2,1)S(1)}) custom-call(f32[16,128,512]{2,1,0:T(8,128)} %bitcast.147, f32[1,512]{1,0:T(1,128)S(1)} %broadcast_in_dim.37.fade, bf16[8,256,512]{2,1,0:T(8,128)(2,1)} %bitcast.168, ...), custom_call_target="tpu_custom_call" | custom-call | bytes 2000000 | tf_op jit(solution)/shard_map/pallas_call | solution.py:481
  605.0 4.2 add_multiply_fusion
  610.7 1.4 copy-done.15
  613.2 2.0 copy-done.27
  615.2 10.8 %convolution_convert_fusion = bf16[2048,1024]{1,0:T(8,128)(2,1)} fusion(bf16[2048,2048]{1,0:T(8,128)(2,1)S(1)} %bitcast.200, bf16[2048,1024]{1,0:T(8,128)(2,1)S(1)} %constant_dynamic-update-slice_fusion), kind=kOutput, calls=%fused_computation.18 | convolution fusion | flops 8592031744 | bytes 16777216 | tf_op jit(solution)/shard_map/dot_general | solution.py:57
  626.6 1.1 convert_element_type.193
  629.7 50.1 %shard_map.296 = f32[256,2048]{1,0:T(8,128)} custom-call(bf16[8,256,1024]{2,1,0:T(8,128)(2,1)} %bitcast.159, bf16[8,256,512]{2,1,0:T(8,128)(2,1)} %bitcast.148, bf16[2048,1536]{1,0:T(8,128)(2,1)} %get-tuple-element.62.refs_2_), custom_call_target="tpu_custom_call" | custom-call | bytes 2000000 | tf_op jit(solution)/shard_map/pallas_call | solution.py:481
  679.9 2.7 fusion.11
  682.6 2.3 fusion.25
  685.8 12.3 %shard_map.297 = f32[8,128]{1,0:T(8,128)} custom-call(f32[32,8,128]{2,1,0:T(8,128)} %bitcast.172), custom_call_target="tpu_custom_call" | custom-call | bytes 1000000 | tf_op jit(solution)/shard_map/pallas_call | solution.py:1077
  698.1 16.4 %shard_map.300 = (bf16[2048,128]{1,0:T(8,128)(2,1)S(1)}, bf16[128,2048]{1,0:T(8,128)(2,1)S(1)}) custom-call(bf16[4,128,512]{2,1,0:T(8,128)(2,1)S(1)} %bitcast.126, bf16[4,128,512]{2,1,0:T(8,128)(2,1)} %bitcast.171), custom_call_target="tpu_custom_call" | custom-call | bytes 2000000 | tf_op jit(solution)/shard_map/pallas_call | solution.py:481
  715.6 4.8 add_convert_fusion.2
  720.4 2.9 shard_map.299
  723.3 1.1 convert_element_type.189
  724.4 2.8 shard_map.298
  729.1 16.3 %shard_map.301 = (bf16[128,1024]{1,0:T(8,128)(2,1)S(1)}, bf16[128,1024]{1,0:T(8,128)(2,1)S(1)}, bf16[128,2048]{1,0:T(8,128)(2,1)S(1)}) custom-call(bf16[4,128,1024]{2,1,0:T(8,128)(2,1)} %bitcast.170), custom_call_target="tpu_custom_call" | custom-call | bytes 2000000 | tf_op jit(solution)/shard_map/pallas_call | solution.py:481
  748.2 1.3 copy.65
  750.5 1.3 copy.66
  (195 shorter events, 35.0 us)
Async XLA Ops:
  7.2 227.3 %all-gather.3.cloned.1.call-start = ((), (), s32[]{:S(2)}) async-start(), calls=%async_computation.4 | async-start | bytes 2621440 | tf_op jit(solution)/shard_map/all_gather | solution.py:1135
  131.5 217.4 %all-gather.5.cloned.1.call-start = ((), (), s32[]{:S(2)}) async-start(), calls=%async_computation.5 | async-start | bytes 7864320 | tf_op jit(solution)/shard_map/all_gather | solution.py:1135
  151.0 2.5 copy-start.45
  153.5 345.6 %copy-start.10 = (bf16[2048,512]{1,0:T(8,128)(2,1)}, bf16[2048,512]{1,0:T(8,128)(2,1)S(1)}, u32[]{:S(2)}) copy-start(bf16[2048,512]{1,0:T(8,128)(2,1)S(1)} %slice.201) | copy-start | bytes 6291460
  156.1 5.1 copy-start.39
  156.2 7.9 %copy-start.36 = (f32[256]{0:T(256)}, f32[256]{0:T(256)S(1)}, u32[]{:S(2)}) copy-start(f32[256]{0:T(256)S(1)} %compare_convert_fusion) | copy-start | bytes 3076
  161.2 2.8 copy-start.28
  164.3 55.5 %copy-start.32 = (bf16[4,128,2048]{2,1,0:T(8,128)(2,1)S(1)}, bf16[4,128,2048]{2,1,0:T(8,128)(2,1)}, u32[]{:S(2)}) copy-start(bf16[4,128,2048]{2,1,0:T(8,128)(2,1)} %get-tuple-element.68) | copy-start | bytes 6291460
  221.0 296.6 %reduce-scatter.7.cloned.1.call-start = ((), (), s32[]{:S(2)}) async-start(), calls=%async_computation.7 | async-start | bytes 7864320 | tf_op jit(solution)/shard_map/reduce_scatter | solution.py:1206
  223.4 2.6 copy-start.33
  225.2 2.0 copy-start.19
  225.2 2.0 copy-start.23
  225.2 2.2 copy-start.25
  225.2 2.2 copy-start.41
  228.2 2.0 copy-start.5
  234.5 46.2 %copy-start.12 = (bf16[2,256,2048]{2,1,0:T(8,128)(2,1)S(1)}, bf16[2,256,2048]{2,1,0:T(8,128)(2,1)}, u32[]{:S(2)}) copy-start(bf16[2,256,2048]{2,1,0:T(8,128)(2,1)} %param.17) | copy-start | bytes 6291460
  282.8 1.3 copy-start.7
  385.2 219.1 %reduce-scatter.5.cloned.1.call-start = ((), (), s32[]{:S(2)}) async-start(), calls=%async_computation.6 | async-start | bytes 2621440 | tf_op jit(solution)/shard_map/reduce_scatter | solution.py:1206
  385.2 49.9 %copy-start.8 = (f32[256,2048]{1,0:T(8,128)S(1)}, f32[256,2048]{1,0:T(8,128)}, u32[]{:S(2)}) copy-start(f32[256,2048]{1,0:T(8,128)} %copy-done.7) | copy-start | bytes 6291460
  435.1 2.6 copy-start.14
  437.7 2.0 copy-start.29
  437.7 2.0 copy-start.37
  438.3 1.3 copy-start.13
  438.3 1.7 copy-start.43
  440.0 45.6 %copy-start.6 = (f32[8,256,512]{2,1,0:T(8,128)S(1)}, f32[8,256,512]{2,1,0:T(8,128)}, u32[]{:S(2)}) copy-start(f32[8,256,512]{2,1,0:T(8,128)} %copy-done.5) | copy-start | bytes 12582916
  496.5 183.4 %reduce-scatter.9.cloned.1.call-start = ((), (), s32[]{:S(2)}) async-start(), calls=%async_computation.8 | async-start | bytes 2621440 | tf_op jit(solution)/shard_map/reduce_scatter | solution.py:1206
  496.6 2.6 copy-start.34
  499.2 1.2 copy-start.26
  502.9 3.0 copy-start.31
  502.9 8.1 %slice-start = ((s8[8388608]{0:T(1024)(128)(4,1)}), s8[4194304]{0:T(1024)(128)(4,1)S(1)}, s32[]{:S(2)}) async-start(s8[8388608]{0:T(1024)(128)(4,1)} %bitcast.195), calls=%async_computation.10 | async-start | bytes 8388608
  505.9 2.9 copy-start.20
  505.9 5.1 slice-start.1
  508.8 3.1 copy-start.16
  604.3 122.9 %reduce-scatter.11.cloned.1.call-start = ((), (), s32[]{:S(2)}) async-start(), calls=%async_computation.9 | async-start | bytes 5242880 | tf_op jit(solution)/shard_map/reduce_scatter | solution.py:1206
  604.9 4.2 copy-start.18
  605.0 10.3 %slice-start.2 = ((s8[8388608]{0:T(1024)(128)(4,1)}), s8[4194304]{0:T(1024)(128)(4,1)S(1)}, s32[]{:S(2)}) async-start(s8[8388608]{0:T(1024)(128)(4,1)} %bitcast.198), calls=%async_computation.12 | async-start | bytes 8388608
  609.2 1.6 copy-start.17
  609.7 2.4 copy-start.15
  609.9 5.4 slice-start.3
  613.2 2.0 copy-start.27
  679.8 2.8 copy-start.11
  682.6 15.5 %copy-start.2 = (bf16[512,512]{1,0:T(8,128)(2,1)S(1)}, bf16[512,512]{1,0:T(8,128)(2,1)}, u32[]{:S(2)}) copy-start(bf16[512,512]{1,0:T(8,128)(2,1)} %reduce-scatter.5.cloned.1.call-done) | copy-start | bytes 1572868
  684.9 30.6 %copy-start.9 = (f32[256,2048]{1,0:T(8,128)S(1)}, f32[256,2048]{1,0:T(8,128)}, u32[]{:S(2)}) copy-start(f32[256,2048]{1,0:T(8,128)} %copy-done.7) | copy-start | bytes 6291460
  684.9 30.6 %copy-start.38 = (f32[256]{0:T(256)S(1)}, f32[256]{0:T(256)}, u32[]{:S(2)}) copy-start(f32[256]{0:T(256)} %copy-done.36) | copy-start | bytes 3076
  684.9 30.6 %copy-start.44 = (f32[256]{0:T(256)S(1)}, f32[256]{0:T(256)}, u32[]{:S(2)}) copy-start(f32[256]{0:T(256)} %copy-done.43) | copy-start | bytes 3076
  723.3 3.9 copy-start.35
  729.1 19.1 %copy-start.22 = (bf16[2,256,2048]{2,1,0:T(8,128)(2,1)S(1)}, bf16[2,256,2048]{2,1,0:T(8,128)(2,1)}, u32[]{:S(2)}) copy-start(bf16[2,256,2048]{2,1,0:T(8,128)(2,1)} %shard_map.298) | copy-start | bytes 6291460
  748.2 2.3 copy-start.21
  (8 other events, 7.4 us)
Sparse Core Ops, SparseCore 0:
  131.6 46.0 all-gather.2
  221.2 127.6 all-gather.4
  385.3 108.9 reduce-scatter.6
  496.6 57.2 reduce-scatter.4
  604.5 40.0 reduce-scatter.8
  646.7 78.4 reduce-scatter.10

commit v7 on v6

--- a/solution.py
+++ b/solution.py
@@ -1,4 +1,5 @@
 import functools
+import math
 
 import jax
 import jax.numpy as jnp
@@ -9,6 +10,7 @@
 from jax.sharding import PartitionSpec as P
 
 eps = 1e-05
+SPARE = 6 << 20
 group_floor = 1.0
 f32 = jnp.float32
 bf16 = jnp.bfloat16
@@ -433,6 +435,7 @@
         own,
         in_eights(left),
         right,
+        tight=True,
     )
     return grad, back.reshape(8 * rows, size)
 
@@ -476,8 +479,19 @@
     done()
 
 
-def call(kernel, collective_id, outs, ins, scratch, *args):
+def held_bytes(array):
+    last = -(-array.shape[-1] // 128) * 128
+    return math.prod(array.shape[:-1]) * last * jnp.dtype(array.dtype).itemsize
+
+
+def call(kernel, collective_id, outs, ins, scratch, *args, tight=False):
     shapes, spaces = zip(*outs)
+    limit = 52 << 20
+    held = [shape for shape, space in outs if space == pltpu.VMEM]
+    held += [arg for arg, spec in zip(args, ins) if spec.memory_space == pltpu.VMEM]
+    held += [one for one in scratch if getattr(one, "memory_space", None) == pltpu.VMEM]
+    if tight:
+        limit = sum(held_bytes(one) for one in held) + SPARE
     return pl.pallas_call(
         kernel,
         out_shape=shapes,
@@ -485,7 +499,7 @@
         out_specs=tuple(pl.BlockSpec(memory_space=space) for space in spaces),
         scratch_shapes=scratch,
         compiler_params=pltpu.CompilerParams(
-            collective_id=collective_id, has_side_effects=True, vmem_limit_bytes=52 << 20
+            collective_id=collective_id, has_side_effects=True, vmem_limit_bytes=limit
         ),
         cost_estimate=pl.CostEstimate(flops=0, bytes_accessed=2_000_000, transcendentals=0),
     )(*args)
@@ -753,6 +767,9 @@
     weights = list(refs[:count])
     attn, rest, full, everyone = refs[count : count + 4]
     (
+        brought,
+        untouched,
+        fetch,
         turns,
         gains,
         normed,
@@ -775,6 +792,18 @@
     across = [weights[i] for i in turned]
     for n, i in enumerate(turned):
         weights[i] = turns.at[n]
+    rows = normed.shape[0]
+    fetched = [
+        pltpu.make_async_copy(
+            own.at[pl.ds(pl.multiple_of(t * rows, rows), rows)], brought, fetch.at[0]
+        )
+    ]
+    fetched += [
+        pltpu.make_async_copy(matrix, untouched.at[n], fetch.at[n + 1])
+        for n, matrix in enumerate(across)
+    ]
+    for copy in fetched:
+        copy.start()
     near = beside(f)
     starts = [sum(sizes[:i]) if i < split else sum(sizes[split:i]) for i in range(count)]
 
@@ -851,9 +880,8 @@
     for i in range(places):
         for j in range(2):
             gains[j : j + 1, i * depth : (i + 1) * depth] = everyone[i, j : j + 1, :depth]
-    rows = normed.shape[0]
-    mine = own[pl.ds(pl.multiple_of(t * rows, rows), rows), :].astype(f32)
-    normed[...] = layer_norm(mine, gains[0:1, :], gains[1:2, :]).astype(bf16)
+    fetched[0].wait()
+    normed[...] = layer_norm(brought[...].astype(f32), gains[0:1, :], gains[1:2, :]).astype(bf16)
     begin, relay, others, diagonal, finish = gather_steps(
         normed, full, mixed, gather_keep, gather_send, gather_recv
     )
@@ -863,7 +891,8 @@
     step(1, 0)
     relay()
     for n in range(len(turned)):
-        turns[n] = across[n][...].T
+        fetched[n + 1].wait()
+        turns[n] = untouched[n].T
     for i in range(split, count):
         hold(i).start()
         for n in range(3):
@@ -900,9 +929,11 @@
             (jax.ShapeDtypeStruct((8, rows, width), bf16), pl.ANY),
             (jax.ShapeDtypeStruct((count, *small.shape), f32), pltpu.VMEM),
         ],
-        [vmem(), vmem()]
-        + [vmem() if i in turned else anywhere for i in range(len(weights))],
+        [anywhere, vmem()] + [anywhere] * len(weights),
         [
+            pltpu.VMEM((rows, width), bf16),
+            pltpu.VMEM((len(turned), *weights[turned[0]].shape), bf16),
+            pltpu.SemaphoreType.DMA((len(turned) + 1,)),
             pltpu.VMEM((len(turned), depth, sizes[turned[0]] * nf), bf16),
             pltpu.VMEM((8, width), f32),
             pltpu.VMEM((rows, width), bf16),
@@ -1009,49 +1040,26 @@
         [vmem()] * len(parts),
         hand_scratch(parts),
         *parts,
+        tight=True,
     )
     return [out.astype(f32) for out in outs]
 
 
-def halves_kernel(own, out, keep, send, recv):
-    t = lax.axis_index("tp")
-    core = {"tp": 1 - t}
-    barrier = pltpu.get_barrier_semaphore()
-    pl.semaphore_signal(barrier, inc=1, device_id=core, device_id_type=MESH)
-    pl.semaphore_wait(barrier, 1)
-    copy = remote(own, out.at[t], send, recv, core)
-    copy.start()
-    local = pltpu.make_async_copy(own, out.at[t], keep)
-    local.start()
-    local.wait()
-    copy.wait()
-
-
-def both_halves(own, collective_id):
-    (out,) = call(
-        halves_kernel,
-        collective_id,
-        [(jax.ShapeDtypeStruct((2, *own.shape), own.dtype), pl.ANY)],
-        [pl.BlockSpec(memory_space=pl.ANY)],
-        [pltpu.SemaphoreType.DMA] * 3,
-        own,
-    )
-    return out
-
-
-def total_kernel(parts, out, slots, send, recv):
+def total_steps(parts, out, slots, send, recv):
     nc, nt = lax.axis_size("ctx"), lax.axis_size("tp")
     count = parts.shape[0]
     place = (lax.axis_index("fsdp") * nc + lax.axis_index("ctx")) * nt + lax.axis_index("tp")
-    barrier = pltpu.get_barrier_semaphore()
-
-    def hello(i, carry):
-        other = peer_of(lax.rem(place + i, count), nc, nt)
-        pl.semaphore_signal(barrier, inc=1, device_id=other, device_id_type=MESH)
-        return carry
-
-    lax.fori_loop(1, count, hello, 0)
-    pl.semaphore_wait(barrier, count - 1)
+
+    def hello():
+        barrier = pltpu.get_barrier_semaphore()
+
+        def one(i, carry):
+            other = peer_of(lax.rem(place + i, count), nc, nt)
+            pl.semaphore_signal(barrier, inc=1, device_id=other, device_id_type=MESH)
+            return carry
+
+        lax.fori_loop(1, count, one, 0)
+        pl.semaphore_wait(barrier, count - 1)
 
     def copy(i):
         other = lax.rem(place + i, count)
@@ -1059,34 +1067,77 @@
             parts.at[other], slots.at[i], send.at[i], recv.at[i], peer_of(other, nc, nt)
         )
 
-    def go(i, carry):
-        copy(i).start()
-        return carry
-
-    lax.fori_loop(1, count, go, 0)
-
-    def add(i, carry):
-        copy(i).wait()
-        return carry + slots[i]
-
-    out[...] = lax.fori_loop(1, count, add, parts[place])
-
-
-def total_small(parts, collective_id):
+    def begin():
+        def go(i, carry):
+            copy(i).start()
+            return carry
+
+        lax.fori_loop(1, count, go, 0)
+
+    def end():
+        def add(i, carry):
+            copy(i).wait()
+            return carry + slots[i]
+
+        out[...] = lax.fori_loop(1, count, add, parts[place])
+
+    return hello, begin, end
+
+
+def close_kernel(
+    parts, first, second, one, two, out, wide, tall, one_both, two_both, slots, send, recv, *scratch
+):
+    hand, keep, core_send, core_recv = scratch[:3], *scratch[3:]
+    t = lax.axis_index("tp")
+    hello, begin, end = total_steps(parts, out, slots, send, recv)
+    hand_over, take = hand_steps([first, second], [[(wide, True)], [(tall, False)]], *hand)
+    hello()
+    begin()
+    copies = []
+    for i, (own, both) in enumerate(((one, one_both), (two, two_both))):
+        copies.append(pltpu.make_async_copy(own, both.at[t], keep.at[i]))
+        copies.append(
+            remote(own, both.at[t], core_send.at[i], core_recv.at[i], {"tp": 1 - t})
+        )
+    for copy in copies:
+        copy.start()
+    end()
+    for copy in copies:
+        copy.wait()
+    hand_over()
+    take()
+
+
+def close(parts, first, second, one, two, collective_id):
     count = parts.shape[0]
-    return pl.pallas_call(
-        total_kernel,
-        out_shape=jax.ShapeDtypeStruct(parts.shape[1:], parts.dtype),
-        in_specs=[pl.BlockSpec(memory_space=pltpu.VMEM)],
-        out_specs=pl.BlockSpec(memory_space=pltpu.VMEM),
-        scratch_shapes=[
-            pltpu.VMEM(parts.shape, parts.dtype),
+    both = (jax.ShapeDtypeStruct((2, *one.shape), one.dtype), pltpu.VMEM)
+    return call(
+        close_kernel,
+        collective_id,
+        [
+            (jax.ShapeDtypeStruct(parts.shape[1:], f32), pltpu.VMEM),
+            *handed(first, [first.shape[2]], True),
+            *handed(second, [second.shape[2]]),
+            both,
+            both,
+        ],
+        [vmem()] * 5,
+        [
+            pltpu.VMEM(parts.shape, f32),
             pltpu.SemaphoreType.DMA((count,)),
             pltpu.SemaphoreType.DMA((count,)),
+            *hand_scratch([first, second]),
+            pltpu.SemaphoreType.DMA((2,)),
+            pltpu.SemaphoreType.DMA((2,)),
+            pltpu.SemaphoreType.DMA((2,)),
         ],
-        compiler_params=pltpu.CompilerParams(collective_id=collective_id, has_side_effects=True),
-        cost_estimate=pl.CostEstimate(flops=0, bytes_accessed=1_000_000, transcendentals=0),
-    )(parts)
+        parts,
+        first,
+        second,
+        one,
+        two,
+        tight=True,
+    )
 
 
 def shards(
@@ -1227,8 +1278,7 @@
     )
     out_sum, swish_part, later = lax.optimization_barrier((out_sum, swish_part, later))
     swish_sum = sum_depths(swish_part)
-    block_own = (own_valid * (hidden + mlp_out)).astype(bf16)
-    block_out = both_halves(block_own, 8).reshape(tokens.shape)
+    block_own = (hidden + mlp_out).astype(bf16)
     query_grad = blocks("sij,sjd->sid", score_low, keys) + query_fade * blocks(
         "sie,sde->sid", mixed_low, entering
     )
@@ -1255,14 +1305,7 @@
     swish_sum, normed_grad = lax.optimization_barrier((swish_sum, normed_grad))
     input_norm_grad, grad_pre_gain, grad_pre_bias = norm_in_back(normed_grad)
     tokens_own = (hidden_grad + input_norm_grad).astype(bf16)
-    grad_tokens = both_halves(tokens_own, 8).reshape(tokens.shape)
-
-    early_grads = finish(
-        [out_sum, swish_sum],
-        [[value_size], [value_size]],
-        [True, False],
-        9,
-    )
+
     norm_parts = jnp.stack([grad_pre_gain, grad_pre_bias, grad_mlp_gain, grad_mlp_bias])
     norm_parts = norm_parts.reshape(4, nf * nc, 1, depth).transpose(1, 2, 0, 3)
     norm_parts = jnp.broadcast_to(norm_parts, (nf * nc, nt, 4, depth)).reshape(nf * nc, nt, -1)
@@ -1272,11 +1315,17 @@
     group_parts = group_parts.reshape(nt, heads_local, 2, nf * nc, -1).transpose(3, 0, 2, 1, 4)
     parts = jnp.concatenate([norm_parts, group_parts.reshape(nf * nc, nt, -1)], -1)
     parts = parts.reshape(nf * nc * nt, -1)
-    sums = total_small(pad_tile(parts), 5).reshape(-1)[: parts.shape[1]]
-    sums, attn_sum, block_out, grad_tokens, early_grads = lax.optimization_barrier(
-        (sums, attn_sum, block_out, grad_tokens, early_grads)
-    )
-    grad_out, grad_swish = early_grads
+    sums, grad_out, grad_swish, block_out, grad_tokens = close(
+        pad_tile(parts), out_sum, swish_sum, block_own, tokens_own, 5
+    )
+    block_valid = (positions[None, :] < lengths[:, None]).astype(bf16)[:, :, None]
+    block_out = block_out.reshape(tokens.shape) * block_valid
+    grad_tokens = grad_tokens.reshape(tokens.shape) * block_valid
+    grad_out, grad_swish = grad_out.astype(f32), grad_swish.astype(f32)
+    sums, attn_sum, block_out, grad_tokens, grad_out, grad_swish = lax.optimization_barrier(
+        (sums, attn_sum, block_out, grad_tokens, grad_out, grad_swish)
+    )
+    sums = sums.reshape(-1)[: parts.shape[1]]
     grad_query, grad_key, grad_value = finish(
         [attn_sum], [[key_size, key_size, value_size]], [False], 11
     )

time: 767 us -> 759 us (0.990)
  Pallas kernels: 575 us -> 563 us
    pallas_call x1 -> x0, Pallas kernels: 12.3 us -> none  [total_small(): pl.pallas_call(total_kernel, out_shape=jax.ShapeDtypeStruct(parts.shape[1...]
    pallas_call x12 -> x10, Pallas kernels: 526 us -> 527 us  [call(): pl.pallas_call(kernel, out_shape=shapes, in_specs=ins, out_specs=tuple((p...]
    unnamed x110 -> x112, local copies, waits for them, and re-layouts: 19.1 us -> 19.2 us
  transfers between devices with their start and end apart: 6 -> 6, of which waited for: 1 -> 2; matrix products, arithmetic and copies ran while one was open for 15% -> 15% of each run, Pallas kernels for 54% -> 53%
where the time goes in v7:
time: 759 us; the launch traced here: 751 us
  Pallas kernels  563 us (74%)
  matrix products  58 us (8%)
  other arithmetic  49.4 us (7%)
  local copies, waits for them, and re-layouts  33.8 us (4%)
  waiting for transfers between devices  30.4 us (4%)
  between operations  15.3 us (2%)
    pallas_call x10, Pallas kernels, call(): pl.pallas_call(kernel, out_shape=shapes, in_specs=ins, out_specs=tuple((p...  527 us
    pallas_call x1, Pallas kernels, feed_forward(): pl.pallas_call(feed_forward_kernel, grid=(count // block,), out_shape=(ja...  36.7 us
    all_gather x2, waiting for transfers between devices, all_depths(): return lax.all_gather(mine, 'ctx', axis=0, tiled=True).reshape(width, -1)  25.8 us
    dot_general x12, matrix products, blocks(): return jnp.einsum(spec, left, right, preferred_element_type=f32)  22.2 us
    dot_general x1, matrix products, product(): return jnp.dot(left, right, preferred_element_type=f32)  19.2 us
    unnamed x112, local copies, waits for them, and re-layouts  19.2 us
    dot_general x2, matrix products, product_left(): lax.dot_general(left, right, (((0,), (0,)), ((), ())), preferred_element_...  16.6 us
  transfers between devices with their start and end apart: 6, of which 2 were waited for; matrix products, arithmetic and copies ran while one was open for 15% of the time, Pallas kernels for 53%

profile of v7, /device:TPU:0, one launch (start us, length us, event | category | flops | bytes accessed | tf_op | source)
XLA Modules:
  0.0 751.3 jit_solution(10053999297988712831)
XLA Ops:
  14.8 113.0 %shard_map.288 = (bf16[2048,1536]{1,0:T(8,128)(2,1)}, bf16[4,128,2048]{2,1,0:T(8,128)(2,1)}, bf16[8,256,2048]{2,1,0:T(8,128)(2,1)}, f32[16,8,128]{2,1,0:T(8,128)S(1)}) custom-call(bf16[512,2048]{1,0:T(8,128)(2,1)} %bitcast.152, f32[8,128]{1,0:T(8,128)S(1)} %stack.79.small, bf16[128,1024]{1,0:T(8,128)(2,1)S(1)} %copy-done.7, bf16[128,1024]{1,0:T(8,128)(2,1)S(1)} %copy-done.8, ...), custom_call_target="tpu_custom_call" | custom-call | bytes 2000000 | tf_op jit(solution)/shard_map/pallas_call | solution.py:495
  127.8 1.9 slice.113
  130.3 19.2 %fusion.34 = f32[2048,1536]{1,0:T(8,128)} fusion(bf16[2048,2048]{1,0:T(8,128)(2,1)} %bitcast.200, bf16[2048,1536]{1,0:T(8,128)(2,1)} %get-tuple-element.65.refs_2_), kind=kOutput, calls=%fused_computation.140 | convolution fusion | flops 12884901888 | bytes 27262976 | tf_op jit(solution)/shard_map/dot_general | solution.py:55
  149.8 2.5 slice.177
  152.3 1.4 compare_select_fusion.2
  155.4 2.5 fusion.30
  158.0 1.5 subtract_convert_fusion.2
  159.9 2.8 fusion.16
  163.0 54.9 %shard_map.289 = (bf16[16,128,512]{2,1,0:T(8,128)(2,1)}, bf16[8,256,2048]{2,1,0:T(8,128)(2,1)}) custom-call(f32[16,128,512]{2,1,0:T(8,128)} %bitcast.157, f32[1,512]{1,0:T(1,128)S(1)} %broadcast_in_dim.37.fade, bf16[256,2048]{1,0:T(8,128)(2,1)S(1)} %fusion.13.own), custom_call_target="tpu_custom_call" | custom-call | bytes 2000000 | tf_op jit(solution)/shard_map/pallas_call | solution.py:495
  217.9 1.3 slice.116
  221.3 1.8 multiply_convert_fusion.4
  227.1 1.1 copy-done.9
  228.2 4.3 multiply_convert_fusion
  232.4 46.1 %shard_map.290 = f32[256,2048]{1,0:T(8,128)} custom-call(bf16[8,256,512]{2,1,0:T(8,128)(2,1)} %bitcast.132, bf16[2048,512]{1,0:T(8,128)(2,1)} %bitcast.134), custom_call_target="tpu_custom_call" | custom-call | bytes 2000000 | tf_op jit(solution)/shard_map/pallas_call | solution.py:495
  278.6 2.1 fusion.29
  282.0 39.1 %shard_map.291 = bf16[8,256,2048]{2,1,0:T(8,128)(2,1)} custom-call(bf16[256,2048]{1,0:T(8,128)(2,1)S(1)} %add_convert_fusion.4.refs_0_), custom_call_target="tpu_custom_call" | custom-call | bytes 2000000 | tf_op jit(solution)/shard_map/pallas_call | solution.py:495
  321.1 25.8 %all-gather.5.cloned.1.call-done = bf16[16,128,1536]{2,1,0:T(8,128)(2,1)} async-done(((bf16[4,128,1536]{2,1,0:T(8,128)(2,1)}), bf16[16,128,1536]{2,1,0:T(8,128)(2,1)}) %all-gather.5.cloned.1.call-update) | async-done | bytes 6291472 | tf_op jit(solution)/shard_map/all_gather | solution.py:1186
  346.9 36.7 %shard_map.292 = (bf16[2048,512]{1,0:T(8,128)(2,1)}, bf16[2048,1024]{1,0:T(8,128)(2,1)}, bf16[2048,1536]{1,0:T(8,128)(2,1)}) custom-call(bf16[2048,2048]{1,0:T(8,128)(2,1)} %bitcast.163, bf16[2048,2048]{1,0:T(8,128)(2,1)} %bitcast.207, bf16[2048,1536]{1,0:T(8,128)(2,1)} %bitcast.149), custom_call_target="tpu_custom_call" | custom-call | flops 30064771072 | bytes 40000000 | tf_op jit(solution)/shard_map/pallas_call | solution.py:645
  383.7 49.8 %shard_map.293 = f32[256,2048]{1,0:T(8,128)} custom-call(bf16[8,256,1024]{2,1,0:T(8,128)(2,1)} %bitcast.172, bf16[2048,1536]{1,0:T(8,128)(2,1)} %bitcast.150), custom_call_target="tpu_custom_call" | custom-call | bytes 2000000 | tf_op jit(solution)/shard_map/pallas_call | solution.py:495
  433.5 2.5 multiply_reduce_fusion.3
  438.0 1.2 copy-done
  439.9 41.9 %shard_map.294 = (bf16[2048,512]{1,0:T(8,128)(2,1)}, f32[8,256,512]{2,1,0:T(8,128)S(1)}) custom-call(bf16[256,2048]{1,0:T(8,128)(2,1)S(1)} %fusion.14.own, bf16[8,256,512]{2,1,0:T(8,128)(2,1)S(1)} %bitcast.133, bf16[2048,512]{1,0:T(8,128)(2,1)S(1)} %bitcast.135), custom_call_target="tpu_custom_call" | custom-call | bytes 2000000 | tf_op jit(solution)/shard_map/pallas_call | solution.py:495
  481.9 6.8 multiply_reduce_fusion.1
  488.7 3.2 fusion.27
  492.0 2.6 add_convert_fusion.1
  495.9 1.8 fusion.25
  498.4 3.0 fusion.15
  501.4 2.9 fusion.37
  504.3 2.2 multiply_add_fusion.1
  507.4 5.7 convolution_convert_fusion.1
  513.1 89.8 %shard_map.295 = (bf16[16,128,512]{2,1,0:T(8,128)(2,1)}, f32[256,2048]{1,0:T(8,128)}, bf16[128,2048]{1,0:T(8,128)(2,1)S(1)}, bf16[128,2048]{1,0:T(8,128)(2,1)S(1)}, bf16[2048,128]{1,0:T(8,128)(2,1)S(1)}) custom-call(f32[16,128,512]{2,1,0:T(8,128)} %bitcast.158, f32[1,512]{1,0:T(1,128)S(1)} %broadcast_in_dim.37.fade, bf16[8,256,512]{2,1,0:T(8,128)(2,1)} %bitcast.177, ...), custom_call_target="tpu_custom_call" | custom-call | bytes 2000000 | tf_op jit(solution)/shard_map/pallas_call | solution.py:495
  603.6 4.2 add_multiply_fusion
  609.4 1.4 copy-done.20
  611.8 2.0 copy-done.30
  613.9 10.8 %convolution_convert_fusion = bf16[2048,1024]{1,0:T(8,128)(2,1)} fusion(bf16[2048,2048]{1,0:T(8,128)(2,1)S(1)} %bitcast.206, bf16[2048,1024]{1,0:T(8,128)(2,1)S(1)} %constant_dynamic-update-slice_fusion), kind=kOutput, calls=%fused_computation.18 | convolution fusion | flops 8592031744 | bytes 16777216 | tf_op jit(solution)/shard_map/dot_general | solution.py:59
  625.9 1.1 convert_element_type.201
  626.9 1.1 convert_element_type.202
  629.1 50.0 %shard_map.296 = f32[256,2048]{1,0:T(8,128)} custom-call(bf16[8,256,1024]{2,1,0:T(8,128)(2,1)} %bitcast.168, bf16[8,256,512]{2,1,0:T(8,128)(2,1)} %bitcast.159, bf16[2048,1536]{1,0:T(8,128)(2,1)} %get-tuple-element.65.refs_2_), custom_call_target="tpu_custom_call" | custom-call | bytes 2000000 | tf_op jit(solution)/shard_map/pallas_call | solution.py:495
  679.4 1.3 copy-done.14
  680.7 1.9 fusion.11
  683.9 3.4 add_convert_fusion.2.two
  687.3 27.5 %shard_map.297 = (f32[8,128]{1,0:T(8,128)S(1)}, bf16[2048,128]{1,0:T(8,128)(2,1)S(1)}, bf16[128,2048]{1,0:T(8,128)(2,1)S(1)}, bf16[2,256,2048]{2,1,0:T(8,128)(2,1)S(1)}, bf16[2,256,2048]{2,1,0:T(8,128)(2,1)S(1)}) custom-call(f32[32,8,128]{2,1,0:T(8,128)S(1)} %bitcast.139, bf16[4,128,512]{2,1,0:T(8,128)(2,1)S(1)} %bitcast.137, ...), custom_call_target="tpu_custom_call" | custom-call | bytes 2000000 | tf_op jit(solution)/shard_map/pallas_call | solution.py:495
  715.8 1.1 convert_element_type.197
  716.9 2.3 broadcast_multiply_fusion
  719.3 4.4 reduce-scatter.11.cloned.1.call-done
  725.5 1.2 copy-done.2
  726.7 14.7 %shard_map.298 = (bf16[128,1024]{1,0:T(8,128)(2,1)S(1)}, bf16[128,1024]{1,0:T(8,128)(2,1)S(1)}, bf16[128,2048]{1,0:T(8,128)(2,1)S(1)}) custom-call(bf16[4,128,1024]{2,1,0:T(8,128)(2,1)S(1)} %bitcast.136), custom_call_target="tpu_custom_call" | custom-call | bytes 2000000 | tf_op jit(solution)/shard_map/pallas_call | solution.py:495
  743.2 1.1 convert_element_type.200
  (196 shorter events, 35.0 us)
Async XLA Ops:
  7.2 225.3 %all-gather.3.cloned.1.call-start = ((), (), s32[]{:S(2)}) async-start(), calls=%async_computation.4 | async-start | bytes 2621440 | tf_op jit(solution)/shard_map/all_gather | solution.py:1186
  14.8 115.0 %copy-start.45 = (s32[2]{0:T(128)S(1)}, s32[2]{0:T(128)}, u32[]{:S(2)}) copy-start(s32[2]{0:T(128)} %param.18) | copy-start | bytes 28
  129.7 217.2 %all-gather.5.cloned.1.call-start = ((), (), s32[]{:S(2)}) async-start(), calls=%async_computation.5 | async-start | bytes 7864320 | tf_op jit(solution)/shard_map/all_gather | solution.py:1186
  152.3 342.4 %copy-start.15 = (bf16[2048,512]{1,0:T(8,128)(2,1)}, bf16[2048,512]{1,0:T(8,128)(2,1)S(1)}, u32[]{:S(2)}) copy-start(bf16[2048,512]{1,0:T(8,128)(2,1)S(1)} %slice.177) | copy-start | bytes 6291460
  154.2 5.6 copy-start.41
  154.8 7.9 %copy-start.39 = (f32[256]{0:T(256)}, f32[256]{0:T(256)S(1)}, u32[]{:S(2)}) copy-start(f32[256]{0:T(256)S(1)} %compare_convert_fusion.1) | copy-start | bytes 3076
  159.9 2.8 copy-start.31
  163.0 55.0 %copy-start.35 = (bf16[4,128,2048]{2,1,0:T(8,128)(2,1)S(1)}, bf16[4,128,2048]{2,1,0:T(8,128)(2,1)}, u32[]{:S(2)}) copy-start(bf16[4,128,2048]{2,1,0:T(8,128)(2,1)} %get-tuple-element.71) | copy-start | bytes 6291460
  219.2 293.9 %reduce-scatter.7.cloned.1.call-start = ((), (), s32[]{:S(2)}) async-start(), calls=%async_computation.7 | async-start | bytes 7864320 | tf_op jit(solution)/shard_map/reduce_scatter | solution.py:1257
  221.3 2.6 copy-start.37
  223.1 2.0 copy-start.24
  223.1 2.0 copy-start.26
  223.2 2.2 copy-start.28
  223.2 2.2 copy-start.43
  226.2 2.0 copy-start.9
  232.4 46.1 %copy-start.17 = (bf16[2,256,2048]{2,1,0:T(8,128)(2,1)S(1)}, bf16[2,256,2048]{2,1,0:T(8,128)(2,1)}, u32[]{:S(2)}) copy-start(bf16[2,256,2048]{2,1,0:T(8,128)(2,1)} %param.17) | copy-start | bytes 6291460
  280.7 1.3 copy-start.11
  383.6 219.3 %reduce-scatter.5.cloned.1.call-start = ((), (), s32[]{:S(2)}) async-start(), calls=%async_computation.6 | async-start | bytes 2621440 | tf_op jit(solution)/shard_map/reduce_scatter | solution.py:1257
  383.6 49.8 %copy-start.12 = (f32[256,2048]{1,0:T(8,128)S(1)}, f32[256,2048]{1,0:T(8,128)}, u32[]{:S(2)}) copy-start(f32[256,2048]{1,0:T(8,128)} %copy-done.11) | copy-start | bytes 6291460
  433.5 2.5 copy-start.19
  436.0 1.6 copy-start.32
  436.0 1.6 copy-start.40
  436.7 52.0 %copy-start.16 = (f32[256,2048]{1,0:T(8,128)}, f32[256,2048]{1,0:T(8,128)S(1)}, u32[]{:S(2)}) copy-start(f32[256,2048]{1,0:T(8,128)S(1)} %get-tuple-element.125) | copy-start | bytes 6291460
  437.6 1.6 copy-start
  437.6 2.3 copy-start.1
  439.9 42.0 %copy-start.10 = (f32[8,256,512]{2,1,0:T(8,128)S(1)}, f32[8,256,512]{2,1,0:T(8,128)}, u32[]{:S(2)}) copy-start(f32[8,256,512]{2,1,0:T(8,128)} %copy-done.9) | copy-start | bytes 12582916
  491.9 187.5 %reduce-scatter.9.cloned.1.call-start = ((), (), s32[]{:S(2)}) async-start(), calls=%async_computation.8 | async-start | bytes 2621440 | tf_op jit(solution)/shard_map/reduce_scatter | solution.py:1257
  492.0 2.7 copy-start.38
  494.7 1.2 copy-start.29
  498.4 3.0 copy-start.34
  498.4 8.1 %slice-start = ((s8[8388608]{0:T(1024)(128)(4,1)}), s8[4194304]{0:T(1024)(128)(4,1)S(1)}, s32[]{:S(2)}) async-start(s8[8388608]{0:T(1024)(128)(4,1)} %bitcast.201), calls=%async_computation.10 | async-start | bytes 8388608
  501.4 2.9 copy-start.25
  501.4 5.1 slice-start.1
  504.3 3.0 copy-start.21
  602.9 120.7 %reduce-scatter.11.cloned.1.call-start = ((), (), s32[]{:S(2)}) async-start(), calls=%async_computation.9 | async-start | bytes 5242880 | tf_op jit(solution)/shard_map/reduce_scatter | solution.py:1257
  603.6 4.2 copy-start.23
  603.6 10.3 %slice-start.2 = ((s8[8388608]{0:T(1024)(128)(4,1)}), s8[4194304]{0:T(1024)(128)(4,1)S(1)}, s32[]{:S(2)}) async-start(s8[8388608]{0:T(1024)(128)(4,1)} %bitcast.204), calls=%async_computation.12 | async-start | bytes 8388608
  607.8 1.6 copy-start.22
  608.3 2.4 copy-start.20
  608.5 5.4 slice-start.3
  611.8 2.0 copy-start.30
  629.1 50.0 %copy-start.13 = (f32[256,2048]{1,0:T(8,128)S(1)}, f32[256,2048]{1,0:T(8,128)}, u32[]{:S(2)}) copy-start(f32[256,2048]{1,0:T(8,128)} %copy-done.11) | copy-start | bytes 6291460
  629.1 50.0 %copy-start.36 = (f32[256,2048]{1,0:T(8,128)S(1)}, f32[256,2048]{1,0:T(8,128)}, u32[]{:S(2)}) copy-start(f32[256,2048]{1,0:T(8,128)} %get-tuple-element.87) | copy-start | bytes 6291460
  679.0 1.7 copy-start.14
  679.4 3.2 copy-start.18
  683.9 3.4 copy-start.5
  683.9 3.4 copy-start.6
  725.5 1.2 copy-start.2
  (10 other events, 8.7 us)
Sparse Core Ops, SparseCore 0:
  129.8 45.4 all-gather.2
  219.3 127.5 all-gather.4
  383.7 108.9 reduce-scatter.6
  494.9 60.3 reduce-scatter.4
  603.1 40.1 reduce-scatter.8
  645.4 78.1 reduce-scatter.10

commit v8 on v7

--- a/solution.py
+++ b/solution.py
@@ -444,8 +444,8 @@
     begin, relay, rest, diagonal, end = gather_with(own, full, *scratch)
     run, done = pass_steps(by, local, fade, out, held, send, recv)
     greet_plane(by)
+    run(-1)
     begin()
-    run(-1)
     run(0)
     relay()
     run(1)
@@ -468,10 +468,10 @@
     run(-1)
     diagonal()
     straight()
+    hand_over()
     run(0)
+    relay()
     run(1)
-    relay()
-    hand_over()
     run(2)
     run(3)
     end()
@@ -575,7 +575,7 @@
 
 def pass_and_gather(local, fade, own, by, collective_id):
     shape = local.shape
-    local = local.reshape(2 * shape[0], -1, shape[2])
+    local = local.reshape(4 * shape[0], -1, shape[2])
     own = ready(own)
     out, full = call(
         functools.partial(pass_gather_kernel, by),
@@ -662,7 +662,7 @@
 
 def pass_and_scatter(local, fade, left, right, start, ff, by, collective_id):
     shape = local.shape
-    local = local.reshape(2 * shape[0], -1, shape[2])
+    local = local.reshape(4 * shape[0], -1, shape[2])
     out, own, *grads = call(
         functools.partial(pass_scatter_kernel, by, start),
         collective_id,

time: 759 us -> 750 us (0.988)
  Pallas kernels: 563 us -> 554 us
    pallas_call x10, Pallas kernels: 527 us -> 517 us  [call(): pl.pallas_call(kernel, out_shape=shapes, in_specs=ins, out_specs=tuple((p...]
  transfers between devices with their start and end apart: 6 -> 6, of which waited for: 2 -> 2; matrix products, arithmetic and copies ran while one was open for 15% -> 15% of each run, Pallas kernels for 53% -> 52%
where the time goes in v8:
time: 750 us; the launch traced here: 743 us
  Pallas kernels  554 us (74%)
  matrix products  57.6 us (8%)
  other arithmetic  49.3 us (7%)
  local copies, waits for them, and re-layouts  34 us (5%)
  waiting for transfers between devices  32.1 us (4%)
  between operations  15.3 us (2%)
    pallas_call x10, Pallas kernels, call(): pl.pallas_call(kernel, out_shape=shapes, in_specs=ins, out_specs=tuple((p...  517 us
    pallas_call x1, Pallas kernels, feed_forward(): pl.pallas_call(feed_forward_kernel, grid=(count // block,), out_shape=(ja...  36.7 us
    all_gather x2, waiting for transfers between devices, all_depths(): return lax.all_gather(mine, 'ctx', axis=0, tiled=True).reshape(width, -1)  24.3 us
    dot_general x12, matrix products, blocks(): return jnp.einsum(spec, left, right, preferred_element_type=f32)  21.8 us
    unnamed x112, local copies, waits for them, and re-layouts  19.3 us
    dot_general x1, matrix products, product(): return jnp.dot(left, right, preferred_element_type=f32)  19.2 us
    dot_general x2, matrix products, product_left(): lax.dot_general(left, right, (((0,), (0,)), ((), ())), preferred_element_...  16.5 us
  transfers between devices with their start and end apart: 6, of which 2 were waited for; matrix products, arithmetic and copies ran while one was open for 15% of the time, Pallas kernels for 52%

profile of v8, /device:TPU:0, one launch (start us, length us, event | category | flops | bytes accessed | tf_op | source)
XLA Modules:
  0.0 742.8 jit_solution(14231539001812012160)
XLA Ops:
  14.8 113.0 %shard_map.288 = (bf16[2048,1536]{1,0:T(8,128)(2,1)}, bf16[4,128,2048]{2,1,0:T(8,128)(2,1)}, bf16[8,256,2048]{2,1,0:T(8,128)(2,1)}, f32[16,8,128]{2,1,0:T(8,128)S(1)}) custom-call(bf16[512,2048]{1,0:T(8,128)(2,1)} %bitcast.152, f32[8,128]{1,0:T(8,128)S(1)} %stack.79.small, bf16[128,1024]{1,0:T(8,128)(2,1)S(1)} %copy-done.7, bf16[128,1024]{1,0:T(8,128)(2,1)S(1)} %copy-done.8, ...), custom_call_target="tpu_custom_call" | custom-call | bytes 2000000 | tf_op jit(solution)/shard_map/pallas_call | solution.py:495
  127.8 1.9 slice.113
  130.3 19.2 %fusion.34 = f32[2048,1536]{1,0:T(8,128)} fusion(bf16[2048,2048]{1,0:T(8,128)(2,1)} %bitcast.200, bf16[2048,1536]{1,0:T(8,128)(2,1)} %get-tuple-element.65.refs_2_), kind=kOutput, calls=%fused_computation.140 | convolution fusion | flops 12884901888 | bytes 27262976 | tf_op jit(solution)/shard_map/dot_general | solution.py:55
  149.8 2.5 slice.177
  152.3 1.4 compare_select_fusion.2
  155.4 2.5 fusion.30
  158.0 1.5 subtract_convert_fusion.2
  159.9 2.8 fusion.16
  163.0 55.2 %shard_map.289 = (bf16[32,64,512]{2,1,0:T(8,128)(2,1)}, bf16[8,256,2048]{2,1,0:T(8,128)(2,1)}) custom-call(f32[32,64,512]{2,1,0:T(8,128)} %bitcast.157, f32[1,512]{1,0:T(1,128)S(1)} %broadcast_in_dim.37.fade, bf16[256,2048]{1,0:T(8,128)(2,1)S(1)} %fusion.13.own), custom_call_target="tpu_custom_call" | custom-call | bytes 2000000 | tf_op jit(solution)/shard_map/pallas_call | solution.py:495
  218.2 1.3 slice.116
  221.6 1.8 multiply_convert_fusion.4
  227.3 1.1 copy-done.9
  228.4 4.3 multiply_convert_fusion
  232.7 46.1 %shard_map.290 = f32[256,2048]{1,0:T(8,128)} custom-call(bf16[8,256,512]{2,1,0:T(8,128)(2,1)} %bitcast.132, bf16[2048,512]{1,0:T(8,128)(2,1)} %bitcast.134), custom_call_target="tpu_custom_call" | custom-call | bytes 2000000 | tf_op jit(solution)/shard_map/pallas_call | solution.py:495
  278.8 2.1 fusion.29
  282.3 39.1 %shard_map.291 = bf16[8,256,2048]{2,1,0:T(8,128)(2,1)} custom-call(bf16[256,2048]{1,0:T(8,128)(2,1)S(1)} %add_convert_fusion.4.refs_0_), custom_call_target="tpu_custom_call" | custom-call | bytes 2000000 | tf_op jit(solution)/shard_map/pallas_call | solution.py:495
  321.4 24.3 %all-gather.5.cloned.1.call-done = bf16[16,128,1536]{2,1,0:T(8,128)(2,1)} async-done(((bf16[4,128,1536]{2,1,0:T(8,128)(2,1)}), bf16[16,128,1536]{2,1,0:T(8,128)(2,1)}) %all-gather.5.cloned.1.call-update) | async-done | bytes 6291472 | tf_op jit(solution)/shard_map/all_gather | solution.py:1186
  345.6 36.7 %shard_map.292 = (bf16[2048,512]{1,0:T(8,128)(2,1)}, bf16[2048,1024]{1,0:T(8,128)(2,1)}, bf16[2048,1536]{1,0:T(8,128)(2,1)}) custom-call(bf16[2048,2048]{1,0:T(8,128)(2,1)} %bitcast.163, bf16[2048,2048]{1,0:T(8,128)(2,1)} %bitcast.207, bf16[2048,1536]{1,0:T(8,128)(2,1)} %bitcast.149), custom_call_target="tpu_custom_call" | custom-call | flops 30064771072 | bytes 40000000 | tf_op jit(solution)/shard_map/pallas_call | solution.py:645
  382.4 49.8 %shard_map.293 = f32[256,2048]{1,0:T(8,128)} custom-call(bf16[8,256,1024]{2,1,0:T(8,128)(2,1)} %bitcast.172, bf16[2048,1536]{1,0:T(8,128)(2,1)} %bitcast.150), custom_call_target="tpu_custom_call" | custom-call | bytes 2000000 | tf_op jit(solution)/shard_map/pallas_call | solution.py:495
  432.2 2.5 multiply_reduce_fusion.3
  436.7 1.2 copy-done
  438.6 41.9 %shard_map.294 = (bf16[2048,512]{1,0:T(8,128)(2,1)}, f32[8,256,512]{2,1,0:T(8,128)S(1)}) custom-call(bf16[256,2048]{1,0:T(8,128)(2,1)S(1)} %fusion.14.own, bf16[8,256,512]{2,1,0:T(8,128)(2,1)S(1)} %bitcast.133, bf16[2048,512]{1,0:T(8,128)(2,1)S(1)} %bitcast.135), custom_call_target="tpu_custom_call" | custom-call | bytes 2000000 | tf_op jit(solution)/shard_map/pallas_call | solution.py:495
  480.6 6.8 multiply_reduce_fusion.1
  487.4 3.2 fusion.27
  490.7 2.6 add_convert_fusion.1
  494.6 1.9 fusion.25
  497.1 3.0 fusion.15
  500.2 2.9 fusion.37
  503.1 2.2 multiply_add_fusion.1
  506.1 5.7 convolution_convert_fusion.1
  511.8 80.8 %shard_map.295 = (bf16[32,64,512]{2,1,0:T(8,128)(2,1)}, f32[256,2048]{1,0:T(8,128)}, bf16[128,2048]{1,0:T(8,128)(2,1)S(1)}, bf16[128,2048]{1,0:T(8,128)(2,1)S(1)}, bf16[2048,128]{1,0:T(8,128)(2,1)S(1)}) custom-call(f32[32,64,512]{2,1,0:T(8,128)} %bitcast.158, f32[1,512]{1,0:T(1,128)S(1)} %broadcast_in_dim.37.fade, bf16[8,256,512]{2,1,0:T(8,128)(2,1)} %bitcast.177, ...), custom_call_target="tpu_custom_call" | custom-call | bytes 2000000 | tf_op jit(solution)/shard_map/pallas_call | solution.py:495
  593.3 3.8 add_multiply_fusion
  599.0 1.3 copy-done.20
  601.4 2.0 copy-done.30
  603.4 10.8 %convolution_convert_fusion = bf16[2048,1024]{1,0:T(8,128)(2,1)} fusion(bf16[2048,2048]{1,0:T(8,128)(2,1)S(1)} %bitcast.206, bf16[2048,1024]{1,0:T(8,128)(2,1)S(1)} %constant_dynamic-update-slice_fusion), kind=kOutput, calls=%fused_computation.18 | convolution fusion | flops 8592031744 | bytes 16777216 | tf_op jit(solution)/shard_map/dot_general | solution.py:59
  615.5 1.1 convert_element_type.201
  616.5 1.1 convert_element_type.202
  618.6 51.3 %shard_map.296 = f32[256,2048]{1,0:T(8,128)} custom-call(bf16[8,256,1024]{2,1,0:T(8,128)(2,1)} %bitcast.168, bf16[8,256,512]{2,1,0:T(8,128)(2,1)} %bitcast.159, bf16[2048,1536]{1,0:T(8,128)(2,1)} %get-tuple-element.65.refs_2_), custom_call_target="tpu_custom_call" | custom-call | bytes 2000000 | tf_op jit(solution)/shard_map/pallas_call | solution.py:495
  670.4 1.2 copy-done.14
  671.6 1.9 fusion.11
  674.8 3.3 add_convert_fusion.2.two
  678.1 25.0 %shard_map.297 = (f32[8,128]{1,0:T(8,128)S(1)}, bf16[2048,128]{1,0:T(8,128)(2,1)S(1)}, bf16[128,2048]{1,0:T(8,128)(2,1)S(1)}, bf16[2,256,2048]{2,1,0:T(8,128)(2,1)S(1)}, bf16[2,256,2048]{2,1,0:T(8,128)(2,1)S(1)}) custom-call(f32[32,8,128]{2,1,0:T(8,128)S(1)} %bitcast.139, bf16[4,128,512]{2,1,0:T(8,128)(2,1)S(1)} %bitcast.137, ...), custom_call_target="tpu_custom_call" | custom-call | bytes 2000000 | tf_op jit(solution)/shard_map/pallas_call | solution.py:495
  704.1 1.1 convert_element_type.197
  705.2 2.3 broadcast_multiply_fusion
  707.6 7.7 %reduce-scatter.11.cloned.1.call-done = bf16[512,1024]{1,0:T(8,128)(2,1)} async-done(((bf16[2048,1024]{1,0:T(8,128)(2,1)}), bf16[512,1024]{1,0:T(8,128)(2,1)}) %reduce-scatter.11.cloned.1.call-update) | async-done | bytes 1048592 | tf_op jit(solution)/shard_map/reduce_scatter | solution.py:1257
  717.1 1.2 copy-done.2
  718.3 14.7 %shard_map.298 = (bf16[128,1024]{1,0:T(8,128)(2,1)S(1)}, bf16[128,1024]{1,0:T(8,128)(2,1)S(1)}, bf16[128,2048]{1,0:T(8,128)(2,1)S(1)}) custom-call(bf16[4,128,1024]{2,1,0:T(8,128)(2,1)S(1)} %bitcast.136), custom_call_target="tpu_custom_call" | custom-call | bytes 2000000 | tf_op jit(solution)/shard_map/pallas_call | solution.py:495
  734.7 1.1 convert_element_type.200
  (196 shorter events, 35.3 us)
Async XLA Ops:
  7.2 225.5 %all-gather.3.cloned.1.call-start = ((), (), s32[]{:S(2)}) async-start(), calls=%async_computation.4 | async-start | bytes 2621440 | tf_op jit(solution)/shard_map/all_gather | solution.py:1186
  14.8 115.0 %copy-start.45 = (s32[2]{0:T(128)S(1)}, s32[2]{0:T(128)}, u32[]{:S(2)}) copy-start(s32[2]{0:T(128)} %param.18) | copy-start | bytes 28
  129.7 216.0 %all-gather.5.cloned.1.call-start = ((), (), s32[]{:S(2)}) async-start(), calls=%async_computation.5 | async-start | bytes 7864320 | tf_op jit(solution)/shard_map/all_gather | solution.py:1186
  152.3 341.1 %copy-start.15 = (bf16[2048,512]{1,0:T(8,128)(2,1)}, bf16[2048,512]{1,0:T(8,128)(2,1)S(1)}, u32[]{:S(2)}) copy-start(bf16[2048,512]{1,0:T(8,128)(2,1)S(1)} %slice.177) | copy-start | bytes 6291460
  154.2 5.6 copy-start.41
  154.8 7.9 %copy-start.39 = (f32[256]{0:T(256)}, f32[256]{0:T(256)S(1)}, u32[]{:S(2)}) copy-start(f32[256]{0:T(256)S(1)} %compare_convert_fusion.1) | copy-start | bytes 3076
  159.9 2.8 copy-start.31
  163.0 55.2 %copy-start.35 = (bf16[4,128,2048]{2,1,0:T(8,128)(2,1)S(1)}, bf16[4,128,2048]{2,1,0:T(8,128)(2,1)}, u32[]{:S(2)}) copy-start(bf16[4,128,2048]{2,1,0:T(8,128)(2,1)} %get-tuple-element.71) | copy-start | bytes 6291460
  219.4 292.3 %reduce-scatter.7.cloned.1.call-start = ((), (), s32[]{:S(2)}) async-start(), calls=%async_computation.7 | async-start | bytes 7864320 | tf_op jit(solution)/shard_map/reduce_scatter | solution.py:1257
  221.6 2.6 copy-start.37
  223.4 2.0 copy-start.24
  223.4 2.0 copy-start.26
  223.4 2.2 copy-start.28
  223.4 2.2 copy-start.43
  226.4 2.0 copy-start.9
  232.7 46.1 %copy-start.17 = (bf16[2,256,2048]{2,1,0:T(8,128)(2,1)S(1)}, bf16[2,256,2048]{2,1,0:T(8,128)(2,1)}, u32[]{:S(2)}) copy-start(bf16[2,256,2048]{2,1,0:T(8,128)(2,1)} %param.17) | copy-start | bytes 6291460
  281.0 1.3 copy-start.11
  382.3 210.3 %reduce-scatter.5.cloned.1.call-start = ((), (), s32[]{:S(2)}) async-start(), calls=%async_computation.6 | async-start | bytes 2621440 | tf_op jit(solution)/shard_map/reduce_scatter | solution.py:1257
  382.4 49.8 %copy-start.12 = (f32[256,2048]{1,0:T(8,128)S(1)}, f32[256,2048]{1,0:T(8,128)}, u32[]{:S(2)}) copy-start(f32[256,2048]{1,0:T(8,128)} %copy-done.11) | copy-start | bytes 6291460
  432.2 2.5 copy-start.19
  434.8 1.6 copy-start.32
  434.8 1.6 copy-start.40
  435.4 52.0 %copy-start.16 = (f32[256,2048]{1,0:T(8,128)}, f32[256,2048]{1,0:T(8,128)S(1)}, u32[]{:S(2)}) copy-start(f32[256,2048]{1,0:T(8,128)S(1)} %get-tuple-element.125) | copy-start | bytes 6291460
  436.4 1.6 copy-start
  436.4 2.3 copy-start.1
  438.6 42.0 %copy-start.10 = (f32[8,256,512]{2,1,0:T(8,128)S(1)}, f32[8,256,512]{2,1,0:T(8,128)}, u32[]{:S(2)}) copy-start(f32[8,256,512]{2,1,0:T(8,128)} %copy-done.9) | copy-start | bytes 12582916
  490.7 179.7 %reduce-scatter.9.cloned.1.call-start = ((), (), s32[]{:S(2)}) async-start(), calls=%async_computation.8 | async-start | bytes 2621440 | tf_op jit(solution)/shard_map/reduce_scatter | solution.py:1257
  490.7 2.7 copy-start.38
  493.4 1.2 copy-start.29
  497.1 3.0 copy-start.34
  497.1 8.1 %slice-start = ((s8[8388608]{0:T(1024)(128)(4,1)}), s8[4194304]{0:T(1024)(128)(4,1)S(1)}, s32[]{:S(2)}) async-start(s8[8388608]{0:T(1024)(128)(4,1)} %bitcast.201), calls=%async_computation.10 | async-start | bytes 8388608
  500.2 2.9 copy-start.25
  500.2 5.1 slice-start.1
  503.1 3.0 copy-start.21
  592.7 122.6 %reduce-scatter.11.cloned.1.call-start = ((), (), s32[]{:S(2)}) async-start(), calls=%async_computation.9 | async-start | bytes 5242880 | tf_op jit(solution)/shard_map/reduce_scatter | solution.py:1257
  593.3 3.8 copy-start.23
  593.3 10.1 %slice-start.2 = ((s8[8388608]{0:T(1024)(128)(4,1)}), s8[4194304]{0:T(1024)(128)(4,1)S(1)}, s32[]{:S(2)}) async-start(s8[8388608]{0:T(1024)(128)(4,1)} %bitcast.204), calls=%async_computation.12 | async-start | bytes 8388608
  597.1 1.9 copy-start.22
  597.7 2.6 copy-start.20
  597.8 5.6 slice-start.3
  601.4 2.0 copy-start.30
  618.6 51.3 %copy-start.13 = (f32[256,2048]{1,0:T(8,128)S(1)}, f32[256,2048]{1,0:T(8,128)}, u32[]{:S(2)}) copy-start(f32[256,2048]{1,0:T(8,128)} %copy-done.11) | copy-start | bytes 6291460
  618.6 51.3 %copy-start.36 = (f32[256,2048]{1,0:T(8,128)S(1)}, f32[256,2048]{1,0:T(8,128)}, u32[]{:S(2)}) copy-start(f32[256,2048]{1,0:T(8,128)} %get-tuple-element.87) | copy-start | bytes 6291460
  670.0 1.6 copy-start.14
  670.3 3.1 copy-start.18
  674.8 3.3 copy-start.5
  674.8 3.3 copy-start.6
  717.1 1.2 copy-start.2
  (10 other events, 8.7 us)
Sparse Core Ops, SparseCore 0:
  129.8 45.6 all-gather.2
  219.6 126.0 all-gather.4
  382.5 108.9 reduce-scatter.6
  493.6 60.3 reduce-scatter.4
  592.8 42.0 reduce-scatter.8
  637.0 78.1 reduce-scatter.10

commit v9 on v8

--- a/solution.py
+++ b/solution.py
@@ -662,7 +662,7 @@
 
 def pass_and_scatter(local, fade, left, right, start, ff, by, collective_id):
     shape = local.shape
-    local = local.reshape(4 * shape[0], -1, shape[2])
+    local = local.reshape(8 * shape[0], -1, shape[2])
     out, own, *grads = call(
         functools.partial(pass_scatter_kernel, by, start),
         collective_id,

time: 750 us -> 750 us (level)
  no operation moved by 1% of the time
where the time goes in v9:
time: 750 us; the launch traced here: 743 us
  Pallas kernels  553 us (74%)
  matrix products  57.6 us (8%)
  other arithmetic  49.4 us (7%)
  local copies, waits for them, and re-layouts  34 us (5%)
  waiting for transfers between devices  32.3 us (4%)
  between operations  15.3 us (2%)
    pallas_call x10, Pallas kernels, call(): pl.pallas_call(kernel, out_shape=shapes, in_specs=ins, out_specs=tuple((p...  517 us
    pallas_call x1, Pallas kernels, feed_forward(): pl.pallas_call(feed_forward_kernel, grid=(count // block,), out_shape=(ja...  36.7 us
    all_gather x2, waiting for transfers between devices, all_depths(): return lax.all_gather(mine, 'ctx', axis=0, tiled=True).reshape(width, -1)  24.3 us
    dot_general x12, matrix products, blocks(): return jnp.einsum(spec, left, right, preferred_element_type=f32)  21.8 us
    unnamed x112, local copies, waits for them, and re-layouts  19.3 us
    dot_general x1, matrix products, product(): return jnp.dot(left, right, preferred_element_type=f32)  19.2 us
    dot_general x2, matrix products, product_left(): lax.dot_general(left, right, (((0,), (0,)), ((), ())), preferred_element_...  16.5 us
  transfers between devices with their start and end apart: 6, of which 2 were waited for; matrix products, arithmetic and copies ran while one was open for 15% of the time, Pallas kernels for 52%

profile of v9, /device:TPU:0, one launch (start us, length us, event | category | flops | bytes accessed | tf_op | source)
XLA Modules:
  0.0 742.6 jit_solution(8275883611507496293)
XLA Ops:
  14.8 113.0 %shard_map.288 = (bf16[2048,1536]{1,0:T(8,128)(2,1)}, bf16[4,128,2048]{2,1,0:T(8,128)(2,1)}, bf16[8,256,2048]{2,1,0:T(8,128)(2,1)}, f32[16,8,128]{2,1,0:T(8,128)S(1)}) custom-call(bf16[512,2048]{1,0:T(8,128)(2,1)} %bitcast.152, f32[8,128]{1,0:T(8,128)S(1)} %stack.79.small, bf16[128,1024]{1,0:T(8,128)(2,1)S(1)} %copy-done.7, bf16[128,1024]{1,0:T(8,128)(2,1)S(1)} %copy-done.8, ...), custom_call_target="tpu_custom_call" | custom-call | bytes 2000000 | tf_op jit(solution)/shard_map/pallas_call | solution.py:495
  127.8 1.9 slice.113
  130.3 19.2 %fusion.34 = f32[2048,1536]{1,0:T(8,128)} fusion(bf16[2048,2048]{1,0:T(8,128)(2,1)} %bitcast.200, bf16[2048,1536]{1,0:T(8,128)(2,1)} %get-tuple-element.65.refs_2_), kind=kOutput, calls=%fused_computation.140 | convolution fusion | flops 12884901888 | bytes 27262976 | tf_op jit(solution)/shard_map/dot_general | solution.py:55
  149.8 2.5 slice.177
  152.3 1.4 compare_select_fusion.2
  155.4 2.5 fusion.30
  158.0 1.5 subtract_convert_fusion.2
  159.9 2.8 fusion.16
  163.0 55.2 %shard_map.289 = (bf16[32,64,512]{2,1,0:T(8,128)(2,1)}, bf16[8,256,2048]{2,1,0:T(8,128)(2,1)}) custom-call(f32[32,64,512]{2,1,0:T(8,128)} %bitcast.157, f32[1,512]{1,0:T(1,128)S(1)} %broadcast_in_dim.37.fade, bf16[256,2048]{1,0:T(8,128)(2,1)S(1)} %fusion.13.own), custom_call_target="tpu_custom_call" | custom-call | bytes 2000000 | tf_op jit(solution)/shard_map/pallas_call | solution.py:495
  218.2 1.3 slice.116
  221.6 1.8 multiply_convert_fusion.4
  227.3 1.1 copy-done.9
  228.4 4.3 multiply_convert_fusion
  232.7 46.1 %shard_map.290 = f32[256,2048]{1,0:T(8,128)} custom-call(bf16[8,256,512]{2,1,0:T(8,128)(2,1)} %bitcast.132, bf16[2048,512]{1,0:T(8,128)(2,1)} %bitcast.134), custom_call_target="tpu_custom_call" | custom-call | bytes 2000000 | tf_op jit(solution)/shard_map/pallas_call | solution.py:495
  278.8 2.1 fusion.29
  282.3 39.1 %shard_map.291 = bf16[8,256,2048]{2,1,0:T(8,128)(2,1)} custom-call(bf16[256,2048]{1,0:T(8,128)(2,1)S(1)} %add_convert_fusion.4.refs_0_), custom_call_target="tpu_custom_call" | custom-call | bytes 2000000 | tf_op jit(solution)/shard_map/pallas_call | solution.py:495
  321.4 24.3 %all-gather.5.cloned.1.call-done = bf16[16,128,1536]{2,1,0:T(8,128)(2,1)} async-done(((bf16[4,128,1536]{2,1,0:T(8,128)(2,1)}), bf16[16,128,1536]{2,1,0:T(8,128)(2,1)}) %all-gather.5.cloned.1.call-update) | async-done | bytes 6291472 | tf_op jit(solution)/shard_map/all_gather | solution.py:1186
  345.6 36.7 %shard_map.292 = (bf16[2048,512]{1,0:T(8,128)(2,1)}, bf16[2048,1024]{1,0:T(8,128)(2,1)}, bf16[2048,1536]{1,0:T(8,128)(2,1)}) custom-call(bf16[2048,2048]{1,0:T(8,128)(2,1)} %bitcast.163, bf16[2048,2048]{1,0:T(8,128)(2,1)} %bitcast.207, bf16[2048,1536]{1,0:T(8,128)(2,1)} %bitcast.149), custom_call_target="tpu_custom_call" | custom-call | flops 30064771072 | bytes 40000000 | tf_op jit(solution)/shard_map/pallas_call | solution.py:645
  382.4 49.8 %shard_map.293 = f32[256,2048]{1,0:T(8,128)} custom-call(bf16[8,256,1024]{2,1,0:T(8,128)(2,1)} %bitcast.172, bf16[2048,1536]{1,0:T(8,128)(2,1)} %bitcast.150), custom_call_target="tpu_custom_call" | custom-call | bytes 2000000 | tf_op jit(solution)/shard_map/pallas_call | solution.py:495
  432.2 2.5 multiply_reduce_fusion.3
  436.7 1.2 copy-done
  438.6 41.9 %shard_map.294 = (bf16[2048,512]{1,0:T(8,128)(2,1)}, f32[8,256,512]{2,1,0:T(8,128)S(1)}) custom-call(bf16[256,2048]{1,0:T(8,128)(2,1)S(1)} %fusion.14.own, bf16[8,256,512]{2,1,0:T(8,128)(2,1)S(1)} %bitcast.133, bf16[2048,512]{1,0:T(8,128)(2,1)S(1)} %bitcast.135), custom_call_target="tpu_custom_call" | custom-call | bytes 2000000 | tf_op jit(solution)/shard_map/pallas_call | solution.py:495
  480.6 6.8 multiply_reduce_fusion.1
  487.4 3.2 fusion.27
  490.7 2.6 add_convert_fusion.1
  494.6 1.9 fusion.25
  497.1 3.0 fusion.15
  500.2 2.9 fusion.37
  503.1 2.2 multiply_add_fusion.1
  506.1 5.7 convolution_convert_fusion.1
  511.8 80.6 %shard_map.295 = (bf16[64,32,512]{2,1,0:T(8,128)(2,1)}, f32[256,2048]{1,0:T(8,128)}, bf16[128,2048]{1,0:T(8,128)(2,1)S(1)}, bf16[128,2048]{1,0:T(8,128)(2,1)S(1)}, bf16[2048,128]{1,0:T(8,128)(2,1)S(1)}) custom-call(f32[64,32,512]{2,1,0:T(8,128)} %bitcast.158, f32[1,512]{1,0:T(1,128)S(1)} %broadcast_in_dim.37.fade, bf16[8,256,512]{2,1,0:T(8,128)(2,1)} %bitcast.177, ...), custom_call_target="tpu_custom_call" | custom-call | bytes 2000000 | tf_op jit(solution)/shard_map/pallas_call | solution.py:495
  593.1 3.8 add_multiply_fusion
  598.8 1.3 copy-done.20
  601.2 2.0 copy-done.30
  603.2 10.8 %convolution_convert_fusion = bf16[2048,1024]{1,0:T(8,128)(2,1)} fusion(bf16[2048,2048]{1,0:T(8,128)(2,1)S(1)} %bitcast.206, bf16[2048,1024]{1,0:T(8,128)(2,1)S(1)} %constant_dynamic-update-slice_fusion), kind=kOutput, calls=%fused_computation.18 | convolution fusion | flops 8592031744 | bytes 16777216 | tf_op jit(solution)/shard_map/dot_general | solution.py:59
  615.3 1.1 convert_element_type.201
  616.3 1.1 convert_element_type.202
  618.5 51.0 %shard_map.296 = f32[256,2048]{1,0:T(8,128)} custom-call(bf16[8,256,1024]{2,1,0:T(8,128)(2,1)} %bitcast.168, bf16[8,256,512]{2,1,0:T(8,128)(2,1)} %bitcast.159, bf16[2048,1536]{1,0:T(8,128)(2,1)} %get-tuple-element.65.refs_2_), custom_call_target="tpu_custom_call" | custom-call | bytes 2000000 | tf_op jit(solution)/shard_map/pallas_call | solution.py:495
  669.9 1.2 copy-done.14
  671.1 1.9 fusion.11
  674.3 3.3 add_convert_fusion.2.two
  677.7 25.0 %shard_map.297 = (f32[8,128]{1,0:T(8,128)S(1)}, bf16[2048,128]{1,0:T(8,128)(2,1)S(1)}, bf16[128,2048]{1,0:T(8,128)(2,1)S(1)}, bf16[2,256,2048]{2,1,0:T(8,128)(2,1)S(1)}, bf16[2,256,2048]{2,1,0:T(8,128)(2,1)S(1)}) custom-call(f32[32,8,128]{2,1,0:T(8,128)S(1)} %bitcast.139, bf16[4,128,512]{2,1,0:T(8,128)(2,1)S(1)} %bitcast.137, ...), custom_call_target="tpu_custom_call" | custom-call | bytes 2000000 | tf_op jit(solution)/shard_map/pallas_call | solution.py:495
  703.7 1.1 convert_element_type.197
  704.8 2.3 broadcast_multiply_fusion
  707.1 7.9 %reduce-scatter.11.cloned.1.call-done = bf16[512,1024]{1,0:T(8,128)(2,1)} async-done(((bf16[2048,1024]{1,0:T(8,128)(2,1)}), bf16[512,1024]{1,0:T(8,128)(2,1)}) %reduce-scatter.11.cloned.1.call-update) | async-done | bytes 1048592 | tf_op jit(solution)/shard_map/reduce_scatter | solution.py:1257
  716.9 1.2 copy-done.2
  718.1 14.7 %shard_map.298 = (bf16[128,1024]{1,0:T(8,128)(2,1)S(1)}, bf16[128,1024]{1,0:T(8,128)(2,1)S(1)}, bf16[128,2048]{1,0:T(8,128)(2,1)S(1)}) custom-call(bf16[4,128,1024]{2,1,0:T(8,128)(2,1)S(1)} %bitcast.136), custom_call_target="tpu_custom_call" | custom-call | bytes 2000000 | tf_op jit(solution)/shard_map/pallas_call | solution.py:495
  734.5 1.1 convert_element_type.200
  (196 shorter events, 35.3 us)
Async XLA Ops:
  7.2 225.5 %all-gather.3.cloned.1.call-start = ((), (), s32[]{:S(2)}) async-start(), calls=%async_computation.4 | async-start | bytes 2621440 | tf_op jit(solution)/shard_map/all_gather | solution.py:1186
  14.8 115.0 %copy-start.45 = (s32[2]{0:T(128)S(1)}, s32[2]{0:T(128)}, u32[]{:S(2)}) copy-start(s32[2]{0:T(128)} %param.18) | copy-start | bytes 28
  129.7 216.0 %all-gather.5.cloned.1.call-start = ((), (), s32[]{:S(2)}) async-start(), calls=%async_computation.5 | async-start | bytes 7864320 | tf_op jit(solution)/shard_map/all_gather | solution.py:1186
  152.3 341.1 %copy-start.15 = (bf16[2048,512]{1,0:T(8,128)(2,1)}, bf16[2048,512]{1,0:T(8,128)(2,1)S(1)}, u32[]{:S(2)}) copy-start(bf16[2048,512]{1,0:T(8,128)(2,1)S(1)} %slice.177) | copy-start | bytes 6291460
  154.2 5.6 copy-start.41
  154.8 7.9 %copy-start.39 = (f32[256]{0:T(256)}, f32[256]{0:T(256)S(1)}, u32[]{:S(2)}) copy-start(f32[256]{0:T(256)S(1)} %compare_convert_fusion.1) | copy-start | bytes 3076
  159.9 2.8 copy-start.31
  163.0 55.2 %copy-start.35 = (bf16[4,128,2048]{2,1,0:T(8,128)(2,1)S(1)}, bf16[4,128,2048]{2,1,0:T(8,128)(2,1)}, u32[]{:S(2)}) copy-start(bf16[4,128,2048]{2,1,0:T(8,128)(2,1)} %get-tuple-element.71) | copy-start | bytes 6291460
  219.4 292.3 %reduce-scatter.7.cloned.1.call-start = ((), (), s32[]{:S(2)}) async-start(), calls=%async_computation.7 | async-start | bytes 7864320 | tf_op jit(solution)/shard_map/reduce_scatter | solution.py:1257
  221.6 2.6 copy-start.37
  223.4 2.0 copy-start.24
  223.4 2.0 copy-start.26
  223.4 2.2 copy-start.28
  223.4 2.2 copy-start.43
  226.4 2.0 copy-start.9
  232.7 46.1 %copy-start.17 = (bf16[2,256,2048]{2,1,0:T(8,128)(2,1)S(1)}, bf16[2,256,2048]{2,1,0:T(8,128)(2,1)}, u32[]{:S(2)}) copy-start(bf16[2,256,2048]{2,1,0:T(8,128)(2,1)} %param.17) | copy-start | bytes 6291460
  281.0 1.3 copy-start.11
  382.3 210.1 %reduce-scatter.5.cloned.1.call-start = ((), (), s32[]{:S(2)}) async-start(), calls=%async_computation.6 | async-start | bytes 2621440 | tf_op jit(solution)/shard_map/reduce_scatter | solution.py:1257
  382.4 49.8 %copy-start.12 = (f32[256,2048]{1,0:T(8,128)S(1)}, f32[256,2048]{1,0:T(8,128)}, u32[]{:S(2)}) copy-start(f32[256,2048]{1,0:T(8,128)} %copy-done.11) | copy-start | bytes 6291460
  432.2 2.5 copy-start.19
  434.8 1.6 copy-start.32
  434.8 1.6 copy-start.40
  435.4 52.0 %copy-start.16 = (f32[256,2048]{1,0:T(8,128)}, f32[256,2048]{1,0:T(8,128)S(1)}, u32[]{:S(2)}) copy-start(f32[256,2048]{1,0:T(8,128)S(1)} %get-tuple-element.125) | copy-start | bytes 6291460
  436.4 1.6 copy-start
  436.4 2.3 copy-start.1
  438.6 42.0 %copy-start.10 = (f32[8,256,512]{2,1,0:T(8,128)S(1)}, f32[8,256,512]{2,1,0:T(8,128)}, u32[]{:S(2)}) copy-start(f32[8,256,512]{2,1,0:T(8,128)} %copy-done.9) | copy-start | bytes 12582916
  490.7 179.2 %reduce-scatter.9.cloned.1.call-start = ((), (), s32[]{:S(2)}) async-start(), calls=%async_computation.8 | async-start | bytes 2621440 | tf_op jit(solution)/shard_map/reduce_scatter | solution.py:1257
  490.7 2.7 copy-start.38
  493.4 1.2 copy-start.29
  497.1 3.0 copy-start.34
  497.1 8.1 %slice-start = ((s8[8388608]{0:T(1024)(128)(4,1)}), s8[4194304]{0:T(1024)(128)(4,1)S(1)}, s32[]{:S(2)}) async-start(s8[8388608]{0:T(1024)(128)(4,1)} %bitcast.201), calls=%async_computation.10 | async-start | bytes 8388608
  500.2 2.9 copy-start.25
  500.2 5.1 slice-start.1
  503.1 3.0 copy-start.21
  592.5 122.5 %reduce-scatter.11.cloned.1.call-start = ((), (), s32[]{:S(2)}) async-start(), calls=%async_computation.9 | async-start | bytes 5242880 | tf_op jit(solution)/shard_map/reduce_scatter | solution.py:1257
  593.1 3.8 copy-start.23
  593.1 10.1 %slice-start.2 = ((s8[8388608]{0:T(1024)(128)(4,1)}), s8[4194304]{0:T(1024)(128)(4,1)S(1)}, s32[]{:S(2)}) async-start(s8[8388608]{0:T(1024)(128)(4,1)} %bitcast.204), calls=%async_computation.12 | async-start | bytes 8388608
  596.9 1.9 copy-start.22
  597.5 2.6 copy-start.20
  597.7 5.6 slice-start.3
  601.2 2.0 copy-start.30
  618.5 51.1 %copy-start.13 = (f32[256,2048]{1,0:T(8,128)S(1)}, f32[256,2048]{1,0:T(8,128)}, u32[]{:S(2)}) copy-start(f32[256,2048]{1,0:T(8,128)} %copy-done.11) | copy-start | bytes 6291460
  618.5 51.1 %copy-start.36 = (f32[256,2048]{1,0:T(8,128)S(1)}, f32[256,2048]{1,0:T(8,128)}, u32[]{:S(2)}) copy-start(f32[256,2048]{1,0:T(8,128)} %get-tuple-element.87) | copy-start | bytes 6291460
  669.5 1.6 copy-start.14
  669.9 3.1 copy-start.18
  674.3 3.3 copy-start.5
  674.3 3.3 copy-start.6
  716.9 1.2 copy-start.2
  (10 other events, 8.7 us)
Sparse Core Ops, SparseCore 0:
  129.8 45.6 all-gather.2
  219.6 126.0 all-gather.4
  382.5 108.9 reduce-scatter.6
  493.6 60.3 reduce-scatter.4
  592.6 41.9 reduce-scatter.8
  636.8 78.1 reduce-scatter.10
